TPU v7x, 32 devices: a whole 2x2x4 slice. The times are simulated.
32 devices in a mesh: blk: 8 (over z, y), grp: 4 (over x, core).
Axes of the slice: x: 2, y: 2, z: 4, core: 2. Of those that a mesh axis runs over, the one named last changes fastest.
Arguments:
- points: bfloat16 [32768, 768], P(('blk', 'grp')), may hold values from -6 to 6, as said below
- counts: int32 [64], P(('blk', 'grp')), may hold values from 256 to 512, as said below
- pair_rows: int32 [512], P('blk'), may hold values from 0 to 7, as said below
- pair_cols: int32 [512], P('blk'), may hold values from 0 to 15, as said below
- pair_live: int32 [8], P('blk'), may hold values from 1 to 64, as said below
- start: float32 [64, 32768], P(None, ('blk', 'grp')), may hold values from -6 to 6
Outputs:
- embed: float32 [64, 32768], P(None, ('blk', 'grp'))
Inputs may be any that keep to these rules, and one draw needn't show every extreme that they name: Padding points are drawn like the others. `counts`: points of a block beyond its count are padding; block 0 is full. `pair_rows`: the live slots of a slab list distinct pairs. `pair_cols`: in a live slot, a value under 8 is above the slot's pair_rows; larger values, naming a block of the next slab, stand in live slots only of slabs below the last. Slots 0 to pair_live - 1 of a slab are live; slab 0 has all 64.
All inputs are finite; a program needn't handle non-finite values.
Results may differ from a plain program's by a relative error of at most 0.0042.
Values may be sent and summed in bfloat16 or wider, within the bound.
No kernel may reach another device: no remote copies, remote signals or barrier semaphores. Data moves between devices by JAX's collectives and lax.ppermute only.
A program may use at most 64 MiB of HBM per device.

v0:
```python
import functools

import jax
import jax.numpy as jnp
from jax import lax
from jax.experimental import pallas as pl
from jax.experimental.pallas import tpu as pltpu
from jax.sharding import PartitionSpec as P

PTS = 512
LOG2E = 1.4426950408889634
DEAD = 65536.0
EXTRA = 16
HOME_EARLY, HOME_LAST, FROM_SLAB, FROM_FAR, TO_OWN = range(5)
KINDS = 5
VMEM = pltpu.VMEM
SMEM = pltpu.SMEM
HIGHEST = lax.Precision.HIGHEST


def cost(flops, moved):
    return pl.CostEstimate(flops=int(flops), bytes_accessed=int(moved), transcendentals=0)


def spec(space):
    return pl.BlockSpec(memory_space=space)


def swap(value, axis, bit):
    count = lax.axis_size(axis)
    return lax.ppermute(value, axis, [(source, source ^ bit) for source in range(count)])


def from_behind(value, axis, steps):
    count = lax.axis_size(axis)
    initial, last = (max(0, -steps), min(count, count - steps))
    return lax.ppermute(value, axis, [(source, source + steps) for source in range(initial, last)])


def bits_of(count):
    bits = []
    bit = 1
    while bit < count:
        bits.append(bit)
        bit *= 2
    return bits


def gather_near(value, axis):
    held = {0: value}
    for bit in reversed(bits_of(lax.axis_size(axis))):
        for rel in list(held):
            held[rel ^ bit] = swap(held[rel], axis, bit)
    return [held[rel] for rel in range(len(held))]


def gather_far_bits(value):
    held = {0: value}
    for bit in reversed(bits_of(lax.axis_size("grp"))[1:]):
        for rel in list(held):
            held[rel ^ bit] = swap(held[rel], "grp", bit)
    held.pop(0)
    return held


def opening_kernel(start, counts, out):
    columns, total = start.shape
    for block in range(total // PTS):
        lanes = slice(block * PTS, (block + 1) * PTS)
        used = lax.broadcasted_iota(jnp.int32, (columns, PTS), 1) < counts[block]
        out[0:columns, lanes] = jnp.where(used, start[:, lanes], 0.0).astype(jnp.bfloat16)
        which = lax.broadcasted_iota(jnp.int32, (EXTRA, PTS), 0)
        place_in = lax.broadcasted_iota(jnp.int32, (EXTRA, PTS), 1)
        ones = jnp.logical_and(which == 0, place_in < counts[block])
        out[columns : columns + EXTRA, lanes] = jnp.where(ones, 1.0, 0.0).astype(jnp.bfloat16)


def opening(start, counts):
    columns, total = start.shape
    return pl.pallas_call(
        opening_kernel,
        out_shape=jax.ShapeDtypeStruct((columns + EXTRA, total), jnp.bfloat16),
        in_specs=[spec(VMEM), spec(SMEM)],
        out_specs=spec(VMEM),
        cost_estimate=cost(2**20, 2**19),
        compiler_params=pltpu.CompilerParams(vmem_limit_bytes=2 * 2**20),
        name="opening",
    )(start, counts)


def stage_of(place, group, blocks_dev):
    piece = lax.div(place, blocks_dev)
    first_half = lax.rem(place, blocks_dev) < blocks_dev // 2
    later = jnp.where(first_half, jnp.where(lax.rem(piece, 2) == 0, 0, 1), 2)
    return jnp.where(piece < min(2, group), 0, later)


def listing_kernel(
    group,
    cap,
    blocks_dev,
    rows,
    cols,
    live,
    out_rows,
    out_cols,
    out_n,
    tiles,
    sources,
    targets,
    bounds,
    owners,
):
    slab = blocks_dev * group
    slots = rows.shape[0]
    member = lax.axis_index("grp")

    def local_near(block, device):
        return (lax.div(block, blocks_dev) ^ device) * blocks_dev + lax.rem(block, blocks_dev)

    def local_far(block):
        return slab + lax.rem(block - slab, blocks_dev)

    def count_far(slot, carry):
        col = cols[slot]
        far = jnp.logical_and(slot < live[0], col >= slab)
        owner = lax.div(col - slab, blocks_dev)
        owners[slot] = jnp.where(far, owner, -1)
        return tuple(
            old + jnp.where(jnp.logical_and(far, owner == device), 1, 0)
            for device, old in enumerate(carry)
        )

    loads = lax.fori_loop(0, slots, count_far, (jnp.int32(0),) * group)

    def give(slot, loads):
        row, col = rows[slot], cols[slot]
        near = jnp.logical_and(slot < live[0], col < slab)
        best = jnp.int32(2**30)
        owner = jnp.int32(0)
        for device in range(group):
            stage = jnp.maximum(
                stage_of(local_near(row, device), group, blocks_dev),
                stage_of(local_near(col, device), group, blocks_dev),
            )
            score = loads[device] + 64 * stage + jnp.where(loads[device] < cap, 0, 2**20)
            owner = jnp.where(score < best, device, owner)
            best = jnp.minimum(score, best)

        @pl.when(near)
        def _():
            owners[slot] = owner

        return tuple(
            load + jnp.where(jnp.logical_and(near, owner == device), 1, 0)
            for device, load in enumerate(loads)
        )

    lax.fori_loop(0, slots, give, loads)

    def place_those(wanted, filled):
        def place(slot, filled):
            row, col = rows[slot], cols[slot]
            row_place = local_near(row, member)
            col_place = jnp.where(col >= slab, local_far(col), local_near(col, member))
            stage = jnp.maximum(
                stage_of(row_place, group, blocks_dev), stage_of(col_place, group, blocks_dev)
            )
            mine = jnp.logical_and(owners[slot] == member, stage == wanted)

            @pl.when(mine)
            def _():
                out_rows[filled] = row_place
                out_cols[filled] = col_place

            return filled + jnp.where(mine, 1, 0)

        return lax.fori_loop(0, slots, place, filled)

    count = jnp.int32(0)
    out_n[0] = count
    for wanted in range(3):
        count = place_those(wanted, count)
        out_n[wanted + 1] = count

    home = min(2, group) * blocks_dev
    bounds[0] = jnp.int32(0)
    filled = jnp.int32(0)
    for kind in range(KINDS):
        for to_row in (True, False):

            def enter(index, filled):
                source = (out_cols if to_row else out_rows)[index]
                target = (out_rows if to_row else out_cols)[index]
                own_target = jnp.logical_and(source >= home, target < blocks_dev)
                other_target = jnp.logical_and(source >= home, target >= blocks_dev)
                if kind == HOME_EARLY:
                    wanted = jnp.logical_and(source < home, index < out_n[2])
                elif kind == HOME_LAST:
                    wanted = jnp.logical_and(source < home, index >= out_n[2])
                elif kind == FROM_SLAB:
                    wanted = jnp.logical_and(other_target, source < slab)
                elif kind == FROM_FAR:
                    wanted = jnp.logical_and(other_target, source >= slab)
                else:
                    wanted = own_target

                @pl.when(wanted)
                def _():
                    tiles[filled] = index
                    sources[filled] = source
                    targets[filled] = target

                return filled + jnp.where(wanted, 1, 0)

            filled = lax.fori_loop(0, count, enter, filled)
            bounds[2 * kind + (1 if to_row else 2)] = filled


def listing(rows, cols, live, group, cap, blocks_dev):
    return pl.pallas_call(
        functools.partial(listing_kernel, group, cap, blocks_dev),
        out_shape=(
            jax.ShapeDtypeStruct((cap,), jnp.int32),
            jax.ShapeDtypeStruct((cap,), jnp.int32),
            jax.ShapeDtypeStruct((4,), jnp.int32),
            jax.ShapeDtypeStruct((2 * cap,), jnp.int32),
            jax.ShapeDtypeStruct((2 * cap,), jnp.int32),
            jax.ShapeDtypeStruct((2 * cap,), jnp.int32),
            jax.ShapeDtypeStruct((2 * KINDS + 1,), jnp.int32),
        ),
        in_specs=[spec(SMEM)] * 3,
        out_specs=(spec(SMEM),) * 7,
        scratch_shapes=[SMEM((rows.shape[0],), jnp.int32)],
        cost_estimate=cost(2**20, 2**10),
        compiler_params=pltpu.CompilerParams(vmem_limit_bytes=2**20),
        name="listing",
    )(rows, cols, live)


def set_levels(place, window, level_row, level_col, scale):
    block = window[place * PTS : (place + 1) * PTS, :]
    width = block.shape[1]
    part = jnp.zeros((PTS, 128), jnp.float32)
    for lane in range(0, width, 128):
        wide = block[:, lane : lane + 128].astype(jnp.float32)
        part = part + wide * wide
    level_row[place] = scale * lax.dot_general(
        jnp.ones((8, 128), jnp.float32),
        part,
        (((1,), (1,)), ((), ())),
        precision=HIGHEST,
        preferred_element_type=jnp.float32,
    )
    if place < level_col.shape[0]:
        total = jnp.sum(part, axis=1, keepdims=True) * scale
        level_col[place] = jnp.broadcast_to(total, (PTS, 128))


def make_tiles(low, high, rows, cols, window, level_row, level_col, kept, buffers):
    width = window.shape[1]
    scale = 6.0 / width * LOG2E
    count = high - low
    spare = kept.shape[0] - 1

    def cross(tile, buffer):
        index = low + jnp.minimum(tile, count - 1)
        left = window[pl.ds(pl.multiple_of(rows[index] * PTS, PTS), PTS), :]
        right = window[pl.ds(pl.multiple_of(cols[index] * PTS, PTS), PTS), :]
        buffer[...] = lax.dot_general(
            left, right, (((1,), (1,)), ((), ())), preferred_element_type=jnp.float32
        )

    def finish(tile, buffer):
        valid = jnp.logical_and(tile >= 0, tile < count)
        index = low + jnp.clip(tile, 0, count - 1)
        row, col = rows[index], cols[index]
        right_level = level_row[col][0:1, :]
        left_level = jnp.concatenate([level_col[row]] * (PTS // 128), axis=1)
        value = jnp.exp2(buffer[...] * scale - left_level - right_level)
        kept[jnp.where(valid, index, spare)] = value.astype(jnp.bfloat16)

    def body(pair, carry):
        cross(2 * pair, buffers[0])
        finish(2 * pair - 1, buffers[1])
        cross(2 * pair + 1, buffers[1])
        finish(2 * pair, buffers[0])
        return carry

    @pl.when(count > 0)
    def _():
        buffers[1][...] = jnp.zeros((PTS, PTS), jnp.float32)

    lax.fori_loop(0, jnp.where(count > 0, lax.div(count, 2) + 1, 0), body, 0)


def build_tiles(stage, fresh, n, rows, cols, state, group, blocks_dev, cap, name):
    places = list(fresh)
    pts = list(fresh.values())
    width = pts[0].shape[1]
    total = (group + 1) * blocks_dev
    near = group * blocks_dev
    shapes = [
        jax.ShapeDtypeStruct((total * PTS, width), jnp.bfloat16),
        jax.ShapeDtypeStruct((total, 8, PTS), jnp.float32),
        jax.ShapeDtypeStruct((near, PTS, 128), jnp.float32),
    ]
    makes = stage is not None
    if makes:
        shapes.append(jax.ShapeDtypeStruct((cap + 1, PTS, PTS), jnp.bfloat16))
    state = state[: len(shapes)]
    scalars = (n, rows, cols) if makes else ()
    first = len(scalars) + len(pts)

    def kernel(*refs):
        pt_refs = refs[len(scalars) : first]
        window, level_row, level_col, *rest = refs[first + len(state) :]
        for place, piece in zip(places, pt_refs):
            blocks = piece.shape[0] // PTS
            window[place * PTS : (place + blocks) * PTS, :] = piece[...]
            for block in range(place, place + blocks):
                set_levels(block, window, level_row, level_col, 3.0 / width * LOG2E)
        if makes:
            n_ref, row_ref, col_ref = refs[:3]
            kept, *buffers = rest
            make_tiles(
                n_ref[stage],
                n_ref[stage + 1],
                row_ref,
                col_ref,
                window,
                level_row,
                level_col,
                kept,
                buffers,
            )

    return pl.pallas_call(
        kernel,
        out_shape=shapes,
        in_specs=[spec(SMEM)] * len(scalars) + [spec(VMEM)] * (len(pts) + len(state)),
        out_specs=[spec(VMEM)] * len(shapes),
        input_output_aliases={first + index: index for index in range(len(state))},
        scratch_shapes=[VMEM((PTS, PTS), jnp.float32)] * (2 if makes else 0),
        cost_estimate=cost(2**32 if stage == 2 else 2**20, 2**20),
        compiler_params=pltpu.CompilerParams(vmem_limit_bytes=6 * 2**20),
        name=name,
    )(*scalars, *pts, *state)


def products(entries, kinds, vecs, tiles, start, targets, height, folds):
    firsts = sorted(vecs)
    tall, held = vecs[firsts[0]].shape
    blocks_dev = held // PTS
    begun = list(start)
    source_low, source_high = firsts[0], firsts[-1] + blocks_dev
    low = min(first for ranges in targets for first, _ in ranges)
    high = max(last for ranges in targets for _, last in ranges)
    shapes = [
        jax.ShapeDtypeStruct((sum(last - first for first, last in ranges), height, PTS), jnp.float32)
        for ranges in targets
    ]

    def pieces(refs):
        for ranges, ref in zip(targets, refs):
            at = 0
            for first, last in ranges:
                yield ref, slice(at, at + last - first), slice(first - low, last - low)
                at += last - first

    def fold(value):
        out = value[:height]
        for index in range(1, folds):
            out = out + value[index * height : (index + 1) * height]
        return out

    def kernel(*refs):
        tile_ref, source_ref, target_ref, bounds = refs[:4]
        vec_refs = refs[4 : 4 + len(firsts)]
        kept = refs[4 + len(firsts)]
        start_refs = refs[5 + len(firsts) : 5 + len(firsts) + len(begun)]
        outs = refs[5 + len(firsts) + len(begun) : -2]
        u_win, acc = refs[-2:]
        for first, ref in zip(firsts, vec_refs):
            for block in range(blocks_dev):
                lanes = slice(block * PTS, (block + 1) * PTS)
                u_win[first - source_low + block] = ref[:, lanes]
        if begun:
            for ref, inside, places in pieces(start_refs):
                acc[places] = ref[inside]
        else:
            for place in range(high - low + 1):
                acc[place] = jnp.zeros((height, PTS), jnp.float32)

        spare = high - low
        unroll = 4

        def several(begin, end, transposed):
            def body(step, carry):
                done = []
                for lane in range(unroll):
                    index = begin + step * unroll + lane
                    valid = index < end
                    index = jnp.minimum(index, end - 1)
                    vec = u_win[source_ref[index] - source_low]
                    tile = kept[tile_ref[index]]
                    if transposed:
                        value = lax.dot_general(
                            vec,
                            tile,
                            (((1,), (1,)), ((), ())),
                            preferred_element_type=jnp.float32,
                        )
                    else:
                        value = jnp.dot(vec, tile, preferred_element_type=jnp.float32)
                    done.append((jnp.where(valid, target_ref[index] - low, spare), fold(value)))
                for target, value in done:
                    acc[target] += value
                return carry

            lax.fori_loop(0, lax.div(end - begin + unroll - 1, unroll), body, 0)

        for kind in kinds:
            several(bounds[2 * kind], bounds[2 * kind + 1], True)
            several(bounds[2 * kind + 1], bounds[2 * kind + 2], False)
        for out, inside, places in pieces(outs):
            out[inside] = acc[places]

    call = pl.pallas_call(
        kernel,
        out_shape=shapes,
        in_specs=[spec(SMEM)] * 4 + [spec(VMEM)] * (len(firsts) + 1 + len(begun)),
        out_specs=[spec(VMEM)] * len(shapes),
        scratch_shapes=[
            VMEM((source_high - source_low, tall, PTS), jnp.bfloat16),
            VMEM((high - low + 1, height, PTS), jnp.float32),
        ],
        cost_estimate=cost(2**31 if FROM_FAR in kinds else 2**20, 2**20),
        compiler_params=pltpu.CompilerParams(vmem_limit_bytes=10 * 2**20),
        name="products",
    )
    return list(call(*entries, *[vecs[first] for first in firsts], tiles, *begun))


def urgent_ranges(group, blocks_dev):
    messages = [
        [rel for rel in range(group) if rel & bit and rel % bit == 0] for bit in bits_of(group)
    ]
    return [
        [(rel * blocks_dev, (rel + 1) * blocks_dev) for rel in rels]
        for rels in messages + [[group]]
    ]


def send_urgent(results, later, group, blocks_dev):
    final = []
    *messages, far = results
    parts = {}
    behind = None
    for bit, message in zip(bits_of(group), messages):
        rels = [rel for rel in range(group) if rel & bit and rel % bit == 0]
        for index, rel in enumerate(rels):
            if rel in parts:
                held = message[index * blocks_dev : (index + 1) * blocks_dev]
                message = held + parts[rel] if len(rels) == 1 else message.at[
                    index * blocks_dev : (index + 1) * blocks_dev
                ].add(parts[rel])
        if bit > 1:
            message, *later = lax.optimization_barrier((message, *later))
        got = swap(message, "grp", bit)
        if behind is None:
            got, far = lax.optimization_barrier((got, far))
            behind = from_behind(far, "blk", 1)
        final.append(got)
        for index, rel in enumerate(rels):
            if rel ^ bit:
                piece = got[index * blocks_dev : (index + 1) * blocks_dev]
                parts[rel ^ bit] = parts[rel ^ bit] + piece if rel ^ bit in parts else piece
    if behind is None:
        behind = from_behind(far, "blk", 1)
    return [behind] + final, later


def finish_home(entries, vecs, tiles, start, blocks_dev, height, folds):
    return products(entries, (TO_OWN,), vecs, tiles, [start], [[(0, blocks_dev)]], height, folds)


def scaled_gram(parts, own, counts, degree, earlier):
    columns = own.shape[0] if degree is not None else own.shape[0] - EXTRA
    total = own.shape[1]
    first = degree is None
    shapes = [
        jax.ShapeDtypeStruct((columns, total), jnp.float32),
        jax.ShapeDtypeStruct((columns, columns * (1 if first else 2)), jnp.float32),
    ]
    if first:
        shapes.append(jax.ShapeDtypeStruct((2 * columns, total), jnp.bfloat16))
        shapes.append(jax.ShapeDtypeStruct((8, total), jnp.float32))
    operands = list(parts) + [own]
    operands += [] if first else [degree, earlier]

    def kernel(count_ref, *refs):
        ins = list(refs[: len(operands)])
        outs = list(refs[len(operands) :])
        part_refs = ins[: len(parts)]
        own_ref = ins[len(parts)]
        z_out, gram_out = outs[:2]
        gram = jnp.zeros((columns, columns), jnp.float32)
        for block in range(total // PTS):
            lanes = slice(block * PTS, (block + 1) * PTS)
            sums = part_refs[0][block]
            for part in part_refs[1:]:
                sums = sums + part[block]
            if first:
                level = 1.0 + sums[columns : columns + 1, :]
                outs[-1][:, lanes] = jnp.broadcast_to(level, (8, PTS))
            else:
                level = ins[len(parts) + 1][0:1, lanes]
            used = lax.broadcasted_iota(jnp.int32, (columns, PTS), 1) < count_ref[block]
            held = own_ref[0:columns, lanes].astype(jnp.float32)
            z = (held + jnp.where(used, sums[0:columns], 0.0)) / level
            z_out[:, lanes] = z
            if first:
                high = z.astype(jnp.bfloat16)
                outs[2][0:columns, lanes] = high
                rest = z - high.astype(jnp.float32)
                outs[2][columns : 2 * columns, lanes] = rest.astype(jnp.bfloat16)
            gram = gram + lax.dot_general(
                z, z, (((1,), (1,)), ((), ())), precision=HIGHEST, preferred_element_type=jnp.float32
            )
        if not first:
            gram = jnp.concatenate([ins[-1][...], gram], axis=1)
        gram_out[...] = gram

    return pl.pallas_call(
        kernel,
        out_shape=tuple(shapes),
        in_specs=[spec(SMEM)] + [spec(VMEM)] * len(operands),
        out_specs=(spec(VMEM),) * len(shapes),
        cost_estimate=cost(2**26, 2**21),
        compiler_params=pltpu.CompilerParams(vmem_limit_bytes=6 * 2**20),
        name="scaled_gram",
    )(counts, *operands)


def inverse_factor(gram):
    size = gram.shape[0]
    row_id = lax.broadcasted_iota(jnp.int32, (size, size), 0)
    col_id = lax.broadcasted_iota(jnp.int32, (size, size), 1)
    eye = jnp.where(row_id == col_id, 1.0, 0.0)
    whole = jnp.concatenate([gram, eye], axis=1)
    wide = 2 * size
    count = size // 8
    groups = [whole[8 * g : 8 * g + 8, :] for g in range(count)]
    within = lax.broadcasted_iota(jnp.int32, (8, wide), 0)

    def spread_row(value, row):
        return jnp.broadcast_to(value[row : row + 1, :], (8, wide))

    results = []
    for g in range(count):
        spread = [
            [
                jnp.broadcast_to(groups[other][:, 8 * g + k : 8 * g + k + 1], (8, wide))
                for other in range(g, count)
            ]
            for k in range(8)
        ]
        pivots = jnp.ones((8, wide), jnp.float32)
        for j in range(8):
            column = spread[j]
            pivot = spread_row(column[0], j)
            pivots = jnp.where(within == j, pivot, pivots)
            over = 1.0 / pivot
            below = jnp.where(within > j, column[0], 0.0)
            for k in range(j + 1, 8):
                share = spread_row(column[0], k) * over
                spread[k][0] = spread[k][0] - below * share
                for other in range(1, count - g):
                    spread[k][other] = spread[k][other] - column[other] * share
            top = spread_row(groups[g], j) * over
            groups[g] = groups[g] - below * top
            for other in range(1, count - g):
                groups[g + other] = groups[g + other] - column[other] * top
        results.append(groups[g] * lax.rsqrt(pivots))
    return jnp.concatenate(results, axis=0)[:, size:wide]


def exact_dot(left, right, contract):
    return lax.dot_general(
        left,
        right,
        (contract, ((), ())),
        precision=HIGHEST,
        preferred_element_type=jnp.float32,
    )


def factors_kernel(grams, both_out, first_out, sound_out):
    columns = grams.shape[0]
    plain = ((1,), (0,))
    turned = ((1,), (1,))
    second = grams[:, columns : 2 * columns]
    first_inverse = inverse_factor(grams[:, 0:columns])
    middle = exact_dot(exact_dot(first_inverse, second, plain), first_inverse, turned)
    both = exact_dot(inverse_factor(middle), first_inverse, plain)
    both_out[...] = both
    first_out[...] = first_inverse
    row_id = lax.broadcasted_iota(jnp.int32, (columns, columns), 0)
    col_id = lax.broadcasted_iota(jnp.int32, (columns, columns), 1)
    trace = jnp.sum(jnp.where(row_id == col_id, second, 0.0))
    spread = jnp.sum(both * both) * trace / (columns * columns)
    sound_out[0] = jnp.where(spread < 64.0, 1, 0)


def factors(grams):
    columns = grams.shape[0]
    square = jax.ShapeDtypeStruct((columns, columns), jnp.float32)
    return pl.pallas_call(
        factors_kernel,
        out_shape=(square, square, jax.ShapeDtypeStruct((1,), jnp.int32)),
        in_specs=[spec(VMEM)],
        out_specs=(spec(VMEM), spec(VMEM), spec(SMEM)),
        cost_estimate=cost(2**30, 2**16),
        compiler_params=pltpu.CompilerParams(vmem_limit_bytes=2 * 2**20),
        name="factors",
    )(grams)


def apply_kernel(factor, z, out, *gram):
    value = exact_dot(factor[...], z[...], ((1,), (0,)))
    out[...] = value
    if gram:
        gram[0][...] = exact_dot(value, value, ((1,), (1,)))


def applied(factor, z, with_gram):
    shapes = [jax.ShapeDtypeStruct(z.shape, jnp.float32)]
    if with_gram:
        shapes.append(jax.ShapeDtypeStruct(factor.shape, jnp.float32))
    return pl.pallas_call(
        apply_kernel,
        out_shape=shapes,
        in_specs=[spec(VMEM)] * 2,
        out_specs=[spec(VMEM)] * len(shapes),
        compiler_params=pltpu.CompilerParams(vmem_limit_bytes=4 * 2**20),
        name="applied",
    )(factor, z)


def second_kernel(gram, first, out):
    out[...] = exact_dot(inverse_factor(gram[...]), first[...], ((1,), (0,)))


def second_factor(gram, first):
    return pl.pallas_call(
        second_kernel,
        out_shape=jax.ShapeDtypeStruct(gram.shape, jnp.float32),
        in_specs=[spec(VMEM)] * 2,
        out_specs=spec(VMEM),
        compiler_params=pltpu.CompilerParams(vmem_limit_bytes=2 * 2**20),
        name="second_factor",
    )(gram, first)


def sum_stages():
    return bits_of(lax.axis_size("blk") * lax.axis_size("grp"))


def pairs_of(bits):
    return [bits[first : first + 2] for first in range(0, len(bits), 2)]


def all_sum(value, stages, beside=None):
    count = lax.axis_size("blk") * lax.axis_size("grp")
    for bits in stages:
        moves = [0]
        for bit in bits if isinstance(bits, list) else [bits]:
            moves += [move ^ bit for move in moves]
        terms = [value] + [
            lax.ppermute(value, ("blk", "grp"), [(source, source ^ move) for source in range(count)])
            for move in moves[1:]
        ]
        if beside is not None:
            terms[0], beside = lax.optimization_barrier((terms[0], beside))
        while len(terms) > 1:
            terms = [left + right for left, right in zip(terms[::2], terms[1::2])]
        value = terms[0]
    return value if beside is None else (value, beside)


def per_device(points, counts, pair_rows, pair_cols, pair_live, start):
    group = lax.axis_size("grp")
    blocks_dev = counts.shape[0]
    columns = start.shape[0]
    slots = pair_rows.shape[0]
    cap = max(-(-slots // group), blocks_dev * blocks_dev * group)
    half = (blocks_dev // 2) * PTS

    home = min(2, group) * blocks_dev

    rows, cols, n, *entries = listing(
        pair_rows, pair_cols, pair_live, group, cap, blocks_dev
    )
    mate = swap(points, "grp", 1)
    chunks = [points[:half], points[half:]]
    far = [from_behind(chunk, "blk", -1) for chunk in chunks]
    crossed = [gather_far_bits(chunk) for chunk in chunks]
    begin, mate = lax.optimization_barrier((start, mate))
    vec = opening(begin, counts)
    tied = lax.optimization_barrier((vec, n, rows, cols, far[0], *crossed[0].values()))
    vec, n, rows, cols, far[0] = tied[:5]
    crossed[0] = dict(zip(crossed[0], tied[5:]))
    cross_vec = gather_far_bits(vec)
    far_vec = from_behind(vec, "blk", -1)
    mate_vec = swap(vec, "grp", 1)

    def direct(index):
        offset = index * (blocks_dev // 2)
        found = {group * blocks_dev + offset: far[index]}
        for rel, value in crossed[index].items():
            found[rel * blocks_dev + offset] = value
        return found

    def passed_on(index):
        offset = index * (blocks_dev // 2)
        found = {}
        for rel, value in crossed[index].items():
            cut = value.shape[0] // (1 if index else 2)
            parts = [swap(value[at : at + cut], "grp", 1) for at in range(0, value.shape[0], cut)]
            found[(rel ^ 1) * blocks_dev + offset] = jnp.concatenate(parts, 0)
        return found

    def build(stage, fresh, state, name):
        return list(
            build_tiles(stage, fresh, n, rows, cols, state, group, blocks_dev, cap, name)
        )

    state = build(0, {0: points, blocks_dev: mate, **direct(0)}, (), "first_tiles")
    state = build(1, passed_on(0), state, "second_tiles")
    urgent = urgent_ranges(group, blocks_dev)
    ranges = [[(0, blocks_dev)]] + urgent
    height = columns + 8
    vecs_home = {0: vec, blocks_dev: mate_vec}
    begun = products(entries, (HOME_EARLY,), vecs_home, state[3], (), ranges, height, 1)
    tied = lax.optimization_barrier((far[1], begun[0], state[1], *crossed[1].values()))
    far[1], begun[0], state[1] = tied[:3]
    crossed[1] = dict(zip(crossed[1], tied[3:]))
    last = passed_on(1)
    *grown, kept = state
    state = build(None, direct(1), grown, "more_blocks") + [kept]
    state = build(2, last, state, "last_tiles")
    kept = state[-1]
    tied = lax.optimization_barrier((kept, *cross_vec.values()))
    kept = tied[0]
    cross_vec = dict(zip(cross_vec, tied[1:]))

    def window_of(own, mate, crossed, far):
        found = {0: own, blocks_dev: mate, group * blocks_dev: far}
        for rel, value in crossed.items():
            found[rel * blocks_dev] = value
            found[(rel ^ 1) * blocks_dev] = swap(value, "grp", 1)
        return found

    def beyond(vecs):
        return {place: value for place, value in vecs.items() if place >= home}

    vecs = window_of(vec, mate_vec, cross_vec, far_vec)
    at_home, *results = products(
        entries, (HOME_LAST,), vecs_home, kept, begun, ranges, height, 1
    )
    results = products(
        entries, (FROM_SLAB, FROM_FAR), beyond(vecs), kept, results, urgent, height, 1
    )
    sums, (at_home,) = send_urgent(results, (at_home,), group, blocks_dev)
    sums = finish_home(entries, beyond(vecs), kept, at_home, blocks_dev, height, 1) + sums
    z, gram, parts, degree = scaled_gram(sums, vec, counts, None, None)

    far_part = from_behind(parts, "blk", -1)
    crossed = gather_far_bits(parts)
    mate_part = swap(parts, "grp", 1)
    at_home, *results = products(
        entries,
        (HOME_EARLY, HOME_LAST),
        {0: parts, blocks_dev: mate_part},
        kept,
        (),
        ranges,
        columns,
        2,
    )
    at_home, *tied = lax.optimization_barrier((at_home, *crossed.values()))
    crossed = dict(zip(crossed, tied))
    vecs = beyond(window_of(parts, mate_part, crossed, far_part))
    results = products(
        entries, (FROM_SLAB, FROM_FAR), vecs, kept, results, urgent, columns, 2
    )
    sums, (at_home,) = send_urgent(results, (at_home,), group, blocks_dev)
    sums = finish_home(entries, vecs, kept, at_home, blocks_dev, columns, 2) + sums
    z, grams = scaled_gram(sums, z, counts, degree, gram)

    stages = sum_stages()
    stages = stages[:1] + pairs_of(stages[1:])
    both, first, sound = factors(all_sum(grams, stages))

    def at_once(both, first, z):
        return both

    def in_two(both, first, z):
        return second_factor(all_sum(applied(first, z, True)[1], stages), first)

    return applied(lax.cond(sound[0] == 1, at_once, in_two, both, first, z), z, False)[0]


def solution(mesh):
    in_specs = (
        P(("blk", "grp"), None),
        P(("blk", "grp")),
        P("blk"),
        P("blk"),
        P("blk"),
        P(None, ("blk", "grp")),
    )
    out_specs = P(None, ("blk", "grp"))
    return jax.shard_map(
        per_device, mesh=mesh, in_specs=in_specs, out_specs=out_specs, check_vma=False
    )
```

profile of v0, /device:TPU:0, one launch (start us, length us, event | category | flops | bytes accessed | tf_op | source)
XLA Modules:
  0.0 129.2 jit_solution(18052787520455681226)
XLA Ops:
  0.0 0.5 collective-permute-start.7
  0.5 1.5 %fusion = (bf16[512,768]{1,0:T(8,128)(2,1)S(1)}, bf16[512,768]{1,0:T(8,128)(2,1)S(1)}) fusion(bf16[1024,768]{1,0:T(8,128)(2,1)} %refs_3_.1), kind=kLoop, calls=%fused_computation.7 | loop fusion | bytes 3145728 | tf_op jit(solution)/shard_map/slice | solution.py:706
  2.1 1.3 %collective-permute-start.8 = (bf16[512,768]{1,0:T(8,128)(2,1)S(1)}, bf16[512,768]{1,0:T(8,128)(2,1)S(1)}, u32[]{:S(2)}, u32[]{:S(2)}) collective-permute-start(bf16[512,768]{1,0:T(8,128)(2,1)S(1)} %get-tuple-element.157), channel_id=1, source_target_pairs={{4,0},{8,4},{12,8},{16,12},{20,16},{24,20},{28,24},{5,1},{9,5},{13... | collective-permute-start | bytes 2359304 | tf_op jit(solution)/shard_map/ppermute | solution.py:37
  3.4 2.7 %collective-permute-start.9 = (bf16[512,768]{1,0:T(8,128)(2,1)S(1)}, bf16[512,768]{1,0:T(8,128)(2,1)S(1)}, u32[]{:S(2)}, u32[]{:S(2)}) collective-permute-start(bf16[512,768]{1,0:T(8,128)(2,1)S(1)} %get-tuple-element.157), channel_id=1, source_target_pairs={{0,2},{1,3},{2,0},{3,1},{4,6},{5,7},{6,4},{7,5},{8,10},{9,11},{10,... | collective-permute-start | bytes 2359304 | tf_op jit(solution)/shard_map/ppermute | solution.py:31
  6.0 1.3 collective-permute-start.10
  7.3 0.1 collective-permute-start.14
  8.1 15.1 %listing.1 = (s32[16]{0:T(128)S(1)}, s32[16]{0:T(128)S(1)}, s32[4]{0:T(128)S(1)}, s32[32]{0:T(128)S(1)}, s32[32]{0:T(128)S(1)}, /*index=5*/s32[32]{0:T(128)S(1)}, s32[11]{0:T(128)S(1)}) custom-call(s32[64]{0:T(128)S(1)} %copy-done.3, s32[64]{0:T(128)S(1)} %copy-done.4, s32[1]{0:T(128)S(6)} %copy.31.live), custom_call_target="tpu_custom_call" | custom-call | flops 1048576 | bytes 1024 | tf_op jit(solution)/shard_map/listing/pallas_call | solution.py:221
  23.2 0.6 opening.1.refs_4_
  23.8 1.2 collective-permute-done.8.refs_5_
  25.0 0.1 fusion.1
  25.0 0.1 collective-permute-start.12
  25.1 0.5 collective-permute-start.13
  25.6 0.1 collective-permute-start.11
  25.7 6.8 %first_tiles.1 = (bf16[5120,768]{1,0:T(8,128)(2,1)S(1)}, f32[10,8,512]{2,1,0:T(8,128)S(1)}, f32[8,512,128]{2,1,0:T(8,128)S(1)}, bf16[17,512,512]{2,1,0:T(8,128)(2,1)S(1)}) custom-call(s32[4]{0:T(128)S(1)} %get-tuple-element.94.refs_0_, s32[16]{0:T(128)S(1)} %get-tuple-element.95.refs_1_, s32[16]{0:T(128)S(1)} %get-tuple-element.96.refs_2_, ...), custom_call_target="tpu_custom_call" | custom-call | flops 1048576 | bytes 1048576 | tf_op jit(solution)/shard_map/first_tiles/pallas_call | solution.py:338
  32.5 0.0 collective-permute-done.13
  32.5 0.1 pad_maximum_fusion.refs_3_
  32.6 2.1 %second_tiles.1 = (bf16[5120,768]{1,0:T(8,128)(2,1)S(1)}, f32[10,8,512]{2,1,0:T(8,128)S(1)}, f32[8,512,128]{2,1,0:T(8,128)S(1)}, bf16[17,512,512]{2,1,0:T(8,128)(2,1)S(1)}) custom-call(s32[4]{0:T(128)S(1)} %get-tuple-element.94.refs_0_, s32[16]{0:T(128)S(1)} %get-tuple-element.95.refs_1_, ...), custom_call_target="tpu_custom_call", output_to_operand_aliasing={{0}: (4, {}), {1}: (5, {}), {2}: (6, {}), {3}: (7, {})} | custom-call | flops 1048576 | bytes 1048576 | tf_op jit(solution)/shard_map/second_tiles/pallas_call | solution.py:338
  34.7 0.0 collective-permute-done.11.refs_5_
  34.7 2.5 %products.7 = (f32[2,72,512]{2,1,0:T(8,128)S(1)}, f32[4,72,512]{2,1,0:T(8,128)S(1)}, f32[2,72,512]{2,1,0:T(8,128)S(1)}, f32[2,72,512]{2,1,0:T(8,128)S(1)}) custom-call(s32[32]{0:T(128)S(1)} %get-tuple-element.86.refs_0_, s32[32]{0:T(128)S(1)} %get-tuple-element.87.refs_1_, s32[32]{0:T(128)S(1)} %get-tuple-element.88.refs_2_, ...), custom_call_target="tpu_custom_call" | custom-call | flops 1048576 | bytes 1048576 | tf_op jit(solution)/shard_map/products/pallas_call | solution.py:442
  37.3 4.3 %collective-permute-done.10.refs_0_ = bf16[512,768]{1,0:T(8,128)(2,1)S(1)} collective-permute-done((bf16[512,768]{1,0:T(8,128)(2,1)S(1)}, bf16[512,768]{1,0:T(8,128)(2,1)S(1)}, u32[]{:S(2)}, u32[]{:S(2)}) %collective-permute-start.10) | collective-permute-done | bytes 786464 | tf_op jit(solution)/shard_map/ppermute | solution.py:37
  41.5 0.0 collective-permute-done.14.refs_1_
  41.5 0.0 collective-permute-start.15
  41.5 1.7 %collective-permute-start.16 = (bf16[80,1024]{1,0:T(8,128)(2,1)S(1)}, bf16[80,1024]{1,0:T(8,128)(2,1)S(1)}, u32[]{:S(2)}, u32[]{:S(2)}) collective-permute-start(bf16[80,1024]{1,0:T(8,128)(2,1)S(1)} %opening.1.refs_4_), channel_id=1, source_target_pairs={{0,2},{1,3},{2,0},{3,1},{4,6},{5,7},{6,4},{7,5},{8,10},{9,11},{10,... | collective-permute-start | bytes 491528 | tf_op jit(solution)/shard_map/ppermute | solution.py:31
  43.2 1.3 collective-permute-start.18
  44.5 0.8 more_blocks.1
  45.3 6.5 %last_tiles.1 = (bf16[5120,768]{1,0:T(8,128)(2,1)S(1)}, f32[10,8,512]{2,1,0:T(8,128)S(1)}, f32[8,512,128]{2,1,0:T(8,128)S(1)}, bf16[17,512,512]{2,1,0:T(8,128)(2,1)S(1)}) custom-call(s32[4]{0:T(128)S(1)} %get-tuple-element.94.refs_0_, s32[16]{0:T(128)S(1)} %get-tuple-element.95.refs_1_, ...), custom_call_target="tpu_custom_call", output_to_operand_aliasing={{0}: (4, {}), {1}: (5, {}), {2}: (6, {}), {3}: (7, {})} | custom-call | flops 4294967296 | bytes 1048576 | tf_op jit(solution)/shard_map/last_tiles/pallas_call | solution.py:338
  51.8 0.1 collective-permute-start.17
  51.8 1.3 products.8
  53.1 0.1 collective-permute-done.17.refs_5_
  53.2 4.8 %products.9 = (f32[4,72,512]{2,1,0:T(8,128)S(1)}, f32[2,72,512]{2,1,0:T(8,128)S(1)}, f32[2,72,512]{2,1,0:T(8,128)S(1)}) custom-call(s32[32]{0:T(128)S(1)} %get-tuple-element.86.refs_0_, s32[32]{0:T(128)S(1)} %get-tuple-element.87.refs_1_, s32[32]{0:T(128)S(1)} %get-tuple-element.88.refs_2_, s32[11]{0:T(128)S(1)} %get-tuple-element.89.refs_3_, ...), custom_call_target="tpu_custom_call" | custom-call | flops 2147483648 | bytes 1048576 | tf_op jit(solution)/shard_map/products/pallas_call | solution.py:442
  58.0 0.5 collective-permute-start.19
  58.5 1.6 %collective-permute-done.19.refs_2_ = f32[4,72,512]{2,1,0:T(8,128)S(1)} collective-permute-done((f32[4,72,512]{2,1,0:T(8,128)S(1)}, f32[4,72,512]{2,1,0:T(8,128)S(1)}, u32[]{:S(2)}, u32[]{:S(2)}) %collective-permute-start.19) | collective-permute-done | bytes 589856 | tf_op jit(solution)/shard_map/ppermute | solution.py:31
  60.2 1.3 %collective-permute-start.21 = (f32[2,72,512]{2,1,0:T(8,128)S(1)}, f32[2,72,512]{2,1,0:T(8,128)S(1)}, u32[]{:S(2)}, u32[]{:S(2)}) collective-permute-start(f32[2,72,512]{2,1,0:T(8,128)S(1)} %slice_add_fusion), channel_id=1, source_target_pairs={{0,2},{1,3},{2,0},{3,1},{4,6},{5,7},{6,4},{7,5},{8,10},{9,11},{10,... | collective-permute-start | bytes 884744 | tf_op jit(solution)/shard_map/ppermute | solution.py:31
  61.5 1.3 %collective-permute-start.20 = (f32[2,72,512]{2,1,0:T(8,128)S(1)}, f32[2,72,512]{2,1,0:T(8,128)S(1)}, u32[]{:S(2)}, u32[]{:S(2)}) collective-permute-start(f32[2,72,512]{2,1,0:T(8,128)S(1)} %get-tuple-element.132), channel_id=1, source_target_pairs={{0,4},{4,8},{8,12},{12,16},{16,20},{20,24},{24,28},{1,5},{5,9},{9,... | collective-permute-start | bytes 884744 | tf_op jit(solution)/shard_map/ppermute | solution.py:37
  62.8 1.6 %products.10.refs_0_ = f32[2,72,512]{2,1,0:T(8,128)S(1)} custom-call(s32[32]{0:T(128)S(1)} %get-tuple-element.86.refs_0_, s32[32]{0:T(128)S(1)} %get-tuple-element.87.refs_1_, s32[32]{0:T(128)S(1)} %get-tuple-element.88.refs_2_, s32[11]{0:T(128)S(1)} %get-tuple-element.89.refs_3_, bf16[80,1024]{1,0:T(8,128)(2,1)S(1)} %collective-permute-done.16.refs_4_, ...), custom_call_target="tpu_custom_call" | custom-call | flops 1048576 | bytes 1048576 | tf_op jit(solution)/shard_map/products/pallas_call | solution.py:442
  64.4 5.1 %collective-permute-done.21.refs_3_ = f32[2,72,512]{2,1,0:T(8,128)S(1)} collective-permute-done((f32[2,72,512]{2,1,0:T(8,128)S(1)}, f32[2,72,512]{2,1,0:T(8,128)S(1)}, u32[]{:S(2)}, u32[]{:S(2)}) %collective-permute-start.21) | collective-permute-done | bytes 294944 | tf_op jit(solution)/shard_map/ppermute | solution.py:31
  69.6 1.0 scaled_gram.2
  70.5 0.1 collective-permute-start.22
  70.6 1.3 %collective-permute-start.23 = (bf16[128,1024]{1,0:T(8,128)(2,1)S(1)}, bf16[128,1024]{1,0:T(8,128)(2,1)S(1)}, u32[]{:S(2)}, u32[]{:S(2)}) collective-permute-start(bf16[128,1024]{1,0:T(8,128)(2,1)S(1)} %get-tuple-element.134.refs_4_), channel_id=1, source_target_pairs={{0,2},{1,3},{2,0},{3,1},{4,6},{5,7},{6,4},{7,5},{8,10},{9,11},{10,... | collective-permute-start | bytes 786440 | tf_op jit(solution)/shard_map/ppermute | solution.py:31
  71.9 1.3 collective-permute-start.25
  73.2 3.0 %products.11 = (f32[2,64,512]{2,1,0:T(8,128)S(1)}, f32[4,64,512]{2,1,0:T(8,128)S(1)}, f32[2,64,512]{2,1,0:T(8,128)S(1)}, f32[2,64,512]{2,1,0:T(8,128)S(1)}) custom-call(s32[32]{0:T(128)S(1)} %get-tuple-element.86.refs_0_, s32[32]{0:T(128)S(1)} %get-tuple-element.87.refs_1_, s32[32]{0:T(128)S(1)} %get-tuple-element.88.refs_2_, ...), custom_call_target="tpu_custom_call" | custom-call | flops 1048576 | bytes 1048576 | tf_op jit(solution)/shard_map/products/pallas_call | solution.py:442
  76.2 3.1 %collective-permute-done.23.refs_4_ = bf16[128,1024]{1,0:T(8,128)(2,1)S(1)} collective-permute-done((bf16[128,1024]{1,0:T(8,128)(2,1)S(1)}, bf16[128,1024]{1,0:T(8,128)(2,1)S(1)}, u32[]{:S(2)}, u32[]{:S(2)}) %collective-permute-start.23) | collective-permute-done | bytes 262176 | tf_op jit(solution)/shard_map/ppermute | solution.py:31
  79.3 3.6 %collective-permute-done.25.refs_6_ = bf16[128,1024]{1,0:T(8,128)(2,1)S(1)} collective-permute-done((bf16[128,1024]{1,0:T(8,128)(2,1)S(1)}, bf16[128,1024]{1,0:T(8,128)(2,1)S(1)}, u32[]{:S(2)}, u32[]{:S(2)}) %collective-permute-start.25) | collective-permute-done | bytes 262176 | tf_op jit(solution)/shard_map/ppermute | solution.py:37
  82.9 4.9 %products.12 = (f32[4,64,512]{2,1,0:T(8,128)S(1)}, f32[2,64,512]{2,1,0:T(8,128)S(1)}, f32[2,64,512]{2,1,0:T(8,128)S(1)}) custom-call(s32[32]{0:T(128)S(1)} %get-tuple-element.86.refs_0_, s32[32]{0:T(128)S(1)} %get-tuple-element.87.refs_1_, s32[32]{0:T(128)S(1)} %get-tuple-element.88.refs_2_, s32[11]{0:T(128)S(1)} %get-tuple-element.89.refs_3_, ...), custom_call_target="tpu_custom_call" | custom-call | flops 2147483648 | bytes 1048576 | tf_op jit(solution)/shard_map/products/pallas_call | solution.py:442
  87.9 0.1 collective-permute-start.26
  88.0 1.9 %collective-permute-done.26.refs_2_ = f32[4,64,512]{2,1,0:T(8,128)S(1)} collective-permute-done((f32[4,64,512]{2,1,0:T(8,128)S(1)}, f32[4,64,512]{2,1,0:T(8,128)S(1)}, u32[]{:S(2)}, u32[]{:S(2)}) %collective-permute-start.26) | collective-permute-done | bytes 524320 | tf_op jit(solution)/shard_map/ppermute | solution.py:31
  89.9 0.1 collective-permute-start.28
  90.0 4.3 %collective-permute-start.27 = (f32[2,64,512]{2,1,0:T(8,128)S(1)}, f32[2,64,512]{2,1,0:T(8,128)S(1)}, u32[]{:S(2)}, u32[]{:S(2)}) collective-permute-start(f32[2,64,512]{2,1,0:T(8,128)S(1)} %get-tuple-element.146), channel_id=1, source_target_pairs={{0,4},{4,8},{8,12},{12,16},{16,20},{20,24},{24,28},{1,5},{5,9},{9,... | collective-permute-start | bytes 786440 | tf_op jit(solution)/shard_map/ppermute | solution.py:37
  94.3 1.5 %products.13.refs_0_ = f32[2,64,512]{2,1,0:T(8,128)S(1)} custom-call(s32[32]{0:T(128)S(1)} %get-tuple-element.86.refs_0_, s32[32]{0:T(128)S(1)} %get-tuple-element.87.refs_1_, s32[32]{0:T(128)S(1)} %get-tuple-element.88.refs_2_, s32[11]{0:T(128)S(1)} %get-tuple-element.89.refs_3_, bf16[128,1024]{1,0:T(8,128)(2,1)S(1)} %collective-permute-done.23.refs_4_, ...), custom_call_target="tpu_custom_call" | custom-call | flops 1048576 | bytes 1048576 | tf_op jit(solution)/shard_map/products/pallas_call | solution.py:442
  95.8 2.6 %collective-permute-done.28.refs_3_ = f32[2,64,512]{2,1,0:T(8,128)S(1)} collective-permute-done((f32[2,64,512]{2,1,0:T(8,128)S(1)}, f32[2,64,512]{2,1,0:T(8,128)S(1)}, u32[]{:S(2)}, u32[]{:S(2)}) %collective-permute-start.28) | collective-permute-done | bytes 262176 | tf_op jit(solution)/shard_map/ppermute | solution.py:31
  98.3 1.8 %collective-permute-done.27.refs_1_ = f32[2,64,512]{2,1,0:T(8,128)S(1)} collective-permute-done((f32[2,64,512]{2,1,0:T(8,128)S(1)}, f32[2,64,512]{2,1,0:T(8,128)S(1)}, u32[]{:S(2)}, u32[]{:S(2)}) %collective-permute-start.27) | collective-permute-done | bytes 262176 | tf_op jit(solution)/shard_map/ppermute | solution.py:37
  100.1 1.0 scaled_gram.3
  101.1 0.1 collective-permute-start.29
  101.2 1.2 collective-permute-done.29
  102.4 1.7 %collective-permute-start.30 = (f32[64,128]{1,0:T(8,128)S(1)}, f32[64,128]{1,0:T(8,128)S(1)}, u32[]{:S(2)}, u32[]{:S(2)}) collective-permute-start(f32[64,128]{1,0:T(8,128)S(1)} %add.50), channel_id=1, source_target_pairs={{0,2},{1,3},{2,0},{3,1},{4,6},{5,7},{6,4},{7,5},{8,10},{9,11},{10,... | collective-permute-start | bytes 98312 | tf_op jit(solution)/shard_map/ppermute | solution.py:681
  104.1 2.5 %collective-permute-start.31 = (f32[64,128]{1,0:T(8,128)S(1)}, f32[64,128]{1,0:T(8,128)S(1)}, u32[]{:S(2)}, u32[]{:S(2)}) collective-permute-start(f32[64,128]{1,0:T(8,128)S(1)} %add.50), channel_id=1, source_target_pairs={{0,4},{1,5},{2,6},{3,7},{4,0},{5,1},{6,2},{7,3},{8,12},{9,13},{10,... | collective-permute-start | bytes 98312 | tf_op jit(solution)/shard_map/ppermute | solution.py:681
  106.6 1.9 %collective-permute-done.31 = f32[64,128]{1,0:T(8,128)S(1)} collective-permute-done((f32[64,128]{1,0:T(8,128)S(1)}, f32[64,128]{1,0:T(8,128)S(1)}, u32[]{:S(2)}, u32[]{:S(2)}) %collective-permute-start.31) | collective-permute-done | bytes 32800 | tf_op jit(solution)/shard_map/ppermute | solution.py:681
  108.5 2.9 %collective-permute-done.32 = f32[64,128]{1,0:T(8,128)S(1)} collective-permute-done((f32[64,128]{1,0:T(8,128)S(1)}, f32[64,128]{1,0:T(8,128)S(1)}, u32[]{:S(2)}, u32[]{:S(2)}) %collective-permute-start.32) | collective-permute-done | bytes 32800 | tf_op jit(solution)/shard_map/ppermute | solution.py:681
  111.4 5.3 %collective-permute-start.33 = (f32[64,128]{1,0:T(8,128)S(1)}, f32[64,128]{1,0:T(8,128)S(1)}, u32[]{:S(2)}, u32[]{:S(2)}) collective-permute-start(f32[64,128]{1,0:T(8,128)S(1)} %add_add_fusion.3), channel_id=1, source_target_pairs={{0,8},{1,9},{2,10},{3,11},{4,12},{5,13},{6,14},{7,15},{8,0},{9,1},... | collective-permute-start | bytes 98312 | tf_op jit(solution)/shard_map/ppermute | solution.py:681
  116.8 2.4 %collective-permute-start.35 = (f32[64,128]{1,0:T(8,128)S(1)}, f32[64,128]{1,0:T(8,128)S(1)}, u32[]{:S(2)}, u32[]{:S(2)}) collective-permute-start(f32[64,128]{1,0:T(8,128)S(1)} %add_add_fusion.3), channel_id=1, source_target_pairs={{0,24},{1,25},{2,26},{3,27},{4,28},{5,29},{6,30},{7,31},{8,16},{9,... | collective-permute-start | bytes 98312 | tf_op jit(solution)/shard_map/ppermute | solution.py:681
  119.2 2.4 %collective-permute-done.34 = f32[64,128]{1,0:T(8,128)S(1)} collective-permute-done((f32[64,128]{1,0:T(8,128)S(1)}, f32[64,128]{1,0:T(8,128)S(1)}, u32[]{:S(2)}, u32[]{:S(2)}) %collective-permute-start.34) | collective-permute-done | bytes 32800 | tf_op jit(solution)/shard_map/ppermute | solution.py:681
  121.6 0.9 collective-permute-done.35
  122.5 4.9 %factors.1 = (f32[64,64]{1,0:T(8,128)S(1)}, f32[64,64]{1,0:T(8,128)S(1)}, s32[1]{0:T(128)}) custom-call(f32[64,128]{1,0:T(8,128)S(1)} %add_add_fusion.2.grams), custom_call_target="tpu_custom_call" | custom-call | flops 1073741824 | bytes 65536 | tf_op jit(solution)/shard_map/factors/pallas_call | solution.py:619
  128.1 1.1 applied.3
  (30 shorter events, 0.2 us)
Async XLA Ops:
  0.0 25.7 %copy-start = (bf16[1024,768]{1,0:T(8,128)(2,1)S(1)}, bf16[1024,768]{1,0:T(8,128)(2,1)}, u32[]{:S(2)}) copy-start(bf16[1024,768]{1,0:T(8,128)(2,1)} %refs_3_.1) | copy-start | bytes 4718596
  0.0 8.1 %copy-start.3 = (s32[64]{0:T(128)S(1)}, s32[64]{0:T(128)}, u32[]{:S(2)}) copy-start(s32[64]{0:T(128)} %rows.1) | copy-start | bytes 772
  0.0 8.1 %copy-start.4 = (s32[64]{0:T(128)S(1)}, s32[64]{0:T(128)}, u32[]{:S(2)}) copy-start(s32[64]{0:T(128)} %cols.1) | copy-start | bytes 772
  0.0 23.2 %copy-start.1 = (f32[64,1024]{1,0:T(8,128)S(1)}, f32[64,1024]{1,0:T(8,128)}, u32[]{:S(2)}) copy-start(f32[64,1024]{1,0:T(8,128)} %start) | copy-start | bytes 786436
  0.0 23.2 %copy-start.2 = (s32[2]{0:T(128)S(1)}, s32[2]{0:T(128)}, u32[]{:S(2)}) copy-start(s32[2]{0:T(128)} %count_ref.3) | copy-start | bytes 28
  0.0 23.2 %collective-permute-start.7 = (bf16[1024,768]{1,0:T(8,128)(2,1)}, bf16[1024,768]{1,0:T(8,128)(2,1)S(1)}, u32[]{:S(2)}, u32[]{:S(2)}) collective-permute-start(bf16[1024,768]{1,0:T(8,128)(2,1)} %refs_3_.1), channel_id=1, source_target_pairs={{0,1},{1,0},{2,3},{3,2},{4,5},{5,4},{6,7},{7,6},{8,9},{9,8},{10,11... | collective-permute-start | bytes 4718600 | tf_op jit(solution)/shard_map/ppermute | solution.py:31
  2.1 22.9 %collective-permute-start.8 = (bf16[512,768]{1,0:T(8,128)(2,1)S(1)}, bf16[512,768]{1,0:T(8,128)(2,1)S(1)}, u32[]{:S(2)}, u32[]{:S(2)}) collective-permute-start(bf16[512,768]{1,0:T(8,128)(2,1)S(1)} %get-tuple-element.157), channel_id=1, source_target_pairs={{4,0},{8,4},{12,8},{16,12},{20,16},{24,20},{28,24},{5,1},{9,5},{13... | collective-permute-start | bytes 2359304 | tf_op jit(solution)/shard_map/ppermute | solution.py:37
  3.4 21.6 %collective-permute-start.9 = (bf16[512,768]{1,0:T(8,128)(2,1)S(1)}, bf16[512,768]{1,0:T(8,128)(2,1)S(1)}, u32[]{:S(2)}, u32[]{:S(2)}) collective-permute-start(bf16[512,768]{1,0:T(8,128)(2,1)S(1)} %get-tuple-element.157), channel_id=1, source_target_pairs={{0,2},{1,3},{2,0},{3,1},{4,6},{5,7},{6,4},{7,5},{8,10},{9,11},{10,... | collective-permute-start | bytes 2359304 | tf_op jit(solution)/shard_map/ppermute | solution.py:31
  6.0 35.5 %collective-permute-start.10 = (bf16[512,768]{1,0:T(8,128)(2,1)S(1)}, bf16[512,768]{1,0:T(8,128)(2,1)S(1)}, u32[]{:S(2)}, u32[]{:S(2)}) collective-permute-start(bf16[512,768]{1,0:T(8,128)(2,1)S(1)} %get-tuple-element.156), channel_id=1, source_target_pairs={{4,0},{8,4},{12,8},{16,12},{20,16},{24,20},{28,24},{5,1},{9,5},{13... | collective-permute-start | bytes 2359304 | tf_op jit(solution)/shard_map/ppermute | solution.py:37
  7.3 34.2 %collective-permute-start.14 = (bf16[512,768]{1,0:T(8,128)(2,1)S(1)}, bf16[512,768]{1,0:T(8,128)(2,1)S(1)}, u32[]{:S(2)}, u32[]{:S(2)}) collective-permute-start(bf16[512,768]{1,0:T(8,128)(2,1)S(1)} %get-tuple-element.156), channel_id=1, source_target_pairs={{0,2},{1,3},{2,0},{3,1},{4,6},{5,7},{6,4},{7,5},{8,10},{9,11},{10,... | collective-permute-start | bytes 2359304 | tf_op jit(solution)/shard_map/ppermute | solution.py:31
  25.0 7.5 %collective-permute-start.12 = (bf16[256,768]{1,0:T(8,128)(2,1)S(1)}, bf16[256,768]{1,0:T(8,128)(2,1)S(1)}, u32[]{:S(2)}, u32[]{:S(2)}) collective-permute-start(bf16[256,768]{1,0:T(8,128)(2,1)S(1)} %get-tuple-element.158), channel_id=1, source_target_pairs={{0,1},{1,0},{2,3},{3,2},{4,5},{5,4},{6,7},{7,6},{8,9},{9,8},{10,11... | collective-permute-start | bytes 1179656 | tf_op jit(solution)/shard_map/ppermute | solution.py:31
  25.1 7.4 %collective-permute-start.13 = (bf16[256,768]{1,0:T(8,128)(2,1)S(1)}, bf16[256,768]{1,0:T(8,128)(2,1)S(1)}, u32[]{:S(2)}, u32[]{:S(2)}) collective-permute-start(bf16[256,768]{1,0:T(8,128)(2,1)S(1)} %get-tuple-element.159), channel_id=1, source_target_pairs={{0,1},{1,0},{2,3},{3,2},{4,5},{5,4},{6,7},{7,6},{8,9},{9,8},{10,11... | collective-permute-start | bytes 1179656 | tf_op jit(solution)/shard_map/ppermute | solution.py:31
  25.6 9.1 %collective-permute-start.11 = (bf16[80,1024]{1,0:T(8,128)(2,1)S(1)}, bf16[80,1024]{1,0:T(8,128)(2,1)S(1)}, u32[]{:S(2)}, u32[]{:S(2)}) collective-permute-start(bf16[80,1024]{1,0:T(8,128)(2,1)S(1)} %opening.1.refs_4_), channel_id=1, source_target_pairs={{0,1},{1,0},{2,3},{3,2},{4,5},{5,4},{6,7},{7,6},{8,9},{9,8},{10,11... | collective-permute-start | bytes 491528 | tf_op jit(solution)/shard_map/ppermute | solution.py:31
  41.5 3.8 %collective-permute-start.15 = (bf16[512,768]{1,0:T(8,128)(2,1)S(1)}, bf16[512,768]{1,0:T(8,128)(2,1)S(1)}, u32[]{:S(2)}, u32[]{:S(2)}) collective-permute-start(bf16[512,768]{1,0:T(8,128)(2,1)S(1)} %collective-permute-done.14.refs_1_), channel_id=1, source_target_pairs={{0,1},{1,0},{2,3},{3,2},{4,5},{5,4},{6,7},{7,6},{8,9},{9,8},{10,11... | collective-permute-start | bytes 2359304 | tf_op jit(solution)/shard_map/ppermute | solution.py:31
  41.5 10.2 %collective-permute-start.16 = (bf16[80,1024]{1,0:T(8,128)(2,1)S(1)}, bf16[80,1024]{1,0:T(8,128)(2,1)S(1)}, u32[]{:S(2)}, u32[]{:S(2)}) collective-permute-start(bf16[80,1024]{1,0:T(8,128)(2,1)S(1)} %opening.1.refs_4_), channel_id=1, source_target_pairs={{0,2},{1,3},{2,0},{3,1},{4,6},{5,7},{6,4},{7,5},{8,10},{9,11},{10,... | collective-permute-start | bytes 491528 | tf_op jit(solution)/shard_map/ppermute | solution.py:31
  43.2 9.9 %collective-permute-start.18 = (bf16[80,1024]{1,0:T(8,128)(2,1)S(1)}, bf16[80,1024]{1,0:T(8,128)(2,1)S(1)}, u32[]{:S(2)}, u32[]{:S(2)}) collective-permute-start(bf16[80,1024]{1,0:T(8,128)(2,1)S(1)} %opening.1.refs_4_), channel_id=1, source_target_pairs={{4,0},{8,4},{12,8},{16,12},{20,16},{24,20},{28,24},{5,1},{9,5},{13... | collective-permute-start | bytes 491528 | tf_op jit(solution)/shard_map/ppermute | solution.py:37
  51.8 1.5 %collective-permute-start.17 = (bf16[80,1024]{1,0:T(8,128)(2,1)S(1)}, bf16[80,1024]{1,0:T(8,128)(2,1)S(1)}, u32[]{:S(2)}, u32[]{:S(2)}) collective-permute-start(bf16[80,1024]{1,0:T(8,128)(2,1)S(1)} %collective-permute-done.16.refs_4_), channel_id=1, source_target_pairs={{0,1},{1,0},{2,3},{3,2},{4,5},{5,4},{6,7},{7,6},{8,9},{9,8},{10,11... | collective-permute-start | bytes 491528 | tf_op jit(solution)/shard_map/ppermute | solution.py:31
  58.0 2.1 %collective-permute-start.19 = (f32[4,72,512]{2,1,0:T(8,128)S(1)}, f32[4,72,512]{2,1,0:T(8,128)S(1)}, u32[]{:S(2)}, u32[]{:S(2)}) collective-permute-start(f32[4,72,512]{2,1,0:T(8,128)S(1)} %get-tuple-element.127), channel_id=1, source_target_pairs={{0,1},{1,0},{2,3},{3,2},{4,5},{5,4},{6,7},{7,6},{8,9},{9,8},{10,11... | collective-permute-start | bytes 1769480 | tf_op jit(solution)/shard_map/ppermute | solution.py:31
  60.2 9.4 %collective-permute-start.21 = (f32[2,72,512]{2,1,0:T(8,128)S(1)}, f32[2,72,512]{2,1,0:T(8,128)S(1)}, u32[]{:S(2)}, u32[]{:S(2)}) collective-permute-start(f32[2,72,512]{2,1,0:T(8,128)S(1)} %slice_add_fusion), channel_id=1, source_target_pairs={{0,2},{1,3},{2,0},{3,1},{4,6},{5,7},{6,4},{7,5},{8,10},{9,11},{10,... | collective-permute-start | bytes 884744 | tf_op jit(solution)/shard_map/ppermute | solution.py:31
  61.5 8.0 %collective-permute-start.20 = (f32[2,72,512]{2,1,0:T(8,128)S(1)}, f32[2,72,512]{2,1,0:T(8,128)S(1)}, u32[]{:S(2)}, u32[]{:S(2)}) collective-permute-start(f32[2,72,512]{2,1,0:T(8,128)S(1)} %get-tuple-element.132), channel_id=1, source_target_pairs={{0,4},{4,8},{8,12},{12,16},{16,20},{20,24},{24,28},{1,5},{5,9},{9,... | collective-permute-start | bytes 884744 | tf_op jit(solution)/shard_map/ppermute | solution.py:37
  70.5 2.7 %collective-permute-start.22 = (bf16[128,1024]{1,0:T(8,128)(2,1)S(1)}, bf16[128,1024]{1,0:T(8,128)(2,1)S(1)}, u32[]{:S(2)}, u32[]{:S(2)}) collective-permute-start(bf16[128,1024]{1,0:T(8,128)(2,1)S(1)} %get-tuple-element.134.refs_4_), channel_id=1, source_target_pairs={{0,1},{1,0},{2,3},{3,2},{4,5},{5,4},{6,7},{7,6},{8,9},{9,8},{10,11... | collective-permute-start | bytes 786440 | tf_op jit(solution)/shard_map/ppermute | solution.py:31
  70.6 8.7 %collective-permute-start.23 = (bf16[128,1024]{1,0:T(8,128)(2,1)S(1)}, bf16[128,1024]{1,0:T(8,128)(2,1)S(1)}, u32[]{:S(2)}, u32[]{:S(2)}) collective-permute-start(bf16[128,1024]{1,0:T(8,128)(2,1)S(1)} %get-tuple-element.134.refs_4_), channel_id=1, source_target_pairs={{0,2},{1,3},{2,0},{3,1},{4,6},{5,7},{6,4},{7,5},{8,10},{9,11},{10,... | collective-permute-start | bytes 786440 | tf_op jit(solution)/shard_map/ppermute | solution.py:31
  71.9 11.0 %collective-permute-start.25 = (bf16[128,1024]{1,0:T(8,128)(2,1)S(1)}, bf16[128,1024]{1,0:T(8,128)(2,1)S(1)}, u32[]{:S(2)}, u32[]{:S(2)}) collective-permute-start(bf16[128,1024]{1,0:T(8,128)(2,1)S(1)} %get-tuple-element.134.refs_4_), channel_id=1, source_target_pairs={{4,0},{8,4},{12,8},{16,12},{20,16},{24,20},{28,24},{5,1},{9,5},{13... | collective-permute-start | bytes 786440 | tf_op jit(solution)/shard_map/ppermute | solution.py:37
  79.3 3.6 %collective-permute-start.24 = (bf16[128,1024]{1,0:T(8,128)(2,1)S(1)}, bf16[128,1024]{1,0:T(8,128)(2,1)S(1)}, u32[]{:S(2)}, u32[]{:S(2)}) collective-permute-start(bf16[128,1024]{1,0:T(8,128)(2,1)S(1)} %collective-permute-done.23.refs_4_), channel_id=1, source_target_pairs={{0,1},{1,0},{2,3},{3,2},{4,5},{5,4},{6,7},{7,6},{8,9},{9,8},{10,11... | collective-permute-start | bytes 786440 | tf_op jit(solution)/shard_map/ppermute | solution.py:31
  87.9 2.0 %collective-permute-start.26 = (f32[4,64,512]{2,1,0:T(8,128)S(1)}, f32[4,64,512]{2,1,0:T(8,128)S(1)}, u32[]{:S(2)}, u32[]{:S(2)}) collective-permute-start(f32[4,64,512]{2,1,0:T(8,128)S(1)} %get-tuple-element.141), channel_id=1, source_target_pairs={{0,1},{1,0},{2,3},{3,2},{4,5},{5,4},{6,7},{7,6},{8,9},{9,8},{10,11... | collective-permute-start | bytes 1572872 | tf_op jit(solution)/shard_map/ppermute | solution.py:31
  89.9 8.4 %collective-permute-start.28 = (f32[2,64,512]{2,1,0:T(8,128)S(1)}, f32[2,64,512]{2,1,0:T(8,128)S(1)}, u32[]{:S(2)}, u32[]{:S(2)}) collective-permute-start(f32[2,64,512]{2,1,0:T(8,128)S(1)} %slice_add_fusion.1), channel_id=1, source_target_pairs={{0,2},{1,3},{2,0},{3,1},{4,6},{5,7},{6,4},{7,5},{8,10},{9,11},{10,... | collective-permute-start | bytes 786440 | tf_op jit(solution)/shard_map/ppermute | solution.py:31
  90.0 10.1 %collective-permute-start.27 = (f32[2,64,512]{2,1,0:T(8,128)S(1)}, f32[2,64,512]{2,1,0:T(8,128)S(1)}, u32[]{:S(2)}, u32[]{:S(2)}) collective-permute-start(f32[2,64,512]{2,1,0:T(8,128)S(1)} %get-tuple-element.146), channel_id=1, source_target_pairs={{0,4},{4,8},{8,12},{12,16},{16,20},{20,24},{24,28},{1,5},{5,9},{9,... | collective-permute-start | bytes 786440 | tf_op jit(solution)/shard_map/ppermute | solution.py:37
  101.1 1.3 collective-permute-start.29
  102.4 4.2 %collective-permute-start.30 = (f32[64,128]{1,0:T(8,128)S(1)}, f32[64,128]{1,0:T(8,128)S(1)}, u32[]{:S(2)}, u32[]{:S(2)}) collective-permute-start(f32[64,128]{1,0:T(8,128)S(1)} %add.50), channel_id=1, source_target_pairs={{0,2},{1,3},{2,0},{3,1},{4,6},{5,7},{6,4},{7,5},{8,10},{9,11},{10,... | collective-permute-start | bytes 98312 | tf_op jit(solution)/shard_map/ppermute | solution.py:681
  104.1 4.4 %collective-permute-start.31 = (f32[64,128]{1,0:T(8,128)S(1)}, f32[64,128]{1,0:T(8,128)S(1)}, u32[]{:S(2)}, u32[]{:S(2)}) collective-permute-start(f32[64,128]{1,0:T(8,128)S(1)} %add.50), channel_id=1, source_target_pairs={{0,4},{1,5},{2,6},{3,7},{4,0},{5,1},{6,2},{7,3},{8,12},{9,13},{10,... | collective-permute-start | bytes 98312 | tf_op jit(solution)/shard_map/ppermute | solution.py:681
  106.6 4.8 %collective-permute-start.32 = (f32[64,128]{1,0:T(8,128)S(1)}, f32[64,128]{1,0:T(8,128)S(1)}, u32[]{:S(2)}, u32[]{:S(2)}) collective-permute-start(f32[64,128]{1,0:T(8,128)S(1)} %add.50), channel_id=1, source_target_pairs={{0,6},{1,7},{2,4},{3,5},{4,2},{5,3},{6,0},{7,1},{8,14},{9,15},{10,... | collective-permute-start | bytes 98312 | tf_op jit(solution)/shard_map/ppermute | solution.py:681
  111.4 7.8 %collective-permute-start.33 = (f32[64,128]{1,0:T(8,128)S(1)}, f32[64,128]{1,0:T(8,128)S(1)}, u32[]{:S(2)}, u32[]{:S(2)}) collective-permute-start(f32[64,128]{1,0:T(8,128)S(1)} %add_add_fusion.3), channel_id=1, source_target_pairs={{0,8},{1,9},{2,10},{3,11},{4,12},{5,13},{6,14},{7,15},{8,0},{9,1},... | collective-permute-start | bytes 98312 | tf_op jit(solution)/shard_map/ppermute | solution.py:681
  116.8 4.8 %collective-permute-start.34 = (f32[64,128]{1,0:T(8,128)S(1)}, f32[64,128]{1,0:T(8,128)S(1)}, u32[]{:S(2)}, u32[]{:S(2)}) collective-permute-start(f32[64,128]{1,0:T(8,128)S(1)} %add_add_fusion.3), channel_id=1, source_target_pairs={{0,16},{1,17},{2,18},{3,19},{4,20},{5,21},{6,22},{7,23},{8,24},{9,... | collective-permute-start | bytes 98312 | tf_op jit(solution)/shard_map/ppermute | solution.py:681
  116.8 5.7 %collective-permute-start.35 = (f32[64,128]{1,0:T(8,128)S(1)}, f32[64,128]{1,0:T(8,128)S(1)}, u32[]{:S(2)}, u32[]{:S(2)}) collective-permute-start(f32[64,128]{1,0:T(8,128)S(1)} %add_add_fusion.3), channel_id=1, source_target_pairs={{0,24},{1,25},{2,26},{3,27},{4,28},{5,29},{6,30},{7,31},{8,16},{9,... | collective-permute-start | bytes 98312 | tf_op jit(solution)/shard_map/ppermute | solution.py:681
where the time goes:
time: 129 us
  Pallas kernels  59.4 us (46%)
  waiting for transfers between devices  34.5 us (27%)
  starting transfers between devices  31.9 us (25%)
  between operations  1.65 us (1%)
  local copies, waits for them, and re-layouts  1.57 us (1%)
    pallas_call x7, Pallas kernels, products(): call(*entries, *[vecs[first] for first in firsts], tiles, *begun)  19.6 us
    pallas_call x4, Pallas kernels, build_tiles(): pl.pallas_call(kernel, out_shape=shapes, in_specs=[spec(SMEM)] * len(scal...  16.2 us
    pallas_call x1, Pallas kernels, listing(): pl.pallas_call(functools.partial(listing_kernel, group, cap, blocks_dev),...  15.1 us
    ppermute x16, waiting for transfers between devices, swap(): lax.ppermute(value, axis, [(source, source ^ bit) for source in range(cou...  14.4 us
    ppermute x7, starting transfers between devices, all_sum(): lax.ppermute(value, ('blk', 'grp'), [(source, source ^ move) for source i...  12.1 us
    ppermute x6, waiting for transfers between devices, from_behind(): lax.ppermute(value, axis, [(source, source + steps) for source in range(i...  10.8 us
    ppermute x6, starting transfers between devices, from_behind(): lax.ppermute(value, axis, [(source, source + steps) for source in range(i...  10.7 us
    ppermute x7, waiting for transfers between devices, all_sum(): lax.ppermute(value, ('blk', 'grp'), [(source, source ^ move) for source i...  9.28 us
  transfers between devices with their start and end apart: 29, of which 15 were waited for; matrix products, arithmetic and copies ran while one was open for 1% of the time, Pallas kernels for 32%

commit v1 on v0

--- a/solution.py
+++ b/solution.py
@@ -11,8 +11,8 @@
 LOG2E = 1.4426950408889634
 DEAD = 65536.0
 EXTRA = 16
-HOME_EARLY, HOME_LAST, FROM_SLAB, FROM_FAR, TO_OWN = range(5)
-KINDS = 5
+HOME_EARLY, HOME_LAST, TO_OTHERS, TO_OWN = range(4)
+KINDS = 4
 VMEM = pltpu.VMEM
 SMEM = pltpu.SMEM
 HIGHEST = lax.Precision.HIGHEST
@@ -198,10 +198,8 @@
                     wanted = jnp.logical_and(source < home, index < out_n[2])
                 elif kind == HOME_LAST:
                     wanted = jnp.logical_and(source < home, index >= out_n[2])
-                elif kind == FROM_SLAB:
-                    wanted = jnp.logical_and(other_target, source < slab)
-                elif kind == FROM_FAR:
-                    wanted = jnp.logical_and(other_target, source >= slab)
+                elif kind == TO_OTHERS:
+                    wanted = other_target
                 else:
                     wanted = own_target
 
@@ -435,7 +433,7 @@
             VMEM((source_high - source_low, tall, PTS), jnp.bfloat16),
             VMEM((high - low + 1, height, PTS), jnp.float32),
         ],
-        cost_estimate=cost(2**31 if FROM_FAR in kinds else 2**20, 2**20),
+        cost_estimate=cost(2**31 if TO_OTHERS in kinds else 2**20, 2**20),
         compiler_params=pltpu.CompilerParams(vmem_limit_bytes=10 * 2**20),
         name="products",
     )
@@ -769,9 +767,7 @@
     at_home, *results = products(
         entries, (HOME_LAST,), vecs_home, kept, begun, ranges, height, 1
     )
-    results = products(
-        entries, (FROM_SLAB, FROM_FAR), beyond(vecs), kept, results, urgent, height, 1
-    )
+    results = products(entries, (TO_OTHERS,), beyond(vecs), kept, results, urgent, height, 1)
     sums, (at_home,) = send_urgent(results, (at_home,), group, blocks_dev)
     sums = finish_home(entries, beyond(vecs), kept, at_home, blocks_dev, height, 1) + sums
     z, gram, parts, degree = scaled_gram(sums, vec, counts, None, None)
@@ -792,9 +788,7 @@
     at_home, *tied = lax.optimization_barrier((at_home, *crossed.values()))
     crossed = dict(zip(crossed, tied))
     vecs = beyond(window_of(parts, mate_part, crossed, far_part))
-    results = products(
-        entries, (FROM_SLAB, FROM_FAR), vecs, kept, results, urgent, columns, 2
-    )
+    results = products(entries, (TO_OTHERS,), vecs, kept, results, urgent, columns, 2)
     sums, (at_home,) = send_urgent(results, (at_home,), group, blocks_dev)
     sums = finish_home(entries, vecs, kept, at_home, blocks_dev, columns, 2) + sums
     z, grams = scaled_gram(sums, z, counts, degree, gram)

time: 129 us -> 126 us (0.977); the launches traced: 129 us -> 124 us
  starting transfers between devices: 31.9 us -> 28.4 us
  Pallas kernels: 59.4 us -> 57.4 us
    ppermute x16, waiting for transfers between devices: 14.4 us -> 16.6 us  [swap(): lax.ppermute(value, axis, [(source, source ^ bit) for source in range(cou...]
    pallas_call x7, Pallas kernels: 19.6 us -> 18 us  [products(): call(*entries, *[vecs[first] for first in firsts], tiles, *begun)]
    ppermute x6, waiting for transfers between devices: 10.8 us -> 9.45 us  [from_behind(): lax.ppermute(value, axis, [(source, source + steps) for source in range(i...]
    ppermute x7, starting transfers between devices: 12.1 us -> 10.8 us  [all_sum(): lax.ppermute(value, ('blk', 'grp'), [(source, source ^ move) for source i...]
    ppermute x6, starting transfers between devices: 10.7 us -> 9.41 us  [from_behind(): lax.ppermute(value, axis, [(source, source + steps) for source in range(i...]
  transfers between devices with their start and end apart: 29 -> 29, of which waited for: 15 -> 14; matrix products, arithmetic and copies ran while one was open for 1% -> 1% of each run, Pallas kernels for 32% -> 33%
where the time goes in v1:
time: 126 us; the launch traced here: 124 us
  Pallas kernels  57.4 us (46%)
  waiting for transfers between devices  35.1 us (28%)
  starting transfers between devices  28.4 us (23%)
  between operations  1.64 us (1%)
  local copies, waits for them, and re-layouts  1.57 us (1%)
    pallas_call x7, Pallas kernels, products(): call(*entries, *[vecs[first] for first in firsts], tiles, *begun)  18 us
    ppermute x16, waiting for transfers between devices, swap(): lax.ppermute(value, axis, [(source, source ^ bit) for source in range(cou...  16.6 us
    pallas_call x4, Pallas kernels, build_tiles(): pl.pallas_call(kernel, out_shape=shapes, in_specs=[spec(SMEM)] * len(scal...  16.2 us
    pallas_call x1, Pallas kernels, listing(): pl.pallas_call(functools.partial(listing_kernel, group, cap, blocks_dev),...  14.7 us
    ppermute x7, starting transfers between devices, all_sum(): lax.ppermute(value, ('blk', 'grp'), [(source, source ^ move) for source i...  10.8 us
    ppermute x6, waiting for transfers between devices, from_behind(): lax.ppermute(value, axis, [(source, source + steps) for source in range(i...  9.45 us
    ppermute x6, starting transfers between devices, from_behind(): lax.ppermute(value, axis, [(source, source + steps) for source in range(i...  9.41 us
    ppermute x7, waiting for transfers between devices, all_sum(): lax.ppermute(value, ('blk', 'grp'), [(source, source ^ move) for source i...  9.07 us
  transfers between devices with their start and end apart: 29, of which 14 were waited for; matrix products, arithmetic and copies ran while one was open for 1% of the time, Pallas kernels for 33%

profile of v1, /device:TPU:0, one launch (start us, length us, event | category | flops | bytes accessed | tf_op | source)
XLA Modules:
  0.0 124.2 jit_solution(6218303518252207207)
XLA Ops:
  0.0 0.5 collective-permute-start.7
  0.5 1.5 %fusion = (bf16[512,768]{1,0:T(8,128)(2,1)S(1)}, bf16[512,768]{1,0:T(8,128)(2,1)S(1)}) fusion(bf16[1024,768]{1,0:T(8,128)(2,1)} %refs_3_.1), kind=kLoop, calls=%fused_computation.7 | loop fusion | bytes 3145728 | tf_op jit(solution)/shard_map/slice | solution.py:704
  2.1 1.3 %collective-permute-start.8 = (bf16[512,768]{1,0:T(8,128)(2,1)S(1)}, bf16[512,768]{1,0:T(8,128)(2,1)S(1)}, u32[]{:S(2)}, u32[]{:S(2)}) collective-permute-start(bf16[512,768]{1,0:T(8,128)(2,1)S(1)} %get-tuple-element.157), channel_id=1, source_target_pairs={{4,0},{8,4},{12,8},{16,12},{20,16},{24,20},{28,24},{5,1},{9,5},{13... | collective-permute-start | bytes 2359304 | tf_op jit(solution)/shard_map/ppermute | solution.py:37
  3.4 2.7 %collective-permute-start.9 = (bf16[512,768]{1,0:T(8,128)(2,1)S(1)}, bf16[512,768]{1,0:T(8,128)(2,1)S(1)}, u32[]{:S(2)}, u32[]{:S(2)}) collective-permute-start(bf16[512,768]{1,0:T(8,128)(2,1)S(1)} %get-tuple-element.157), channel_id=1, source_target_pairs={{0,2},{1,3},{2,0},{3,1},{4,6},{5,7},{6,4},{7,5},{8,10},{9,11},{10,... | collective-permute-start | bytes 2359304 | tf_op jit(solution)/shard_map/ppermute | solution.py:31
  6.0 1.3 %collective-permute-start.10 = (bf16[512,768]{1,0:T(8,128)(2,1)S(1)}, bf16[512,768]{1,0:T(8,128)(2,1)S(1)}, u32[]{:S(2)}, u32[]{:S(2)}) collective-permute-start(bf16[512,768]{1,0:T(8,128)(2,1)S(1)} %get-tuple-element.156), channel_id=1, source_target_pairs={{4,0},{8,4},{12,8},{16,12},{20,16},{24,20},{28,24},{5,1},{9,5},{13... | collective-permute-start | bytes 2359304 | tf_op jit(solution)/shard_map/ppermute | solution.py:37
  7.3 0.1 collective-permute-start.14
  8.1 14.7 %listing.1 = (s32[16]{0:T(128)S(1)}, s32[16]{0:T(128)S(1)}, s32[4]{0:T(128)S(1)}, s32[32]{0:T(128)S(1)}, s32[32]{0:T(128)S(1)}, /*index=5*/s32[32]{0:T(128)S(1)}, s32[9]{0:T(128)S(1)}) custom-call(s32[64]{0:T(128)S(1)} %copy-done.3, s32[64]{0:T(128)S(1)} %copy-done.4, s32[1]{0:T(128)S(6)} %copy.31.live), custom_call_target="tpu_custom_call" | custom-call | flops 1048576 | bytes 1024 | tf_op jit(solution)/shard_map/listing/pallas_call | solution.py:219
  22.8 0.6 opening.1.refs_4_
  23.4 1.6 %collective-permute-done.8.refs_5_ = bf16[512,768]{1,0:T(8,128)(2,1)S(1)} collective-permute-done((bf16[512,768]{1,0:T(8,128)(2,1)S(1)}, bf16[512,768]{1,0:T(8,128)(2,1)S(1)}, u32[]{:S(2)}, u32[]{:S(2)}) %collective-permute-start.8) | collective-permute-done | bytes 786464 | tf_op jit(solution)/shard_map/ppermute | solution.py:37
  25.0 0.1 fusion.1
  25.0 0.1 collective-permute-start.12
  25.1 0.5 collective-permute-start.13
  25.6 0.1 collective-permute-start.11
  25.7 6.8 %first_tiles.1 = (bf16[5120,768]{1,0:T(8,128)(2,1)S(1)}, f32[10,8,512]{2,1,0:T(8,128)S(1)}, f32[8,512,128]{2,1,0:T(8,128)S(1)}, bf16[17,512,512]{2,1,0:T(8,128)(2,1)S(1)}) custom-call(s32[4]{0:T(128)S(1)} %get-tuple-element.94.refs_0_, s32[16]{0:T(128)S(1)} %get-tuple-element.95.refs_1_, s32[16]{0:T(128)S(1)} %get-tuple-element.96.refs_2_, ...), custom_call_target="tpu_custom_call" | custom-call | flops 1048576 | bytes 1048576 | tf_op jit(solution)/shard_map/first_tiles/pallas_call | solution.py:336
  32.5 0.0 collective-permute-done.13
  32.5 0.1 pad_maximum_fusion.refs_3_
  32.6 2.1 %second_tiles.1 = (bf16[5120,768]{1,0:T(8,128)(2,1)S(1)}, f32[10,8,512]{2,1,0:T(8,128)S(1)}, f32[8,512,128]{2,1,0:T(8,128)S(1)}, bf16[17,512,512]{2,1,0:T(8,128)(2,1)S(1)}) custom-call(s32[4]{0:T(128)S(1)} %get-tuple-element.94.refs_0_, s32[16]{0:T(128)S(1)} %get-tuple-element.95.refs_1_, ...), custom_call_target="tpu_custom_call", output_to_operand_aliasing={{0}: (4, {}), {1}: (5, {}), {2}: (6, {}), {3}: (7, {})} | custom-call | flops 1048576 | bytes 1048576 | tf_op jit(solution)/shard_map/second_tiles/pallas_call | solution.py:336
  34.7 0.0 collective-permute-done.11.refs_5_
  34.7 2.5 %products.7 = (f32[2,72,512]{2,1,0:T(8,128)S(1)}, f32[4,72,512]{2,1,0:T(8,128)S(1)}, f32[2,72,512]{2,1,0:T(8,128)S(1)}, f32[2,72,512]{2,1,0:T(8,128)S(1)}) custom-call(s32[32]{0:T(128)S(1)} %get-tuple-element.86.refs_0_, s32[32]{0:T(128)S(1)} %get-tuple-element.87.refs_1_, s32[32]{0:T(128)S(1)} %get-tuple-element.88.refs_2_, ...), custom_call_target="tpu_custom_call" | custom-call | flops 1048576 | bytes 1048576 | tf_op jit(solution)/shard_map/products/pallas_call | solution.py:440
  37.3 4.3 %collective-permute-done.10.refs_0_ = bf16[512,768]{1,0:T(8,128)(2,1)S(1)} collective-permute-done((bf16[512,768]{1,0:T(8,128)(2,1)S(1)}, bf16[512,768]{1,0:T(8,128)(2,1)S(1)}, u32[]{:S(2)}, u32[]{:S(2)}) %collective-permute-start.10) | collective-permute-done | bytes 786464 | tf_op jit(solution)/shard_map/ppermute | solution.py:37
  41.5 0.0 collective-permute-done.14.refs_1_
  41.5 0.0 collective-permute-start.15
  41.5 1.7 %collective-permute-start.16 = (bf16[80,1024]{1,0:T(8,128)(2,1)S(1)}, bf16[80,1024]{1,0:T(8,128)(2,1)S(1)}, u32[]{:S(2)}, u32[]{:S(2)}) collective-permute-start(bf16[80,1024]{1,0:T(8,128)(2,1)S(1)} %opening.1.refs_4_), channel_id=1, source_target_pairs={{0,2},{1,3},{2,0},{3,1},{4,6},{5,7},{6,4},{7,5},{8,10},{9,11},{10,... | collective-permute-start | bytes 491528 | tf_op jit(solution)/shard_map/ppermute | solution.py:31
  43.2 1.3 %collective-permute-start.18 = (bf16[80,1024]{1,0:T(8,128)(2,1)S(1)}, bf16[80,1024]{1,0:T(8,128)(2,1)S(1)}, u32[]{:S(2)}, u32[]{:S(2)}) collective-permute-start(bf16[80,1024]{1,0:T(8,128)(2,1)S(1)} %opening.1.refs_4_), channel_id=1, source_target_pairs={{4,0},{8,4},{12,8},{16,12},{20,16},{24,20},{28,24},{5,1},{9,5},{13... | collective-permute-start | bytes 491528 | tf_op jit(solution)/shard_map/ppermute | solution.py:37
  44.5 0.8 more_blocks.1
  45.3 6.5 %last_tiles.1 = (bf16[5120,768]{1,0:T(8,128)(2,1)S(1)}, f32[10,8,512]{2,1,0:T(8,128)S(1)}, f32[8,512,128]{2,1,0:T(8,128)S(1)}, bf16[17,512,512]{2,1,0:T(8,128)(2,1)S(1)}) custom-call(s32[4]{0:T(128)S(1)} %get-tuple-element.94.refs_0_, s32[16]{0:T(128)S(1)} %get-tuple-element.95.refs_1_, ...), custom_call_target="tpu_custom_call", output_to_operand_aliasing={{0}: (4, {}), {1}: (5, {}), {2}: (6, {}), {3}: (7, {})} | custom-call | flops 4294967296 | bytes 1048576 | tf_op jit(solution)/shard_map/last_tiles/pallas_call | solution.py:336
  51.8 0.3 collective-permute-start.17
  52.0 1.3 %products.8 = (f32[2,72,512]{2,1,0:T(8,128)S(1)}, f32[4,72,512]{2,1,0:T(8,128)S(1)}, f32[2,72,512]{2,1,0:T(8,128)S(1)}, f32[2,72,512]{2,1,0:T(8,128)S(1)}) custom-call(s32[32]{0:T(128)S(1)} %get-tuple-element.86.refs_0_, s32[32]{0:T(128)S(1)} %get-tuple-element.87.refs_1_, s32[32]{0:T(128)S(1)} %get-tuple-element.88.refs_2_, ...), custom_call_target="tpu_custom_call" | custom-call | flops 1048576 | bytes 1048576 | tf_op jit(solution)/shard_map/products/pallas_call | solution.py:440
  53.3 4.0 %products.9 = (f32[4,72,512]{2,1,0:T(8,128)S(1)}, f32[2,72,512]{2,1,0:T(8,128)S(1)}, f32[2,72,512]{2,1,0:T(8,128)S(1)}) custom-call(s32[32]{0:T(128)S(1)} %get-tuple-element.86.refs_0_, s32[32]{0:T(128)S(1)} %get-tuple-element.87.refs_1_, s32[32]{0:T(128)S(1)} %get-tuple-element.88.refs_2_, s32[9]{0:T(128)S(1)} %get-tuple-element.89.refs_3_, ...), custom_call_target="tpu_custom_call" | custom-call | flops 2147483648 | bytes 1048576 | tf_op jit(solution)/shard_map/products/pallas_call | solution.py:440
  57.4 0.4 collective-permute-start.19
  57.7 1.7 %collective-permute-done.19.refs_2_ = f32[4,72,512]{2,1,0:T(8,128)S(1)} collective-permute-done((f32[4,72,512]{2,1,0:T(8,128)S(1)}, f32[4,72,512]{2,1,0:T(8,128)S(1)}, u32[]{:S(2)}, u32[]{:S(2)}) %collective-permute-start.19) | collective-permute-done | bytes 589856 | tf_op jit(solution)/shard_map/ppermute | solution.py:31
  59.5 0.4 collective-permute-start.21
  59.9 1.5 %collective-permute-start.20 = (f32[2,72,512]{2,1,0:T(8,128)S(1)}, f32[2,72,512]{2,1,0:T(8,128)S(1)}, u32[]{:S(2)}, u32[]{:S(2)}) collective-permute-start(f32[2,72,512]{2,1,0:T(8,128)S(1)} %get-tuple-element.132), channel_id=1, source_target_pairs={{0,4},{4,8},{8,12},{12,16},{16,20},{20,24},{24,28},{1,5},{5,9},{9,... | collective-permute-start | bytes 884744 | tf_op jit(solution)/shard_map/ppermute | solution.py:37
  61.4 1.4 %products.10.refs_0_ = f32[2,72,512]{2,1,0:T(8,128)S(1)} custom-call(s32[32]{0:T(128)S(1)} %get-tuple-element.86.refs_0_, s32[32]{0:T(128)S(1)} %get-tuple-element.87.refs_1_, s32[32]{0:T(128)S(1)} %get-tuple-element.88.refs_2_, s32[9]{0:T(128)S(1)} %get-tuple-element.89.refs_3_, bf16[80,1024]{1,0:T(8,128)(2,1)S(1)} %collective-permute-done.16.refs_4_, ...), custom_call_target="tpu_custom_call" | custom-call | flops 1048576 | bytes 1048576 | tf_op jit(solution)/shard_map/products/pallas_call | solution.py:440
  62.8 6.0 %collective-permute-done.21.refs_3_ = f32[2,72,512]{2,1,0:T(8,128)S(1)} collective-permute-done((f32[2,72,512]{2,1,0:T(8,128)S(1)}, f32[2,72,512]{2,1,0:T(8,128)S(1)}, u32[]{:S(2)}, u32[]{:S(2)}) %collective-permute-start.21) | collective-permute-done | bytes 294944 | tf_op jit(solution)/shard_map/ppermute | solution.py:31
  68.8 1.0 scaled_gram.2
  69.7 0.1 collective-permute-start.22
  69.8 0.9 collective-permute-start.23
  70.7 1.3 %collective-permute-start.25 = (bf16[128,1024]{1,0:T(8,128)(2,1)S(1)}, bf16[128,1024]{1,0:T(8,128)(2,1)S(1)}, u32[]{:S(2)}, u32[]{:S(2)}) collective-permute-start(bf16[128,1024]{1,0:T(8,128)(2,1)S(1)} %get-tuple-element.134.refs_4_), channel_id=1, source_target_pairs={{4,0},{8,4},{12,8},{16,12},{20,16},{24,20},{28,24},{5,1},{9,5},{13... | collective-permute-start | bytes 786440 | tf_op jit(solution)/shard_map/ppermute | solution.py:37
  72.0 3.2 %products.11 = (f32[2,64,512]{2,1,0:T(8,128)S(1)}, f32[4,64,512]{2,1,0:T(8,128)S(1)}, f32[2,64,512]{2,1,0:T(8,128)S(1)}, f32[2,64,512]{2,1,0:T(8,128)S(1)}) custom-call(s32[32]{0:T(128)S(1)} %get-tuple-element.86.refs_0_, s32[32]{0:T(128)S(1)} %get-tuple-element.87.refs_1_, s32[32]{0:T(128)S(1)} %get-tuple-element.88.refs_2_, ...), custom_call_target="tpu_custom_call" | custom-call | flops 1048576 | bytes 1048576 | tf_op jit(solution)/shard_map/products/pallas_call | solution.py:440
  75.2 3.4 %collective-permute-done.23.refs_4_ = bf16[128,1024]{1,0:T(8,128)(2,1)S(1)} collective-permute-done((bf16[128,1024]{1,0:T(8,128)(2,1)S(1)}, bf16[128,1024]{1,0:T(8,128)(2,1)S(1)}, u32[]{:S(2)}, u32[]{:S(2)}) %collective-permute-start.23) | collective-permute-done | bytes 262176 | tf_op jit(solution)/shard_map/ppermute | solution.py:31
  78.5 3.2 %collective-permute-done.25.refs_6_ = bf16[128,1024]{1,0:T(8,128)(2,1)S(1)} collective-permute-done((bf16[128,1024]{1,0:T(8,128)(2,1)S(1)}, bf16[128,1024]{1,0:T(8,128)(2,1)S(1)}, u32[]{:S(2)}, u32[]{:S(2)}) %collective-permute-start.25) | collective-permute-done | bytes 262176 | tf_op jit(solution)/shard_map/ppermute | solution.py:37
  81.7 4.1 %products.12 = (f32[4,64,512]{2,1,0:T(8,128)S(1)}, f32[2,64,512]{2,1,0:T(8,128)S(1)}, f32[2,64,512]{2,1,0:T(8,128)S(1)}) custom-call(s32[32]{0:T(128)S(1)} %get-tuple-element.86.refs_0_, s32[32]{0:T(128)S(1)} %get-tuple-element.87.refs_1_, s32[32]{0:T(128)S(1)} %get-tuple-element.88.refs_2_, s32[9]{0:T(128)S(1)} %get-tuple-element.89.refs_3_, ...), custom_call_target="tpu_custom_call" | custom-call | flops 2147483648 | bytes 1048576 | tf_op jit(solution)/shard_map/products/pallas_call | solution.py:440
  85.8 0.1 collective-permute-start.26
  85.9 1.9 %collective-permute-done.26.refs_2_ = f32[4,64,512]{2,1,0:T(8,128)S(1)} collective-permute-done((f32[4,64,512]{2,1,0:T(8,128)S(1)}, f32[4,64,512]{2,1,0:T(8,128)S(1)}, u32[]{:S(2)}, u32[]{:S(2)}) %collective-permute-start.26) | collective-permute-done | bytes 524320 | tf_op jit(solution)/shard_map/ppermute | solution.py:31
  87.8 0.5 collective-permute-start.28
  88.4 2.8 %collective-permute-start.27 = (f32[2,64,512]{2,1,0:T(8,128)S(1)}, f32[2,64,512]{2,1,0:T(8,128)S(1)}, u32[]{:S(2)}, u32[]{:S(2)}) collective-permute-start(f32[2,64,512]{2,1,0:T(8,128)S(1)} %get-tuple-element.146), channel_id=1, source_target_pairs={{0,4},{4,8},{8,12},{12,16},{16,20},{20,24},{24,28},{1,5},{5,9},{9,... | collective-permute-start | bytes 786440 | tf_op jit(solution)/shard_map/ppermute | solution.py:37
  91.1 1.5 %products.13.refs_0_ = f32[2,64,512]{2,1,0:T(8,128)S(1)} custom-call(s32[32]{0:T(128)S(1)} %get-tuple-element.86.refs_0_, s32[32]{0:T(128)S(1)} %get-tuple-element.87.refs_1_, s32[32]{0:T(128)S(1)} %get-tuple-element.88.refs_2_, s32[9]{0:T(128)S(1)} %get-tuple-element.89.refs_3_, bf16[128,1024]{1,0:T(8,128)(2,1)S(1)} %collective-permute-done.23.refs_4_, ...), custom_call_target="tpu_custom_call" | custom-call | flops 1048576 | bytes 1048576 | tf_op jit(solution)/shard_map/products/pallas_call | solution.py:440
  92.6 3.6 %collective-permute-done.28.refs_3_ = f32[2,64,512]{2,1,0:T(8,128)S(1)} collective-permute-done((f32[2,64,512]{2,1,0:T(8,128)S(1)}, f32[2,64,512]{2,1,0:T(8,128)S(1)}, u32[]{:S(2)}, u32[]{:S(2)}) %collective-permute-start.28) | collective-permute-done | bytes 262176 | tf_op jit(solution)/shard_map/ppermute | solution.py:31
  96.3 0.4 collective-permute-done.27.refs_1_
  96.7 1.0 scaled_gram.3
  97.7 0.1 collective-permute-start.29
  97.8 1.2 collective-permute-done.29
  99.0 1.2 %collective-permute-start.30 = (f32[64,128]{1,0:T(8,128)S(1)}, f32[64,128]{1,0:T(8,128)S(1)}, u32[]{:S(2)}, u32[]{:S(2)}) collective-permute-start(f32[64,128]{1,0:T(8,128)S(1)} %add.50), channel_id=1, source_target_pairs={{0,2},{1,3},{2,0},{3,1},{4,6},{5,7},{6,4},{7,5},{8,10},{9,11},{10,... | collective-permute-start | bytes 98312 | tf_op jit(solution)/shard_map/ppermute | solution.py:679
  100.2 2.5 %collective-permute-start.31 = (f32[64,128]{1,0:T(8,128)S(1)}, f32[64,128]{1,0:T(8,128)S(1)}, u32[]{:S(2)}, u32[]{:S(2)}) collective-permute-start(f32[64,128]{1,0:T(8,128)S(1)} %add.50), channel_id=1, source_target_pairs={{0,4},{1,5},{2,6},{3,7},{4,0},{5,1},{6,2},{7,3},{8,12},{9,13},{10,... | collective-permute-start | bytes 98312 | tf_op jit(solution)/shard_map/ppermute | solution.py:679
  102.7 0.2 collective-permute-start.32
  102.9 1.7 %collective-permute-done.31 = f32[64,128]{1,0:T(8,128)S(1)} collective-permute-done((f32[64,128]{1,0:T(8,128)S(1)}, f32[64,128]{1,0:T(8,128)S(1)}, u32[]{:S(2)}, u32[]{:S(2)}) %collective-permute-start.31) | collective-permute-done | bytes 32800 | tf_op jit(solution)/shard_map/ppermute | solution.py:679
  104.6 2.9 %collective-permute-done.32 = f32[64,128]{1,0:T(8,128)S(1)} collective-permute-done((f32[64,128]{1,0:T(8,128)S(1)}, f32[64,128]{1,0:T(8,128)S(1)}, u32[]{:S(2)}, u32[]{:S(2)}) %collective-permute-start.32) | collective-permute-done | bytes 32800 | tf_op jit(solution)/shard_map/ppermute | solution.py:679
  107.6 4.3 %collective-permute-start.33 = (f32[64,128]{1,0:T(8,128)S(1)}, f32[64,128]{1,0:T(8,128)S(1)}, u32[]{:S(2)}, u32[]{:S(2)}) collective-permute-start(f32[64,128]{1,0:T(8,128)S(1)} %add_add_fusion.3), channel_id=1, source_target_pairs={{0,8},{1,9},{2,10},{3,11},{4,12},{5,13},{6,14},{7,15},{8,0},{9,1},... | collective-permute-start | bytes 98312 | tf_op jit(solution)/shard_map/ppermute | solution.py:679
  111.9 2.4 %collective-permute-start.35 = (f32[64,128]{1,0:T(8,128)S(1)}, f32[64,128]{1,0:T(8,128)S(1)}, u32[]{:S(2)}, u32[]{:S(2)}) collective-permute-start(f32[64,128]{1,0:T(8,128)S(1)} %add_add_fusion.3), channel_id=1, source_target_pairs={{0,24},{1,25},{2,26},{3,27},{4,28},{5,29},{6,30},{7,31},{8,16},{9,... | collective-permute-start | bytes 98312 | tf_op jit(solution)/shard_map/ppermute | solution.py:679
  114.3 2.4 %collective-permute-done.34 = f32[64,128]{1,0:T(8,128)S(1)} collective-permute-done((f32[64,128]{1,0:T(8,128)S(1)}, f32[64,128]{1,0:T(8,128)S(1)}, u32[]{:S(2)}, u32[]{:S(2)}) %collective-permute-start.34) | collective-permute-done | bytes 32800 | tf_op jit(solution)/shard_map/ppermute | solution.py:679
  116.7 0.9 collective-permute-done.35
  117.6 4.9 %factors.1 = (f32[64,64]{1,0:T(8,128)S(1)}, f32[64,64]{1,0:T(8,128)S(1)}, s32[1]{0:T(128)}) custom-call(f32[64,128]{1,0:T(8,128)S(1)} %add_add_fusion.2.grams), custom_call_target="tpu_custom_call" | custom-call | flops 1073741824 | bytes 65536 | tf_op jit(solution)/shard_map/factors/pallas_call | solution.py:617
  123.2 1.1 applied.3
  (30 shorter events, 0.2 us)
Async XLA Ops:
  0.0 25.7 %copy-start = (bf16[1024,768]{1,0:T(8,128)(2,1)S(1)}, bf16[1024,768]{1,0:T(8,128)(2,1)}, u32[]{:S(2)}) copy-start(bf16[1024,768]{1,0:T(8,128)(2,1)} %refs_3_.1) | copy-start | bytes 4718596
  0.0 8.1 %copy-start.3 = (s32[64]{0:T(128)S(1)}, s32[64]{0:T(128)}, u32[]{:S(2)}) copy-start(s32[64]{0:T(128)} %rows.1) | copy-start | bytes 772
  0.0 8.1 %copy-start.4 = (s32[64]{0:T(128)S(1)}, s32[64]{0:T(128)}, u32[]{:S(2)}) copy-start(s32[64]{0:T(128)} %cols.1) | copy-start | bytes 772
  0.0 22.8 %copy-start.1 = (f32[64,1024]{1,0:T(8,128)S(1)}, f32[64,1024]{1,0:T(8,128)}, u32[]{:S(2)}) copy-start(f32[64,1024]{1,0:T(8,128)} %start) | copy-start | bytes 786436
  0.0 22.8 %copy-start.2 = (s32[2]{0:T(128)S(1)}, s32[2]{0:T(128)}, u32[]{:S(2)}) copy-start(s32[2]{0:T(128)} %count_ref.3) | copy-start | bytes 28
  0.0 22.8 %collective-permute-start.7 = (bf16[1024,768]{1,0:T(8,128)(2,1)}, bf16[1024,768]{1,0:T(8,128)(2,1)S(1)}, u32[]{:S(2)}, u32[]{:S(2)}) collective-permute-start(bf16[1024,768]{1,0:T(8,128)(2,1)} %refs_3_.1), channel_id=1, source_target_pairs={{0,1},{1,0},{2,3},{3,2},{4,5},{5,4},{6,7},{7,6},{8,9},{9,8},{10,11... | collective-permute-start | bytes 4718600 | tf_op jit(solution)/shard_map/ppermute | solution.py:31
  2.1 22.9 %collective-permute-start.8 = (bf16[512,768]{1,0:T(8,128)(2,1)S(1)}, bf16[512,768]{1,0:T(8,128)(2,1)S(1)}, u32[]{:S(2)}, u32[]{:S(2)}) collective-permute-start(bf16[512,768]{1,0:T(8,128)(2,1)S(1)} %get-tuple-element.157), channel_id=1, source_target_pairs={{4,0},{8,4},{12,8},{16,12},{20,16},{24,20},{28,24},{5,1},{9,5},{13... | collective-permute-start | bytes 2359304 | tf_op jit(solution)/shard_map/ppermute | solution.py:37
  3.4 21.6 %collective-permute-start.9 = (bf16[512,768]{1,0:T(8,128)(2,1)S(1)}, bf16[512,768]{1,0:T(8,128)(2,1)S(1)}, u32[]{:S(2)}, u32[]{:S(2)}) collective-permute-start(bf16[512,768]{1,0:T(8,128)(2,1)S(1)} %get-tuple-element.157), channel_id=1, source_target_pairs={{0,2},{1,3},{2,0},{3,1},{4,6},{5,7},{6,4},{7,5},{8,10},{9,11},{10,... | collective-permute-start | bytes 2359304 | tf_op jit(solution)/shard_map/ppermute | solution.py:31
  6.0 35.5 %collective-permute-start.10 = (bf16[512,768]{1,0:T(8,128)(2,1)S(1)}, bf16[512,768]{1,0:T(8,128)(2,1)S(1)}, u32[]{:S(2)}, u32[]{:S(2)}) collective-permute-start(bf16[512,768]{1,0:T(8,128)(2,1)S(1)} %get-tuple-element.156), channel_id=1, source_target_pairs={{4,0},{8,4},{12,8},{16,12},{20,16},{24,20},{28,24},{5,1},{9,5},{13... | collective-permute-start | bytes 2359304 | tf_op jit(solution)/shard_map/ppermute | solution.py:37
  7.3 34.2 %collective-permute-start.14 = (bf16[512,768]{1,0:T(8,128)(2,1)S(1)}, bf16[512,768]{1,0:T(8,128)(2,1)S(1)}, u32[]{:S(2)}, u32[]{:S(2)}) collective-permute-start(bf16[512,768]{1,0:T(8,128)(2,1)S(1)} %get-tuple-element.156), channel_id=1, source_target_pairs={{0,2},{1,3},{2,0},{3,1},{4,6},{5,7},{6,4},{7,5},{8,10},{9,11},{10,... | collective-permute-start | bytes 2359304 | tf_op jit(solution)/shard_map/ppermute | solution.py:31
  25.0 7.5 %collective-permute-start.12 = (bf16[256,768]{1,0:T(8,128)(2,1)S(1)}, bf16[256,768]{1,0:T(8,128)(2,1)S(1)}, u32[]{:S(2)}, u32[]{:S(2)}) collective-permute-start(bf16[256,768]{1,0:T(8,128)(2,1)S(1)} %get-tuple-element.158), channel_id=1, source_target_pairs={{0,1},{1,0},{2,3},{3,2},{4,5},{5,4},{6,7},{7,6},{8,9},{9,8},{10,11... | collective-permute-start | bytes 1179656 | tf_op jit(solution)/shard_map/ppermute | solution.py:31
  25.1 7.4 %collective-permute-start.13 = (bf16[256,768]{1,0:T(8,128)(2,1)S(1)}, bf16[256,768]{1,0:T(8,128)(2,1)S(1)}, u32[]{:S(2)}, u32[]{:S(2)}) collective-permute-start(bf16[256,768]{1,0:T(8,128)(2,1)S(1)} %get-tuple-element.159), channel_id=1, source_target_pairs={{0,1},{1,0},{2,3},{3,2},{4,5},{5,4},{6,7},{7,6},{8,9},{9,8},{10,11... | collective-permute-start | bytes 1179656 | tf_op jit(solution)/shard_map/ppermute | solution.py:31
  25.6 9.1 %collective-permute-start.11 = (bf16[80,1024]{1,0:T(8,128)(2,1)S(1)}, bf16[80,1024]{1,0:T(8,128)(2,1)S(1)}, u32[]{:S(2)}, u32[]{:S(2)}) collective-permute-start(bf16[80,1024]{1,0:T(8,128)(2,1)S(1)} %opening.1.refs_4_), channel_id=1, source_target_pairs={{0,1},{1,0},{2,3},{3,2},{4,5},{5,4},{6,7},{7,6},{8,9},{9,8},{10,11... | collective-permute-start | bytes 491528 | tf_op jit(solution)/shard_map/ppermute | solution.py:31
  41.5 3.8 %collective-permute-start.15 = (bf16[512,768]{1,0:T(8,128)(2,1)S(1)}, bf16[512,768]{1,0:T(8,128)(2,1)S(1)}, u32[]{:S(2)}, u32[]{:S(2)}) collective-permute-start(bf16[512,768]{1,0:T(8,128)(2,1)S(1)} %collective-permute-done.14.refs_1_), channel_id=1, source_target_pairs={{0,1},{1,0},{2,3},{3,2},{4,5},{5,4},{6,7},{7,6},{8,9},{9,8},{10,11... | collective-permute-start | bytes 2359304 | tf_op jit(solution)/shard_map/ppermute | solution.py:31
  41.5 10.2 %collective-permute-start.16 = (bf16[80,1024]{1,0:T(8,128)(2,1)S(1)}, bf16[80,1024]{1,0:T(8,128)(2,1)S(1)}, u32[]{:S(2)}, u32[]{:S(2)}) collective-permute-start(bf16[80,1024]{1,0:T(8,128)(2,1)S(1)} %opening.1.refs_4_), channel_id=1, source_target_pairs={{0,2},{1,3},{2,0},{3,1},{4,6},{5,7},{6,4},{7,5},{8,10},{9,11},{10,... | collective-permute-start | bytes 491528 | tf_op jit(solution)/shard_map/ppermute | solution.py:31
  43.2 10.1 %collective-permute-start.18 = (bf16[80,1024]{1,0:T(8,128)(2,1)S(1)}, bf16[80,1024]{1,0:T(8,128)(2,1)S(1)}, u32[]{:S(2)}, u32[]{:S(2)}) collective-permute-start(bf16[80,1024]{1,0:T(8,128)(2,1)S(1)} %opening.1.refs_4_), channel_id=1, source_target_pairs={{4,0},{8,4},{12,8},{16,12},{20,16},{24,20},{28,24},{5,1},{9,5},{13... | collective-permute-start | bytes 491528 | tf_op jit(solution)/shard_map/ppermute | solution.py:37
  51.8 1.6 %collective-permute-start.17 = (bf16[80,1024]{1,0:T(8,128)(2,1)S(1)}, bf16[80,1024]{1,0:T(8,128)(2,1)S(1)}, u32[]{:S(2)}, u32[]{:S(2)}) collective-permute-start(bf16[80,1024]{1,0:T(8,128)(2,1)S(1)} %collective-permute-done.16.refs_4_), channel_id=1, source_target_pairs={{0,1},{1,0},{2,3},{3,2},{4,5},{5,4},{6,7},{7,6},{8,9},{9,8},{10,11... | collective-permute-start | bytes 491528 | tf_op jit(solution)/shard_map/ppermute | solution.py:31
  57.4 2.1 %collective-permute-start.19 = (f32[4,72,512]{2,1,0:T(8,128)S(1)}, f32[4,72,512]{2,1,0:T(8,128)S(1)}, u32[]{:S(2)}, u32[]{:S(2)}) collective-permute-start(f32[4,72,512]{2,1,0:T(8,128)S(1)} %get-tuple-element.127), channel_id=1, source_target_pairs={{0,1},{1,0},{2,3},{3,2},{4,5},{5,4},{6,7},{7,6},{8,9},{9,8},{10,11... | collective-permute-start | bytes 1769480 | tf_op jit(solution)/shard_map/ppermute | solution.py:31
  59.5 9.3 %collective-permute-start.21 = (f32[2,72,512]{2,1,0:T(8,128)S(1)}, f32[2,72,512]{2,1,0:T(8,128)S(1)}, u32[]{:S(2)}, u32[]{:S(2)}) collective-permute-start(f32[2,72,512]{2,1,0:T(8,128)S(1)} %slice_add_fusion), channel_id=1, source_target_pairs={{0,2},{1,3},{2,0},{3,1},{4,6},{5,7},{6,4},{7,5},{8,10},{9,11},{10,... | collective-permute-start | bytes 884744 | tf_op jit(solution)/shard_map/ppermute | solution.py:31
  59.9 8.9 %collective-permute-start.20 = (f32[2,72,512]{2,1,0:T(8,128)S(1)}, f32[2,72,512]{2,1,0:T(8,128)S(1)}, u32[]{:S(2)}, u32[]{:S(2)}) collective-permute-start(f32[2,72,512]{2,1,0:T(8,128)S(1)} %get-tuple-element.132), channel_id=1, source_target_pairs={{0,4},{4,8},{8,12},{12,16},{16,20},{20,24},{24,28},{1,5},{5,9},{9,... | collective-permute-start | bytes 884744 | tf_op jit(solution)/shard_map/ppermute | solution.py:37
  69.7 2.2 %collective-permute-start.22 = (bf16[128,1024]{1,0:T(8,128)(2,1)S(1)}, bf16[128,1024]{1,0:T(8,128)(2,1)S(1)}, u32[]{:S(2)}, u32[]{:S(2)}) collective-permute-start(bf16[128,1024]{1,0:T(8,128)(2,1)S(1)} %get-tuple-element.134.refs_4_), channel_id=1, source_target_pairs={{0,1},{1,0},{2,3},{3,2},{4,5},{5,4},{6,7},{7,6},{8,9},{9,8},{10,11... | collective-permute-start | bytes 786440 | tf_op jit(solution)/shard_map/ppermute | solution.py:31
  69.8 8.7 %collective-permute-start.23 = (bf16[128,1024]{1,0:T(8,128)(2,1)S(1)}, bf16[128,1024]{1,0:T(8,128)(2,1)S(1)}, u32[]{:S(2)}, u32[]{:S(2)}) collective-permute-start(bf16[128,1024]{1,0:T(8,128)(2,1)S(1)} %get-tuple-element.134.refs_4_), channel_id=1, source_target_pairs={{0,2},{1,3},{2,0},{3,1},{4,6},{5,7},{6,4},{7,5},{8,10},{9,11},{10,... | collective-permute-start | bytes 786440 | tf_op jit(solution)/shard_map/ppermute | solution.py:31
  70.7 11.0 %collective-permute-start.25 = (bf16[128,1024]{1,0:T(8,128)(2,1)S(1)}, bf16[128,1024]{1,0:T(8,128)(2,1)S(1)}, u32[]{:S(2)}, u32[]{:S(2)}) collective-permute-start(bf16[128,1024]{1,0:T(8,128)(2,1)S(1)} %get-tuple-element.134.refs_4_), channel_id=1, source_target_pairs={{4,0},{8,4},{12,8},{16,12},{20,16},{24,20},{28,24},{5,1},{9,5},{13... | collective-permute-start | bytes 786440 | tf_op jit(solution)/shard_map/ppermute | solution.py:37
  78.5 3.2 %collective-permute-start.24 = (bf16[128,1024]{1,0:T(8,128)(2,1)S(1)}, bf16[128,1024]{1,0:T(8,128)(2,1)S(1)}, u32[]{:S(2)}, u32[]{:S(2)}) collective-permute-start(bf16[128,1024]{1,0:T(8,128)(2,1)S(1)} %collective-permute-done.23.refs_4_), channel_id=1, source_target_pairs={{0,1},{1,0},{2,3},{3,2},{4,5},{5,4},{6,7},{7,6},{8,9},{9,8},{10,11... | collective-permute-start | bytes 786440 | tf_op jit(solution)/shard_map/ppermute | solution.py:31
  85.8 2.0 %collective-permute-start.26 = (f32[4,64,512]{2,1,0:T(8,128)S(1)}, f32[4,64,512]{2,1,0:T(8,128)S(1)}, u32[]{:S(2)}, u32[]{:S(2)}) collective-permute-start(f32[4,64,512]{2,1,0:T(8,128)S(1)} %get-tuple-element.141), channel_id=1, source_target_pairs={{0,1},{1,0},{2,3},{3,2},{4,5},{5,4},{6,7},{7,6},{8,9},{9,8},{10,11... | collective-permute-start | bytes 1572872 | tf_op jit(solution)/shard_map/ppermute | solution.py:31
  87.8 8.4 %collective-permute-start.28 = (f32[2,64,512]{2,1,0:T(8,128)S(1)}, f32[2,64,512]{2,1,0:T(8,128)S(1)}, u32[]{:S(2)}, u32[]{:S(2)}) collective-permute-start(f32[2,64,512]{2,1,0:T(8,128)S(1)} %slice_add_fusion.1), channel_id=1, source_target_pairs={{0,2},{1,3},{2,0},{3,1},{4,6},{5,7},{6,4},{7,5},{8,10},{9,11},{10,... | collective-permute-start | bytes 786440 | tf_op jit(solution)/shard_map/ppermute | solution.py:31
  88.4 8.3 %collective-permute-start.27 = (f32[2,64,512]{2,1,0:T(8,128)S(1)}, f32[2,64,512]{2,1,0:T(8,128)S(1)}, u32[]{:S(2)}, u32[]{:S(2)}) collective-permute-start(f32[2,64,512]{2,1,0:T(8,128)S(1)} %get-tuple-element.146), channel_id=1, source_target_pairs={{0,4},{4,8},{8,12},{12,16},{16,20},{20,24},{24,28},{1,5},{5,9},{9,... | collective-permute-start | bytes 786440 | tf_op jit(solution)/shard_map/ppermute | solution.py:37
  97.7 1.3 %collective-permute-start.29 = (f32[64,128]{1,0:T(8,128)S(1)}, f32[64,128]{1,0:T(8,128)S(1)}, u32[]{:S(2)}, u32[]{:S(2)}) collective-permute-start(f32[64,128]{1,0:T(8,128)S(1)} %get-tuple-element.151), channel_id=1, source_target_pairs={{0,1},{1,0},{2,3},{3,2},{4,5},{5,4},{6,7},{7,6},{8,9},{9,8},{10,11... | collective-permute-start | bytes 98312 | tf_op jit(solution)/shard_map/ppermute | solution.py:679
  99.0 4.0 %collective-permute-start.30 = (f32[64,128]{1,0:T(8,128)S(1)}, f32[64,128]{1,0:T(8,128)S(1)}, u32[]{:S(2)}, u32[]{:S(2)}) collective-permute-start(f32[64,128]{1,0:T(8,128)S(1)} %add.50), channel_id=1, source_target_pairs={{0,2},{1,3},{2,0},{3,1},{4,6},{5,7},{6,4},{7,5},{8,10},{9,11},{10,... | collective-permute-start | bytes 98312 | tf_op jit(solution)/shard_map/ppermute | solution.py:679
  100.2 4.4 %collective-permute-start.31 = (f32[64,128]{1,0:T(8,128)S(1)}, f32[64,128]{1,0:T(8,128)S(1)}, u32[]{:S(2)}, u32[]{:S(2)}) collective-permute-start(f32[64,128]{1,0:T(8,128)S(1)} %add.50), channel_id=1, source_target_pairs={{0,4},{1,5},{2,6},{3,7},{4,0},{5,1},{6,2},{7,3},{8,12},{9,13},{10,... | collective-permute-start | bytes 98312 | tf_op jit(solution)/shard_map/ppermute | solution.py:679
  102.7 4.8 %collective-permute-start.32 = (f32[64,128]{1,0:T(8,128)S(1)}, f32[64,128]{1,0:T(8,128)S(1)}, u32[]{:S(2)}, u32[]{:S(2)}) collective-permute-start(f32[64,128]{1,0:T(8,128)S(1)} %add.50), channel_id=1, source_target_pairs={{0,6},{1,7},{2,4},{3,5},{4,2},{5,3},{6,0},{7,1},{8,14},{9,15},{10,... | collective-permute-start | bytes 98312 | tf_op jit(solution)/shard_map/ppermute | solution.py:679
  107.6 6.7 %collective-permute-start.33 = (f32[64,128]{1,0:T(8,128)S(1)}, f32[64,128]{1,0:T(8,128)S(1)}, u32[]{:S(2)}, u32[]{:S(2)}) collective-permute-start(f32[64,128]{1,0:T(8,128)S(1)} %add_add_fusion.3), channel_id=1, source_target_pairs={{0,8},{1,9},{2,10},{3,11},{4,12},{5,13},{6,14},{7,15},{8,0},{9,1},... | collective-permute-start | bytes 98312 | tf_op jit(solution)/shard_map/ppermute | solution.py:679
  111.9 4.8 %collective-permute-start.34 = (f32[64,128]{1,0:T(8,128)S(1)}, f32[64,128]{1,0:T(8,128)S(1)}, u32[]{:S(2)}, u32[]{:S(2)}) collective-permute-start(f32[64,128]{1,0:T(8,128)S(1)} %add_add_fusion.3), channel_id=1, source_target_pairs={{0,16},{1,17},{2,18},{3,19},{4,20},{5,21},{6,22},{7,23},{8,24},{9,... | collective-permute-start | bytes 98312 | tf_op jit(solution)/shard_map/ppermute | solution.py:679
  111.9 5.7 %collective-permute-start.35 = (f32[64,128]{1,0:T(8,128)S(1)}, f32[64,128]{1,0:T(8,128)S(1)}, u32[]{:S(2)}, u32[]{:S(2)}) collective-permute-start(f32[64,128]{1,0:T(8,128)S(1)} %add_add_fusion.3), channel_id=1, source_target_pairs={{0,24},{1,25},{2,26},{3,27},{4,28},{5,29},{6,30},{7,31},{8,16},{9,... | collective-permute-start | bytes 98312 | tf_op jit(solution)/shard_map/ppermute | solution.py:679

commit v2 on v1

--- a/solution.py
+++ b/solution.py
@@ -451,10 +451,9 @@
 
 
 def send_urgent(results, later, group, blocks_dev):
-    final = []
     *messages, far = results
+    final = [from_behind(far, "blk", 1)]
     parts = {}
-    behind = None
     for bit, message in zip(bits_of(group), messages):
         rels = [rel for rel in range(group) if rel & bit and rel % bit == 0]
         for index, rel in enumerate(rels):
@@ -466,17 +465,12 @@
         if bit > 1:
             message, *later = lax.optimization_barrier((message, *later))
         got = swap(message, "grp", bit)
-        if behind is None:
-            got, far = lax.optimization_barrier((got, far))
-            behind = from_behind(far, "blk", 1)
         final.append(got)
         for index, rel in enumerate(rels):
             if rel ^ bit:
                 piece = got[index * blocks_dev : (index + 1) * blocks_dev]
                 parts[rel ^ bit] = parts[rel ^ bit] + piece if rel ^ bit in parts else piece
-    if behind is None:
-        behind = from_behind(far, "blk", 1)
-    return [behind] + final, later
+    return final, later
 
 
 def finish_home(entries, vecs, tiles, start, blocks_dev, height, folds):
@@ -700,8 +694,10 @@
     rows, cols, n, *entries = listing(
         pair_rows, pair_cols, pair_live, group, cap, blocks_dev
     )
-    mate = swap(points, "grp", 1)
-    chunks = [points[:half], points[half:]]
+    first_chunk = points[:half]
+    rest, first_chunk = lax.optimization_barrier((points, first_chunk))
+    mate = swap(rest, "grp", 1)
+    chunks = [first_chunk, rest[half:]]
     far = [from_behind(chunk, "blk", -1) for chunk in chunks]
     crossed = [gather_far_bits(chunk) for chunk in chunks]
     begin, mate = lax.optimization_barrier((start, mate))

time: 126 us -> 125 us (level); the launches traced: 124 us -> 125 us
  starting transfers between devices: 28.4 us -> 32 us
  waiting for transfers between devices: 35.1 us -> 32 us
    ppermute x16, waiting for transfers between devices: 16.6 us -> 9.12 us  [swap(): lax.ppermute(value, axis, [(source, source ^ bit) for source in range(cou...]
    ppermute x6, waiting for transfers between devices: 9.45 us -> 14.7 us  [from_behind(): lax.ppermute(value, axis, [(source, source + steps) for source in range(i...]
    ppermute x16, starting transfers between devices: 8.22 us -> 10.9 us  [swap(): lax.ppermute(value, axis, [(source, source ^ bit) for source in range(cou...]
    ppermute x7, starting transfers between devices: 10.8 us -> 13.1 us  [all_sum(): lax.ppermute(value, ('blk', 'grp'), [(source, source ^ move) for source i...]
    ppermute x6, starting transfers between devices: 9.41 us -> 7.99 us  [from_behind(): lax.ppermute(value, axis, [(source, source + steps) for source in range(i...]
  transfers between devices with their start and end apart: 29 -> 29, of which waited for: 14 -> 16; matrix products, arithmetic and copies ran while one was open for 1% -> 0% of each run, Pallas kernels for 33% -> 33%
where the time goes in v2:
time: 125 us
  Pallas kernels  57.4 us (46%)
  starting transfers between devices  32 us (26%)
  waiting for transfers between devices  32 us (26%)
  between operations  1.65 us (1%)
  local copies, waits for them, and re-layouts  1.44 us (1%)
    pallas_call x7, Pallas kernels, products(): call(*entries, *[vecs[first] for first in firsts], tiles, *begun)  18 us
    pallas_call x4, Pallas kernels, build_tiles(): pl.pallas_call(kernel, out_shape=shapes, in_specs=[spec(SMEM)] * len(scal...  16.1 us
    ppermute x6, waiting for transfers between devices, from_behind(): lax.ppermute(value, axis, [(source, source + steps) for source in range(i...  14.7 us
    pallas_call x1, Pallas kernels, listing(): pl.pallas_call(functools.partial(listing_kernel, group, cap, blocks_dev),...  14.7 us
    ppermute x7, starting transfers between devices, all_sum(): lax.ppermute(value, ('blk', 'grp'), [(source, source ^ move) for source i...  13.1 us
    ppermute x16, starting transfers between devices, swap(): lax.ppermute(value, axis, [(source, source ^ bit) for source in range(cou...  10.9 us
    ppermute x16, waiting for transfers between devices, swap(): lax.ppermute(value, axis, [(source, source ^ bit) for source in range(cou...  9.12 us
    ppermute x7, waiting for transfers between devices, all_sum(): lax.ppermute(value, ('blk', 'grp'), [(source, source ^ move) for source i...  8.14 us
  transfers between devices with their start and end apart: 29, of which 16 were waited for; matrix products, arithmetic and copies ran while one was open for 0% of the time, Pallas kernels for 33%

profile of v2, /device:TPU:0, one launch (start us, length us, event | category | flops | bytes accessed | tf_op | source)
XLA Modules:
  0.0 124.7 jit_solution(9538295331232860968)
XLA Ops:
  0.0 1.3 %slice.18 = bf16[512,768]{1,0:T(8,128)(2,1)S(1)} slice(bf16[1024,768]{1,0:T(8,128)(2,1)} %refs_3_.1), slice={[0:512], [0:768]} | slice | bytes 1572864 | tf_op jit(solution)/shard_map/slice | solution.py:697
  1.3 0.5 collective-permute-start.7
  1.9 1.3 %collective-permute-start.8 = (bf16[512,768]{1,0:T(8,128)(2,1)S(1)}, bf16[512,768]{1,0:T(8,128)(2,1)S(1)}, u32[]{:S(2)}, u32[]{:S(2)}) collective-permute-start(bf16[512,768]{1,0:T(8,128)(2,1)S(1)} %slice.18), channel_id=1, source_target_pairs={{4,0},{8,4},{12,8},{16,12},{20,16},{24,20},{28,24},{5,1},{9,5},{13... | collective-permute-start | bytes 2359304 | tf_op jit(solution)/shard_map/ppermute | solution.py:37
  3.2 2.6 %collective-permute-start.9 = (bf16[512,768]{1,0:T(8,128)(2,1)S(1)}, bf16[512,768]{1,0:T(8,128)(2,1)S(1)}, u32[]{:S(2)}, u32[]{:S(2)}) collective-permute-start(bf16[512,768]{1,0:T(8,128)(2,1)S(1)} %slice.18), channel_id=1, source_target_pairs={{0,2},{1,3},{2,0},{3,1},{4,6},{5,7},{6,4},{7,5},{8,10},{9,11},{10,... | collective-permute-start | bytes 2359304 | tf_op jit(solution)/shard_map/ppermute | solution.py:31
  5.7 0.1 slice.19
  5.8 1.3 %collective-permute-start.10 = (bf16[512,768]{1,0:T(8,128)(2,1)S(1)}, bf16[512,768]{1,0:T(8,128)(2,1)S(1)}, u32[]{:S(2)}, u32[]{:S(2)}) collective-permute-start(bf16[512,768]{1,0:T(8,128)(2,1)S(1)} %slice.19), channel_id=1, source_target_pairs={{4,0},{8,4},{12,8},{16,12},{20,16},{24,20},{28,24},{5,1},{9,5},{13... | collective-permute-start | bytes 2359304 | tf_op jit(solution)/shard_map/ppermute | solution.py:37
  7.1 0.1 collective-permute-start.14
  7.9 14.7 %listing.1 = (s32[16]{0:T(128)S(1)}, s32[16]{0:T(128)S(1)}, s32[4]{0:T(128)S(1)}, s32[32]{0:T(128)S(1)}, s32[32]{0:T(128)S(1)}, /*index=5*/s32[32]{0:T(128)S(1)}, s32[9]{0:T(128)S(1)}) custom-call(s32[64]{0:T(128)S(1)} %copy-done.3, s32[64]{0:T(128)S(1)} %copy-done.4, s32[1]{0:T(128)S(6)} %copy.31.live), custom_call_target="tpu_custom_call" | custom-call | flops 1048576 | bytes 1024 | tf_op jit(solution)/shard_map/listing/pallas_call | solution.py:219
  22.6 0.6 opening.1.refs_4_
  23.1 1.5 %collective-permute-done.8.refs_5_ = bf16[512,768]{1,0:T(8,128)(2,1)S(1)} collective-permute-done((bf16[512,768]{1,0:T(8,128)(2,1)S(1)}, bf16[512,768]{1,0:T(8,128)(2,1)S(1)}, u32[]{:S(2)}, u32[]{:S(2)}) %collective-permute-start.8) | collective-permute-done | bytes 786464 | tf_op jit(solution)/shard_map/ppermute | solution.py:37
  24.7 0.1 fusion
  24.7 0.1 collective-permute-start.12
  24.8 0.5 collective-permute-start.13
  25.3 0.1 collective-permute-start.11
  25.4 7.9 %first_tiles.1 = (bf16[5120,768]{1,0:T(8,128)(2,1)S(1)}, f32[10,8,512]{2,1,0:T(8,128)S(1)}, f32[8,512,128]{2,1,0:T(8,128)S(1)}, bf16[17,512,512]{2,1,0:T(8,128)(2,1)S(1)}) custom-call(s32[4]{0:T(128)S(1)} %get-tuple-element.94.refs_0_, s32[16]{0:T(128)S(1)} %get-tuple-element.95.refs_1_, s32[16]{0:T(128)S(1)} %get-tuple-element.96.refs_2_, ...), custom_call_target="tpu_custom_call" | custom-call | flops 1048576 | bytes 1048576 | tf_op jit(solution)/shard_map/first_tiles/pallas_call | solution.py:336
  33.3 0.1 pad_maximum_fusion.refs_3_
  33.4 2.1 %second_tiles.1 = (bf16[5120,768]{1,0:T(8,128)(2,1)S(1)}, f32[10,8,512]{2,1,0:T(8,128)S(1)}, f32[8,512,128]{2,1,0:T(8,128)S(1)}, bf16[17,512,512]{2,1,0:T(8,128)(2,1)S(1)}) custom-call(s32[4]{0:T(128)S(1)} %get-tuple-element.94.refs_0_, s32[16]{0:T(128)S(1)} %get-tuple-element.95.refs_1_, ...), custom_call_target="tpu_custom_call", output_to_operand_aliasing={{0}: (4, {}), {1}: (5, {}), {2}: (6, {}), {3}: (7, {})} | custom-call | flops 1048576 | bytes 1048576 | tf_op jit(solution)/shard_map/second_tiles/pallas_call | solution.py:336
  35.5 2.5 %products.7 = (f32[2,72,512]{2,1,0:T(8,128)S(1)}, f32[4,72,512]{2,1,0:T(8,128)S(1)}, f32[2,72,512]{2,1,0:T(8,128)S(1)}, f32[2,72,512]{2,1,0:T(8,128)S(1)}) custom-call(s32[32]{0:T(128)S(1)} %get-tuple-element.84.refs_0_, s32[32]{0:T(128)S(1)} %get-tuple-element.85.refs_1_, s32[32]{0:T(128)S(1)} %get-tuple-element.86.refs_2_, ...), custom_call_target="tpu_custom_call" | custom-call | flops 1048576 | bytes 1048576 | tf_op jit(solution)/shard_map/products/pallas_call | solution.py:440
  38.0 3.3 %collective-permute-done.10.refs_0_ = bf16[512,768]{1,0:T(8,128)(2,1)S(1)} collective-permute-done((bf16[512,768]{1,0:T(8,128)(2,1)S(1)}, bf16[512,768]{1,0:T(8,128)(2,1)S(1)}, u32[]{:S(2)}, u32[]{:S(2)}) %collective-permute-start.10) | collective-permute-done | bytes 786464 | tf_op jit(solution)/shard_map/ppermute | solution.py:37
  41.3 1.7 %collective-permute-start.16 = (bf16[80,1024]{1,0:T(8,128)(2,1)S(1)}, bf16[80,1024]{1,0:T(8,128)(2,1)S(1)}, u32[]{:S(2)}, u32[]{:S(2)}) collective-permute-start(bf16[80,1024]{1,0:T(8,128)(2,1)S(1)} %opening.1.refs_4_), channel_id=1, source_target_pairs={{0,2},{1,3},{2,0},{3,1},{4,6},{5,7},{6,4},{7,5},{8,10},{9,11},{10,... | collective-permute-start | bytes 491528 | tf_op jit(solution)/shard_map/ppermute | solution.py:31
  43.1 1.3 %collective-permute-start.18 = (bf16[80,1024]{1,0:T(8,128)(2,1)S(1)}, bf16[80,1024]{1,0:T(8,128)(2,1)S(1)}, u32[]{:S(2)}, u32[]{:S(2)}) collective-permute-start(bf16[80,1024]{1,0:T(8,128)(2,1)S(1)} %opening.1.refs_4_), channel_id=1, source_target_pairs={{4,0},{8,4},{12,8},{16,12},{20,16},{24,20},{28,24},{5,1},{9,5},{13... | collective-permute-start | bytes 491528 | tf_op jit(solution)/shard_map/ppermute | solution.py:37
  44.3 0.8 more_blocks.1
  45.1 5.4 %last_tiles.1 = (bf16[5120,768]{1,0:T(8,128)(2,1)S(1)}, f32[10,8,512]{2,1,0:T(8,128)S(1)}, f32[8,512,128]{2,1,0:T(8,128)S(1)}, bf16[17,512,512]{2,1,0:T(8,128)(2,1)S(1)}) custom-call(s32[4]{0:T(128)S(1)} %get-tuple-element.94.refs_0_, s32[16]{0:T(128)S(1)} %get-tuple-element.95.refs_1_, ...), custom_call_target="tpu_custom_call", output_to_operand_aliasing={{0}: (4, {}), {1}: (5, {}), {2}: (6, {}), {3}: (7, {})} | custom-call | flops 4294967296 | bytes 1048576 | tf_op jit(solution)/shard_map/last_tiles/pallas_call | solution.py:336
  50.5 1.4 %collective-permute-start.17 = (bf16[80,1024]{1,0:T(8,128)(2,1)S(1)}, bf16[80,1024]{1,0:T(8,128)(2,1)S(1)}, u32[]{:S(2)}, u32[]{:S(2)}) collective-permute-start(bf16[80,1024]{1,0:T(8,128)(2,1)S(1)} %collective-permute-done.16.refs_4_), channel_id=1, source_target_pairs={{0,1},{1,0},{2,3},{3,2},{4,5},{5,4},{6,7},{7,6},{8,9},{9,8},{10,11... | collective-permute-start | bytes 491528 | tf_op jit(solution)/shard_map/ppermute | solution.py:31
  51.9 1.3 %products.8 = (f32[2,72,512]{2,1,0:T(8,128)S(1)}, f32[4,72,512]{2,1,0:T(8,128)S(1)}, f32[2,72,512]{2,1,0:T(8,128)S(1)}, f32[2,72,512]{2,1,0:T(8,128)S(1)}) custom-call(s32[32]{0:T(128)S(1)} %get-tuple-element.84.refs_0_, s32[32]{0:T(128)S(1)} %get-tuple-element.85.refs_1_, s32[32]{0:T(128)S(1)} %get-tuple-element.86.refs_2_, ...), custom_call_target="tpu_custom_call" | custom-call | flops 1048576 | bytes 1048576 | tf_op jit(solution)/shard_map/products/pallas_call | solution.py:440
  53.2 4.0 %products.9 = (f32[4,72,512]{2,1,0:T(8,128)S(1)}, f32[2,72,512]{2,1,0:T(8,128)S(1)}, f32[2,72,512]{2,1,0:T(8,128)S(1)}) custom-call(s32[32]{0:T(128)S(1)} %get-tuple-element.84.refs_0_, s32[32]{0:T(128)S(1)} %get-tuple-element.85.refs_1_, s32[32]{0:T(128)S(1)} %get-tuple-element.86.refs_2_, s32[9]{0:T(128)S(1)} %get-tuple-element.87.refs_3_, ...), custom_call_target="tpu_custom_call" | custom-call | flops 2147483648 | bytes 1048576 | tf_op jit(solution)/shard_map/products/pallas_call | solution.py:440
  57.2 0.1 collective-permute-start.19
  57.3 1.6 %collective-permute-start.20 = (f32[2,72,512]{2,1,0:T(8,128)S(1)}, f32[2,72,512]{2,1,0:T(8,128)S(1)}, u32[]{:S(2)}, u32[]{:S(2)}) collective-permute-start(f32[2,72,512]{2,1,0:T(8,128)S(1)} %get-tuple-element.130), channel_id=1, source_target_pairs={{0,4},{4,8},{8,12},{12,16},{16,20},{20,24},{24,28},{1,5},{5,9},{9,... | collective-permute-start | bytes 884744 | tf_op jit(solution)/shard_map/ppermute | solution.py:37
  58.9 0.4 collective-permute-done.19.refs_2_
  59.3 1.4 %collective-permute-start.21 = (f32[2,72,512]{2,1,0:T(8,128)S(1)}, f32[2,72,512]{2,1,0:T(8,128)S(1)}, u32[]{:S(2)}, u32[]{:S(2)}) collective-permute-start(f32[2,72,512]{2,1,0:T(8,128)S(1)} %slice_add_fusion), channel_id=1, source_target_pairs={{0,2},{1,3},{2,0},{3,1},{4,6},{5,7},{6,4},{7,5},{8,10},{9,11},{10,... | collective-permute-start | bytes 884744 | tf_op jit(solution)/shard_map/ppermute | solution.py:31
  60.7 1.4 %products.10.refs_0_ = f32[2,72,512]{2,1,0:T(8,128)S(1)} custom-call(s32[32]{0:T(128)S(1)} %get-tuple-element.84.refs_0_, s32[32]{0:T(128)S(1)} %get-tuple-element.85.refs_1_, s32[32]{0:T(128)S(1)} %get-tuple-element.86.refs_2_, s32[9]{0:T(128)S(1)} %get-tuple-element.87.refs_3_, bf16[80,1024]{1,0:T(8,128)(2,1)S(1)} %collective-permute-done.16.refs_4_, ...), custom_call_target="tpu_custom_call" | custom-call | flops 1048576 | bytes 1048576 | tf_op jit(solution)/shard_map/products/pallas_call | solution.py:440
  62.1 3.7 %collective-permute-done.20.refs_1_ = f32[2,72,512]{2,1,0:T(8,128)S(1)} collective-permute-done((f32[2,72,512]{2,1,0:T(8,128)S(1)}, f32[2,72,512]{2,1,0:T(8,128)S(1)}, u32[]{:S(2)}, u32[]{:S(2)}) %collective-permute-start.20) | collective-permute-done | bytes 294944 | tf_op jit(solution)/shard_map/ppermute | solution.py:37
  65.8 2.7 %collective-permute-done.21.refs_3_ = f32[2,72,512]{2,1,0:T(8,128)S(1)} collective-permute-done((f32[2,72,512]{2,1,0:T(8,128)S(1)}, f32[2,72,512]{2,1,0:T(8,128)S(1)}, u32[]{:S(2)}, u32[]{:S(2)}) %collective-permute-start.21) | collective-permute-done | bytes 294944 | tf_op jit(solution)/shard_map/ppermute | solution.py:31
  68.4 1.0 scaled_gram.2
  69.4 0.1 collective-permute-start.22
  69.5 1.4 %collective-permute-start.23 = (bf16[128,1024]{1,0:T(8,128)(2,1)S(1)}, bf16[128,1024]{1,0:T(8,128)(2,1)S(1)}, u32[]{:S(2)}, u32[]{:S(2)}) collective-permute-start(bf16[128,1024]{1,0:T(8,128)(2,1)S(1)} %get-tuple-element.132.refs_4_), channel_id=1, source_target_pairs={{0,2},{1,3},{2,0},{3,1},{4,6},{5,7},{6,4},{7,5},{8,10},{9,11},{10,... | collective-permute-start | bytes 786440 | tf_op jit(solution)/shard_map/ppermute | solution.py:31
  70.8 1.3 %collective-permute-start.25 = (bf16[128,1024]{1,0:T(8,128)(2,1)S(1)}, bf16[128,1024]{1,0:T(8,128)(2,1)S(1)}, u32[]{:S(2)}, u32[]{:S(2)}) collective-permute-start(bf16[128,1024]{1,0:T(8,128)(2,1)S(1)} %get-tuple-element.132.refs_4_), channel_id=1, source_target_pairs={{4,0},{8,4},{12,8},{16,12},{20,16},{24,20},{28,24},{5,1},{9,5},{13... | collective-permute-start | bytes 786440 | tf_op jit(solution)/shard_map/ppermute | solution.py:37
  72.1 3.2 %products.11 = (f32[2,64,512]{2,1,0:T(8,128)S(1)}, f32[4,64,512]{2,1,0:T(8,128)S(1)}, f32[2,64,512]{2,1,0:T(8,128)S(1)}, f32[2,64,512]{2,1,0:T(8,128)S(1)}) custom-call(s32[32]{0:T(128)S(1)} %get-tuple-element.84.refs_0_, s32[32]{0:T(128)S(1)} %get-tuple-element.85.refs_1_, s32[32]{0:T(128)S(1)} %get-tuple-element.86.refs_2_, ...), custom_call_target="tpu_custom_call" | custom-call | flops 1048576 | bytes 1048576 | tf_op jit(solution)/shard_map/products/pallas_call | solution.py:440
  75.3 2.9 %collective-permute-done.23.refs_4_ = bf16[128,1024]{1,0:T(8,128)(2,1)S(1)} collective-permute-done((bf16[128,1024]{1,0:T(8,128)(2,1)S(1)}, bf16[128,1024]{1,0:T(8,128)(2,1)S(1)}, u32[]{:S(2)}, u32[]{:S(2)}) %collective-permute-start.23) | collective-permute-done | bytes 262176 | tf_op jit(solution)/shard_map/ppermute | solution.py:31
  78.2 2.9 %collective-permute-done.25.refs_6_ = bf16[128,1024]{1,0:T(8,128)(2,1)S(1)} collective-permute-done((bf16[128,1024]{1,0:T(8,128)(2,1)S(1)}, bf16[128,1024]{1,0:T(8,128)(2,1)S(1)}, u32[]{:S(2)}, u32[]{:S(2)}) %collective-permute-start.25) | collective-permute-done | bytes 262176 | tf_op jit(solution)/shard_map/ppermute | solution.py:37
  81.1 4.1 %products.12 = (f32[4,64,512]{2,1,0:T(8,128)S(1)}, f32[2,64,512]{2,1,0:T(8,128)S(1)}, f32[2,64,512]{2,1,0:T(8,128)S(1)}) custom-call(s32[32]{0:T(128)S(1)} %get-tuple-element.84.refs_0_, s32[32]{0:T(128)S(1)} %get-tuple-element.85.refs_1_, s32[32]{0:T(128)S(1)} %get-tuple-element.86.refs_2_, s32[9]{0:T(128)S(1)} %get-tuple-element.87.refs_3_, ...), custom_call_target="tpu_custom_call" | custom-call | flops 2147483648 | bytes 1048576 | tf_op jit(solution)/shard_map/products/pallas_call | solution.py:440
  85.2 0.1 collective-permute-start.26
  85.3 1.3 %collective-permute-start.27 = (f32[2,64,512]{2,1,0:T(8,128)S(1)}, f32[2,64,512]{2,1,0:T(8,128)S(1)}, u32[]{:S(2)}, u32[]{:S(2)}) collective-permute-start(f32[2,64,512]{2,1,0:T(8,128)S(1)} %get-tuple-element.142), channel_id=1, source_target_pairs={{0,4},{4,8},{8,12},{12,16},{16,20},{20,24},{24,28},{1,5},{5,9},{9,... | collective-permute-start | bytes 786440 | tf_op jit(solution)/shard_map/ppermute | solution.py:37
  86.6 0.6 collective-permute-done.26.refs_2_
  87.2 1.0 collective-permute-start.28
  88.3 1.5 %products.13.refs_0_ = f32[2,64,512]{2,1,0:T(8,128)S(1)} custom-call(s32[32]{0:T(128)S(1)} %get-tuple-element.84.refs_0_, s32[32]{0:T(128)S(1)} %get-tuple-element.85.refs_1_, s32[32]{0:T(128)S(1)} %get-tuple-element.86.refs_2_, s32[9]{0:T(128)S(1)} %get-tuple-element.87.refs_3_, bf16[128,1024]{1,0:T(8,128)(2,1)S(1)} %collective-permute-done.23.refs_4_, ...), custom_call_target="tpu_custom_call" | custom-call | flops 1048576 | bytes 1048576 | tf_op jit(solution)/shard_map/products/pallas_call | solution.py:440
  89.7 3.3 %collective-permute-done.27.refs_1_ = f32[2,64,512]{2,1,0:T(8,128)S(1)} collective-permute-done((f32[2,64,512]{2,1,0:T(8,128)S(1)}, f32[2,64,512]{2,1,0:T(8,128)S(1)}, u32[]{:S(2)}, u32[]{:S(2)}) %collective-permute-start.27) | collective-permute-done | bytes 262176 | tf_op jit(solution)/shard_map/ppermute | solution.py:37
  93.1 2.6 %collective-permute-done.28.refs_3_ = f32[2,64,512]{2,1,0:T(8,128)S(1)} collective-permute-done((f32[2,64,512]{2,1,0:T(8,128)S(1)}, f32[2,64,512]{2,1,0:T(8,128)S(1)}, u32[]{:S(2)}, u32[]{:S(2)}) %collective-permute-start.28) | collective-permute-done | bytes 262176 | tf_op jit(solution)/shard_map/ppermute | solution.py:31
  95.7 1.0 scaled_gram.3
  96.7 0.1 collective-permute-start.29
  96.8 1.2 collective-permute-done.29
  98.0 1.0 collective-permute-start.30
  99.0 0.3 collective-permute-start.31
  99.3 2.2 %collective-permute-start.32 = (f32[64,128]{1,0:T(8,128)S(1)}, f32[64,128]{1,0:T(8,128)S(1)}, u32[]{:S(2)}, u32[]{:S(2)}) collective-permute-start(f32[64,128]{1,0:T(8,128)S(1)} %add.50), channel_id=1, source_target_pairs={{0,6},{1,7},{2,4},{3,5},{4,2},{5,3},{6,0},{7,1},{8,14},{9,15},{10,... | collective-permute-start | bytes 98312 | tf_op jit(solution)/shard_map/ppermute | solution.py:673
  101.4 0.4 collective-permute-done.30
  101.9 1.2 collective-permute-done.31
  103.1 1.0 collective-permute-done.32
  104.1 6.1 %collective-permute-start.33 = (f32[64,128]{1,0:T(8,128)S(1)}, f32[64,128]{1,0:T(8,128)S(1)}, u32[]{:S(2)}, u32[]{:S(2)}) collective-permute-start(f32[64,128]{1,0:T(8,128)S(1)} %add_add_fusion.3), channel_id=1, source_target_pairs={{0,8},{1,9},{2,10},{3,11},{4,12},{5,13},{6,14},{7,15},{8,0},{9,1},... | collective-permute-start | bytes 98312 | tf_op jit(solution)/shard_map/ppermute | solution.py:673
  110.2 2.1 %collective-permute-start.34 = (f32[64,128]{1,0:T(8,128)S(1)}, f32[64,128]{1,0:T(8,128)S(1)}, u32[]{:S(2)}, u32[]{:S(2)}) collective-permute-start(f32[64,128]{1,0:T(8,128)S(1)} %add_add_fusion.3), channel_id=1, source_target_pairs={{0,16},{1,17},{2,18},{3,19},{4,20},{5,21},{6,22},{7,23},{8,24},{9,... | collective-permute-start | bytes 98312 | tf_op jit(solution)/shard_map/ppermute | solution.py:673
  112.3 1.4 %collective-permute-start.35 = (f32[64,128]{1,0:T(8,128)S(1)}, f32[64,128]{1,0:T(8,128)S(1)}, u32[]{:S(2)}, u32[]{:S(2)}) collective-permute-start(f32[64,128]{1,0:T(8,128)S(1)} %add_add_fusion.3), channel_id=1, source_target_pairs={{0,24},{1,25},{2,26},{3,27},{4,28},{5,29},{6,30},{7,31},{8,16},{9,... | collective-permute-start | bytes 98312 | tf_op jit(solution)/shard_map/ppermute | solution.py:673
  113.7 1.4 %collective-permute-done.34 = f32[64,128]{1,0:T(8,128)S(1)} collective-permute-done((f32[64,128]{1,0:T(8,128)S(1)}, f32[64,128]{1,0:T(8,128)S(1)}, u32[]{:S(2)}, u32[]{:S(2)}) %collective-permute-start.34) | collective-permute-done | bytes 32800 | tf_op jit(solution)/shard_map/ppermute | solution.py:673
  115.0 3.0 %collective-permute-done.35 = f32[64,128]{1,0:T(8,128)S(1)} collective-permute-done((f32[64,128]{1,0:T(8,128)S(1)}, f32[64,128]{1,0:T(8,128)S(1)}, u32[]{:S(2)}, u32[]{:S(2)}) %collective-permute-start.35) | collective-permute-done | bytes 32800 | tf_op jit(solution)/shard_map/ppermute | solution.py:673
  118.0 4.9 %factors.1 = (f32[64,64]{1,0:T(8,128)S(1)}, f32[64,64]{1,0:T(8,128)S(1)}, s32[1]{0:T(128)}) custom-call(f32[64,128]{1,0:T(8,128)S(1)} %add_add_fusion.2.grams), custom_call_target="tpu_custom_call" | custom-call | flops 1073741824 | bytes 65536 | tf_op jit(solution)/shard_map/factors/pallas_call | solution.py:611
  123.6 1.1 applied.3
  (31 shorter events, 0.2 us)
Async XLA Ops:
  0.0 5.7 %copy-start = (bf16[1024,768]{1,0:T(8,128)(2,1)S(1)}, bf16[1024,768]{1,0:T(8,128)(2,1)}, u32[]{:S(2)}) copy-start(bf16[1024,768]{1,0:T(8,128)(2,1)} %refs_3_.1) | copy-start | bytes 4718596
  0.0 7.8 %copy-start.3 = (s32[64]{0:T(128)S(1)}, s32[64]{0:T(128)}, u32[]{:S(2)}) copy-start(s32[64]{0:T(128)} %rows.1) | copy-start | bytes 772
  0.0 7.8 %copy-start.4 = (s32[64]{0:T(128)S(1)}, s32[64]{0:T(128)}, u32[]{:S(2)}) copy-start(s32[64]{0:T(128)} %cols.1) | copy-start | bytes 772
  0.0 22.5 %copy-start.1 = (f32[64,1024]{1,0:T(8,128)S(1)}, f32[64,1024]{1,0:T(8,128)}, u32[]{:S(2)}) copy-start(f32[64,1024]{1,0:T(8,128)} %start) | copy-start | bytes 786436
  0.0 22.6 %copy-start.2 = (s32[2]{0:T(128)S(1)}, s32[2]{0:T(128)}, u32[]{:S(2)}) copy-start(s32[2]{0:T(128)} %count_ref.3) | copy-start | bytes 28
  1.3 21.2 %collective-permute-start.7 = (bf16[1024,768]{1,0:T(8,128)(2,1)}, bf16[1024,768]{1,0:T(8,128)(2,1)S(1)}, u32[]{:S(2)}, u32[]{:S(2)}) collective-permute-start(bf16[1024,768]{1,0:T(8,128)(2,1)} %refs_3_.1), channel_id=1, source_target_pairs={{0,1},{1,0},{2,3},{3,2},{4,5},{5,4},{6,7},{7,6},{8,9},{9,8},{10,11... | collective-permute-start | bytes 4718600 | tf_op jit(solution)/shard_map/ppermute | solution.py:31
  1.9 22.8 %collective-permute-start.8 = (bf16[512,768]{1,0:T(8,128)(2,1)S(1)}, bf16[512,768]{1,0:T(8,128)(2,1)S(1)}, u32[]{:S(2)}, u32[]{:S(2)}) collective-permute-start(bf16[512,768]{1,0:T(8,128)(2,1)S(1)} %slice.18), channel_id=1, source_target_pairs={{4,0},{8,4},{12,8},{16,12},{20,16},{24,20},{28,24},{5,1},{9,5},{13... | collective-permute-start | bytes 2359304 | tf_op jit(solution)/shard_map/ppermute | solution.py:37
  3.2 21.5 %collective-permute-start.9 = (bf16[512,768]{1,0:T(8,128)(2,1)S(1)}, bf16[512,768]{1,0:T(8,128)(2,1)S(1)}, u32[]{:S(2)}, u32[]{:S(2)}) collective-permute-start(bf16[512,768]{1,0:T(8,128)(2,1)S(1)} %slice.18), channel_id=1, source_target_pairs={{0,2},{1,3},{2,0},{3,1},{4,6},{5,7},{6,4},{7,5},{8,10},{9,11},{10,... | collective-permute-start | bytes 2359304 | tf_op jit(solution)/shard_map/ppermute | solution.py:31
  5.8 35.5 %collective-permute-start.10 = (bf16[512,768]{1,0:T(8,128)(2,1)S(1)}, bf16[512,768]{1,0:T(8,128)(2,1)S(1)}, u32[]{:S(2)}, u32[]{:S(2)}) collective-permute-start(bf16[512,768]{1,0:T(8,128)(2,1)S(1)} %slice.19), channel_id=1, source_target_pairs={{4,0},{8,4},{12,8},{16,12},{20,16},{24,20},{28,24},{5,1},{9,5},{13... | collective-permute-start | bytes 2359304 | tf_op jit(solution)/shard_map/ppermute | solution.py:37
  7.1 34.2 %collective-permute-start.14 = (bf16[512,768]{1,0:T(8,128)(2,1)S(1)}, bf16[512,768]{1,0:T(8,128)(2,1)S(1)}, u32[]{:S(2)}, u32[]{:S(2)}) collective-permute-start(bf16[512,768]{1,0:T(8,128)(2,1)S(1)} %slice.19), channel_id=1, source_target_pairs={{0,2},{1,3},{2,0},{3,1},{4,6},{5,7},{6,4},{7,5},{8,10},{9,11},{10,... | collective-permute-start | bytes 2359304 | tf_op jit(solution)/shard_map/ppermute | solution.py:31
  24.7 8.5 %collective-permute-start.12 = (bf16[256,768]{1,0:T(8,128)(2,1)S(1)}, bf16[256,768]{1,0:T(8,128)(2,1)S(1)}, u32[]{:S(2)}, u32[]{:S(2)}) collective-permute-start(bf16[256,768]{1,0:T(8,128)(2,1)S(1)} %get-tuple-element.152), channel_id=1, source_target_pairs={{0,1},{1,0},{2,3},{3,2},{4,5},{5,4},{6,7},{7,6},{8,9},{9,8},{10,11... | collective-permute-start | bytes 1179656 | tf_op jit(solution)/shard_map/ppermute | solution.py:31
  24.8 8.5 %collective-permute-start.13 = (bf16[256,768]{1,0:T(8,128)(2,1)S(1)}, bf16[256,768]{1,0:T(8,128)(2,1)S(1)}, u32[]{:S(2)}, u32[]{:S(2)}) collective-permute-start(bf16[256,768]{1,0:T(8,128)(2,1)S(1)} %get-tuple-element.153), channel_id=1, source_target_pairs={{0,1},{1,0},{2,3},{3,2},{4,5},{5,4},{6,7},{7,6},{8,9},{9,8},{10,11... | collective-permute-start | bytes 1179656 | tf_op jit(solution)/shard_map/ppermute | solution.py:31
  25.3 10.2 %collective-permute-start.11 = (bf16[80,1024]{1,0:T(8,128)(2,1)S(1)}, bf16[80,1024]{1,0:T(8,128)(2,1)S(1)}, u32[]{:S(2)}, u32[]{:S(2)}) collective-permute-start(bf16[80,1024]{1,0:T(8,128)(2,1)S(1)} %opening.1.refs_4_), channel_id=1, source_target_pairs={{0,1},{1,0},{2,3},{3,2},{4,5},{5,4},{6,7},{7,6},{8,9},{9,8},{10,11... | collective-permute-start | bytes 491528 | tf_op jit(solution)/shard_map/ppermute | solution.py:31
  41.3 3.8 %collective-permute-start.15 = (bf16[512,768]{1,0:T(8,128)(2,1)S(1)}, bf16[512,768]{1,0:T(8,128)(2,1)S(1)}, u32[]{:S(2)}, u32[]{:S(2)}) collective-permute-start(bf16[512,768]{1,0:T(8,128)(2,1)S(1)} %collective-permute-done.14.refs_1_), channel_id=1, source_target_pairs={{0,1},{1,0},{2,3},{3,2},{4,5},{5,4},{6,7},{7,6},{8,9},{9,8},{10,11... | collective-permute-start | bytes 2359304 | tf_op jit(solution)/shard_map/ppermute | solution.py:31
  41.3 9.1 %collective-permute-start.16 = (bf16[80,1024]{1,0:T(8,128)(2,1)S(1)}, bf16[80,1024]{1,0:T(8,128)(2,1)S(1)}, u32[]{:S(2)}, u32[]{:S(2)}) collective-permute-start(bf16[80,1024]{1,0:T(8,128)(2,1)S(1)} %opening.1.refs_4_), channel_id=1, source_target_pairs={{0,2},{1,3},{2,0},{3,1},{4,6},{5,7},{6,4},{7,5},{8,10},{9,11},{10,... | collective-permute-start | bytes 491528 | tf_op jit(solution)/shard_map/ppermute | solution.py:31
  43.1 10.1 %collective-permute-start.18 = (bf16[80,1024]{1,0:T(8,128)(2,1)S(1)}, bf16[80,1024]{1,0:T(8,128)(2,1)S(1)}, u32[]{:S(2)}, u32[]{:S(2)}) collective-permute-start(bf16[80,1024]{1,0:T(8,128)(2,1)S(1)} %opening.1.refs_4_), channel_id=1, source_target_pairs={{4,0},{8,4},{12,8},{16,12},{20,16},{24,20},{28,24},{5,1},{9,5},{13... | collective-permute-start | bytes 491528 | tf_op jit(solution)/shard_map/ppermute | solution.py:37
  50.5 2.7 %collective-permute-start.17 = (bf16[80,1024]{1,0:T(8,128)(2,1)S(1)}, bf16[80,1024]{1,0:T(8,128)(2,1)S(1)}, u32[]{:S(2)}, u32[]{:S(2)}) collective-permute-start(bf16[80,1024]{1,0:T(8,128)(2,1)S(1)} %collective-permute-done.16.refs_4_), channel_id=1, source_target_pairs={{0,1},{1,0},{2,3},{3,2},{4,5},{5,4},{6,7},{7,6},{8,9},{9,8},{10,11... | collective-permute-start | bytes 491528 | tf_op jit(solution)/shard_map/ppermute | solution.py:31
  57.2 2.1 %collective-permute-start.19 = (f32[4,72,512]{2,1,0:T(8,128)S(1)}, f32[4,72,512]{2,1,0:T(8,128)S(1)}, u32[]{:S(2)}, u32[]{:S(2)}) collective-permute-start(f32[4,72,512]{2,1,0:T(8,128)S(1)} %get-tuple-element.127), channel_id=1, source_target_pairs={{0,1},{1,0},{2,3},{3,2},{4,5},{5,4},{6,7},{7,6},{8,9},{9,8},{10,11... | collective-permute-start | bytes 1769480 | tf_op jit(solution)/shard_map/ppermute | solution.py:31
  57.3 8.4 %collective-permute-start.20 = (f32[2,72,512]{2,1,0:T(8,128)S(1)}, f32[2,72,512]{2,1,0:T(8,128)S(1)}, u32[]{:S(2)}, u32[]{:S(2)}) collective-permute-start(f32[2,72,512]{2,1,0:T(8,128)S(1)} %get-tuple-element.130), channel_id=1, source_target_pairs={{0,4},{4,8},{8,12},{12,16},{16,20},{20,24},{24,28},{1,5},{5,9},{9,... | collective-permute-start | bytes 884744 | tf_op jit(solution)/shard_map/ppermute | solution.py:37
  59.3 9.1 %collective-permute-start.21 = (f32[2,72,512]{2,1,0:T(8,128)S(1)}, f32[2,72,512]{2,1,0:T(8,128)S(1)}, u32[]{:S(2)}, u32[]{:S(2)}) collective-permute-start(f32[2,72,512]{2,1,0:T(8,128)S(1)} %slice_add_fusion), channel_id=1, source_target_pairs={{0,2},{1,3},{2,0},{3,1},{4,6},{5,7},{6,4},{7,5},{8,10},{9,11},{10,... | collective-permute-start | bytes 884744 | tf_op jit(solution)/shard_map/ppermute | solution.py:31
  69.4 2.7 %collective-permute-start.22 = (bf16[128,1024]{1,0:T(8,128)(2,1)S(1)}, bf16[128,1024]{1,0:T(8,128)(2,1)S(1)}, u32[]{:S(2)}, u32[]{:S(2)}) collective-permute-start(bf16[128,1024]{1,0:T(8,128)(2,1)S(1)} %get-tuple-element.132.refs_4_), channel_id=1, source_target_pairs={{0,1},{1,0},{2,3},{3,2},{4,5},{5,4},{6,7},{7,6},{8,9},{9,8},{10,11... | collective-permute-start | bytes 786440 | tf_op jit(solution)/shard_map/ppermute | solution.py:31
  69.5 8.7 %collective-permute-start.23 = (bf16[128,1024]{1,0:T(8,128)(2,1)S(1)}, bf16[128,1024]{1,0:T(8,128)(2,1)S(1)}, u32[]{:S(2)}, u32[]{:S(2)}) collective-permute-start(bf16[128,1024]{1,0:T(8,128)(2,1)S(1)} %get-tuple-element.132.refs_4_), channel_id=1, source_target_pairs={{0,2},{1,3},{2,0},{3,1},{4,6},{5,7},{6,4},{7,5},{8,10},{9,11},{10,... | collective-permute-start | bytes 786440 | tf_op jit(solution)/shard_map/ppermute | solution.py:31
  70.8 10.3 %collective-permute-start.25 = (bf16[128,1024]{1,0:T(8,128)(2,1)S(1)}, bf16[128,1024]{1,0:T(8,128)(2,1)S(1)}, u32[]{:S(2)}, u32[]{:S(2)}) collective-permute-start(bf16[128,1024]{1,0:T(8,128)(2,1)S(1)} %get-tuple-element.132.refs_4_), channel_id=1, source_target_pairs={{4,0},{8,4},{12,8},{16,12},{20,16},{24,20},{28,24},{5,1},{9,5},{13... | collective-permute-start | bytes 786440 | tf_op jit(solution)/shard_map/ppermute | solution.py:37
  78.2 2.9 %collective-permute-start.24 = (bf16[128,1024]{1,0:T(8,128)(2,1)S(1)}, bf16[128,1024]{1,0:T(8,128)(2,1)S(1)}, u32[]{:S(2)}, u32[]{:S(2)}) collective-permute-start(bf16[128,1024]{1,0:T(8,128)(2,1)S(1)} %collective-permute-done.23.refs_4_), channel_id=1, source_target_pairs={{0,1},{1,0},{2,3},{3,2},{4,5},{5,4},{6,7},{7,6},{8,9},{9,8},{10,11... | collective-permute-start | bytes 786440 | tf_op jit(solution)/shard_map/ppermute | solution.py:31
  85.2 2.0 %collective-permute-start.26 = (f32[4,64,512]{2,1,0:T(8,128)S(1)}, f32[4,64,512]{2,1,0:T(8,128)S(1)}, u32[]{:S(2)}, u32[]{:S(2)}) collective-permute-start(f32[4,64,512]{2,1,0:T(8,128)S(1)} %get-tuple-element.139), channel_id=1, source_target_pairs={{0,1},{1,0},{2,3},{3,2},{4,5},{5,4},{6,7},{7,6},{8,9},{9,8},{10,11... | collective-permute-start | bytes 1572872 | tf_op jit(solution)/shard_map/ppermute | solution.py:31
  85.3 7.8 %collective-permute-start.27 = (f32[2,64,512]{2,1,0:T(8,128)S(1)}, f32[2,64,512]{2,1,0:T(8,128)S(1)}, u32[]{:S(2)}, u32[]{:S(2)}) collective-permute-start(f32[2,64,512]{2,1,0:T(8,128)S(1)} %get-tuple-element.142), channel_id=1, source_target_pairs={{0,4},{4,8},{8,12},{12,16},{16,20},{20,24},{24,28},{1,5},{5,9},{9,... | collective-permute-start | bytes 786440 | tf_op jit(solution)/shard_map/ppermute | solution.py:37
  87.2 8.4 %collective-permute-start.28 = (f32[2,64,512]{2,1,0:T(8,128)S(1)}, f32[2,64,512]{2,1,0:T(8,128)S(1)}, u32[]{:S(2)}, u32[]{:S(2)}) collective-permute-start(f32[2,64,512]{2,1,0:T(8,128)S(1)} %slice_add_fusion.1), channel_id=1, source_target_pairs={{0,2},{1,3},{2,0},{3,1},{4,6},{5,7},{6,4},{7,5},{8,10},{9,11},{10,... | collective-permute-start | bytes 786440 | tf_op jit(solution)/shard_map/ppermute | solution.py:31
  96.7 1.3 %collective-permute-start.29 = (f32[64,128]{1,0:T(8,128)S(1)}, f32[64,128]{1,0:T(8,128)S(1)}, u32[]{:S(2)}, u32[]{:S(2)}) collective-permute-start(f32[64,128]{1,0:T(8,128)S(1)} %get-tuple-element.147), channel_id=1, source_target_pairs={{0,1},{1,0},{2,3},{3,2},{4,5},{5,4},{6,7},{7,6},{8,9},{9,8},{10,11... | collective-permute-start | bytes 98312 | tf_op jit(solution)/shard_map/ppermute | solution.py:673
  98.0 3.9 %collective-permute-start.30 = (f32[64,128]{1,0:T(8,128)S(1)}, f32[64,128]{1,0:T(8,128)S(1)}, u32[]{:S(2)}, u32[]{:S(2)}) collective-permute-start(f32[64,128]{1,0:T(8,128)S(1)} %add.50), channel_id=1, source_target_pairs={{0,2},{1,3},{2,0},{3,1},{4,6},{5,7},{6,4},{7,5},{8,10},{9,11},{10,... | collective-permute-start | bytes 98312 | tf_op jit(solution)/shard_map/ppermute | solution.py:673
  99.0 4.1 %collective-permute-start.31 = (f32[64,128]{1,0:T(8,128)S(1)}, f32[64,128]{1,0:T(8,128)S(1)}, u32[]{:S(2)}, u32[]{:S(2)}) collective-permute-start(f32[64,128]{1,0:T(8,128)S(1)} %add.50), channel_id=1, source_target_pairs={{0,4},{1,5},{2,6},{3,7},{4,0},{5,1},{6,2},{7,3},{8,12},{9,13},{10,... | collective-permute-start | bytes 98312 | tf_op jit(solution)/shard_map/ppermute | solution.py:673
  99.3 4.8 %collective-permute-start.32 = (f32[64,128]{1,0:T(8,128)S(1)}, f32[64,128]{1,0:T(8,128)S(1)}, u32[]{:S(2)}, u32[]{:S(2)}) collective-permute-start(f32[64,128]{1,0:T(8,128)S(1)} %add.50), channel_id=1, source_target_pairs={{0,6},{1,7},{2,4},{3,5},{4,2},{5,3},{6,0},{7,1},{8,14},{9,15},{10,... | collective-permute-start | bytes 98312 | tf_op jit(solution)/shard_map/ppermute | solution.py:673
  104.1 9.6 %collective-permute-start.33 = (f32[64,128]{1,0:T(8,128)S(1)}, f32[64,128]{1,0:T(8,128)S(1)}, u32[]{:S(2)}, u32[]{:S(2)}) collective-permute-start(f32[64,128]{1,0:T(8,128)S(1)} %add_add_fusion.3), channel_id=1, source_target_pairs={{0,8},{1,9},{2,10},{3,11},{4,12},{5,13},{6,14},{7,15},{8,0},{9,1},... | collective-permute-start | bytes 98312 | tf_op jit(solution)/shard_map/ppermute | solution.py:673
  110.2 4.8 %collective-permute-start.34 = (f32[64,128]{1,0:T(8,128)S(1)}, f32[64,128]{1,0:T(8,128)S(1)}, u32[]{:S(2)}, u32[]{:S(2)}) collective-permute-start(f32[64,128]{1,0:T(8,128)S(1)} %add_add_fusion.3), channel_id=1, source_target_pairs={{0,16},{1,17},{2,18},{3,19},{4,20},{5,21},{6,22},{7,23},{8,24},{9,... | collective-permute-start | bytes 98312 | tf_op jit(solution)/shard_map/ppermute | solution.py:673
  112.3 5.7 %collective-permute-start.35 = (f32[64,128]{1,0:T(8,128)S(1)}, f32[64,128]{1,0:T(8,128)S(1)}, u32[]{:S(2)}, u32[]{:S(2)}) collective-permute-start(f32[64,128]{1,0:T(8,128)S(1)} %add_add_fusion.3), channel_id=1, source_target_pairs={{0,24},{1,25},{2,26},{3,27},{4,28},{5,29},{6,30},{7,31},{8,16},{9,... | collective-permute-start | bytes 98312 | tf_op jit(solution)/shard_map/ppermute | solution.py:673

commit v3 on v2

--- a/solution.py
+++ b/solution.py
@@ -700,8 +700,7 @@
     chunks = [first_chunk, rest[half:]]
     far = [from_behind(chunk, "blk", -1) for chunk in chunks]
     crossed = [gather_far_bits(chunk) for chunk in chunks]
-    begin, mate = lax.optimization_barrier((start, mate))
-    vec = opening(begin, counts)
+    vec = opening(start, counts)
     tied = lax.optimization_barrier((vec, n, rows, cols, far[0], *crossed[0].values()))
     vec, n, rows, cols, far[0] = tied[:5]
     crossed[0] = dict(zip(crossed[0], tied[5:]))

time: 125 us -> 126 us (level)
  starting transfers between devices: 32 us -> 36.8 us
  waiting for transfers between devices: 32 us -> 28.4 us
    ppermute x6, starting transfers between devices: 7.99 us -> 14.6 us  [from_behind(): lax.ppermute(value, axis, [(source, source + steps) for source in range(i...]
    ppermute x7, starting transfers between devices: 13.1 us -> 9.83 us  [all_sum(): lax.ppermute(value, ('blk', 'grp'), [(source, source ^ move) for source i...]
    ppermute x6, waiting for transfers between devices: 14.7 us -> 11.7 us  [from_behind(): lax.ppermute(value, axis, [(source, source + steps) for source in range(i...]
    ppermute x16, starting transfers between devices: 10.9 us -> 12.4 us  [swap(): lax.ppermute(value, axis, [(source, source ^ bit) for source in range(cou...]
  transfers between devices with their start and end apart: 29 -> 29, of which waited for: 16 -> 16; matrix products, arithmetic and copies ran while one was open for 0% -> 0% of each run, Pallas kernels for 33% -> 35%
where the time goes in v3:
time: 126 us
  Pallas kernels  57.4 us (46%)
  starting transfers between devices  36.8 us (29%)
  waiting for transfers between devices  28.4 us (23%)
  between operations  1.64 us (1%)
  local copies, waits for them, and re-layouts  1.44 us (1%)
    pallas_call x7, Pallas kernels, products(): call(*entries, *[vecs[first] for first in firsts], tiles, *begun)  18 us
    pallas_call x4, Pallas kernels, build_tiles(): pl.pallas_call(kernel, out_shape=shapes, in_specs=[spec(SMEM)] * len(scal...  16.2 us
    pallas_call x1, Pallas kernels, listing(): pl.pallas_call(functools.partial(listing_kernel, group, cap, blocks_dev),...  14.7 us
    ppermute x6, starting transfers between devices, from_behind(): lax.ppermute(value, axis, [(source, source + steps) for source in range(i...  14.6 us
    ppermute x16, starting transfers between devices, swap(): lax.ppermute(value, axis, [(source, source ^ bit) for source in range(cou...  12.4 us
    ppermute x6, waiting for transfers between devices, from_behind(): lax.ppermute(value, axis, [(source, source + steps) for source in range(i...  11.7 us
    ppermute x7, starting transfers between devices, all_sum(): lax.ppermute(value, ('blk', 'grp'), [(source, source ^ move) for source i...  9.83 us
    ppermute x16, waiting for transfers between devices, swap(): lax.ppermute(value, axis, [(source, source ^ bit) for source in range(cou...  8.63 us
  transfers between devices with their start and end apart: 29, of which 16 were waited for; matrix products, arithmetic and copies ran while one was open for 0% of the time, Pallas kernels for 35%

profile of v3, /device:TPU:0, one launch (start us, length us, event | category | flops | bytes accessed | tf_op | source)
XLA Modules:
  0.0 125.8 jit_solution(10404982678476360041)
XLA Ops:
  0.0 1.3 %slice.18 = bf16[512,768]{1,0:T(8,128)(2,1)S(1)} slice(bf16[1024,768]{1,0:T(8,128)(2,1)} %refs_3_.1), slice={[0:512], [0:768]} | slice | bytes 1572864 | tf_op jit(solution)/shard_map/slice | solution.py:697
  1.3 1.3 %collective-permute-start.7 = (bf16[512,768]{1,0:T(8,128)(2,1)S(1)}, bf16[512,768]{1,0:T(8,128)(2,1)S(1)}, u32[]{:S(2)}, u32[]{:S(2)}) collective-permute-start(bf16[512,768]{1,0:T(8,128)(2,1)S(1)} %slice.18), channel_id=1, source_target_pairs={{4,0},{8,4},{12,8},{16,12},{20,16},{24,20},{28,24},{5,1},{9,5},{13... | collective-permute-start | bytes 2359304 | tf_op jit(solution)/shard_map/ppermute | solution.py:37
  2.6 3.0 %collective-permute-start.8 = (bf16[512,768]{1,0:T(8,128)(2,1)S(1)}, bf16[512,768]{1,0:T(8,128)(2,1)S(1)}, u32[]{:S(2)}, u32[]{:S(2)}) collective-permute-start(bf16[512,768]{1,0:T(8,128)(2,1)S(1)} %slice.18), channel_id=1, source_target_pairs={{0,2},{1,3},{2,0},{3,1},{4,6},{5,7},{6,4},{7,5},{8,10},{9,11},{10,... | collective-permute-start | bytes 2359304 | tf_op jit(solution)/shard_map/ppermute | solution.py:31
  5.7 0.0 collective-permute-start.13
  5.7 0.1 slice.19
  5.7 0.2 collective-permute-start.14
  5.9 1.3 %collective-permute-start.9 = (bf16[512,768]{1,0:T(8,128)(2,1)S(1)}, bf16[512,768]{1,0:T(8,128)(2,1)S(1)}, u32[]{:S(2)}, u32[]{:S(2)}) collective-permute-start(bf16[512,768]{1,0:T(8,128)(2,1)S(1)} %slice.19), channel_id=1, source_target_pairs={{4,0},{8,4},{12,8},{16,12},{20,16},{24,20},{28,24},{5,1},{9,5},{13... | collective-permute-start | bytes 2359304 | tf_op jit(solution)/shard_map/ppermute | solution.py:37
  7.8 0.6 opening.1.refs_4_
  8.4 14.7 %listing.1 = (s32[16]{0:T(128)S(1)}, s32[16]{0:T(128)S(1)}, s32[4]{0:T(128)S(1)}, s32[32]{0:T(128)S(1)}, s32[32]{0:T(128)S(1)}, /*index=5*/s32[32]{0:T(128)S(1)}, s32[9]{0:T(128)S(1)}) custom-call(s32[64]{0:T(128)S(1)} %copy-done.3, s32[64]{0:T(128)S(1)} %copy-done.4, s32[1]{0:T(128)S(6)} %copy.31.live), custom_call_target="tpu_custom_call" | custom-call | flops 1048576 | bytes 1024 | tf_op jit(solution)/shard_map/listing/pallas_call | solution.py:219
  23.1 1.5 %collective-permute-done.7.refs_5_ = bf16[512,768]{1,0:T(8,128)(2,1)S(1)} collective-permute-done((bf16[512,768]{1,0:T(8,128)(2,1)S(1)}, bf16[512,768]{1,0:T(8,128)(2,1)S(1)}, u32[]{:S(2)}, u32[]{:S(2)}) %collective-permute-start.7) | collective-permute-done | bytes 786464 | tf_op jit(solution)/shard_map/ppermute | solution.py:37
  24.6 0.1 fusion
  24.6 0.1 collective-permute-start.11
  24.7 0.5 collective-permute-start.12
  25.2 1.2 collective-permute-done.11
  26.4 0.1 collective-permute-start.10
  26.6 0.4 collective-permute-done.12
  27.0 0.1 pad_maximum_fusion.refs_3_
  27.1 9.0 %first_tiles.1 = (bf16[5120,768]{1,0:T(8,128)(2,1)S(1)}, f32[10,8,512]{2,1,0:T(8,128)S(1)}, f32[8,512,128]{2,1,0:T(8,128)S(1)}, bf16[17,512,512]{2,1,0:T(8,128)(2,1)S(1)}) custom-call(s32[4]{0:T(128)S(1)} %get-tuple-element.90.refs_0_, s32[16]{0:T(128)S(1)} %get-tuple-element.91.refs_1_, s32[16]{0:T(128)S(1)} %get-tuple-element.92.refs_2_, ...), custom_call_target="tpu_custom_call" | custom-call | flops 1048576 | bytes 1048576 | tf_op jit(solution)/shard_map/first_tiles/pallas_call | solution.py:336
  36.1 1.0 second_tiles.1
  37.1 3.0 %products.7 = (f32[2,72,512]{2,1,0:T(8,128)S(1)}, f32[4,72,512]{2,1,0:T(8,128)S(1)}, f32[2,72,512]{2,1,0:T(8,128)S(1)}, f32[2,72,512]{2,1,0:T(8,128)S(1)}) custom-call(s32[32]{0:T(128)S(1)} %get-tuple-element.82.refs_0_, s32[32]{0:T(128)S(1)} %get-tuple-element.83.refs_1_, s32[32]{0:T(128)S(1)} %get-tuple-element.84.refs_2_, ...), custom_call_target="tpu_custom_call" | custom-call | flops 1048576 | bytes 1048576 | tf_op jit(solution)/shard_map/products/pallas_call | solution.py:440
  40.2 0.4 collective-permute-done.9.refs_0_
  40.6 2.1 %collective-permute-start.16 = (bf16[80,1024]{1,0:T(8,128)(2,1)S(1)}, bf16[80,1024]{1,0:T(8,128)(2,1)S(1)}, u32[]{:S(2)}, u32[]{:S(2)}) collective-permute-start(bf16[80,1024]{1,0:T(8,128)(2,1)S(1)} %opening.1.refs_4_), channel_id=1, source_target_pairs={{0,2},{1,3},{2,0},{3,1},{4,6},{5,7},{6,4},{7,5},{8,10},{9,11},{10,... | collective-permute-start | bytes 491528 | tf_op jit(solution)/shard_map/ppermute | solution.py:31
  42.7 1.3 %collective-permute-start.18 = (bf16[80,1024]{1,0:T(8,128)(2,1)S(1)}, bf16[80,1024]{1,0:T(8,128)(2,1)S(1)}, u32[]{:S(2)}, u32[]{:S(2)}) collective-permute-start(bf16[80,1024]{1,0:T(8,128)(2,1)S(1)} %opening.1.refs_4_), channel_id=1, source_target_pairs={{4,0},{8,4},{12,8},{16,12},{20,16},{24,20},{28,24},{5,1},{9,5},{13... | collective-permute-start | bytes 491528 | tf_op jit(solution)/shard_map/ppermute | solution.py:37
  44.0 0.8 more_blocks.1
  44.7 5.4 %last_tiles.1 = (bf16[5120,768]{1,0:T(8,128)(2,1)S(1)}, f32[10,8,512]{2,1,0:T(8,128)S(1)}, f32[8,512,128]{2,1,0:T(8,128)S(1)}, bf16[17,512,512]{2,1,0:T(8,128)(2,1)S(1)}) custom-call(s32[4]{0:T(128)S(1)} %get-tuple-element.90.refs_0_, s32[16]{0:T(128)S(1)} %get-tuple-element.91.refs_1_, ...), custom_call_target="tpu_custom_call", output_to_operand_aliasing={{0}: (4, {}), {1}: (5, {}), {2}: (6, {}), {3}: (7, {})} | custom-call | flops 4294967296 | bytes 1048576 | tf_op jit(solution)/shard_map/last_tiles/pallas_call | solution.py:336
  50.2 1.0 collective-permute-start.17
  51.2 1.3 %products.8 = (f32[2,72,512]{2,1,0:T(8,128)S(1)}, f32[4,72,512]{2,1,0:T(8,128)S(1)}, f32[2,72,512]{2,1,0:T(8,128)S(1)}, f32[2,72,512]{2,1,0:T(8,128)S(1)}) custom-call(s32[32]{0:T(128)S(1)} %get-tuple-element.82.refs_0_, s32[32]{0:T(128)S(1)} %get-tuple-element.83.refs_1_, s32[32]{0:T(128)S(1)} %get-tuple-element.84.refs_2_, ...), custom_call_target="tpu_custom_call" | custom-call | flops 1048576 | bytes 1048576 | tf_op jit(solution)/shard_map/products/pallas_call | solution.py:440
  52.5 2.8 %products.9 = (f32[4,72,512]{2,1,0:T(8,128)S(1)}, f32[2,72,512]{2,1,0:T(8,128)S(1)}, f32[2,72,512]{2,1,0:T(8,128)S(1)}) custom-call(s32[32]{0:T(128)S(1)} %get-tuple-element.82.refs_0_, s32[32]{0:T(128)S(1)} %get-tuple-element.83.refs_1_, s32[32]{0:T(128)S(1)} %get-tuple-element.84.refs_2_, s32[9]{0:T(128)S(1)} %get-tuple-element.85.refs_3_, ...), custom_call_target="tpu_custom_call" | custom-call | flops 2147483648 | bytes 1048576 | tf_op jit(solution)/shard_map/products/pallas_call | solution.py:440
  55.2 1.4 %collective-permute-start.19 = (f32[4,72,512]{2,1,0:T(8,128)S(1)}, f32[4,72,512]{2,1,0:T(8,128)S(1)}, u32[]{:S(2)}, u32[]{:S(2)}) collective-permute-start(f32[4,72,512]{2,1,0:T(8,128)S(1)} %get-tuple-element.123), channel_id=1, source_target_pairs={{0,1},{1,0},{2,3},{3,2},{4,5},{5,4},{6,7},{7,6},{8,9},{9,8},{10,11... | collective-permute-start | bytes 1769480 | tf_op jit(solution)/shard_map/ppermute | solution.py:31
  56.7 2.0 %collective-permute-start.20 = (f32[2,72,512]{2,1,0:T(8,128)S(1)}, f32[2,72,512]{2,1,0:T(8,128)S(1)}, u32[]{:S(2)}, u32[]{:S(2)}) collective-permute-start(f32[2,72,512]{2,1,0:T(8,128)S(1)} %get-tuple-element.126), channel_id=1, source_target_pairs={{0,4},{4,8},{8,12},{12,16},{16,20},{20,24},{24,28},{1,5},{5,9},{9,... | collective-permute-start | bytes 884744 | tf_op jit(solution)/shard_map/ppermute | solution.py:37
  58.7 1.4 %collective-permute-start.21 = (f32[2,72,512]{2,1,0:T(8,128)S(1)}, f32[2,72,512]{2,1,0:T(8,128)S(1)}, u32[]{:S(2)}, u32[]{:S(2)}) collective-permute-start(f32[2,72,512]{2,1,0:T(8,128)S(1)} %slice_add_fusion), channel_id=1, source_target_pairs={{0,2},{1,3},{2,0},{3,1},{4,6},{5,7},{6,4},{7,5},{8,10},{9,11},{10,... | collective-permute-start | bytes 884744 | tf_op jit(solution)/shard_map/ppermute | solution.py:31
  60.1 2.2 %products.10.refs_0_ = f32[2,72,512]{2,1,0:T(8,128)S(1)} custom-call(s32[32]{0:T(128)S(1)} %get-tuple-element.82.refs_0_, s32[32]{0:T(128)S(1)} %get-tuple-element.83.refs_1_, s32[32]{0:T(128)S(1)} %get-tuple-element.84.refs_2_, s32[9]{0:T(128)S(1)} %get-tuple-element.85.refs_3_, bf16[80,1024]{1,0:T(8,128)(2,1)S(1)} %collective-permute-done.16.refs_4_, ...), custom_call_target="tpu_custom_call" | custom-call | flops 1048576 | bytes 1048576 | tf_op jit(solution)/shard_map/products/pallas_call | solution.py:440
  62.3 3.3 %collective-permute-done.20.refs_1_ = f32[2,72,512]{2,1,0:T(8,128)S(1)} collective-permute-done((f32[2,72,512]{2,1,0:T(8,128)S(1)}, f32[2,72,512]{2,1,0:T(8,128)S(1)}, u32[]{:S(2)}, u32[]{:S(2)}) %collective-permute-start.20) | collective-permute-done | bytes 294944 | tf_op jit(solution)/shard_map/ppermute | solution.py:37
  65.5 2.4 %collective-permute-done.21.refs_3_ = f32[2,72,512]{2,1,0:T(8,128)S(1)} collective-permute-done((f32[2,72,512]{2,1,0:T(8,128)S(1)}, f32[2,72,512]{2,1,0:T(8,128)S(1)}, u32[]{:S(2)}, u32[]{:S(2)}) %collective-permute-start.21) | collective-permute-done | bytes 294944 | tf_op jit(solution)/shard_map/ppermute | solution.py:31
  67.9 0.9 scaled_gram.2
  68.8 0.1 collective-permute-start.22
  68.9 1.5 %collective-permute-start.23 = (bf16[128,1024]{1,0:T(8,128)(2,1)S(1)}, bf16[128,1024]{1,0:T(8,128)(2,1)S(1)}, u32[]{:S(2)}, u32[]{:S(2)}) collective-permute-start(bf16[128,1024]{1,0:T(8,128)(2,1)S(1)} %get-tuple-element.128.refs_4_), channel_id=1, source_target_pairs={{0,2},{1,3},{2,0},{3,1},{4,6},{5,7},{6,4},{7,5},{8,10},{9,11},{10,... | collective-permute-start | bytes 786440 | tf_op jit(solution)/shard_map/ppermute | solution.py:31
  70.5 1.3 %collective-permute-start.25 = (bf16[128,1024]{1,0:T(8,128)(2,1)S(1)}, bf16[128,1024]{1,0:T(8,128)(2,1)S(1)}, u32[]{:S(2)}, u32[]{:S(2)}) collective-permute-start(bf16[128,1024]{1,0:T(8,128)(2,1)S(1)} %get-tuple-element.128.refs_4_), channel_id=1, source_target_pairs={{4,0},{8,4},{12,8},{16,12},{20,16},{24,20},{28,24},{5,1},{9,5},{13... | collective-permute-start | bytes 786440 | tf_op jit(solution)/shard_map/ppermute | solution.py:37
  71.8 3.6 %products.11 = (f32[2,64,512]{2,1,0:T(8,128)S(1)}, f32[4,64,512]{2,1,0:T(8,128)S(1)}, f32[2,64,512]{2,1,0:T(8,128)S(1)}, f32[2,64,512]{2,1,0:T(8,128)S(1)}) custom-call(s32[32]{0:T(128)S(1)} %get-tuple-element.82.refs_0_, s32[32]{0:T(128)S(1)} %get-tuple-element.83.refs_1_, s32[32]{0:T(128)S(1)} %get-tuple-element.84.refs_2_, ...), custom_call_target="tpu_custom_call" | custom-call | flops 1048576 | bytes 1048576 | tf_op jit(solution)/shard_map/products/pallas_call | solution.py:440
  75.4 2.2 %collective-permute-done.23.refs_4_ = bf16[128,1024]{1,0:T(8,128)(2,1)S(1)} collective-permute-done((bf16[128,1024]{1,0:T(8,128)(2,1)S(1)}, bf16[128,1024]{1,0:T(8,128)(2,1)S(1)}, u32[]{:S(2)}, u32[]{:S(2)}) %collective-permute-start.23) | collective-permute-done | bytes 262176 | tf_op jit(solution)/shard_map/ppermute | solution.py:31
  77.6 3.1 %collective-permute-done.25.refs_6_ = bf16[128,1024]{1,0:T(8,128)(2,1)S(1)} collective-permute-done((bf16[128,1024]{1,0:T(8,128)(2,1)S(1)}, bf16[128,1024]{1,0:T(8,128)(2,1)S(1)}, u32[]{:S(2)}, u32[]{:S(2)}) %collective-permute-start.25) | collective-permute-done | bytes 262176 | tf_op jit(solution)/shard_map/ppermute | solution.py:37
  80.7 2.8 %products.12 = (f32[4,64,512]{2,1,0:T(8,128)S(1)}, f32[2,64,512]{2,1,0:T(8,128)S(1)}, f32[2,64,512]{2,1,0:T(8,128)S(1)}) custom-call(s32[32]{0:T(128)S(1)} %get-tuple-element.82.refs_0_, s32[32]{0:T(128)S(1)} %get-tuple-element.83.refs_1_, s32[32]{0:T(128)S(1)} %get-tuple-element.84.refs_2_, s32[9]{0:T(128)S(1)} %get-tuple-element.85.refs_3_, ...), custom_call_target="tpu_custom_call" | custom-call | flops 2147483648 | bytes 1048576 | tf_op jit(solution)/shard_map/products/pallas_call | solution.py:440
  83.6 0.7 collective-permute-start.26
  84.2 7.5 %collective-permute-start.27 = (f32[2,64,512]{2,1,0:T(8,128)S(1)}, f32[2,64,512]{2,1,0:T(8,128)S(1)}, u32[]{:S(2)}, u32[]{:S(2)}) collective-permute-start(f32[2,64,512]{2,1,0:T(8,128)S(1)} %get-tuple-element.138), channel_id=1, source_target_pairs={{0,4},{4,8},{8,12},{12,16},{16,20},{20,24},{24,28},{1,5},{5,9},{9,... | collective-permute-start | bytes 786440 | tf_op jit(solution)/shard_map/ppermute | solution.py:37
  91.8 0.3 collective-permute-start.28
  92.1 2.3 %products.13.refs_0_ = f32[2,64,512]{2,1,0:T(8,128)S(1)} custom-call(s32[32]{0:T(128)S(1)} %get-tuple-element.82.refs_0_, s32[32]{0:T(128)S(1)} %get-tuple-element.83.refs_1_, s32[32]{0:T(128)S(1)} %get-tuple-element.84.refs_2_, s32[9]{0:T(128)S(1)} %get-tuple-element.85.refs_3_, bf16[128,1024]{1,0:T(8,128)(2,1)S(1)} %collective-permute-done.23.refs_4_, ...), custom_call_target="tpu_custom_call" | custom-call | flops 1048576 | bytes 1048576 | tf_op jit(solution)/shard_map/products/pallas_call | solution.py:440
  94.4 3.5 %collective-permute-done.27.refs_1_ = f32[2,64,512]{2,1,0:T(8,128)S(1)} collective-permute-done((f32[2,64,512]{2,1,0:T(8,128)S(1)}, f32[2,64,512]{2,1,0:T(8,128)S(1)}, u32[]{:S(2)}, u32[]{:S(2)}) %collective-permute-start.27) | collective-permute-done | bytes 262176 | tf_op jit(solution)/shard_map/ppermute | solution.py:37
  97.9 2.4 %collective-permute-done.28.refs_3_ = f32[2,64,512]{2,1,0:T(8,128)S(1)} collective-permute-done((f32[2,64,512]{2,1,0:T(8,128)S(1)}, f32[2,64,512]{2,1,0:T(8,128)S(1)}, u32[]{:S(2)}, u32[]{:S(2)}) %collective-permute-start.28) | collective-permute-done | bytes 262176 | tf_op jit(solution)/shard_map/ppermute | solution.py:31
  100.2 1.0 scaled_gram.3
  101.3 0.1 collective-permute-start.29
  101.3 1.2 collective-permute-done.29
  102.5 0.3 collective-permute-start.30
  102.8 0.9 collective-permute-start.31
  103.7 2.3 %collective-permute-start.32 = (f32[64,128]{1,0:T(8,128)S(1)}, f32[64,128]{1,0:T(8,128)S(1)}, u32[]{:S(2)}, u32[]{:S(2)}) collective-permute-start(f32[64,128]{1,0:T(8,128)S(1)} %add.50), channel_id=1, source_target_pairs={{0,6},{1,7},{2,4},{3,5},{4,2},{5,3},{6,0},{7,1},{8,14},{9,15},{10,... | collective-permute-start | bytes 98312 | tf_op jit(solution)/shard_map/ppermute | solution.py:673
  106.0 0.4 collective-permute-done.30
  106.4 0.3 collective-permute-done.31
  106.7 1.8 %collective-permute-done.32 = f32[64,128]{1,0:T(8,128)S(1)} collective-permute-done((f32[64,128]{1,0:T(8,128)S(1)}, f32[64,128]{1,0:T(8,128)S(1)}, u32[]{:S(2)}, u32[]{:S(2)}) %collective-permute-start.32) | collective-permute-done | bytes 32800 | tf_op jit(solution)/shard_map/ppermute | solution.py:673
  108.6 2.2 %collective-permute-start.33 = (f32[64,128]{1,0:T(8,128)S(1)}, f32[64,128]{1,0:T(8,128)S(1)}, u32[]{:S(2)}, u32[]{:S(2)}) collective-permute-start(f32[64,128]{1,0:T(8,128)S(1)} %add_add_fusion.3), channel_id=1, source_target_pairs={{0,8},{1,9},{2,10},{3,11},{4,12},{5,13},{6,14},{7,15},{8,0},{9,1},... | collective-permute-start | bytes 98312 | tf_op jit(solution)/shard_map/ppermute | solution.py:673
  110.7 2.7 %collective-permute-start.34 = (f32[64,128]{1,0:T(8,128)S(1)}, f32[64,128]{1,0:T(8,128)S(1)}, u32[]{:S(2)}, u32[]{:S(2)}) collective-permute-start(f32[64,128]{1,0:T(8,128)S(1)} %add_add_fusion.3), channel_id=1, source_target_pairs={{0,16},{1,17},{2,18},{3,19},{4,20},{5,21},{6,22},{7,23},{8,24},{9,... | collective-permute-start | bytes 98312 | tf_op jit(solution)/shard_map/ppermute | solution.py:673
  113.5 1.4 %collective-permute-start.35 = (f32[64,128]{1,0:T(8,128)S(1)}, f32[64,128]{1,0:T(8,128)S(1)}, u32[]{:S(2)}, u32[]{:S(2)}) collective-permute-start(f32[64,128]{1,0:T(8,128)S(1)} %add_add_fusion.3), channel_id=1, source_target_pairs={{0,24},{1,25},{2,26},{3,27},{4,28},{5,29},{6,30},{7,31},{8,16},{9,... | collective-permute-start | bytes 98312 | tf_op jit(solution)/shard_map/ppermute | solution.py:673
  114.8 0.9 collective-permute-done.34
  115.7 3.4 %collective-permute-done.35 = f32[64,128]{1,0:T(8,128)S(1)} collective-permute-done((f32[64,128]{1,0:T(8,128)S(1)}, f32[64,128]{1,0:T(8,128)S(1)}, u32[]{:S(2)}, u32[]{:S(2)}) %collective-permute-start.35) | collective-permute-done | bytes 32800 | tf_op jit(solution)/shard_map/ppermute | solution.py:673
  119.2 4.9 %factors.1 = (f32[64,64]{1,0:T(8,128)S(1)}, f32[64,64]{1,0:T(8,128)S(1)}, s32[1]{0:T(128)}) custom-call(f32[64,128]{1,0:T(8,128)S(1)} %add_add_fusion.2.grams), custom_call_target="tpu_custom_call" | custom-call | flops 1073741824 | bytes 65536 | tf_op jit(solution)/shard_map/factors/pallas_call | solution.py:611
  124.8 1.1 applied.3
  (31 shorter events, 0.2 us)
Async XLA Ops:
  0.0 5.7 %copy-start = (bf16[1024,768]{1,0:T(8,128)(2,1)S(1)}, bf16[1024,768]{1,0:T(8,128)(2,1)}, u32[]{:S(2)}) copy-start(bf16[1024,768]{1,0:T(8,128)(2,1)} %refs_3_.1) | copy-start | bytes 4718596
  0.0 7.8 %copy-start.1 = (f32[64,1024]{1,0:T(8,128)S(1)}, f32[64,1024]{1,0:T(8,128)}, u32[]{:S(2)}) copy-start(f32[64,1024]{1,0:T(8,128)} %start.1) | copy-start | bytes 786436
  0.0 7.8 %copy-start.2 = (s32[2]{0:T(128)S(1)}, s32[2]{0:T(128)}, u32[]{:S(2)}) copy-start(s32[2]{0:T(128)} %count_ref.3) | copy-start | bytes 28
  0.0 8.4 %copy-start.3 = (s32[64]{0:T(128)S(1)}, s32[64]{0:T(128)}, u32[]{:S(2)}) copy-start(s32[64]{0:T(128)} %rows.1) | copy-start | bytes 772
  0.0 8.4 %copy-start.4 = (s32[64]{0:T(128)S(1)}, s32[64]{0:T(128)}, u32[]{:S(2)}) copy-start(s32[64]{0:T(128)} %cols.1) | copy-start | bytes 772
  1.3 23.2 %collective-permute-start.7 = (bf16[512,768]{1,0:T(8,128)(2,1)S(1)}, bf16[512,768]{1,0:T(8,128)(2,1)S(1)}, u32[]{:S(2)}, u32[]{:S(2)}) collective-permute-start(bf16[512,768]{1,0:T(8,128)(2,1)S(1)} %slice.18), channel_id=1, source_target_pairs={{4,0},{8,4},{12,8},{16,12},{20,16},{24,20},{28,24},{5,1},{9,5},{13... | collective-permute-start | bytes 2359304 | tf_op jit(solution)/shard_map/ppermute | solution.py:37
  2.6 22.0 %collective-permute-start.8 = (bf16[512,768]{1,0:T(8,128)(2,1)S(1)}, bf16[512,768]{1,0:T(8,128)(2,1)S(1)}, u32[]{:S(2)}, u32[]{:S(2)}) collective-permute-start(bf16[512,768]{1,0:T(8,128)(2,1)S(1)} %slice.18), channel_id=1, source_target_pairs={{0,2},{1,3},{2,0},{3,1},{4,6},{5,7},{6,4},{7,5},{8,10},{9,11},{10,... | collective-permute-start | bytes 2359304 | tf_op jit(solution)/shard_map/ppermute | solution.py:31
  5.7 21.4 %collective-permute-start.13 = (bf16[1024,768]{1,0:T(8,128)(2,1)}, bf16[1024,768]{1,0:T(8,128)(2,1)S(1)}, u32[]{:S(2)}, u32[]{:S(2)}) collective-permute-start(bf16[1024,768]{1,0:T(8,128)(2,1)} %refs_3_.1), channel_id=1, source_target_pairs={{0,1},{1,0},{2,3},{3,2},{4,5},{5,4},{6,7},{7,6},{8,9},{9,8},{10,11... | collective-permute-start | bytes 4718600 | tf_op jit(solution)/shard_map/ppermute | solution.py:31
  5.7 34.5 %collective-permute-start.14 = (bf16[512,768]{1,0:T(8,128)(2,1)S(1)}, bf16[512,768]{1,0:T(8,128)(2,1)S(1)}, u32[]{:S(2)}, u32[]{:S(2)}) collective-permute-start(bf16[512,768]{1,0:T(8,128)(2,1)S(1)} %slice.19), channel_id=1, source_target_pairs={{0,2},{1,3},{2,0},{3,1},{4,6},{5,7},{6,4},{7,5},{8,10},{9,11},{10,... | collective-permute-start | bytes 2359304 | tf_op jit(solution)/shard_map/ppermute | solution.py:31
  5.9 34.7 %collective-permute-start.9 = (bf16[512,768]{1,0:T(8,128)(2,1)S(1)}, bf16[512,768]{1,0:T(8,128)(2,1)S(1)}, u32[]{:S(2)}, u32[]{:S(2)}) collective-permute-start(bf16[512,768]{1,0:T(8,128)(2,1)S(1)} %slice.19), channel_id=1, source_target_pairs={{4,0},{8,4},{12,8},{16,12},{20,16},{24,20},{28,24},{5,1},{9,5},{13... | collective-permute-start | bytes 2359304 | tf_op jit(solution)/shard_map/ppermute | solution.py:37
  24.6 1.8 %collective-permute-start.11 = (bf16[256,768]{1,0:T(8,128)(2,1)S(1)}, bf16[256,768]{1,0:T(8,128)(2,1)S(1)}, u32[]{:S(2)}, u32[]{:S(2)}) collective-permute-start(bf16[256,768]{1,0:T(8,128)(2,1)S(1)} %get-tuple-element.148), channel_id=1, source_target_pairs={{0,1},{1,0},{2,3},{3,2},{4,5},{5,4},{6,7},{7,6},{8,9},{9,8},{10,11... | collective-permute-start | bytes 1179656 | tf_op jit(solution)/shard_map/ppermute | solution.py:31
  24.7 2.3 %collective-permute-start.12 = (bf16[256,768]{1,0:T(8,128)(2,1)S(1)}, bf16[256,768]{1,0:T(8,128)(2,1)S(1)}, u32[]{:S(2)}, u32[]{:S(2)}) collective-permute-start(bf16[256,768]{1,0:T(8,128)(2,1)S(1)} %get-tuple-element.149), channel_id=1, source_target_pairs={{0,1},{1,0},{2,3},{3,2},{4,5},{5,4},{6,7},{7,6},{8,9},{9,8},{10,11... | collective-permute-start | bytes 1179656 | tf_op jit(solution)/shard_map/ppermute | solution.py:31
  26.4 10.7 %collective-permute-start.10 = (bf16[80,1024]{1,0:T(8,128)(2,1)S(1)}, bf16[80,1024]{1,0:T(8,128)(2,1)S(1)}, u32[]{:S(2)}, u32[]{:S(2)}) collective-permute-start(bf16[80,1024]{1,0:T(8,128)(2,1)S(1)} %opening.1.refs_4_), channel_id=1, source_target_pairs={{0,1},{1,0},{2,3},{3,2},{4,5},{5,4},{6,7},{7,6},{8,9},{9,8},{10,11... | collective-permute-start | bytes 491528 | tf_op jit(solution)/shard_map/ppermute | solution.py:31
  40.6 4.1 %collective-permute-start.15 = (bf16[512,768]{1,0:T(8,128)(2,1)S(1)}, bf16[512,768]{1,0:T(8,128)(2,1)S(1)}, u32[]{:S(2)}, u32[]{:S(2)}) collective-permute-start(bf16[512,768]{1,0:T(8,128)(2,1)S(1)} %collective-permute-done.14.refs_1_), channel_id=1, source_target_pairs={{0,1},{1,0},{2,3},{3,2},{4,5},{5,4},{6,7},{7,6},{8,9},{9,8},{10,11... | collective-permute-start | bytes 2359304 | tf_op jit(solution)/shard_map/ppermute | solution.py:31
  40.6 9.5 %collective-permute-start.16 = (bf16[80,1024]{1,0:T(8,128)(2,1)S(1)}, bf16[80,1024]{1,0:T(8,128)(2,1)S(1)}, u32[]{:S(2)}, u32[]{:S(2)}) collective-permute-start(bf16[80,1024]{1,0:T(8,128)(2,1)S(1)} %opening.1.refs_4_), channel_id=1, source_target_pairs={{0,2},{1,3},{2,0},{3,1},{4,6},{5,7},{6,4},{7,5},{8,10},{9,11},{10,... | collective-permute-start | bytes 491528 | tf_op jit(solution)/shard_map/ppermute | solution.py:31
  42.7 9.7 %collective-permute-start.18 = (bf16[80,1024]{1,0:T(8,128)(2,1)S(1)}, bf16[80,1024]{1,0:T(8,128)(2,1)S(1)}, u32[]{:S(2)}, u32[]{:S(2)}) collective-permute-start(bf16[80,1024]{1,0:T(8,128)(2,1)S(1)} %opening.1.refs_4_), channel_id=1, source_target_pairs={{4,0},{8,4},{12,8},{16,12},{20,16},{24,20},{28,24},{5,1},{9,5},{13... | collective-permute-start | bytes 491528 | tf_op jit(solution)/shard_map/ppermute | solution.py:37
  50.2 2.3 %collective-permute-start.17 = (bf16[80,1024]{1,0:T(8,128)(2,1)S(1)}, bf16[80,1024]{1,0:T(8,128)(2,1)S(1)}, u32[]{:S(2)}, u32[]{:S(2)}) collective-permute-start(bf16[80,1024]{1,0:T(8,128)(2,1)S(1)} %collective-permute-done.16.refs_4_), channel_id=1, source_target_pairs={{0,1},{1,0},{2,3},{3,2},{4,5},{5,4},{6,7},{7,6},{8,9},{9,8},{10,11... | collective-permute-start | bytes 491528 | tf_op jit(solution)/shard_map/ppermute | solution.py:31
  55.2 3.4 %collective-permute-start.19 = (f32[4,72,512]{2,1,0:T(8,128)S(1)}, f32[4,72,512]{2,1,0:T(8,128)S(1)}, u32[]{:S(2)}, u32[]{:S(2)}) collective-permute-start(f32[4,72,512]{2,1,0:T(8,128)S(1)} %get-tuple-element.123), channel_id=1, source_target_pairs={{0,1},{1,0},{2,3},{3,2},{4,5},{5,4},{6,7},{7,6},{8,9},{9,8},{10,11... | collective-permute-start | bytes 1769480 | tf_op jit(solution)/shard_map/ppermute | solution.py:31
  56.7 8.9 %collective-permute-start.20 = (f32[2,72,512]{2,1,0:T(8,128)S(1)}, f32[2,72,512]{2,1,0:T(8,128)S(1)}, u32[]{:S(2)}, u32[]{:S(2)}) collective-permute-start(f32[2,72,512]{2,1,0:T(8,128)S(1)} %get-tuple-element.126), channel_id=1, source_target_pairs={{0,4},{4,8},{8,12},{12,16},{16,20},{20,24},{24,28},{1,5},{5,9},{9,... | collective-permute-start | bytes 884744 | tf_op jit(solution)/shard_map/ppermute | solution.py:37
  58.7 9.2 %collective-permute-start.21 = (f32[2,72,512]{2,1,0:T(8,128)S(1)}, f32[2,72,512]{2,1,0:T(8,128)S(1)}, u32[]{:S(2)}, u32[]{:S(2)}) collective-permute-start(f32[2,72,512]{2,1,0:T(8,128)S(1)} %slice_add_fusion), channel_id=1, source_target_pairs={{0,2},{1,3},{2,0},{3,1},{4,6},{5,7},{6,4},{7,5},{8,10},{9,11},{10,... | collective-permute-start | bytes 884744 | tf_op jit(solution)/shard_map/ppermute | solution.py:31
  68.8 2.9 %collective-permute-start.22 = (bf16[128,1024]{1,0:T(8,128)(2,1)S(1)}, bf16[128,1024]{1,0:T(8,128)(2,1)S(1)}, u32[]{:S(2)}, u32[]{:S(2)}) collective-permute-start(bf16[128,1024]{1,0:T(8,128)(2,1)S(1)} %get-tuple-element.128.refs_4_), channel_id=1, source_target_pairs={{0,1},{1,0},{2,3},{3,2},{4,5},{5,4},{6,7},{7,6},{8,9},{9,8},{10,11... | collective-permute-start | bytes 786440 | tf_op jit(solution)/shard_map/ppermute | solution.py:31
  68.9 8.7 %collective-permute-start.23 = (bf16[128,1024]{1,0:T(8,128)(2,1)S(1)}, bf16[128,1024]{1,0:T(8,128)(2,1)S(1)}, u32[]{:S(2)}, u32[]{:S(2)}) collective-permute-start(bf16[128,1024]{1,0:T(8,128)(2,1)S(1)} %get-tuple-element.128.refs_4_), channel_id=1, source_target_pairs={{0,2},{1,3},{2,0},{3,1},{4,6},{5,7},{6,4},{7,5},{8,10},{9,11},{10,... | collective-permute-start | bytes 786440 | tf_op jit(solution)/shard_map/ppermute | solution.py:31
  70.5 10.3 %collective-permute-start.25 = (bf16[128,1024]{1,0:T(8,128)(2,1)S(1)}, bf16[128,1024]{1,0:T(8,128)(2,1)S(1)}, u32[]{:S(2)}, u32[]{:S(2)}) collective-permute-start(bf16[128,1024]{1,0:T(8,128)(2,1)S(1)} %get-tuple-element.128.refs_4_), channel_id=1, source_target_pairs={{4,0},{8,4},{12,8},{16,12},{20,16},{24,20},{28,24},{5,1},{9,5},{13... | collective-permute-start | bytes 786440 | tf_op jit(solution)/shard_map/ppermute | solution.py:37
  77.6 3.1 %collective-permute-start.24 = (bf16[128,1024]{1,0:T(8,128)(2,1)S(1)}, bf16[128,1024]{1,0:T(8,128)(2,1)S(1)}, u32[]{:S(2)}, u32[]{:S(2)}) collective-permute-start(bf16[128,1024]{1,0:T(8,128)(2,1)S(1)} %collective-permute-done.23.refs_4_), channel_id=1, source_target_pairs={{0,1},{1,0},{2,3},{3,2},{4,5},{5,4},{6,7},{7,6},{8,9},{9,8},{10,11... | collective-permute-start | bytes 786440 | tf_op jit(solution)/shard_map/ppermute | solution.py:31
  83.6 8.2 %collective-permute-start.26 = (f32[4,64,512]{2,1,0:T(8,128)S(1)}, f32[4,64,512]{2,1,0:T(8,128)S(1)}, u32[]{:S(2)}, u32[]{:S(2)}) collective-permute-start(f32[4,64,512]{2,1,0:T(8,128)S(1)} %get-tuple-element.135), channel_id=1, source_target_pairs={{0,1},{1,0},{2,3},{3,2},{4,5},{5,4},{6,7},{7,6},{8,9},{9,8},{10,11... | collective-permute-start | bytes 1572872 | tf_op jit(solution)/shard_map/ppermute | solution.py:31
  84.2 13.7 %collective-permute-start.27 = (f32[2,64,512]{2,1,0:T(8,128)S(1)}, f32[2,64,512]{2,1,0:T(8,128)S(1)}, u32[]{:S(2)}, u32[]{:S(2)}) collective-permute-start(f32[2,64,512]{2,1,0:T(8,128)S(1)} %get-tuple-element.138), channel_id=1, source_target_pairs={{0,4},{4,8},{8,12},{12,16},{16,20},{20,24},{24,28},{1,5},{5,9},{9,... | collective-permute-start | bytes 786440 | tf_op jit(solution)/shard_map/ppermute | solution.py:37
  91.8 8.5 %collective-permute-start.28 = (f32[2,64,512]{2,1,0:T(8,128)S(1)}, f32[2,64,512]{2,1,0:T(8,128)S(1)}, u32[]{:S(2)}, u32[]{:S(2)}) collective-permute-start(f32[2,64,512]{2,1,0:T(8,128)S(1)} %slice_add_fusion.1), channel_id=1, source_target_pairs={{0,2},{1,3},{2,0},{3,1},{4,6},{5,7},{6,4},{7,5},{8,10},{9,11},{10,... | collective-permute-start | bytes 786440 | tf_op jit(solution)/shard_map/ppermute | solution.py:31
  101.3 1.3 %collective-permute-start.29 = (f32[64,128]{1,0:T(8,128)S(1)}, f32[64,128]{1,0:T(8,128)S(1)}, u32[]{:S(2)}, u32[]{:S(2)}) collective-permute-start(f32[64,128]{1,0:T(8,128)S(1)} %get-tuple-element.143), channel_id=1, source_target_pairs={{0,1},{1,0},{2,3},{3,2},{4,5},{5,4},{6,7},{7,6},{8,9},{9,8},{10,11... | collective-permute-start | bytes 98312 | tf_op jit(solution)/shard_map/ppermute | solution.py:673
  102.5 3.9 %collective-permute-start.30 = (f32[64,128]{1,0:T(8,128)S(1)}, f32[64,128]{1,0:T(8,128)S(1)}, u32[]{:S(2)}, u32[]{:S(2)}) collective-permute-start(f32[64,128]{1,0:T(8,128)S(1)} %add.50), channel_id=1, source_target_pairs={{0,2},{1,3},{2,0},{3,1},{4,6},{5,7},{6,4},{7,5},{8,10},{9,11},{10,... | collective-permute-start | bytes 98312 | tf_op jit(solution)/shard_map/ppermute | solution.py:673
  102.8 3.9 %collective-permute-start.31 = (f32[64,128]{1,0:T(8,128)S(1)}, f32[64,128]{1,0:T(8,128)S(1)}, u32[]{:S(2)}, u32[]{:S(2)}) collective-permute-start(f32[64,128]{1,0:T(8,128)S(1)} %add.50), channel_id=1, source_target_pairs={{0,4},{1,5},{2,6},{3,7},{4,0},{5,1},{6,2},{7,3},{8,12},{9,13},{10,... | collective-permute-start | bytes 98312 | tf_op jit(solution)/shard_map/ppermute | solution.py:673
  103.7 4.8 %collective-permute-start.32 = (f32[64,128]{1,0:T(8,128)S(1)}, f32[64,128]{1,0:T(8,128)S(1)}, u32[]{:S(2)}, u32[]{:S(2)}) collective-permute-start(f32[64,128]{1,0:T(8,128)S(1)} %add.50), channel_id=1, source_target_pairs={{0,6},{1,7},{2,4},{3,5},{4,2},{5,3},{6,0},{7,1},{8,14},{9,15},{10,... | collective-permute-start | bytes 98312 | tf_op jit(solution)/shard_map/ppermute | solution.py:673
  108.6 6.3 %collective-permute-start.33 = (f32[64,128]{1,0:T(8,128)S(1)}, f32[64,128]{1,0:T(8,128)S(1)}, u32[]{:S(2)}, u32[]{:S(2)}) collective-permute-start(f32[64,128]{1,0:T(8,128)S(1)} %add_add_fusion.3), channel_id=1, source_target_pairs={{0,8},{1,9},{2,10},{3,11},{4,12},{5,13},{6,14},{7,15},{8,0},{9,1},... | collective-permute-start | bytes 98312 | tf_op jit(solution)/shard_map/ppermute | solution.py:673
  110.7 5.0 %collective-permute-start.34 = (f32[64,128]{1,0:T(8,128)S(1)}, f32[64,128]{1,0:T(8,128)S(1)}, u32[]{:S(2)}, u32[]{:S(2)}) collective-permute-start(f32[64,128]{1,0:T(8,128)S(1)} %add_add_fusion.3), channel_id=1, source_target_pairs={{0,16},{1,17},{2,18},{3,19},{4,20},{5,21},{6,22},{7,23},{8,24},{9,... | collective-permute-start | bytes 98312 | tf_op jit(solution)/shard_map/ppermute | solution.py:673
  113.5 5.7 %collective-permute-start.35 = (f32[64,128]{1,0:T(8,128)S(1)}, f32[64,128]{1,0:T(8,128)S(1)}, u32[]{:S(2)}, u32[]{:S(2)}) collective-permute-start(f32[64,128]{1,0:T(8,128)S(1)} %add_add_fusion.3), channel_id=1, source_target_pairs={{0,24},{1,25},{2,26},{3,27},{4,28},{5,29},{6,30},{7,31},{8,16},{9,... | collective-permute-start | bytes 98312 | tf_op jit(solution)/shard_map/ppermute | solution.py:673

commit v4 on v3

--- a/solution.py
+++ b/solution.py
@@ -110,9 +110,10 @@
     targets,
     bounds,
     owners,
+    row_places,
+    col_places,
 ):
     slab = blocks_dev * group
-    slots = rows.shape[0]
     member = lax.axis_index("grp")
 
     def local_near(block, device):
@@ -121,9 +122,12 @@
     def local_far(block):
         return slab + lax.rem(block - slab, blocks_dev)
 
+    def far_of(col):
+        return col >= slab
+
     def count_far(slot, carry):
         col = cols[slot]
-        far = jnp.logical_and(slot < live[0], col >= slab)
+        far = far_of(col)
         owner = lax.div(col - slab, blocks_dev)
         owners[slot] = jnp.where(far, owner, -1)
         return tuple(
@@ -131,11 +135,11 @@
             for device, old in enumerate(carry)
         )
 
-    loads = lax.fori_loop(0, slots, count_far, (jnp.int32(0),) * group)
+    loads = lax.fori_loop(0, live[0], count_far, (jnp.int32(0),) * group)
 
     def give(slot, loads):
         row, col = rows[slot], cols[slot]
-        near = jnp.logical_and(slot < live[0], col < slab)
+        near = jnp.logical_not(far_of(col))
         best = jnp.int32(2**30)
         owner = jnp.int32(0)
         for device in range(group):
@@ -147,35 +151,34 @@
             owner = jnp.where(score < best, device, owner)
             best = jnp.minimum(score, best)
 
-        @pl.when(near)
-        def _():
-            owners[slot] = owner
-
+        row_place = local_near(row, member)
+        col_place = jnp.where(far_of(col), local_far(col), local_near(col, member))
+        stage = jnp.maximum(
+            stage_of(row_place, group, blocks_dev), stage_of(col_place, group, blocks_dev)
+        )
+        mine = jnp.where(near, owner, owners[slot]) == member
+        row_places[slot] = row_place
+        col_places[slot] = col_place
+        owners[slot] = jnp.where(mine, stage, -1)
         return tuple(
             load + jnp.where(jnp.logical_and(near, owner == device), 1, 0)
             for device, load in enumerate(loads)
         )
 
-    lax.fori_loop(0, slots, give, loads)
+    lax.fori_loop(0, live[0], give, loads)
 
     def place_those(wanted, filled):
         def place(slot, filled):
-            row, col = rows[slot], cols[slot]
-            row_place = local_near(row, member)
-            col_place = jnp.where(col >= slab, local_far(col), local_near(col, member))
-            stage = jnp.maximum(
-                stage_of(row_place, group, blocks_dev), stage_of(col_place, group, blocks_dev)
-            )
-            mine = jnp.logical_and(owners[slot] == member, stage == wanted)
+            mine = owners[slot] == wanted
 
             @pl.when(mine)
             def _():
-                out_rows[filled] = row_place
-                out_cols[filled] = col_place
+                out_rows[filled] = row_places[slot]
+                out_cols[filled] = col_places[slot]
 
             return filled + jnp.where(mine, 1, 0)
 
-        return lax.fori_loop(0, slots, place, filled)
+        return lax.fori_loop(0, live[0], place, filled)
 
     count = jnp.int32(0)
     out_n[0] = count
@@ -229,7 +232,7 @@
         ),
         in_specs=[spec(SMEM)] * 3,
         out_specs=(spec(SMEM),) * 7,
-        scratch_shapes=[SMEM((rows.shape[0],), jnp.int32)],
+        scratch_shapes=[SMEM((rows.shape[0],), jnp.int32)] * 3,
         cost_estimate=cost(2**20, 2**10),
         compiler_params=pltpu.CompilerParams(vmem_limit_bytes=2**20),
         name="listing",

time: 126 us -> 121 us (0.960)
  starting transfers between devices: 36.8 us -> 28.6 us
  waiting for transfers between devices: 28.4 us -> 32.3 us
    ppermute x6, starting transfers between devices: 14.6 us -> 9.66 us  [from_behind(): lax.ppermute(value, axis, [(source, source + steps) for source in range(i...]
    ppermute x16, waiting for transfers between devices: 8.63 us -> 11.4 us  [swap(): lax.ppermute(value, axis, [(source, source ^ bit) for source in range(cou...]
    pallas_call x1, Pallas kernels: 14.7 us -> 12 us  [listing(): pl.pallas_call(functools.partial(listing_kernel, group, cap, blocks_dev),...]
    pallas_call x7, Pallas kernels: 18 us -> 20.5 us  [products(): call(*entries, *[vecs[first] for first in firsts], tiles, *begun)]
    ppermute x7, starting transfers between devices: 9.83 us -> 8.01 us  [all_sum(): lax.ppermute(value, ('blk', 'grp'), [(source, source ^ move) for source i...]
    ppermute x6, waiting for transfers between devices: 11.7 us -> 13.3 us  [from_behind(): lax.ppermute(value, axis, [(source, source + steps) for source in range(i...]
    ppermute x16, starting transfers between devices: 12.4 us -> 10.9 us  [swap(): lax.ppermute(value, axis, [(source, source ^ bit) for source in range(cou...]
  transfers between devices with their start and end apart: 29 -> 29, of which waited for: 16 -> 18; matrix products, arithmetic and copies ran while one was open for 0% -> 0% of each run, Pallas kernels for 35% -> 34%
where the time goes in v4:
time: 121 us
  Pallas kernels  57.2 us (47%)
  waiting for transfers between devices  32.3 us (27%)
  starting transfers between devices  28.6 us (24%)
  between operations  1.65 us (1%)
  local copies, waits for them, and re-layouts  1.44 us (1%)
    pallas_call x7, Pallas kernels, products(): call(*entries, *[vecs[first] for first in firsts], tiles, *begun)  20.5 us
    pallas_call x4, Pallas kernels, build_tiles(): pl.pallas_call(kernel, out_shape=shapes, in_specs=[spec(SMEM)] * len(scal...  16.2 us
    ppermute x6, waiting for transfers between devices, from_behind(): lax.ppermute(value, axis, [(source, source + steps) for source in range(i...  13.3 us
    pallas_call x1, Pallas kernels, listing(): pl.pallas_call(functools.partial(listing_kernel, group, cap, blocks_dev),...  12 us
    ppermute x16, waiting for transfers between devices, swap(): lax.ppermute(value, axis, [(source, source ^ bit) for source in range(cou...  11.4 us
    ppermute x16, starting transfers between devices, swap(): lax.ppermute(value, axis, [(source, source ^ bit) for source in range(cou...  10.9 us
    ppermute x6, starting transfers between devices, from_behind(): lax.ppermute(value, axis, [(source, source + steps) for source in range(i...  9.66 us
    ppermute x7, starting transfers between devices, all_sum(): lax.ppermute(value, ('blk', 'grp'), [(source, source ^ move) for source i...  8.01 us
  transfers between devices with their start and end apart: 29, of which 18 were waited for; matrix products, arithmetic and copies ran while one was open for 0% of the time, Pallas kernels for 34%

profile of v4, /device:TPU:0, one launch (start us, length us, event | category | flops | bytes accessed | tf_op | source)
XLA Modules:
  0.0 121.4 jit_solution(7146927544669493329)
XLA Ops:
  0.0 1.3 %slice.18 = bf16[512,768]{1,0:T(8,128)(2,1)S(1)} slice(bf16[1024,768]{1,0:T(8,128)(2,1)} %refs_3_.1), slice={[0:512], [0:768]} | slice | bytes 1572864 | tf_op jit(solution)/shard_map/slice | solution.py:700
  1.3 1.3 %collective-permute-start.7 = (bf16[512,768]{1,0:T(8,128)(2,1)S(1)}, bf16[512,768]{1,0:T(8,128)(2,1)S(1)}, u32[]{:S(2)}, u32[]{:S(2)}) collective-permute-start(bf16[512,768]{1,0:T(8,128)(2,1)S(1)} %slice.18), channel_id=1, source_target_pairs={{4,0},{8,4},{12,8},{16,12},{20,16},{24,20},{28,24},{5,1},{9,5},{13... | collective-permute-start | bytes 2359304 | tf_op jit(solution)/shard_map/ppermute | solution.py:37
  2.6 3.0 %collective-permute-start.8 = (bf16[512,768]{1,0:T(8,128)(2,1)S(1)}, bf16[512,768]{1,0:T(8,128)(2,1)S(1)}, u32[]{:S(2)}, u32[]{:S(2)}) collective-permute-start(bf16[512,768]{1,0:T(8,128)(2,1)S(1)} %slice.18), channel_id=1, source_target_pairs={{0,2},{1,3},{2,0},{3,1},{4,6},{5,7},{6,4},{7,5},{8,10},{9,11},{10,... | collective-permute-start | bytes 2359304 | tf_op jit(solution)/shard_map/ppermute | solution.py:31
  5.7 0.1 slice.19
  5.7 0.2 collective-permute-start.14
  5.9 1.3 %collective-permute-start.9 = (bf16[512,768]{1,0:T(8,128)(2,1)S(1)}, bf16[512,768]{1,0:T(8,128)(2,1)S(1)}, u32[]{:S(2)}, u32[]{:S(2)}) collective-permute-start(bf16[512,768]{1,0:T(8,128)(2,1)S(1)} %slice.19), channel_id=1, source_target_pairs={{4,0},{8,4},{12,8},{16,12},{20,16},{24,20},{28,24},{5,1},{9,5},{13... | collective-permute-start | bytes 2359304 | tf_op jit(solution)/shard_map/ppermute | solution.py:37
  7.8 0.6 opening.1.refs_4_
  8.4 12.0 %listing.1 = (s32[16]{0:T(128)S(1)}, s32[16]{0:T(128)S(1)}, s32[4]{0:T(128)S(1)}, s32[32]{0:T(128)S(1)}, s32[32]{0:T(128)S(1)}, /*index=5*/s32[32]{0:T(128)S(1)}, s32[9]{0:T(128)S(1)}) custom-call(s32[64]{0:T(128)S(1)} %copy-done.3, s32[64]{0:T(128)S(1)} %copy-done.4, s32[1]{0:T(128)S(6)} %copy.31.live), custom_call_target="tpu_custom_call" | custom-call | flops 1048576 | bytes 1024 | tf_op jit(solution)/shard_map/listing/pallas_call | solution.py:222
  20.4 4.1 %collective-permute-done.7.refs_5_ = bf16[512,768]{1,0:T(8,128)(2,1)S(1)} collective-permute-done((bf16[512,768]{1,0:T(8,128)(2,1)S(1)}, bf16[512,768]{1,0:T(8,128)(2,1)S(1)}, u32[]{:S(2)}, u32[]{:S(2)}) %collective-permute-start.7) | collective-permute-done | bytes 786464 | tf_op jit(solution)/shard_map/ppermute | solution.py:37
  24.6 0.1 fusion
  24.6 0.1 collective-permute-start.11
  24.7 0.5 collective-permute-start.12
  25.2 1.2 collective-permute-done.11
  26.4 0.1 collective-permute-start.10
  26.6 0.4 collective-permute-done.12
  27.0 0.1 pad_maximum_fusion.refs_3_
  27.1 6.9 %first_tiles.1 = (bf16[5120,768]{1,0:T(8,128)(2,1)S(1)}, f32[10,8,512]{2,1,0:T(8,128)S(1)}, f32[8,512,128]{2,1,0:T(8,128)S(1)}, bf16[17,512,512]{2,1,0:T(8,128)(2,1)S(1)}) custom-call(s32[4]{0:T(128)S(1)} %get-tuple-element.90.refs_0_, s32[16]{0:T(128)S(1)} %get-tuple-element.91.refs_1_, s32[16]{0:T(128)S(1)} %get-tuple-element.92.refs_2_, ...), custom_call_target="tpu_custom_call" | custom-call | flops 1048576 | bytes 1048576 | tf_op jit(solution)/shard_map/first_tiles/pallas_call | solution.py:339
  33.9 2.1 %second_tiles.1 = (bf16[5120,768]{1,0:T(8,128)(2,1)S(1)}, f32[10,8,512]{2,1,0:T(8,128)S(1)}, f32[8,512,128]{2,1,0:T(8,128)S(1)}, bf16[17,512,512]{2,1,0:T(8,128)(2,1)S(1)}) custom-call(s32[4]{0:T(128)S(1)} %get-tuple-element.90.refs_0_, s32[16]{0:T(128)S(1)} %get-tuple-element.91.refs_1_, ...), custom_call_target="tpu_custom_call", output_to_operand_aliasing={{0}: (4, {}), {1}: (5, {}), {2}: (6, {}), {3}: (7, {})} | custom-call | flops 1048576 | bytes 1048576 | tf_op jit(solution)/shard_map/second_tiles/pallas_call | solution.py:339
  36.1 2.5 %products.7 = (f32[2,72,512]{2,1,0:T(8,128)S(1)}, f32[4,72,512]{2,1,0:T(8,128)S(1)}, f32[2,72,512]{2,1,0:T(8,128)S(1)}, f32[2,72,512]{2,1,0:T(8,128)S(1)}) custom-call(s32[32]{0:T(128)S(1)} %get-tuple-element.82.refs_0_, s32[32]{0:T(128)S(1)} %get-tuple-element.83.refs_1_, s32[32]{0:T(128)S(1)} %get-tuple-element.84.refs_2_, ...), custom_call_target="tpu_custom_call" | custom-call | flops 1048576 | bytes 1048576 | tf_op jit(solution)/shard_map/products/pallas_call | solution.py:443
  38.6 1.5 %collective-permute-done.14.refs_1_ = bf16[512,768]{1,0:T(8,128)(2,1)S(1)} collective-permute-done((bf16[512,768]{1,0:T(8,128)(2,1)S(1)}, bf16[512,768]{1,0:T(8,128)(2,1)S(1)}, u32[]{:S(2)}, u32[]{:S(2)}) %collective-permute-start.14) | collective-permute-done | bytes 786464 | tf_op jit(solution)/shard_map/ppermute | solution.py:31
  40.0 0.6 collective-permute-done.9.refs_0_
  40.6 3.2 %collective-permute-start.16 = (bf16[80,1024]{1,0:T(8,128)(2,1)S(1)}, bf16[80,1024]{1,0:T(8,128)(2,1)S(1)}, u32[]{:S(2)}, u32[]{:S(2)}) collective-permute-start(bf16[80,1024]{1,0:T(8,128)(2,1)S(1)} %opening.1.refs_4_), channel_id=1, source_target_pairs={{0,2},{1,3},{2,0},{3,1},{4,6},{5,7},{6,4},{7,5},{8,10},{9,11},{10,... | collective-permute-start | bytes 491528 | tf_op jit(solution)/shard_map/ppermute | solution.py:31
  43.8 1.3 %collective-permute-start.18 = (bf16[80,1024]{1,0:T(8,128)(2,1)S(1)}, bf16[80,1024]{1,0:T(8,128)(2,1)S(1)}, u32[]{:S(2)}, u32[]{:S(2)}) collective-permute-start(bf16[80,1024]{1,0:T(8,128)(2,1)S(1)} %opening.1.refs_4_), channel_id=1, source_target_pairs={{4,0},{8,4},{12,8},{16,12},{20,16},{24,20},{28,24},{5,1},{9,5},{13... | collective-permute-start | bytes 491528 | tf_op jit(solution)/shard_map/ppermute | solution.py:37
  45.1 0.8 more_blocks.1
  45.8 6.5 %last_tiles.1 = (bf16[5120,768]{1,0:T(8,128)(2,1)S(1)}, f32[10,8,512]{2,1,0:T(8,128)S(1)}, f32[8,512,128]{2,1,0:T(8,128)S(1)}, bf16[17,512,512]{2,1,0:T(8,128)(2,1)S(1)}) custom-call(s32[4]{0:T(128)S(1)} %get-tuple-element.90.refs_0_, s32[16]{0:T(128)S(1)} %get-tuple-element.91.refs_1_, ...), custom_call_target="tpu_custom_call", output_to_operand_aliasing={{0}: (4, {}), {1}: (5, {}), {2}: (6, {}), {3}: (7, {})} | custom-call | flops 4294967296 | bytes 1048576 | tf_op jit(solution)/shard_map/last_tiles/pallas_call | solution.py:339
  52.3 0.1 collective-permute-start.17
  52.4 1.8 %products.8 = (f32[2,72,512]{2,1,0:T(8,128)S(1)}, f32[4,72,512]{2,1,0:T(8,128)S(1)}, f32[2,72,512]{2,1,0:T(8,128)S(1)}, f32[2,72,512]{2,1,0:T(8,128)S(1)}) custom-call(s32[32]{0:T(128)S(1)} %get-tuple-element.82.refs_0_, s32[32]{0:T(128)S(1)} %get-tuple-element.83.refs_1_, s32[32]{0:T(128)S(1)} %get-tuple-element.84.refs_2_, ...), custom_call_target="tpu_custom_call" | custom-call | flops 1048576 | bytes 1048576 | tf_op jit(solution)/shard_map/products/pallas_call | solution.py:443
  54.2 4.0 %products.9 = (f32[4,72,512]{2,1,0:T(8,128)S(1)}, f32[2,72,512]{2,1,0:T(8,128)S(1)}, f32[2,72,512]{2,1,0:T(8,128)S(1)}) custom-call(s32[32]{0:T(128)S(1)} %get-tuple-element.82.refs_0_, s32[32]{0:T(128)S(1)} %get-tuple-element.83.refs_1_, s32[32]{0:T(128)S(1)} %get-tuple-element.84.refs_2_, s32[9]{0:T(128)S(1)} %get-tuple-element.85.refs_3_, ...), custom_call_target="tpu_custom_call" | custom-call | flops 2147483648 | bytes 1048576 | tf_op jit(solution)/shard_map/products/pallas_call | solution.py:443
  58.3 0.1 collective-permute-start.19
  58.3 1.3 %collective-permute-start.20 = (f32[2,72,512]{2,1,0:T(8,128)S(1)}, f32[2,72,512]{2,1,0:T(8,128)S(1)}, u32[]{:S(2)}, u32[]{:S(2)}) collective-permute-start(f32[2,72,512]{2,1,0:T(8,128)S(1)} %get-tuple-element.126), channel_id=1, source_target_pairs={{0,4},{4,8},{8,12},{12,16},{16,20},{20,24},{24,28},{1,5},{5,9},{9,... | collective-permute-start | bytes 884744 | tf_op jit(solution)/shard_map/ppermute | solution.py:37
  59.7 0.7 collective-permute-done.19.refs_2_
  60.4 1.0 collective-permute-start.21
  61.4 2.2 %products.10.refs_0_ = f32[2,72,512]{2,1,0:T(8,128)S(1)} custom-call(s32[32]{0:T(128)S(1)} %get-tuple-element.82.refs_0_, s32[32]{0:T(128)S(1)} %get-tuple-element.83.refs_1_, s32[32]{0:T(128)S(1)} %get-tuple-element.84.refs_2_, s32[9]{0:T(128)S(1)} %get-tuple-element.85.refs_3_, bf16[80,1024]{1,0:T(8,128)(2,1)S(1)} %collective-permute-done.16.refs_4_, ...), custom_call_target="tpu_custom_call" | custom-call | flops 1048576 | bytes 1048576 | tf_op jit(solution)/shard_map/products/pallas_call | solution.py:443
  63.6 3.2 %collective-permute-done.20.refs_1_ = f32[2,72,512]{2,1,0:T(8,128)S(1)} collective-permute-done((f32[2,72,512]{2,1,0:T(8,128)S(1)}, f32[2,72,512]{2,1,0:T(8,128)S(1)}, u32[]{:S(2)}, u32[]{:S(2)}) %collective-permute-start.20) | collective-permute-done | bytes 294944 | tf_op jit(solution)/shard_map/ppermute | solution.py:37
  66.8 2.7 %collective-permute-done.21.refs_3_ = f32[2,72,512]{2,1,0:T(8,128)S(1)} collective-permute-done((f32[2,72,512]{2,1,0:T(8,128)S(1)}, f32[2,72,512]{2,1,0:T(8,128)S(1)}, u32[]{:S(2)}, u32[]{:S(2)}) %collective-permute-start.21) | collective-permute-done | bytes 294944 | tf_op jit(solution)/shard_map/ppermute | solution.py:31
  69.5 1.0 scaled_gram.2
  70.4 0.1 collective-permute-start.22
  70.5 1.2 %collective-permute-start.23 = (bf16[128,1024]{1,0:T(8,128)(2,1)S(1)}, bf16[128,1024]{1,0:T(8,128)(2,1)S(1)}, u32[]{:S(2)}, u32[]{:S(2)}) collective-permute-start(bf16[128,1024]{1,0:T(8,128)(2,1)S(1)} %get-tuple-element.128.refs_4_), channel_id=1, source_target_pairs={{0,2},{1,3},{2,0},{3,1},{4,6},{5,7},{6,4},{7,5},{8,10},{9,11},{10,... | collective-permute-start | bytes 786440 | tf_op jit(solution)/shard_map/ppermute | solution.py:31
  71.8 1.3 %collective-permute-start.25 = (bf16[128,1024]{1,0:T(8,128)(2,1)S(1)}, bf16[128,1024]{1,0:T(8,128)(2,1)S(1)}, u32[]{:S(2)}, u32[]{:S(2)}) collective-permute-start(bf16[128,1024]{1,0:T(8,128)(2,1)S(1)} %get-tuple-element.128.refs_4_), channel_id=1, source_target_pairs={{4,0},{8,4},{12,8},{16,12},{20,16},{24,20},{28,24},{5,1},{9,5},{13... | collective-permute-start | bytes 786440 | tf_op jit(solution)/shard_map/ppermute | solution.py:37
  73.1 3.6 %products.11 = (f32[2,64,512]{2,1,0:T(8,128)S(1)}, f32[4,64,512]{2,1,0:T(8,128)S(1)}, f32[2,64,512]{2,1,0:T(8,128)S(1)}, f32[2,64,512]{2,1,0:T(8,128)S(1)}) custom-call(s32[32]{0:T(128)S(1)} %get-tuple-element.82.refs_0_, s32[32]{0:T(128)S(1)} %get-tuple-element.83.refs_1_, s32[32]{0:T(128)S(1)} %get-tuple-element.84.refs_2_, ...), custom_call_target="tpu_custom_call" | custom-call | flops 1048576 | bytes 1048576 | tf_op jit(solution)/shard_map/products/pallas_call | solution.py:443
  76.7 2.5 %collective-permute-done.23.refs_4_ = bf16[128,1024]{1,0:T(8,128)(2,1)S(1)} collective-permute-done((bf16[128,1024]{1,0:T(8,128)(2,1)S(1)}, bf16[128,1024]{1,0:T(8,128)(2,1)S(1)}, u32[]{:S(2)}, u32[]{:S(2)}) %collective-permute-start.23) | collective-permute-done | bytes 262176 | tf_op jit(solution)/shard_map/ppermute | solution.py:31
  79.3 2.8 %collective-permute-done.25.refs_6_ = bf16[128,1024]{1,0:T(8,128)(2,1)S(1)} collective-permute-done((bf16[128,1024]{1,0:T(8,128)(2,1)S(1)}, bf16[128,1024]{1,0:T(8,128)(2,1)S(1)}, u32[]{:S(2)}, u32[]{:S(2)}) %collective-permute-start.25) | collective-permute-done | bytes 262176 | tf_op jit(solution)/shard_map/ppermute | solution.py:37
  82.0 4.1 %products.12 = (f32[4,64,512]{2,1,0:T(8,128)S(1)}, f32[2,64,512]{2,1,0:T(8,128)S(1)}, f32[2,64,512]{2,1,0:T(8,128)S(1)}) custom-call(s32[32]{0:T(128)S(1)} %get-tuple-element.82.refs_0_, s32[32]{0:T(128)S(1)} %get-tuple-element.83.refs_1_, s32[32]{0:T(128)S(1)} %get-tuple-element.84.refs_2_, s32[9]{0:T(128)S(1)} %get-tuple-element.85.refs_3_, ...), custom_call_target="tpu_custom_call" | custom-call | flops 2147483648 | bytes 1048576 | tf_op jit(solution)/shard_map/products/pallas_call | solution.py:443
  86.1 0.1 collective-permute-start.26
  86.2 3.2 %collective-permute-start.27 = (f32[2,64,512]{2,1,0:T(8,128)S(1)}, f32[2,64,512]{2,1,0:T(8,128)S(1)}, u32[]{:S(2)}, u32[]{:S(2)}) collective-permute-start(f32[2,64,512]{2,1,0:T(8,128)S(1)} %get-tuple-element.138), channel_id=1, source_target_pairs={{0,4},{4,8},{8,12},{12,16},{16,20},{20,24},{24,28},{1,5},{5,9},{9,... | collective-permute-start | bytes 786440 | tf_op jit(solution)/shard_map/ppermute | solution.py:37
  89.5 1.3 %collective-permute-start.28 = (f32[2,64,512]{2,1,0:T(8,128)S(1)}, f32[2,64,512]{2,1,0:T(8,128)S(1)}, u32[]{:S(2)}, u32[]{:S(2)}) collective-permute-start(f32[2,64,512]{2,1,0:T(8,128)S(1)} %slice_add_fusion.1), channel_id=1, source_target_pairs={{0,2},{1,3},{2,0},{3,1},{4,6},{5,7},{6,4},{7,5},{8,10},{9,11},{10,... | collective-permute-start | bytes 786440 | tf_op jit(solution)/shard_map/ppermute | solution.py:31
  90.8 2.3 %products.13.refs_0_ = f32[2,64,512]{2,1,0:T(8,128)S(1)} custom-call(s32[32]{0:T(128)S(1)} %get-tuple-element.82.refs_0_, s32[32]{0:T(128)S(1)} %get-tuple-element.83.refs_1_, s32[32]{0:T(128)S(1)} %get-tuple-element.84.refs_2_, s32[9]{0:T(128)S(1)} %get-tuple-element.85.refs_3_, bf16[128,1024]{1,0:T(8,128)(2,1)S(1)} %collective-permute-done.23.refs_4_, ...), custom_call_target="tpu_custom_call" | custom-call | flops 1048576 | bytes 1048576 | tf_op jit(solution)/shard_map/products/pallas_call | solution.py:443
  93.0 2.6 %collective-permute-done.27.refs_1_ = f32[2,64,512]{2,1,0:T(8,128)S(1)} collective-permute-done((f32[2,64,512]{2,1,0:T(8,128)S(1)}, f32[2,64,512]{2,1,0:T(8,128)S(1)}, u32[]{:S(2)}, u32[]{:S(2)}) %collective-permute-start.27) | collective-permute-done | bytes 262176 | tf_op jit(solution)/shard_map/ppermute | solution.py:37
  95.6 2.4 %collective-permute-done.28.refs_3_ = f32[2,64,512]{2,1,0:T(8,128)S(1)} collective-permute-done((f32[2,64,512]{2,1,0:T(8,128)S(1)}, f32[2,64,512]{2,1,0:T(8,128)S(1)}, u32[]{:S(2)}, u32[]{:S(2)}) %collective-permute-start.28) | collective-permute-done | bytes 262176 | tf_op jit(solution)/shard_map/ppermute | solution.py:31
  98.0 1.0 scaled_gram.3
  99.0 0.1 collective-permute-start.29
  99.1 1.2 collective-permute-done.29
  100.3 0.8 collective-permute-start.30
  101.0 1.7 %collective-permute-start.31 = (f32[64,128]{1,0:T(8,128)S(1)}, f32[64,128]{1,0:T(8,128)S(1)}, u32[]{:S(2)}, u32[]{:S(2)}) collective-permute-start(f32[64,128]{1,0:T(8,128)S(1)} %add.50), channel_id=1, source_target_pairs={{0,4},{1,5},{2,6},{3,7},{4,0},{5,1},{6,2},{7,3},{8,12},{9,13},{10,... | collective-permute-start | bytes 98312 | tf_op jit(solution)/shard_map/ppermute | solution.py:676
  102.8 1.0 collective-permute-start.32
  103.8 0.4 collective-permute-done.30
  104.2 0.8 collective-permute-done.31
  104.9 2.6 %collective-permute-done.32 = f32[64,128]{1,0:T(8,128)S(1)} collective-permute-done((f32[64,128]{1,0:T(8,128)S(1)}, f32[64,128]{1,0:T(8,128)S(1)}, u32[]{:S(2)}, u32[]{:S(2)}) %collective-permute-start.32) | collective-permute-done | bytes 32800 | tf_op jit(solution)/shard_map/ppermute | solution.py:676
  107.6 1.4 %collective-permute-start.33 = (f32[64,128]{1,0:T(8,128)S(1)}, f32[64,128]{1,0:T(8,128)S(1)}, u32[]{:S(2)}, u32[]{:S(2)}) collective-permute-start(f32[64,128]{1,0:T(8,128)S(1)} %add_add_fusion.3), channel_id=1, source_target_pairs={{0,8},{1,9},{2,10},{3,11},{4,12},{5,13},{6,14},{7,15},{8,0},{9,1},... | collective-permute-start | bytes 98312 | tf_op jit(solution)/shard_map/ppermute | solution.py:676
  108.9 3.1 %collective-permute-start.35 = (f32[64,128]{1,0:T(8,128)S(1)}, f32[64,128]{1,0:T(8,128)S(1)}, u32[]{:S(2)}, u32[]{:S(2)}) collective-permute-start(f32[64,128]{1,0:T(8,128)S(1)} %add_add_fusion.3), channel_id=1, source_target_pairs={{0,24},{1,25},{2,26},{3,27},{4,28},{5,29},{6,30},{7,31},{8,16},{9,... | collective-permute-start | bytes 98312 | tf_op jit(solution)/shard_map/ppermute | solution.py:676
  112.0 2.1 %collective-permute-done.34 = f32[64,128]{1,0:T(8,128)S(1)} collective-permute-done((f32[64,128]{1,0:T(8,128)S(1)}, f32[64,128]{1,0:T(8,128)S(1)}, u32[]{:S(2)}, u32[]{:S(2)}) %collective-permute-start.34) | collective-permute-done | bytes 32800 | tf_op jit(solution)/shard_map/ppermute | solution.py:676
  114.1 0.6 collective-permute-done.35
  114.7 4.9 %factors.1 = (f32[64,64]{1,0:T(8,128)S(1)}, f32[64,64]{1,0:T(8,128)S(1)}, s32[1]{0:T(128)}) custom-call(f32[64,128]{1,0:T(8,128)S(1)} %add_add_fusion.2.grams), custom_call_target="tpu_custom_call" | custom-call | flops 1073741824 | bytes 65536 | tf_op jit(solution)/shard_map/factors/pallas_call | solution.py:614
  120.3 1.1 applied.3
  (31 shorter events, 0.2 us)
Async XLA Ops:
  0.0 5.7 %copy-start = (bf16[1024,768]{1,0:T(8,128)(2,1)S(1)}, bf16[1024,768]{1,0:T(8,128)(2,1)}, u32[]{:S(2)}) copy-start(bf16[1024,768]{1,0:T(8,128)(2,1)} %refs_3_.1) | copy-start | bytes 4718596
  0.0 7.8 %copy-start.1 = (f32[64,1024]{1,0:T(8,128)S(1)}, f32[64,1024]{1,0:T(8,128)}, u32[]{:S(2)}) copy-start(f32[64,1024]{1,0:T(8,128)} %start.1) | copy-start | bytes 786436
  0.0 7.8 %copy-start.2 = (s32[2]{0:T(128)S(1)}, s32[2]{0:T(128)}, u32[]{:S(2)}) copy-start(s32[2]{0:T(128)} %count_ref.3) | copy-start | bytes 28
  0.0 8.4 %copy-start.3 = (s32[64]{0:T(128)S(1)}, s32[64]{0:T(128)}, u32[]{:S(2)}) copy-start(s32[64]{0:T(128)} %rows.1) | copy-start | bytes 772
  0.0 8.4 %copy-start.4 = (s32[64]{0:T(128)S(1)}, s32[64]{0:T(128)}, u32[]{:S(2)}) copy-start(s32[64]{0:T(128)} %cols.1) | copy-start | bytes 772
  1.3 23.2 %collective-permute-start.7 = (bf16[512,768]{1,0:T(8,128)(2,1)S(1)}, bf16[512,768]{1,0:T(8,128)(2,1)S(1)}, u32[]{:S(2)}, u32[]{:S(2)}) collective-permute-start(bf16[512,768]{1,0:T(8,128)(2,1)S(1)} %slice.18), channel_id=1, source_target_pairs={{4,0},{8,4},{12,8},{16,12},{20,16},{24,20},{28,24},{5,1},{9,5},{13... | collective-permute-start | bytes 2359304 | tf_op jit(solution)/shard_map/ppermute | solution.py:37
  2.6 22.0 %collective-permute-start.8 = (bf16[512,768]{1,0:T(8,128)(2,1)S(1)}, bf16[512,768]{1,0:T(8,128)(2,1)S(1)}, u32[]{:S(2)}, u32[]{:S(2)}) collective-permute-start(bf16[512,768]{1,0:T(8,128)(2,1)S(1)} %slice.18), channel_id=1, source_target_pairs={{0,2},{1,3},{2,0},{3,1},{4,6},{5,7},{6,4},{7,5},{8,10},{9,11},{10,... | collective-permute-start | bytes 2359304 | tf_op jit(solution)/shard_map/ppermute | solution.py:31
  5.7 21.4 %collective-permute-start.13 = (bf16[1024,768]{1,0:T(8,128)(2,1)}, bf16[1024,768]{1,0:T(8,128)(2,1)S(1)}, u32[]{:S(2)}, u32[]{:S(2)}) collective-permute-start(bf16[1024,768]{1,0:T(8,128)(2,1)} %refs_3_.1), channel_id=1, source_target_pairs={{0,1},{1,0},{2,3},{3,2},{4,5},{5,4},{6,7},{7,6},{8,9},{9,8},{10,11... | collective-permute-start | bytes 4718600 | tf_op jit(solution)/shard_map/ppermute | solution.py:31
  5.7 34.3 %collective-permute-start.14 = (bf16[512,768]{1,0:T(8,128)(2,1)S(1)}, bf16[512,768]{1,0:T(8,128)(2,1)S(1)}, u32[]{:S(2)}, u32[]{:S(2)}) collective-permute-start(bf16[512,768]{1,0:T(8,128)(2,1)S(1)} %slice.19), channel_id=1, source_target_pairs={{0,2},{1,3},{2,0},{3,1},{4,6},{5,7},{6,4},{7,5},{8,10},{9,11},{10,... | collective-permute-start | bytes 2359304 | tf_op jit(solution)/shard_map/ppermute | solution.py:31
  5.9 34.7 %collective-permute-start.9 = (bf16[512,768]{1,0:T(8,128)(2,1)S(1)}, bf16[512,768]{1,0:T(8,128)(2,1)S(1)}, u32[]{:S(2)}, u32[]{:S(2)}) collective-permute-start(bf16[512,768]{1,0:T(8,128)(2,1)S(1)} %slice.19), channel_id=1, source_target_pairs={{4,0},{8,4},{12,8},{16,12},{20,16},{24,20},{28,24},{5,1},{9,5},{13... | collective-permute-start | bytes 2359304 | tf_op jit(solution)/shard_map/ppermute | solution.py:37
  24.6 1.8 %collective-permute-start.11 = (bf16[256,768]{1,0:T(8,128)(2,1)S(1)}, bf16[256,768]{1,0:T(8,128)(2,1)S(1)}, u32[]{:S(2)}, u32[]{:S(2)}) collective-permute-start(bf16[256,768]{1,0:T(8,128)(2,1)S(1)} %get-tuple-element.148), channel_id=1, source_target_pairs={{0,1},{1,0},{2,3},{3,2},{4,5},{5,4},{6,7},{7,6},{8,9},{9,8},{10,11... | collective-permute-start | bytes 1179656 | tf_op jit(solution)/shard_map/ppermute | solution.py:31
  24.7 2.3 %collective-permute-start.12 = (bf16[256,768]{1,0:T(8,128)(2,1)S(1)}, bf16[256,768]{1,0:T(8,128)(2,1)S(1)}, u32[]{:S(2)}, u32[]{:S(2)}) collective-permute-start(bf16[256,768]{1,0:T(8,128)(2,1)S(1)} %get-tuple-element.149), channel_id=1, source_target_pairs={{0,1},{1,0},{2,3},{3,2},{4,5},{5,4},{6,7},{7,6},{8,9},{9,8},{10,11... | collective-permute-start | bytes 1179656 | tf_op jit(solution)/shard_map/ppermute | solution.py:31
  26.4 9.6 %collective-permute-start.10 = (bf16[80,1024]{1,0:T(8,128)(2,1)S(1)}, bf16[80,1024]{1,0:T(8,128)(2,1)S(1)}, u32[]{:S(2)}, u32[]{:S(2)}) collective-permute-start(bf16[80,1024]{1,0:T(8,128)(2,1)S(1)} %opening.1.refs_4_), channel_id=1, source_target_pairs={{0,1},{1,0},{2,3},{3,2},{4,5},{5,4},{6,7},{7,6},{8,9},{9,8},{10,11... | collective-permute-start | bytes 491528 | tf_op jit(solution)/shard_map/ppermute | solution.py:31
  40.6 5.2 %collective-permute-start.15 = (bf16[512,768]{1,0:T(8,128)(2,1)S(1)}, bf16[512,768]{1,0:T(8,128)(2,1)S(1)}, u32[]{:S(2)}, u32[]{:S(2)}) collective-permute-start(bf16[512,768]{1,0:T(8,128)(2,1)S(1)} %collective-permute-done.14.refs_1_), channel_id=1, source_target_pairs={{0,1},{1,0},{2,3},{3,2},{4,5},{5,4},{6,7},{7,6},{8,9},{9,8},{10,11... | collective-permute-start | bytes 2359304 | tf_op jit(solution)/shard_map/ppermute | solution.py:31
  40.6 11.7 %collective-permute-start.16 = (bf16[80,1024]{1,0:T(8,128)(2,1)S(1)}, bf16[80,1024]{1,0:T(8,128)(2,1)S(1)}, u32[]{:S(2)}, u32[]{:S(2)}) collective-permute-start(bf16[80,1024]{1,0:T(8,128)(2,1)S(1)} %opening.1.refs_4_), channel_id=1, source_target_pairs={{0,2},{1,3},{2,0},{3,1},{4,6},{5,7},{6,4},{7,5},{8,10},{9,11},{10,... | collective-permute-start | bytes 491528 | tf_op jit(solution)/shard_map/ppermute | solution.py:31
  43.8 10.4 %collective-permute-start.18 = (bf16[80,1024]{1,0:T(8,128)(2,1)S(1)}, bf16[80,1024]{1,0:T(8,128)(2,1)S(1)}, u32[]{:S(2)}, u32[]{:S(2)}) collective-permute-start(bf16[80,1024]{1,0:T(8,128)(2,1)S(1)} %opening.1.refs_4_), channel_id=1, source_target_pairs={{4,0},{8,4},{12,8},{16,12},{20,16},{24,20},{28,24},{5,1},{9,5},{13... | collective-permute-start | bytes 491528 | tf_op jit(solution)/shard_map/ppermute | solution.py:37
  52.3 1.9 %collective-permute-start.17 = (bf16[80,1024]{1,0:T(8,128)(2,1)S(1)}, bf16[80,1024]{1,0:T(8,128)(2,1)S(1)}, u32[]{:S(2)}, u32[]{:S(2)}) collective-permute-start(bf16[80,1024]{1,0:T(8,128)(2,1)S(1)} %collective-permute-done.16.refs_4_), channel_id=1, source_target_pairs={{0,1},{1,0},{2,3},{3,2},{4,5},{5,4},{6,7},{7,6},{8,9},{9,8},{10,11... | collective-permute-start | bytes 491528 | tf_op jit(solution)/shard_map/ppermute | solution.py:31
  58.3 2.1 %collective-permute-start.19 = (f32[4,72,512]{2,1,0:T(8,128)S(1)}, f32[4,72,512]{2,1,0:T(8,128)S(1)}, u32[]{:S(2)}, u32[]{:S(2)}) collective-permute-start(f32[4,72,512]{2,1,0:T(8,128)S(1)} %get-tuple-element.123), channel_id=1, source_target_pairs={{0,1},{1,0},{2,3},{3,2},{4,5},{5,4},{6,7},{7,6},{8,9},{9,8},{10,11... | collective-permute-start | bytes 1769480 | tf_op jit(solution)/shard_map/ppermute | solution.py:31
  58.3 8.5 %collective-permute-start.20 = (f32[2,72,512]{2,1,0:T(8,128)S(1)}, f32[2,72,512]{2,1,0:T(8,128)S(1)}, u32[]{:S(2)}, u32[]{:S(2)}) collective-permute-start(f32[2,72,512]{2,1,0:T(8,128)S(1)} %get-tuple-element.126), channel_id=1, source_target_pairs={{0,4},{4,8},{8,12},{12,16},{16,20},{20,24},{24,28},{1,5},{5,9},{9,... | collective-permute-start | bytes 884744 | tf_op jit(solution)/shard_map/ppermute | solution.py:37
  60.4 9.1 %collective-permute-start.21 = (f32[2,72,512]{2,1,0:T(8,128)S(1)}, f32[2,72,512]{2,1,0:T(8,128)S(1)}, u32[]{:S(2)}, u32[]{:S(2)}) collective-permute-start(f32[2,72,512]{2,1,0:T(8,128)S(1)} %slice_add_fusion), channel_id=1, source_target_pairs={{0,2},{1,3},{2,0},{3,1},{4,6},{5,7},{6,4},{7,5},{8,10},{9,11},{10,... | collective-permute-start | bytes 884744 | tf_op jit(solution)/shard_map/ppermute | solution.py:31
  70.4 2.6 %collective-permute-start.22 = (bf16[128,1024]{1,0:T(8,128)(2,1)S(1)}, bf16[128,1024]{1,0:T(8,128)(2,1)S(1)}, u32[]{:S(2)}, u32[]{:S(2)}) collective-permute-start(bf16[128,1024]{1,0:T(8,128)(2,1)S(1)} %get-tuple-element.128.refs_4_), channel_id=1, source_target_pairs={{0,1},{1,0},{2,3},{3,2},{4,5},{5,4},{6,7},{7,6},{8,9},{9,8},{10,11... | collective-permute-start | bytes 786440 | tf_op jit(solution)/shard_map/ppermute | solution.py:31
  70.5 8.7 %collective-permute-start.23 = (bf16[128,1024]{1,0:T(8,128)(2,1)S(1)}, bf16[128,1024]{1,0:T(8,128)(2,1)S(1)}, u32[]{:S(2)}, u32[]{:S(2)}) collective-permute-start(bf16[128,1024]{1,0:T(8,128)(2,1)S(1)} %get-tuple-element.128.refs_4_), channel_id=1, source_target_pairs={{0,2},{1,3},{2,0},{3,1},{4,6},{5,7},{6,4},{7,5},{8,10},{9,11},{10,... | collective-permute-start | bytes 786440 | tf_op jit(solution)/shard_map/ppermute | solution.py:31
  71.8 10.3 %collective-permute-start.25 = (bf16[128,1024]{1,0:T(8,128)(2,1)S(1)}, bf16[128,1024]{1,0:T(8,128)(2,1)S(1)}, u32[]{:S(2)}, u32[]{:S(2)}) collective-permute-start(bf16[128,1024]{1,0:T(8,128)(2,1)S(1)} %get-tuple-element.128.refs_4_), channel_id=1, source_target_pairs={{4,0},{8,4},{12,8},{16,12},{20,16},{24,20},{28,24},{5,1},{9,5},{13... | collective-permute-start | bytes 786440 | tf_op jit(solution)/shard_map/ppermute | solution.py:37
  79.2 2.8 %collective-permute-start.24 = (bf16[128,1024]{1,0:T(8,128)(2,1)S(1)}, bf16[128,1024]{1,0:T(8,128)(2,1)S(1)}, u32[]{:S(2)}, u32[]{:S(2)}) collective-permute-start(bf16[128,1024]{1,0:T(8,128)(2,1)S(1)} %collective-permute-done.23.refs_4_), channel_id=1, source_target_pairs={{0,1},{1,0},{2,3},{3,2},{4,5},{5,4},{6,7},{7,6},{8,9},{9,8},{10,11... | collective-permute-start | bytes 786440 | tf_op jit(solution)/shard_map/ppermute | solution.py:31
  86.1 3.3 %collective-permute-start.26 = (f32[4,64,512]{2,1,0:T(8,128)S(1)}, f32[4,64,512]{2,1,0:T(8,128)S(1)}, u32[]{:S(2)}, u32[]{:S(2)}) collective-permute-start(f32[4,64,512]{2,1,0:T(8,128)S(1)} %get-tuple-element.135), channel_id=1, source_target_pairs={{0,1},{1,0},{2,3},{3,2},{4,5},{5,4},{6,7},{7,6},{8,9},{9,8},{10,11... | collective-permute-start | bytes 1572872 | tf_op jit(solution)/shard_map/ppermute | solution.py:31
  86.2 9.4 %collective-permute-start.27 = (f32[2,64,512]{2,1,0:T(8,128)S(1)}, f32[2,64,512]{2,1,0:T(8,128)S(1)}, u32[]{:S(2)}, u32[]{:S(2)}) collective-permute-start(f32[2,64,512]{2,1,0:T(8,128)S(1)} %get-tuple-element.138), channel_id=1, source_target_pairs={{0,4},{4,8},{8,12},{12,16},{16,20},{20,24},{24,28},{1,5},{5,9},{9,... | collective-permute-start | bytes 786440 | tf_op jit(solution)/shard_map/ppermute | solution.py:37
  89.5 8.5 %collective-permute-start.28 = (f32[2,64,512]{2,1,0:T(8,128)S(1)}, f32[2,64,512]{2,1,0:T(8,128)S(1)}, u32[]{:S(2)}, u32[]{:S(2)}) collective-permute-start(f32[2,64,512]{2,1,0:T(8,128)S(1)} %slice_add_fusion.1), channel_id=1, source_target_pairs={{0,2},{1,3},{2,0},{3,1},{4,6},{5,7},{6,4},{7,5},{8,10},{9,11},{10,... | collective-permute-start | bytes 786440 | tf_op jit(solution)/shard_map/ppermute | solution.py:31
  99.0 1.3 %collective-permute-start.29 = (f32[64,128]{1,0:T(8,128)S(1)}, f32[64,128]{1,0:T(8,128)S(1)}, u32[]{:S(2)}, u32[]{:S(2)}) collective-permute-start(f32[64,128]{1,0:T(8,128)S(1)} %get-tuple-element.143), channel_id=1, source_target_pairs={{0,1},{1,0},{2,3},{3,2},{4,5},{5,4},{6,7},{7,6},{8,9},{9,8},{10,11... | collective-permute-start | bytes 98312 | tf_op jit(solution)/shard_map/ppermute | solution.py:676
  100.3 3.9 %collective-permute-start.30 = (f32[64,128]{1,0:T(8,128)S(1)}, f32[64,128]{1,0:T(8,128)S(1)}, u32[]{:S(2)}, u32[]{:S(2)}) collective-permute-start(f32[64,128]{1,0:T(8,128)S(1)} %add.50), channel_id=1, source_target_pairs={{0,2},{1,3},{2,0},{3,1},{4,6},{5,7},{6,4},{7,5},{8,10},{9,11},{10,... | collective-permute-start | bytes 98312 | tf_op jit(solution)/shard_map/ppermute | solution.py:676
  101.0 3.9 %collective-permute-start.31 = (f32[64,128]{1,0:T(8,128)S(1)}, f32[64,128]{1,0:T(8,128)S(1)}, u32[]{:S(2)}, u32[]{:S(2)}) collective-permute-start(f32[64,128]{1,0:T(8,128)S(1)} %add.50), channel_id=1, source_target_pairs={{0,4},{1,5},{2,6},{3,7},{4,0},{5,1},{6,2},{7,3},{8,12},{9,13},{10,... | collective-permute-start | bytes 98312 | tf_op jit(solution)/shard_map/ppermute | solution.py:676
  102.8 4.8 %collective-permute-start.32 = (f32[64,128]{1,0:T(8,128)S(1)}, f32[64,128]{1,0:T(8,128)S(1)}, u32[]{:S(2)}, u32[]{:S(2)}) collective-permute-start(f32[64,128]{1,0:T(8,128)S(1)} %add.50), channel_id=1, source_target_pairs={{0,6},{1,7},{2,4},{3,5},{4,2},{5,3},{6,0},{7,1},{8,14},{9,15},{10,... | collective-permute-start | bytes 98312 | tf_op jit(solution)/shard_map/ppermute | solution.py:676
  107.6 4.5 %collective-permute-start.33 = (f32[64,128]{1,0:T(8,128)S(1)}, f32[64,128]{1,0:T(8,128)S(1)}, u32[]{:S(2)}, u32[]{:S(2)}) collective-permute-start(f32[64,128]{1,0:T(8,128)S(1)} %add_add_fusion.3), channel_id=1, source_target_pairs={{0,8},{1,9},{2,10},{3,11},{4,12},{5,13},{6,14},{7,15},{8,0},{9,1},... | collective-permute-start | bytes 98312 | tf_op jit(solution)/shard_map/ppermute | solution.py:676
  108.9 5.2 %collective-permute-start.34 = (f32[64,128]{1,0:T(8,128)S(1)}, f32[64,128]{1,0:T(8,128)S(1)}, u32[]{:S(2)}, u32[]{:S(2)}) collective-permute-start(f32[64,128]{1,0:T(8,128)S(1)} %add_add_fusion.3), channel_id=1, source_target_pairs={{0,16},{1,17},{2,18},{3,19},{4,20},{5,21},{6,22},{7,23},{8,24},{9,... | collective-permute-start | bytes 98312 | tf_op jit(solution)/shard_map/ppermute | solution.py:676
  108.9 5.8 %collective-permute-start.35 = (f32[64,128]{1,0:T(8,128)S(1)}, f32[64,128]{1,0:T(8,128)S(1)}, u32[]{:S(2)}, u32[]{:S(2)}) collective-permute-start(f32[64,128]{1,0:T(8,128)S(1)} %add_add_fusion.3), channel_id=1, source_target_pairs={{0,24},{1,25},{2,26},{3,27},{4,28},{5,29},{6,30},{7,31},{8,16},{9,... | collective-permute-start | bytes 98312 | tf_op jit(solution)/shard_map/ppermute | solution.py:676

commit v5 on v4

--- a/solution.py
+++ b/solution.py
@@ -292,7 +292,11 @@
     def _():
         buffers[1][...] = jnp.zeros((PTS, PTS), jnp.float32)
 
-    lax.fori_loop(0, jnp.where(count > 0, lax.div(count, 2) + 1, 0), body, 0)
+    lax.fori_loop(0, lax.div(count + 1, 2), body, 0)
+
+    @pl.when(jnp.logical_and(count > 0, lax.rem(count, 2) == 0))
+    def _():
+        finish(count - 1, buffers[1])
 
 
 def build_tiles(stage, fresh, n, rows, cols, state, group, blocks_dev, cap, name):

time: 121 us -> 119 us (0.983)
  waiting for transfers between devices: 32.3 us -> 36.3 us
  Pallas kernels: 57.2 us -> 53.8 us
  starting transfers between devices: 28.6 us -> 25.6 us
    ppermute x6, waiting for transfers between devices: 13.3 us -> 16 us  [from_behind(): lax.ppermute(value, axis, [(source, source + steps) for source in range(i...]
    pallas_call x7, Pallas kernels: 20.5 us -> 18 us  [products(): call(*entries, *[vecs[first] for first in firsts], tiles, *begun)]
    ppermute x16, starting transfers between devices: 10.9 us -> 8.83 us  [swap(): lax.ppermute(value, axis, [(source, source ^ bit) for source in range(cou...]
  transfers between devices with their start and end apart: 29 -> 29, of which waited for: 18 -> 19; matrix products, arithmetic and copies ran while one was open for 0% -> 0% of each run, Pallas kernels for 34% -> 32%
where the time goes in v5:
time: 119 us
  Pallas kernels  53.8 us (45%)
  waiting for transfers between devices  36.3 us (31%)
  starting transfers between devices  25.6 us (22%)
  between operations  1.65 us (1%)
  local copies, waits for them, and re-layouts  1.44 us (1%)
    pallas_call x7, Pallas kernels, products(): call(*entries, *[vecs[first] for first in firsts], tiles, *begun)  18 us
    ppermute x6, waiting for transfers between devices, from_behind(): lax.ppermute(value, axis, [(source, source + steps) for source in range(i...  16 us
    pallas_call x4, Pallas kernels, build_tiles(): pl.pallas_call(kernel, out_shape=shapes, in_specs=[spec(SMEM)] * len(scal...  15.3 us
    pallas_call x1, Pallas kernels, listing(): pl.pallas_call(functools.partial(listing_kernel, group, cap, blocks_dev),...  12 us
    ppermute x16, waiting for transfers between devices, swap(): lax.ppermute(value, axis, [(source, source ^ bit) for source in range(cou...  11.6 us
    ppermute x16, starting transfers between devices, swap(): lax.ppermute(value, axis, [(source, source ^ bit) for source in range(cou...  8.83 us
    ppermute x7, waiting for transfers between devices, all_sum(): lax.ppermute(value, ('blk', 'grp'), [(source, source ^ move) for source i...  8.8 us
    ppermute x6, starting transfers between devices, from_behind(): lax.ppermute(value, axis, [(source, source + steps) for source in range(i...  8.54 us
  transfers between devices with their start and end apart: 29, of which 19 were waited for; matrix products, arithmetic and copies ran while one was open for 0% of the time, Pallas kernels for 32%

profile of v5, /device:TPU:0, one launch (start us, length us, event | category | flops | bytes accessed | tf_op | source)
XLA Modules:
  0.0 119.0 jit_solution(15367046659231485077)
XLA Ops:
  0.0 1.3 %slice.18 = bf16[512,768]{1,0:T(8,128)(2,1)S(1)} slice(bf16[1024,768]{1,0:T(8,128)(2,1)} %refs_3_.1), slice={[0:512], [0:768]} | slice | bytes 1572864 | tf_op jit(solution)/shard_map/slice | solution.py:704
  1.3 1.3 %collective-permute-start.7 = (bf16[512,768]{1,0:T(8,128)(2,1)S(1)}, bf16[512,768]{1,0:T(8,128)(2,1)S(1)}, u32[]{:S(2)}, u32[]{:S(2)}) collective-permute-start(bf16[512,768]{1,0:T(8,128)(2,1)S(1)} %slice.18), channel_id=1, source_target_pairs={{4,0},{8,4},{12,8},{16,12},{20,16},{24,20},{28,24},{5,1},{9,5},{13... | collective-permute-start | bytes 2359304 | tf_op jit(solution)/shard_map/ppermute | solution.py:37
  2.6 3.0 %collective-permute-start.8 = (bf16[512,768]{1,0:T(8,128)(2,1)S(1)}, bf16[512,768]{1,0:T(8,128)(2,1)S(1)}, u32[]{:S(2)}, u32[]{:S(2)}) collective-permute-start(bf16[512,768]{1,0:T(8,128)(2,1)S(1)} %slice.18), channel_id=1, source_target_pairs={{0,2},{1,3},{2,0},{3,1},{4,6},{5,7},{6,4},{7,5},{8,10},{9,11},{10,... | collective-permute-start | bytes 2359304 | tf_op jit(solution)/shard_map/ppermute | solution.py:31
  5.7 0.2 collective-permute-start.14
  5.9 1.3 %collective-permute-start.9 = (bf16[512,768]{1,0:T(8,128)(2,1)S(1)}, bf16[512,768]{1,0:T(8,128)(2,1)S(1)}, u32[]{:S(2)}, u32[]{:S(2)}) collective-permute-start(bf16[512,768]{1,0:T(8,128)(2,1)S(1)} %slice.19), channel_id=1, source_target_pairs={{4,0},{8,4},{12,8},{16,12},{20,16},{24,20},{28,24},{5,1},{9,5},{13... | collective-permute-start | bytes 2359304 | tf_op jit(solution)/shard_map/ppermute | solution.py:37
  7.8 0.6 opening.1.refs_4_
  8.4 12.0 %listing.1 = (s32[16]{0:T(128)S(1)}, s32[16]{0:T(128)S(1)}, s32[4]{0:T(128)S(1)}, s32[32]{0:T(128)S(1)}, s32[32]{0:T(128)S(1)}, /*index=5*/s32[32]{0:T(128)S(1)}, s32[9]{0:T(128)S(1)}) custom-call(s32[64]{0:T(128)S(1)} %copy-done.3, s32[64]{0:T(128)S(1)} %copy-done.4, s32[1]{0:T(128)S(6)} %copy.31.live), custom_call_target="tpu_custom_call" | custom-call | flops 1048576 | bytes 1024 | tf_op jit(solution)/shard_map/listing/pallas_call | solution.py:222
  20.4 4.1 %collective-permute-done.7.refs_5_ = bf16[512,768]{1,0:T(8,128)(2,1)S(1)} collective-permute-done((bf16[512,768]{1,0:T(8,128)(2,1)S(1)}, bf16[512,768]{1,0:T(8,128)(2,1)S(1)}, u32[]{:S(2)}, u32[]{:S(2)}) %collective-permute-start.7) | collective-permute-done | bytes 786464 | tf_op jit(solution)/shard_map/ppermute | solution.py:37
  24.6 0.1 collective-permute-start.11
  24.7 0.5 collective-permute-start.12
  25.2 1.2 %collective-permute-done.11 = bf16[256,768]{1,0:T(8,128)(2,1)S(1)} collective-permute-done((bf16[256,768]{1,0:T(8,128)(2,1)S(1)}, bf16[256,768]{1,0:T(8,128)(2,1)S(1)}, u32[]{:S(2)}, u32[]{:S(2)}) %collective-permute-start.11) | collective-permute-done | bytes 393248 | tf_op jit(solution)/shard_map/ppermute | solution.py:31
  26.4 0.1 collective-permute-start.10
  26.6 0.4 collective-permute-done.12
  27.0 0.1 pad_maximum_fusion.refs_3_
  27.1 6.9 %first_tiles.1 = (bf16[5120,768]{1,0:T(8,128)(2,1)S(1)}, f32[10,8,512]{2,1,0:T(8,128)S(1)}, f32[8,512,128]{2,1,0:T(8,128)S(1)}, bf16[17,512,512]{2,1,0:T(8,128)(2,1)S(1)}) custom-call(s32[4]{0:T(128)S(1)} %get-tuple-element.90.refs_0_, s32[16]{0:T(128)S(1)} %get-tuple-element.91.refs_1_, s32[16]{0:T(128)S(1)} %get-tuple-element.92.refs_2_, ...), custom_call_target="tpu_custom_call" | custom-call | flops 1048576 | bytes 1048576 | tf_op jit(solution)/shard_map/first_tiles/pallas_call | solution.py:343
  33.9 2.3 %second_tiles.1 = (bf16[5120,768]{1,0:T(8,128)(2,1)S(1)}, f32[10,8,512]{2,1,0:T(8,128)S(1)}, f32[8,512,128]{2,1,0:T(8,128)S(1)}, bf16[17,512,512]{2,1,0:T(8,128)(2,1)S(1)}) custom-call(s32[4]{0:T(128)S(1)} %get-tuple-element.90.refs_0_, s32[16]{0:T(128)S(1)} %get-tuple-element.91.refs_1_, ...), custom_call_target="tpu_custom_call", output_to_operand_aliasing={{0}: (4, {}), {1}: (5, {}), {2}: (6, {}), {3}: (7, {})} | custom-call | flops 1048576 | bytes 1048576 | tf_op jit(solution)/shard_map/second_tiles/pallas_call | solution.py:343
  36.2 2.5 %products.7 = (f32[2,72,512]{2,1,0:T(8,128)S(1)}, f32[4,72,512]{2,1,0:T(8,128)S(1)}, f32[2,72,512]{2,1,0:T(8,128)S(1)}, f32[2,72,512]{2,1,0:T(8,128)S(1)}) custom-call(s32[32]{0:T(128)S(1)} %get-tuple-element.82.refs_0_, s32[32]{0:T(128)S(1)} %get-tuple-element.83.refs_1_, s32[32]{0:T(128)S(1)} %get-tuple-element.84.refs_2_, ...), custom_call_target="tpu_custom_call" | custom-call | flops 1048576 | bytes 1048576 | tf_op jit(solution)/shard_map/products/pallas_call | solution.py:447
  38.8 1.3 %collective-permute-done.14.refs_1_ = bf16[512,768]{1,0:T(8,128)(2,1)S(1)} collective-permute-done((bf16[512,768]{1,0:T(8,128)(2,1)S(1)}, bf16[512,768]{1,0:T(8,128)(2,1)S(1)}, u32[]{:S(2)}, u32[]{:S(2)}) %collective-permute-start.14) | collective-permute-done | bytes 786464 | tf_op jit(solution)/shard_map/ppermute | solution.py:31
  40.0 0.6 collective-permute-done.9.refs_0_
  40.6 1.7 %collective-permute-start.16 = (bf16[80,1024]{1,0:T(8,128)(2,1)S(1)}, bf16[80,1024]{1,0:T(8,128)(2,1)S(1)}, u32[]{:S(2)}, u32[]{:S(2)}) collective-permute-start(bf16[80,1024]{1,0:T(8,128)(2,1)S(1)} %opening.1.refs_4_), channel_id=1, source_target_pairs={{0,2},{1,3},{2,0},{3,1},{4,6},{5,7},{6,4},{7,5},{8,10},{9,11},{10,... | collective-permute-start | bytes 491528 | tf_op jit(solution)/shard_map/ppermute | solution.py:31
  42.3 1.3 %collective-permute-start.18 = (bf16[80,1024]{1,0:T(8,128)(2,1)S(1)}, bf16[80,1024]{1,0:T(8,128)(2,1)S(1)}, u32[]{:S(2)}, u32[]{:S(2)}) collective-permute-start(bf16[80,1024]{1,0:T(8,128)(2,1)S(1)} %opening.1.refs_4_), channel_id=1, source_target_pairs={{4,0},{8,4},{12,8},{16,12},{20,16},{24,20},{28,24},{5,1},{9,5},{13... | collective-permute-start | bytes 491528 | tf_op jit(solution)/shard_map/ppermute | solution.py:37
  43.6 0.8 more_blocks.1
  44.4 5.4 %last_tiles.1 = (bf16[5120,768]{1,0:T(8,128)(2,1)S(1)}, f32[10,8,512]{2,1,0:T(8,128)S(1)}, f32[8,512,128]{2,1,0:T(8,128)S(1)}, bf16[17,512,512]{2,1,0:T(8,128)(2,1)S(1)}) custom-call(s32[4]{0:T(128)S(1)} %get-tuple-element.90.refs_0_, s32[16]{0:T(128)S(1)} %get-tuple-element.91.refs_1_, ...), custom_call_target="tpu_custom_call", output_to_operand_aliasing={{0}: (4, {}), {1}: (5, {}), {2}: (6, {}), {3}: (7, {})} | custom-call | flops 4294967296 | bytes 1048576 | tf_op jit(solution)/shard_map/last_tiles/pallas_call | solution.py:343
  49.8 0.1 collective-permute-start.17
  49.9 1.3 %products.8 = (f32[2,72,512]{2,1,0:T(8,128)S(1)}, f32[4,72,512]{2,1,0:T(8,128)S(1)}, f32[2,72,512]{2,1,0:T(8,128)S(1)}, f32[2,72,512]{2,1,0:T(8,128)S(1)}) custom-call(s32[32]{0:T(128)S(1)} %get-tuple-element.82.refs_0_, s32[32]{0:T(128)S(1)} %get-tuple-element.83.refs_1_, s32[32]{0:T(128)S(1)} %get-tuple-element.84.refs_2_, ...), custom_call_target="tpu_custom_call" | custom-call | flops 1048576 | bytes 1048576 | tf_op jit(solution)/shard_map/products/pallas_call | solution.py:447
  51.2 0.1 collective-permute-done.18.refs_6_
  51.2 4.0 %products.9 = (f32[4,72,512]{2,1,0:T(8,128)S(1)}, f32[2,72,512]{2,1,0:T(8,128)S(1)}, f32[2,72,512]{2,1,0:T(8,128)S(1)}) custom-call(s32[32]{0:T(128)S(1)} %get-tuple-element.82.refs_0_, s32[32]{0:T(128)S(1)} %get-tuple-element.83.refs_1_, s32[32]{0:T(128)S(1)} %get-tuple-element.84.refs_2_, s32[9]{0:T(128)S(1)} %get-tuple-element.85.refs_3_, ...), custom_call_target="tpu_custom_call" | custom-call | flops 2147483648 | bytes 1048576 | tf_op jit(solution)/shard_map/products/pallas_call | solution.py:447
  55.3 0.5 collective-permute-start.19
  55.8 2.1 %collective-permute-start.20 = (f32[2,72,512]{2,1,0:T(8,128)S(1)}, f32[2,72,512]{2,1,0:T(8,128)S(1)}, u32[]{:S(2)}, u32[]{:S(2)}) collective-permute-start(f32[2,72,512]{2,1,0:T(8,128)S(1)} %get-tuple-element.126), channel_id=1, source_target_pairs={{0,4},{4,8},{8,12},{12,16},{16,20},{20,24},{24,28},{1,5},{5,9},{9,... | collective-permute-start | bytes 884744 | tf_op jit(solution)/shard_map/ppermute | solution.py:37
  57.9 1.1 collective-permute-start.21
  59.1 1.6 %products.10.refs_0_ = f32[2,72,512]{2,1,0:T(8,128)S(1)} custom-call(s32[32]{0:T(128)S(1)} %get-tuple-element.82.refs_0_, s32[32]{0:T(128)S(1)} %get-tuple-element.83.refs_1_, s32[32]{0:T(128)S(1)} %get-tuple-element.84.refs_2_, s32[9]{0:T(128)S(1)} %get-tuple-element.85.refs_3_, bf16[80,1024]{1,0:T(8,128)(2,1)S(1)} %collective-permute-done.16.refs_4_, ...), custom_call_target="tpu_custom_call" | custom-call | flops 1048576 | bytes 1048576 | tf_op jit(solution)/shard_map/products/pallas_call | solution.py:447
  60.7 4.1 %collective-permute-done.20.refs_1_ = f32[2,72,512]{2,1,0:T(8,128)S(1)} collective-permute-done((f32[2,72,512]{2,1,0:T(8,128)S(1)}, f32[2,72,512]{2,1,0:T(8,128)S(1)}, u32[]{:S(2)}, u32[]{:S(2)}) %collective-permute-start.20) | collective-permute-done | bytes 294944 | tf_op jit(solution)/shard_map/ppermute | solution.py:37
  64.8 2.4 %collective-permute-done.21.refs_3_ = f32[2,72,512]{2,1,0:T(8,128)S(1)} collective-permute-done((f32[2,72,512]{2,1,0:T(8,128)S(1)}, f32[2,72,512]{2,1,0:T(8,128)S(1)}, u32[]{:S(2)}, u32[]{:S(2)}) %collective-permute-start.21) | collective-permute-done | bytes 294944 | tf_op jit(solution)/shard_map/ppermute | solution.py:31
  67.1 0.9 scaled_gram.2
  68.1 0.1 collective-permute-start.22
  68.2 1.3 %collective-permute-start.23 = (bf16[128,1024]{1,0:T(8,128)(2,1)S(1)}, bf16[128,1024]{1,0:T(8,128)(2,1)S(1)}, u32[]{:S(2)}, u32[]{:S(2)}) collective-permute-start(bf16[128,1024]{1,0:T(8,128)(2,1)S(1)} %get-tuple-element.128.refs_4_), channel_id=1, source_target_pairs={{0,2},{1,3},{2,0},{3,1},{4,6},{5,7},{6,4},{7,5},{8,10},{9,11},{10,... | collective-permute-start | bytes 786440 | tf_op jit(solution)/shard_map/ppermute | solution.py:31
  69.5 1.3 %collective-permute-start.25 = (bf16[128,1024]{1,0:T(8,128)(2,1)S(1)}, bf16[128,1024]{1,0:T(8,128)(2,1)S(1)}, u32[]{:S(2)}, u32[]{:S(2)}) collective-permute-start(bf16[128,1024]{1,0:T(8,128)(2,1)S(1)} %get-tuple-element.128.refs_4_), channel_id=1, source_target_pairs={{4,0},{8,4},{12,8},{16,12},{20,16},{24,20},{28,24},{5,1},{9,5},{13... | collective-permute-start | bytes 786440 | tf_op jit(solution)/shard_map/ppermute | solution.py:37
  70.8 3.0 %products.11 = (f32[2,64,512]{2,1,0:T(8,128)S(1)}, f32[4,64,512]{2,1,0:T(8,128)S(1)}, f32[2,64,512]{2,1,0:T(8,128)S(1)}, f32[2,64,512]{2,1,0:T(8,128)S(1)}) custom-call(s32[32]{0:T(128)S(1)} %get-tuple-element.82.refs_0_, s32[32]{0:T(128)S(1)} %get-tuple-element.83.refs_1_, s32[32]{0:T(128)S(1)} %get-tuple-element.84.refs_2_, ...), custom_call_target="tpu_custom_call" | custom-call | flops 1048576 | bytes 1048576 | tf_op jit(solution)/shard_map/products/pallas_call | solution.py:447
  73.8 3.1 %collective-permute-done.23.refs_4_ = bf16[128,1024]{1,0:T(8,128)(2,1)S(1)} collective-permute-done((bf16[128,1024]{1,0:T(8,128)(2,1)S(1)}, bf16[128,1024]{1,0:T(8,128)(2,1)S(1)}, u32[]{:S(2)}, u32[]{:S(2)}) %collective-permute-start.23) | collective-permute-done | bytes 262176 | tf_op jit(solution)/shard_map/ppermute | solution.py:31
  76.9 2.8 %collective-permute-done.25.refs_6_ = bf16[128,1024]{1,0:T(8,128)(2,1)S(1)} collective-permute-done((bf16[128,1024]{1,0:T(8,128)(2,1)S(1)}, bf16[128,1024]{1,0:T(8,128)(2,1)S(1)}, u32[]{:S(2)}, u32[]{:S(2)}) %collective-permute-start.25) | collective-permute-done | bytes 262176 | tf_op jit(solution)/shard_map/ppermute | solution.py:37
  79.7 4.1 %products.12 = (f32[4,64,512]{2,1,0:T(8,128)S(1)}, f32[2,64,512]{2,1,0:T(8,128)S(1)}, f32[2,64,512]{2,1,0:T(8,128)S(1)}) custom-call(s32[32]{0:T(128)S(1)} %get-tuple-element.82.refs_0_, s32[32]{0:T(128)S(1)} %get-tuple-element.83.refs_1_, s32[32]{0:T(128)S(1)} %get-tuple-element.84.refs_2_, s32[9]{0:T(128)S(1)} %get-tuple-element.85.refs_3_, ...), custom_call_target="tpu_custom_call" | custom-call | flops 2147483648 | bytes 1048576 | tf_op jit(solution)/shard_map/products/pallas_call | solution.py:447
  83.8 0.1 collective-permute-start.26
  83.9 1.3 %collective-permute-start.27 = (f32[2,64,512]{2,1,0:T(8,128)S(1)}, f32[2,64,512]{2,1,0:T(8,128)S(1)}, u32[]{:S(2)}, u32[]{:S(2)}) collective-permute-start(f32[2,64,512]{2,1,0:T(8,128)S(1)} %get-tuple-element.138), channel_id=1, source_target_pairs={{0,4},{4,8},{8,12},{12,16},{16,20},{20,24},{24,28},{1,5},{5,9},{9,... | collective-permute-start | bytes 786440 | tf_op jit(solution)/shard_map/ppermute | solution.py:37
  85.2 0.6 collective-permute-done.26.refs_2_
  85.8 0.1 collective-permute-start.28
  85.9 1.5 %products.13.refs_0_ = f32[2,64,512]{2,1,0:T(8,128)S(1)} custom-call(s32[32]{0:T(128)S(1)} %get-tuple-element.82.refs_0_, s32[32]{0:T(128)S(1)} %get-tuple-element.83.refs_1_, s32[32]{0:T(128)S(1)} %get-tuple-element.84.refs_2_, s32[9]{0:T(128)S(1)} %get-tuple-element.85.refs_3_, bf16[128,1024]{1,0:T(8,128)(2,1)S(1)} %collective-permute-done.23.refs_4_, ...), custom_call_target="tpu_custom_call" | custom-call | flops 1048576 | bytes 1048576 | tf_op jit(solution)/shard_map/products/pallas_call | solution.py:447
  87.4 4.3 %collective-permute-done.27.refs_1_ = f32[2,64,512]{2,1,0:T(8,128)S(1)} collective-permute-done((f32[2,64,512]{2,1,0:T(8,128)S(1)}, f32[2,64,512]{2,1,0:T(8,128)S(1)}, u32[]{:S(2)}, u32[]{:S(2)}) %collective-permute-start.27) | collective-permute-done | bytes 262176 | tf_op jit(solution)/shard_map/ppermute | solution.py:37
  91.7 2.6 %collective-permute-done.28.refs_3_ = f32[2,64,512]{2,1,0:T(8,128)S(1)} collective-permute-done((f32[2,64,512]{2,1,0:T(8,128)S(1)}, f32[2,64,512]{2,1,0:T(8,128)S(1)}, u32[]{:S(2)}, u32[]{:S(2)}) %collective-permute-start.28) | collective-permute-done | bytes 262176 | tf_op jit(solution)/shard_map/ppermute | solution.py:31
  94.3 1.0 scaled_gram.3
  95.3 0.1 collective-permute-start.29
  95.3 1.2 %collective-permute-done.29 = f32[64,128]{1,0:T(8,128)S(1)} collective-permute-done((f32[64,128]{1,0:T(8,128)S(1)}, f32[64,128]{1,0:T(8,128)S(1)}, u32[]{:S(2)}, u32[]{:S(2)}) %collective-permute-start.29) | collective-permute-done | bytes 32800 | tf_op jit(solution)/shard_map/ppermute | solution.py:680
  96.5 0.3 collective-permute-start.30
  96.8 2.0 %collective-permute-start.31 = (f32[64,128]{1,0:T(8,128)S(1)}, f32[64,128]{1,0:T(8,128)S(1)}, u32[]{:S(2)}, u32[]{:S(2)}) collective-permute-start(f32[64,128]{1,0:T(8,128)S(1)} %add.50), channel_id=1, source_target_pairs={{0,4},{1,5},{2,6},{3,7},{4,0},{5,1},{6,2},{7,3},{8,12},{9,13},{10,... | collective-permute-start | bytes 98312 | tf_op jit(solution)/shard_map/ppermute | solution.py:680
  98.8 1.2 %collective-permute-start.32 = (f32[64,128]{1,0:T(8,128)S(1)}, f32[64,128]{1,0:T(8,128)S(1)}, u32[]{:S(2)}, u32[]{:S(2)}) collective-permute-start(f32[64,128]{1,0:T(8,128)S(1)} %add.50), channel_id=1, source_target_pairs={{0,6},{1,7},{2,4},{3,5},{4,2},{5,3},{6,0},{7,1},{8,14},{9,15},{10,... | collective-permute-start | bytes 98312 | tf_op jit(solution)/shard_map/ppermute | solution.py:680
  100.0 0.4 collective-permute-done.30
  100.5 0.3 collective-permute-done.31
  100.7 2.9 %collective-permute-done.32 = f32[64,128]{1,0:T(8,128)S(1)} collective-permute-done((f32[64,128]{1,0:T(8,128)S(1)}, f32[64,128]{1,0:T(8,128)S(1)}, u32[]{:S(2)}, u32[]{:S(2)}) %collective-permute-start.32) | collective-permute-done | bytes 32800 | tf_op jit(solution)/shard_map/ppermute | solution.py:680
  103.7 2.2 %collective-permute-start.33 = (f32[64,128]{1,0:T(8,128)S(1)}, f32[64,128]{1,0:T(8,128)S(1)}, u32[]{:S(2)}, u32[]{:S(2)}) collective-permute-start(f32[64,128]{1,0:T(8,128)S(1)} %add_add_fusion.3), channel_id=1, source_target_pairs={{0,8},{1,9},{2,10},{3,11},{4,12},{5,13},{6,14},{7,15},{8,0},{9,1},... | collective-permute-start | bytes 98312 | tf_op jit(solution)/shard_map/ppermute | solution.py:680
  105.9 0.7 collective-permute-start.34
  106.6 1.7 %collective-permute-start.35 = (f32[64,128]{1,0:T(8,128)S(1)}, f32[64,128]{1,0:T(8,128)S(1)}, u32[]{:S(2)}, u32[]{:S(2)}) collective-permute-start(f32[64,128]{1,0:T(8,128)S(1)} %add_add_fusion.3), channel_id=1, source_target_pairs={{0,24},{1,25},{2,26},{3,27},{4,28},{5,29},{6,30},{7,31},{8,16},{9,... | collective-permute-start | bytes 98312 | tf_op jit(solution)/shard_map/ppermute | solution.py:680
  108.3 2.4 %collective-permute-done.34 = f32[64,128]{1,0:T(8,128)S(1)} collective-permute-done((f32[64,128]{1,0:T(8,128)S(1)}, f32[64,128]{1,0:T(8,128)S(1)}, u32[]{:S(2)}, u32[]{:S(2)}) %collective-permute-start.34) | collective-permute-done | bytes 32800 | tf_op jit(solution)/shard_map/ppermute | solution.py:680
  110.7 1.6 %collective-permute-done.35 = f32[64,128]{1,0:T(8,128)S(1)} collective-permute-done((f32[64,128]{1,0:T(8,128)S(1)}, f32[64,128]{1,0:T(8,128)S(1)}, u32[]{:S(2)}, u32[]{:S(2)}) %collective-permute-start.35) | collective-permute-done | bytes 32800 | tf_op jit(solution)/shard_map/ppermute | solution.py:680
  112.3 4.9 %factors.1 = (f32[64,64]{1,0:T(8,128)S(1)}, f32[64,64]{1,0:T(8,128)S(1)}, s32[1]{0:T(128)}) custom-call(f32[64,128]{1,0:T(8,128)S(1)} %add_add_fusion.2.grams), custom_call_target="tpu_custom_call" | custom-call | flops 1073741824 | bytes 65536 | tf_op jit(solution)/shard_map/factors/pallas_call | solution.py:618
  117.9 1.1 applied.3
  (31 shorter events, 0.3 us)
Async XLA Ops:
  0.0 5.7 %copy-start = (bf16[1024,768]{1,0:T(8,128)(2,1)S(1)}, bf16[1024,768]{1,0:T(8,128)(2,1)}, u32[]{:S(2)}) copy-start(bf16[1024,768]{1,0:T(8,128)(2,1)} %refs_3_.1) | copy-start | bytes 4718596
  0.0 7.8 %copy-start.1 = (f32[64,1024]{1,0:T(8,128)S(1)}, f32[64,1024]{1,0:T(8,128)}, u32[]{:S(2)}) copy-start(f32[64,1024]{1,0:T(8,128)} %start.1) | copy-start | bytes 786436
  0.0 7.8 %copy-start.2 = (s32[2]{0:T(128)S(1)}, s32[2]{0:T(128)}, u32[]{:S(2)}) copy-start(s32[2]{0:T(128)} %count_ref.3) | copy-start | bytes 28
  0.0 8.4 %copy-start.3 = (s32[64]{0:T(128)S(1)}, s32[64]{0:T(128)}, u32[]{:S(2)}) copy-start(s32[64]{0:T(128)} %rows.1) | copy-start | bytes 772
  0.0 8.4 %copy-start.4 = (s32[64]{0:T(128)S(1)}, s32[64]{0:T(128)}, u32[]{:S(2)}) copy-start(s32[64]{0:T(128)} %cols.1) | copy-start | bytes 772
  1.3 23.2 %collective-permute-start.7 = (bf16[512,768]{1,0:T(8,128)(2,1)S(1)}, bf16[512,768]{1,0:T(8,128)(2,1)S(1)}, u32[]{:S(2)}, u32[]{:S(2)}) collective-permute-start(bf16[512,768]{1,0:T(8,128)(2,1)S(1)} %slice.18), channel_id=1, source_target_pairs={{4,0},{8,4},{12,8},{16,12},{20,16},{24,20},{28,24},{5,1},{9,5},{13... | collective-permute-start | bytes 2359304 | tf_op jit(solution)/shard_map/ppermute | solution.py:37
  2.6 22.0 %collective-permute-start.8 = (bf16[512,768]{1,0:T(8,128)(2,1)S(1)}, bf16[512,768]{1,0:T(8,128)(2,1)S(1)}, u32[]{:S(2)}, u32[]{:S(2)}) collective-permute-start(bf16[512,768]{1,0:T(8,128)(2,1)S(1)} %slice.18), channel_id=1, source_target_pairs={{0,2},{1,3},{2,0},{3,1},{4,6},{5,7},{6,4},{7,5},{8,10},{9,11},{10,... | collective-permute-start | bytes 2359304 | tf_op jit(solution)/shard_map/ppermute | solution.py:31
  5.7 21.4 %collective-permute-start.13 = (bf16[1024,768]{1,0:T(8,128)(2,1)}, bf16[1024,768]{1,0:T(8,128)(2,1)S(1)}, u32[]{:S(2)}, u32[]{:S(2)}) collective-permute-start(bf16[1024,768]{1,0:T(8,128)(2,1)} %refs_3_.1), channel_id=1, source_target_pairs={{0,1},{1,0},{2,3},{3,2},{4,5},{5,4},{6,7},{7,6},{8,9},{9,8},{10,11... | collective-permute-start | bytes 4718600 | tf_op jit(solution)/shard_map/ppermute | solution.py:31
  5.7 34.3 %collective-permute-start.14 = (bf16[512,768]{1,0:T(8,128)(2,1)S(1)}, bf16[512,768]{1,0:T(8,128)(2,1)S(1)}, u32[]{:S(2)}, u32[]{:S(2)}) collective-permute-start(bf16[512,768]{1,0:T(8,128)(2,1)S(1)} %slice.19), channel_id=1, source_target_pairs={{0,2},{1,3},{2,0},{3,1},{4,6},{5,7},{6,4},{7,5},{8,10},{9,11},{10,... | collective-permute-start | bytes 2359304 | tf_op jit(solution)/shard_map/ppermute | solution.py:31
  5.9 34.7 %collective-permute-start.9 = (bf16[512,768]{1,0:T(8,128)(2,1)S(1)}, bf16[512,768]{1,0:T(8,128)(2,1)S(1)}, u32[]{:S(2)}, u32[]{:S(2)}) collective-permute-start(bf16[512,768]{1,0:T(8,128)(2,1)S(1)} %slice.19), channel_id=1, source_target_pairs={{4,0},{8,4},{12,8},{16,12},{20,16},{24,20},{28,24},{5,1},{9,5},{13... | collective-permute-start | bytes 2359304 | tf_op jit(solution)/shard_map/ppermute | solution.py:37
  24.6 1.8 %collective-permute-start.11 = (bf16[256,768]{1,0:T(8,128)(2,1)S(1)}, bf16[256,768]{1,0:T(8,128)(2,1)S(1)}, u32[]{:S(2)}, u32[]{:S(2)}) collective-permute-start(bf16[256,768]{1,0:T(8,128)(2,1)S(1)} %get-tuple-element.148), channel_id=1, source_target_pairs={{0,1},{1,0},{2,3},{3,2},{4,5},{5,4},{6,7},{7,6},{8,9},{9,8},{10,11... | collective-permute-start | bytes 1179656 | tf_op jit(solution)/shard_map/ppermute | solution.py:31
  24.7 2.3 %collective-permute-start.12 = (bf16[256,768]{1,0:T(8,128)(2,1)S(1)}, bf16[256,768]{1,0:T(8,128)(2,1)S(1)}, u32[]{:S(2)}, u32[]{:S(2)}) collective-permute-start(bf16[256,768]{1,0:T(8,128)(2,1)S(1)} %get-tuple-element.149), channel_id=1, source_target_pairs={{0,1},{1,0},{2,3},{3,2},{4,5},{5,4},{6,7},{7,6},{8,9},{9,8},{10,11... | collective-permute-start | bytes 1179656 | tf_op jit(solution)/shard_map/ppermute | solution.py:31
  26.4 9.8 %collective-permute-start.10 = (bf16[80,1024]{1,0:T(8,128)(2,1)S(1)}, bf16[80,1024]{1,0:T(8,128)(2,1)S(1)}, u32[]{:S(2)}, u32[]{:S(2)}) collective-permute-start(bf16[80,1024]{1,0:T(8,128)(2,1)S(1)} %opening.1.refs_4_), channel_id=1, source_target_pairs={{0,1},{1,0},{2,3},{3,2},{4,5},{5,4},{6,7},{7,6},{8,9},{9,8},{10,11... | collective-permute-start | bytes 491528 | tf_op jit(solution)/shard_map/ppermute | solution.py:31
  40.6 3.8 %collective-permute-start.15 = (bf16[512,768]{1,0:T(8,128)(2,1)S(1)}, bf16[512,768]{1,0:T(8,128)(2,1)S(1)}, u32[]{:S(2)}, u32[]{:S(2)}) collective-permute-start(bf16[512,768]{1,0:T(8,128)(2,1)S(1)} %collective-permute-done.14.refs_1_), channel_id=1, source_target_pairs={{0,1},{1,0},{2,3},{3,2},{4,5},{5,4},{6,7},{7,6},{8,9},{9,8},{10,11... | collective-permute-start | bytes 2359304 | tf_op jit(solution)/shard_map/ppermute | solution.py:31
  40.6 9.2 %collective-permute-start.16 = (bf16[80,1024]{1,0:T(8,128)(2,1)S(1)}, bf16[80,1024]{1,0:T(8,128)(2,1)S(1)}, u32[]{:S(2)}, u32[]{:S(2)}) collective-permute-start(bf16[80,1024]{1,0:T(8,128)(2,1)S(1)} %opening.1.refs_4_), channel_id=1, source_target_pairs={{0,2},{1,3},{2,0},{3,1},{4,6},{5,7},{6,4},{7,5},{8,10},{9,11},{10,... | collective-permute-start | bytes 491528 | tf_op jit(solution)/shard_map/ppermute | solution.py:31
  42.3 8.9 %collective-permute-start.18 = (bf16[80,1024]{1,0:T(8,128)(2,1)S(1)}, bf16[80,1024]{1,0:T(8,128)(2,1)S(1)}, u32[]{:S(2)}, u32[]{:S(2)}) collective-permute-start(bf16[80,1024]{1,0:T(8,128)(2,1)S(1)} %opening.1.refs_4_), channel_id=1, source_target_pairs={{4,0},{8,4},{12,8},{16,12},{20,16},{24,20},{28,24},{5,1},{9,5},{13... | collective-permute-start | bytes 491528 | tf_op jit(solution)/shard_map/ppermute | solution.py:37
  49.8 1.5 %collective-permute-start.17 = (bf16[80,1024]{1,0:T(8,128)(2,1)S(1)}, bf16[80,1024]{1,0:T(8,128)(2,1)S(1)}, u32[]{:S(2)}, u32[]{:S(2)}) collective-permute-start(bf16[80,1024]{1,0:T(8,128)(2,1)S(1)} %collective-permute-done.16.refs_4_), channel_id=1, source_target_pairs={{0,1},{1,0},{2,3},{3,2},{4,5},{5,4},{6,7},{7,6},{8,9},{9,8},{10,11... | collective-permute-start | bytes 491528 | tf_op jit(solution)/shard_map/ppermute | solution.py:31
  55.3 2.6 %collective-permute-start.19 = (f32[4,72,512]{2,1,0:T(8,128)S(1)}, f32[4,72,512]{2,1,0:T(8,128)S(1)}, u32[]{:S(2)}, u32[]{:S(2)}) collective-permute-start(f32[4,72,512]{2,1,0:T(8,128)S(1)} %get-tuple-element.123), channel_id=1, source_target_pairs={{0,1},{1,0},{2,3},{3,2},{4,5},{5,4},{6,7},{7,6},{8,9},{9,8},{10,11... | collective-permute-start | bytes 1769480 | tf_op jit(solution)/shard_map/ppermute | solution.py:31
  55.8 9.0 %collective-permute-start.20 = (f32[2,72,512]{2,1,0:T(8,128)S(1)}, f32[2,72,512]{2,1,0:T(8,128)S(1)}, u32[]{:S(2)}, u32[]{:S(2)}) collective-permute-start(f32[2,72,512]{2,1,0:T(8,128)S(1)} %get-tuple-element.126), channel_id=1, source_target_pairs={{0,4},{4,8},{8,12},{12,16},{16,20},{20,24},{24,28},{1,5},{5,9},{9,... | collective-permute-start | bytes 884744 | tf_op jit(solution)/shard_map/ppermute | solution.py:37
  57.9 9.2 %collective-permute-start.21 = (f32[2,72,512]{2,1,0:T(8,128)S(1)}, f32[2,72,512]{2,1,0:T(8,128)S(1)}, u32[]{:S(2)}, u32[]{:S(2)}) collective-permute-start(f32[2,72,512]{2,1,0:T(8,128)S(1)} %slice_add_fusion), channel_id=1, source_target_pairs={{0,2},{1,3},{2,0},{3,1},{4,6},{5,7},{6,4},{7,5},{8,10},{9,11},{10,... | collective-permute-start | bytes 884744 | tf_op jit(solution)/shard_map/ppermute | solution.py:31
  68.1 2.7 %collective-permute-start.22 = (bf16[128,1024]{1,0:T(8,128)(2,1)S(1)}, bf16[128,1024]{1,0:T(8,128)(2,1)S(1)}, u32[]{:S(2)}, u32[]{:S(2)}) collective-permute-start(bf16[128,1024]{1,0:T(8,128)(2,1)S(1)} %get-tuple-element.128.refs_4_), channel_id=1, source_target_pairs={{0,1},{1,0},{2,3},{3,2},{4,5},{5,4},{6,7},{7,6},{8,9},{9,8},{10,11... | collective-permute-start | bytes 786440 | tf_op jit(solution)/shard_map/ppermute | solution.py:31
  68.2 8.7 %collective-permute-start.23 = (bf16[128,1024]{1,0:T(8,128)(2,1)S(1)}, bf16[128,1024]{1,0:T(8,128)(2,1)S(1)}, u32[]{:S(2)}, u32[]{:S(2)}) collective-permute-start(bf16[128,1024]{1,0:T(8,128)(2,1)S(1)} %get-tuple-element.128.refs_4_), channel_id=1, source_target_pairs={{0,2},{1,3},{2,0},{3,1},{4,6},{5,7},{6,4},{7,5},{8,10},{9,11},{10,... | collective-permute-start | bytes 786440 | tf_op jit(solution)/shard_map/ppermute | solution.py:31
  69.5 10.3 %collective-permute-start.25 = (bf16[128,1024]{1,0:T(8,128)(2,1)S(1)}, bf16[128,1024]{1,0:T(8,128)(2,1)S(1)}, u32[]{:S(2)}, u32[]{:S(2)}) collective-permute-start(bf16[128,1024]{1,0:T(8,128)(2,1)S(1)} %get-tuple-element.128.refs_4_), channel_id=1, source_target_pairs={{4,0},{8,4},{12,8},{16,12},{20,16},{24,20},{28,24},{5,1},{9,5},{13... | collective-permute-start | bytes 786440 | tf_op jit(solution)/shard_map/ppermute | solution.py:37
  76.9 2.8 %collective-permute-start.24 = (bf16[128,1024]{1,0:T(8,128)(2,1)S(1)}, bf16[128,1024]{1,0:T(8,128)(2,1)S(1)}, u32[]{:S(2)}, u32[]{:S(2)}) collective-permute-start(bf16[128,1024]{1,0:T(8,128)(2,1)S(1)} %collective-permute-done.23.refs_4_), channel_id=1, source_target_pairs={{0,1},{1,0},{2,3},{3,2},{4,5},{5,4},{6,7},{7,6},{8,9},{9,8},{10,11... | collective-permute-start | bytes 786440 | tf_op jit(solution)/shard_map/ppermute | solution.py:31
  83.8 2.0 %collective-permute-start.26 = (f32[4,64,512]{2,1,0:T(8,128)S(1)}, f32[4,64,512]{2,1,0:T(8,128)S(1)}, u32[]{:S(2)}, u32[]{:S(2)}) collective-permute-start(f32[4,64,512]{2,1,0:T(8,128)S(1)} %get-tuple-element.135), channel_id=1, source_target_pairs={{0,1},{1,0},{2,3},{3,2},{4,5},{5,4},{6,7},{7,6},{8,9},{9,8},{10,11... | collective-permute-start | bytes 1572872 | tf_op jit(solution)/shard_map/ppermute | solution.py:31
  83.9 7.8 %collective-permute-start.27 = (f32[2,64,512]{2,1,0:T(8,128)S(1)}, f32[2,64,512]{2,1,0:T(8,128)S(1)}, u32[]{:S(2)}, u32[]{:S(2)}) collective-permute-start(f32[2,64,512]{2,1,0:T(8,128)S(1)} %get-tuple-element.138), channel_id=1, source_target_pairs={{0,4},{4,8},{8,12},{12,16},{16,20},{20,24},{24,28},{1,5},{5,9},{9,... | collective-permute-start | bytes 786440 | tf_op jit(solution)/shard_map/ppermute | solution.py:37
  85.8 8.4 %collective-permute-start.28 = (f32[2,64,512]{2,1,0:T(8,128)S(1)}, f32[2,64,512]{2,1,0:T(8,128)S(1)}, u32[]{:S(2)}, u32[]{:S(2)}) collective-permute-start(f32[2,64,512]{2,1,0:T(8,128)S(1)} %slice_add_fusion.1), channel_id=1, source_target_pairs={{0,2},{1,3},{2,0},{3,1},{4,6},{5,7},{6,4},{7,5},{8,10},{9,11},{10,... | collective-permute-start | bytes 786440 | tf_op jit(solution)/shard_map/ppermute | solution.py:31
  95.3 1.3 %collective-permute-start.29 = (f32[64,128]{1,0:T(8,128)S(1)}, f32[64,128]{1,0:T(8,128)S(1)}, u32[]{:S(2)}, u32[]{:S(2)}) collective-permute-start(f32[64,128]{1,0:T(8,128)S(1)} %get-tuple-element.143), channel_id=1, source_target_pairs={{0,1},{1,0},{2,3},{3,2},{4,5},{5,4},{6,7},{7,6},{8,9},{9,8},{10,11... | collective-permute-start | bytes 98312 | tf_op jit(solution)/shard_map/ppermute | solution.py:680
  96.5 3.9 %collective-permute-start.30 = (f32[64,128]{1,0:T(8,128)S(1)}, f32[64,128]{1,0:T(8,128)S(1)}, u32[]{:S(2)}, u32[]{:S(2)}) collective-permute-start(f32[64,128]{1,0:T(8,128)S(1)} %add.50), channel_id=1, source_target_pairs={{0,2},{1,3},{2,0},{3,1},{4,6},{5,7},{6,4},{7,5},{8,10},{9,11},{10,... | collective-permute-start | bytes 98312 | tf_op jit(solution)/shard_map/ppermute | solution.py:680
  96.8 3.9 %collective-permute-start.31 = (f32[64,128]{1,0:T(8,128)S(1)}, f32[64,128]{1,0:T(8,128)S(1)}, u32[]{:S(2)}, u32[]{:S(2)}) collective-permute-start(f32[64,128]{1,0:T(8,128)S(1)} %add.50), channel_id=1, source_target_pairs={{0,4},{1,5},{2,6},{3,7},{4,0},{5,1},{6,2},{7,3},{8,12},{9,13},{10,... | collective-permute-start | bytes 98312 | tf_op jit(solution)/shard_map/ppermute | solution.py:680
  98.8 4.8 %collective-permute-start.32 = (f32[64,128]{1,0:T(8,128)S(1)}, f32[64,128]{1,0:T(8,128)S(1)}, u32[]{:S(2)}, u32[]{:S(2)}) collective-permute-start(f32[64,128]{1,0:T(8,128)S(1)} %add.50), channel_id=1, source_target_pairs={{0,6},{1,7},{2,4},{3,5},{4,2},{5,3},{6,0},{7,1},{8,14},{9,15},{10,... | collective-permute-start | bytes 98312 | tf_op jit(solution)/shard_map/ppermute | solution.py:680
  103.7 4.6 %collective-permute-start.33 = (f32[64,128]{1,0:T(8,128)S(1)}, f32[64,128]{1,0:T(8,128)S(1)}, u32[]{:S(2)}, u32[]{:S(2)}) collective-permute-start(f32[64,128]{1,0:T(8,128)S(1)} %add_add_fusion.3), channel_id=1, source_target_pairs={{0,8},{1,9},{2,10},{3,11},{4,12},{5,13},{6,14},{7,15},{8,0},{9,1},... | collective-permute-start | bytes 98312 | tf_op jit(solution)/shard_map/ppermute | solution.py:680
  105.9 4.8 %collective-permute-start.34 = (f32[64,128]{1,0:T(8,128)S(1)}, f32[64,128]{1,0:T(8,128)S(1)}, u32[]{:S(2)}, u32[]{:S(2)}) collective-permute-start(f32[64,128]{1,0:T(8,128)S(1)} %add_add_fusion.3), channel_id=1, source_target_pairs={{0,16},{1,17},{2,18},{3,19},{4,20},{5,21},{6,22},{7,23},{8,24},{9,... | collective-permute-start | bytes 98312 | tf_op jit(solution)/shard_map/ppermute | solution.py:680
  106.6 5.7 %collective-permute-start.35 = (f32[64,128]{1,0:T(8,128)S(1)}, f32[64,128]{1,0:T(8,128)S(1)}, u32[]{:S(2)}, u32[]{:S(2)}) collective-permute-start(f32[64,128]{1,0:T(8,128)S(1)} %add_add_fusion.3), channel_id=1, source_target_pairs={{0,24},{1,25},{2,26},{3,27},{4,28},{5,29},{6,30},{7,31},{8,16},{9,... | collective-permute-start | bytes 98312 | tf_op jit(solution)/shard_map/ppermute | solution.py:680

commit v6 on v5

--- a/solution.py
+++ b/solution.py
@@ -711,8 +711,8 @@
     tied = lax.optimization_barrier((vec, n, rows, cols, far[0], *crossed[0].values()))
     vec, n, rows, cols, far[0] = tied[:5]
     crossed[0] = dict(zip(crossed[0], tied[5:]))
+    far_vec = from_behind(vec, "blk", -1)
     cross_vec = gather_far_bits(vec)
-    far_vec = from_behind(vec, "blk", -1)
     mate_vec = swap(vec, "grp", 1)
 
     def direct(index):
@@ -751,9 +751,9 @@
     state = build(None, direct(1), grown, "more_blocks") + [kept]
     state = build(2, last, state, "last_tiles")
     kept = state[-1]
-    tied = lax.optimization_barrier((kept, *cross_vec.values()))
-    kept = tied[0]
-    cross_vec = dict(zip(cross_vec, tied[1:]))
+    tied = lax.optimization_barrier((kept, far_vec, *cross_vec.values()))
+    kept, far_vec = tied[:2]
+    cross_vec = dict(zip(cross_vec, tied[2:]))
 
     def window_of(own, mate, crossed, far):
         found = {0: own, blocks_dev: mate, group * blocks_dev: far}

time: 119 us -> 122 us (1.025); the launches traced: 119 us -> 120 us
  starting transfers between devices: 25.6 us -> 30.1 us
  waiting for transfers between devices: 36.3 us -> 32.9 us
    ppermute x6, starting transfers between devices: 8.54 us -> 11.7 us  [from_behind(): lax.ppermute(value, axis, [(source, source + steps) for source in range(i...]
    ppermute x7, waiting for transfers between devices: 8.8 us -> 7.24 us  [all_sum(): lax.ppermute(value, ('blk', 'grp'), [(source, source ^ move) for source i...]
    ppermute x16, starting transfers between devices: 8.83 us -> 10.3 us  [swap(): lax.ppermute(value, axis, [(source, source ^ bit) for source in range(cou...]
  transfers between devices with their start and end apart: 29 -> 29, of which waited for: 19 -> 17; matrix products, arithmetic and copies ran while one was open for 0% -> 0% of each run, Pallas kernels for 32% -> 31%
where the time goes in v6:
time: 122 us; the launch traced here: 120 us
  Pallas kernels  53.8 us (44%)
  waiting for transfers between devices  32.9 us (27%)
  starting transfers between devices  30.1 us (25%)
  between operations  1.65 us (1%)
  local copies, waits for them, and re-layouts  1.44 us (1%)
    pallas_call x7, Pallas kernels, products(): call(*entries, *[vecs[first] for first in firsts], tiles, *begun)  18 us
    pallas_call x4, Pallas kernels, build_tiles(): pl.pallas_call(kernel, out_shape=shapes, in_specs=[spec(SMEM)] * len(scal...  15.3 us
    ppermute x6, waiting for transfers between devices, from_behind(): lax.ppermute(value, axis, [(source, source + steps) for source in range(i...  14.9 us
    pallas_call x1, Pallas kernels, listing(): pl.pallas_call(functools.partial(listing_kernel, group, cap, blocks_dev),...  12 us
    ppermute x6, starting transfers between devices, from_behind(): lax.ppermute(value, axis, [(source, source + steps) for source in range(i...  11.7 us
    ppermute x16, waiting for transfers between devices, swap(): lax.ppermute(value, axis, [(source, source ^ bit) for source in range(cou...  10.7 us
    ppermute x16, starting transfers between devices, swap(): lax.ppermute(value, axis, [(source, source ^ bit) for source in range(cou...  10.3 us
    ppermute x7, starting transfers between devices, all_sum(): lax.ppermute(value, ('blk', 'grp'), [(source, source ^ move) for source i...  8.01 us
  transfers between devices with their start and end apart: 29, of which 17 were waited for; matrix products, arithmetic and copies ran while one was open for 0% of the time, Pallas kernels for 31%

profile of v6, /device:TPU:0, one launch (start us, length us, event | category | flops | bytes accessed | tf_op | source)
XLA Modules:
  0.0 120.0 jit_solution(842255137605680380)
XLA Ops:
  0.0 1.3 %slice.18 = bf16[512,768]{1,0:T(8,128)(2,1)S(1)} slice(bf16[1024,768]{1,0:T(8,128)(2,1)} %refs_3_.1), slice={[0:512], [0:768]} | slice | bytes 1572864 | tf_op jit(solution)/shard_map/slice | solution.py:704
  1.3 1.3 %collective-permute-start.7 = (bf16[512,768]{1,0:T(8,128)(2,1)S(1)}, bf16[512,768]{1,0:T(8,128)(2,1)S(1)}, u32[]{:S(2)}, u32[]{:S(2)}) collective-permute-start(bf16[512,768]{1,0:T(8,128)(2,1)S(1)} %slice.18), channel_id=1, source_target_pairs={{4,0},{8,4},{12,8},{16,12},{20,16},{24,20},{28,24},{5,1},{9,5},{13... | collective-permute-start | bytes 2359304 | tf_op jit(solution)/shard_map/ppermute | solution.py:37
  2.6 3.0 %collective-permute-start.8 = (bf16[512,768]{1,0:T(8,128)(2,1)S(1)}, bf16[512,768]{1,0:T(8,128)(2,1)S(1)}, u32[]{:S(2)}, u32[]{:S(2)}) collective-permute-start(bf16[512,768]{1,0:T(8,128)(2,1)S(1)} %slice.18), channel_id=1, source_target_pairs={{0,2},{1,3},{2,0},{3,1},{4,6},{5,7},{6,4},{7,5},{8,10},{9,11},{10,... | collective-permute-start | bytes 2359304 | tf_op jit(solution)/shard_map/ppermute | solution.py:31
  5.7 0.1 slice.19
  5.7 0.2 collective-permute-start.14
  5.9 1.3 %collective-permute-start.9 = (bf16[512,768]{1,0:T(8,128)(2,1)S(1)}, bf16[512,768]{1,0:T(8,128)(2,1)S(1)}, u32[]{:S(2)}, u32[]{:S(2)}) collective-permute-start(bf16[512,768]{1,0:T(8,128)(2,1)S(1)} %slice.19), channel_id=1, source_target_pairs={{4,0},{8,4},{12,8},{16,12},{20,16},{24,20},{28,24},{5,1},{9,5},{13... | collective-permute-start | bytes 2359304 | tf_op jit(solution)/shard_map/ppermute | solution.py:37
  7.8 0.6 opening.1.refs_4_
  8.4 12.0 %listing.1 = (s32[16]{0:T(128)S(1)}, s32[16]{0:T(128)S(1)}, s32[4]{0:T(128)S(1)}, s32[32]{0:T(128)S(1)}, s32[32]{0:T(128)S(1)}, /*index=5*/s32[32]{0:T(128)S(1)}, s32[9]{0:T(128)S(1)}) custom-call(s32[64]{0:T(128)S(1)} %copy-done.3, s32[64]{0:T(128)S(1)} %copy-done.4, s32[1]{0:T(128)S(6)} %copy.31.live), custom_call_target="tpu_custom_call" | custom-call | flops 1048576 | bytes 1024 | tf_op jit(solution)/shard_map/listing/pallas_call | solution.py:222
  20.4 4.1 %collective-permute-done.7.refs_5_ = bf16[512,768]{1,0:T(8,128)(2,1)S(1)} collective-permute-done((bf16[512,768]{1,0:T(8,128)(2,1)S(1)}, bf16[512,768]{1,0:T(8,128)(2,1)S(1)}, u32[]{:S(2)}, u32[]{:S(2)}) %collective-permute-start.7) | collective-permute-done | bytes 786464 | tf_op jit(solution)/shard_map/ppermute | solution.py:37
  24.6 0.1 fusion
  24.6 0.1 collective-permute-start.11
  24.7 0.5 collective-permute-start.12
  25.2 1.2 %collective-permute-done.11 = bf16[256,768]{1,0:T(8,128)(2,1)S(1)} collective-permute-done((bf16[256,768]{1,0:T(8,128)(2,1)S(1)}, bf16[256,768]{1,0:T(8,128)(2,1)S(1)}, u32[]{:S(2)}, u32[]{:S(2)}) %collective-permute-start.11) | collective-permute-done | bytes 393248 | tf_op jit(solution)/shard_map/ppermute | solution.py:31
  26.4 0.1 collective-permute-start.10
  26.6 0.4 collective-permute-done.12
  27.0 0.1 pad_maximum_fusion.refs_3_
  27.1 6.9 %first_tiles.1 = (bf16[5120,768]{1,0:T(8,128)(2,1)S(1)}, f32[10,8,512]{2,1,0:T(8,128)S(1)}, f32[8,512,128]{2,1,0:T(8,128)S(1)}, bf16[17,512,512]{2,1,0:T(8,128)(2,1)S(1)}) custom-call(s32[4]{0:T(128)S(1)} %get-tuple-element.91.refs_0_, s32[16]{0:T(128)S(1)} %get-tuple-element.92.refs_1_, s32[16]{0:T(128)S(1)} %get-tuple-element.93.refs_2_, ...), custom_call_target="tpu_custom_call" | custom-call | flops 1048576 | bytes 1048576 | tf_op jit(solution)/shard_map/first_tiles/pallas_call | solution.py:343
  33.9 2.1 %second_tiles.1 = (bf16[5120,768]{1,0:T(8,128)(2,1)S(1)}, f32[10,8,512]{2,1,0:T(8,128)S(1)}, f32[8,512,128]{2,1,0:T(8,128)S(1)}, bf16[17,512,512]{2,1,0:T(8,128)(2,1)S(1)}) custom-call(s32[4]{0:T(128)S(1)} %get-tuple-element.91.refs_0_, s32[16]{0:T(128)S(1)} %get-tuple-element.92.refs_1_, ...), custom_call_target="tpu_custom_call", output_to_operand_aliasing={{0}: (4, {}), {1}: (5, {}), {2}: (6, {}), {3}: (7, {})} | custom-call | flops 1048576 | bytes 1048576 | tf_op jit(solution)/shard_map/second_tiles/pallas_call | solution.py:343
  36.1 2.5 %products.7 = (f32[2,72,512]{2,1,0:T(8,128)S(1)}, f32[4,72,512]{2,1,0:T(8,128)S(1)}, f32[2,72,512]{2,1,0:T(8,128)S(1)}, f32[2,72,512]{2,1,0:T(8,128)S(1)}) custom-call(s32[32]{0:T(128)S(1)} %get-tuple-element.83.refs_0_, s32[32]{0:T(128)S(1)} %get-tuple-element.84.refs_1_, s32[32]{0:T(128)S(1)} %get-tuple-element.85.refs_2_, ...), custom_call_target="tpu_custom_call" | custom-call | flops 1048576 | bytes 1048576 | tf_op jit(solution)/shard_map/products/pallas_call | solution.py:447
  38.6 1.4 %collective-permute-done.14.refs_1_ = bf16[512,768]{1,0:T(8,128)(2,1)S(1)} collective-permute-done((bf16[512,768]{1,0:T(8,128)(2,1)S(1)}, bf16[512,768]{1,0:T(8,128)(2,1)S(1)}, u32[]{:S(2)}, u32[]{:S(2)}) %collective-permute-start.14) | collective-permute-done | bytes 786464 | tf_op jit(solution)/shard_map/ppermute | solution.py:31
  40.0 0.6 collective-permute-done.9.refs_0_
  40.6 1.3 %collective-permute-start.16 = (bf16[80,1024]{1,0:T(8,128)(2,1)S(1)}, bf16[80,1024]{1,0:T(8,128)(2,1)S(1)}, u32[]{:S(2)}, u32[]{:S(2)}) collective-permute-start(bf16[80,1024]{1,0:T(8,128)(2,1)S(1)} %opening.1.refs_4_), channel_id=1, source_target_pairs={{4,0},{8,4},{12,8},{16,12},{20,16},{24,20},{28,24},{5,1},{9,5},{13... | collective-permute-start | bytes 491528 | tf_op jit(solution)/shard_map/ppermute | solution.py:37
  41.9 1.8 %collective-permute-start.17 = (bf16[80,1024]{1,0:T(8,128)(2,1)S(1)}, bf16[80,1024]{1,0:T(8,128)(2,1)S(1)}, u32[]{:S(2)}, u32[]{:S(2)}) collective-permute-start(bf16[80,1024]{1,0:T(8,128)(2,1)S(1)} %opening.1.refs_4_), channel_id=1, source_target_pairs={{0,2},{1,3},{2,0},{3,1},{4,6},{5,7},{6,4},{7,5},{8,10},{9,11},{10,... | collective-permute-start | bytes 491528 | tf_op jit(solution)/shard_map/ppermute | solution.py:31
  43.7 0.7 more_blocks.1
  44.4 5.6 %last_tiles.1 = (bf16[5120,768]{1,0:T(8,128)(2,1)S(1)}, f32[10,8,512]{2,1,0:T(8,128)S(1)}, f32[8,512,128]{2,1,0:T(8,128)S(1)}, bf16[17,512,512]{2,1,0:T(8,128)(2,1)S(1)}) custom-call(s32[4]{0:T(128)S(1)} %get-tuple-element.91.refs_0_, s32[16]{0:T(128)S(1)} %get-tuple-element.92.refs_1_, ...), custom_call_target="tpu_custom_call", output_to_operand_aliasing={{0}: (4, {}), {1}: (5, {}), {2}: (6, {}), {3}: (7, {})} | custom-call | flops 4294967296 | bytes 1048576 | tf_op jit(solution)/shard_map/last_tiles/pallas_call | solution.py:343
  50.0 0.0 collective-permute-done.16.refs_6_
  50.0 0.3 collective-permute-start.18
  50.3 1.3 %products.8 = (f32[2,72,512]{2,1,0:T(8,128)S(1)}, f32[4,72,512]{2,1,0:T(8,128)S(1)}, f32[2,72,512]{2,1,0:T(8,128)S(1)}, f32[2,72,512]{2,1,0:T(8,128)S(1)}) custom-call(s32[32]{0:T(128)S(1)} %get-tuple-element.83.refs_0_, s32[32]{0:T(128)S(1)} %get-tuple-element.84.refs_1_, s32[32]{0:T(128)S(1)} %get-tuple-element.85.refs_2_, ...), custom_call_target="tpu_custom_call" | custom-call | flops 1048576 | bytes 1048576 | tf_op jit(solution)/shard_map/products/pallas_call | solution.py:447
  51.6 4.0 %products.9 = (f32[4,72,512]{2,1,0:T(8,128)S(1)}, f32[2,72,512]{2,1,0:T(8,128)S(1)}, f32[2,72,512]{2,1,0:T(8,128)S(1)}) custom-call(s32[32]{0:T(128)S(1)} %get-tuple-element.83.refs_0_, s32[32]{0:T(128)S(1)} %get-tuple-element.84.refs_1_, s32[32]{0:T(128)S(1)} %get-tuple-element.85.refs_2_, s32[9]{0:T(128)S(1)} %get-tuple-element.86.refs_3_, ...), custom_call_target="tpu_custom_call" | custom-call | flops 2147483648 | bytes 1048576 | tf_op jit(solution)/shard_map/products/pallas_call | solution.py:447
  55.6 0.3 collective-permute-start.19
  56.0 3.2 %collective-permute-start.20 = (f32[2,72,512]{2,1,0:T(8,128)S(1)}, f32[2,72,512]{2,1,0:T(8,128)S(1)}, u32[]{:S(2)}, u32[]{:S(2)}) collective-permute-start(f32[2,72,512]{2,1,0:T(8,128)S(1)} %get-tuple-element.128), channel_id=1, source_target_pairs={{0,4},{4,8},{8,12},{12,16},{16,20},{20,24},{24,28},{1,5},{5,9},{9,... | collective-permute-start | bytes 884744 | tf_op jit(solution)/shard_map/ppermute | solution.py:37
  59.3 1.2 collective-permute-start.21
  60.4 1.6 %products.10.refs_0_ = f32[2,72,512]{2,1,0:T(8,128)S(1)} custom-call(s32[32]{0:T(128)S(1)} %get-tuple-element.83.refs_0_, s32[32]{0:T(128)S(1)} %get-tuple-element.84.refs_1_, s32[32]{0:T(128)S(1)} %get-tuple-element.85.refs_2_, s32[9]{0:T(128)S(1)} %get-tuple-element.86.refs_3_, bf16[80,1024]{1,0:T(8,128)(2,1)S(1)} %collective-permute-done.17.refs_4_, ...), custom_call_target="tpu_custom_call" | custom-call | flops 1048576 | bytes 1048576 | tf_op jit(solution)/shard_map/products/pallas_call | solution.py:447
  62.0 3.7 %collective-permute-done.20.refs_1_ = f32[2,72,512]{2,1,0:T(8,128)S(1)} collective-permute-done((f32[2,72,512]{2,1,0:T(8,128)S(1)}, f32[2,72,512]{2,1,0:T(8,128)S(1)}, u32[]{:S(2)}, u32[]{:S(2)}) %collective-permute-start.20) | collective-permute-done | bytes 294944 | tf_op jit(solution)/shard_map/ppermute | solution.py:37
  65.7 2.4 %collective-permute-done.21.refs_3_ = f32[2,72,512]{2,1,0:T(8,128)S(1)} collective-permute-done((f32[2,72,512]{2,1,0:T(8,128)S(1)}, f32[2,72,512]{2,1,0:T(8,128)S(1)}, u32[]{:S(2)}, u32[]{:S(2)}) %collective-permute-start.21) | collective-permute-done | bytes 294944 | tf_op jit(solution)/shard_map/ppermute | solution.py:31
  68.1 0.9 scaled_gram.2
  69.0 0.1 collective-permute-start.22
  69.1 1.6 %collective-permute-start.23 = (bf16[128,1024]{1,0:T(8,128)(2,1)S(1)}, bf16[128,1024]{1,0:T(8,128)(2,1)S(1)}, u32[]{:S(2)}, u32[]{:S(2)}) collective-permute-start(bf16[128,1024]{1,0:T(8,128)(2,1)S(1)} %get-tuple-element.130.refs_4_), channel_id=1, source_target_pairs={{0,2},{1,3},{2,0},{3,1},{4,6},{5,7},{6,4},{7,5},{8,10},{9,11},{10,... | collective-permute-start | bytes 786440 | tf_op jit(solution)/shard_map/ppermute | solution.py:31
  70.7 1.3 %collective-permute-start.25 = (bf16[128,1024]{1,0:T(8,128)(2,1)S(1)}, bf16[128,1024]{1,0:T(8,128)(2,1)S(1)}, u32[]{:S(2)}, u32[]{:S(2)}) collective-permute-start(bf16[128,1024]{1,0:T(8,128)(2,1)S(1)} %get-tuple-element.130.refs_4_), channel_id=1, source_target_pairs={{4,0},{8,4},{12,8},{16,12},{20,16},{24,20},{28,24},{5,1},{9,5},{13... | collective-permute-start | bytes 786440 | tf_op jit(solution)/shard_map/ppermute | solution.py:37
  72.0 3.0 %products.11 = (f32[2,64,512]{2,1,0:T(8,128)S(1)}, f32[4,64,512]{2,1,0:T(8,128)S(1)}, f32[2,64,512]{2,1,0:T(8,128)S(1)}, f32[2,64,512]{2,1,0:T(8,128)S(1)}) custom-call(s32[32]{0:T(128)S(1)} %get-tuple-element.83.refs_0_, s32[32]{0:T(128)S(1)} %get-tuple-element.84.refs_1_, s32[32]{0:T(128)S(1)} %get-tuple-element.85.refs_2_, ...), custom_call_target="tpu_custom_call" | custom-call | flops 1048576 | bytes 1048576 | tf_op jit(solution)/shard_map/products/pallas_call | solution.py:447
  75.0 2.9 %collective-permute-done.23.refs_4_ = bf16[128,1024]{1,0:T(8,128)(2,1)S(1)} collective-permute-done((bf16[128,1024]{1,0:T(8,128)(2,1)S(1)}, bf16[128,1024]{1,0:T(8,128)(2,1)S(1)}, u32[]{:S(2)}, u32[]{:S(2)}) %collective-permute-start.23) | collective-permute-done | bytes 262176 | tf_op jit(solution)/shard_map/ppermute | solution.py:31
  77.8 3.1 %collective-permute-done.25.refs_6_ = bf16[128,1024]{1,0:T(8,128)(2,1)S(1)} collective-permute-done((bf16[128,1024]{1,0:T(8,128)(2,1)S(1)}, bf16[128,1024]{1,0:T(8,128)(2,1)S(1)}, u32[]{:S(2)}, u32[]{:S(2)}) %collective-permute-start.25) | collective-permute-done | bytes 262176 | tf_op jit(solution)/shard_map/ppermute | solution.py:37
  80.9 4.1 %products.12 = (f32[4,64,512]{2,1,0:T(8,128)S(1)}, f32[2,64,512]{2,1,0:T(8,128)S(1)}, f32[2,64,512]{2,1,0:T(8,128)S(1)}) custom-call(s32[32]{0:T(128)S(1)} %get-tuple-element.83.refs_0_, s32[32]{0:T(128)S(1)} %get-tuple-element.84.refs_1_, s32[32]{0:T(128)S(1)} %get-tuple-element.85.refs_2_, s32[9]{0:T(128)S(1)} %get-tuple-element.86.refs_3_, ...), custom_call_target="tpu_custom_call" | custom-call | flops 2147483648 | bytes 1048576 | tf_op jit(solution)/shard_map/products/pallas_call | solution.py:447
  85.0 0.1 collective-permute-start.26
  85.1 3.4 %collective-permute-start.27 = (f32[2,64,512]{2,1,0:T(8,128)S(1)}, f32[2,64,512]{2,1,0:T(8,128)S(1)}, u32[]{:S(2)}, u32[]{:S(2)}) collective-permute-start(f32[2,64,512]{2,1,0:T(8,128)S(1)} %get-tuple-element.140), channel_id=1, source_target_pairs={{0,4},{4,8},{8,12},{12,16},{16,20},{20,24},{24,28},{1,5},{5,9},{9,... | collective-permute-start | bytes 786440 | tf_op jit(solution)/shard_map/ppermute | solution.py:37
  88.6 1.2 collective-permute-start.28
  89.7 1.5 %products.13.refs_0_ = f32[2,64,512]{2,1,0:T(8,128)S(1)} custom-call(s32[32]{0:T(128)S(1)} %get-tuple-element.83.refs_0_, s32[32]{0:T(128)S(1)} %get-tuple-element.84.refs_1_, s32[32]{0:T(128)S(1)} %get-tuple-element.85.refs_2_, s32[9]{0:T(128)S(1)} %get-tuple-element.86.refs_3_, bf16[128,1024]{1,0:T(8,128)(2,1)S(1)} %collective-permute-done.23.refs_4_, ...), custom_call_target="tpu_custom_call" | custom-call | flops 1048576 | bytes 1048576 | tf_op jit(solution)/shard_map/products/pallas_call | solution.py:447
  91.2 3.5 %collective-permute-done.27.refs_1_ = f32[2,64,512]{2,1,0:T(8,128)S(1)} collective-permute-done((f32[2,64,512]{2,1,0:T(8,128)S(1)}, f32[2,64,512]{2,1,0:T(8,128)S(1)}, u32[]{:S(2)}, u32[]{:S(2)}) %collective-permute-start.27) | collective-permute-done | bytes 262176 | tf_op jit(solution)/shard_map/ppermute | solution.py:37
  94.7 2.4 %collective-permute-done.28.refs_3_ = f32[2,64,512]{2,1,0:T(8,128)S(1)} collective-permute-done((f32[2,64,512]{2,1,0:T(8,128)S(1)}, f32[2,64,512]{2,1,0:T(8,128)S(1)}, u32[]{:S(2)}, u32[]{:S(2)}) %collective-permute-start.28) | collective-permute-done | bytes 262176 | tf_op jit(solution)/shard_map/ppermute | solution.py:31
  97.0 1.0 scaled_gram.3
  98.1 0.1 collective-permute-start.29
  98.1 1.2 collective-permute-done.29
  99.3 1.1 collective-permute-start.30
  100.4 0.9 collective-permute-start.31
  101.4 1.5 %collective-permute-start.32 = (f32[64,128]{1,0:T(8,128)S(1)}, f32[64,128]{1,0:T(8,128)S(1)}, u32[]{:S(2)}, u32[]{:S(2)}) collective-permute-start(f32[64,128]{1,0:T(8,128)S(1)} %add.50), channel_id=1, source_target_pairs={{0,6},{1,7},{2,4},{3,5},{4,2},{5,3},{6,0},{7,1},{8,14},{9,15},{10,... | collective-permute-start | bytes 98312 | tf_op jit(solution)/shard_map/ppermute | solution.py:680
  102.8 0.4 collective-permute-done.30
  103.2 1.1 collective-permute-done.31
  104.4 1.8 %collective-permute-done.32 = f32[64,128]{1,0:T(8,128)S(1)} collective-permute-done((f32[64,128]{1,0:T(8,128)S(1)}, f32[64,128]{1,0:T(8,128)S(1)}, u32[]{:S(2)}, u32[]{:S(2)}) %collective-permute-start.32) | collective-permute-done | bytes 32800 | tf_op jit(solution)/shard_map/ppermute | solution.py:680
  106.2 1.4 %collective-permute-start.33 = (f32[64,128]{1,0:T(8,128)S(1)}, f32[64,128]{1,0:T(8,128)S(1)}, u32[]{:S(2)}, u32[]{:S(2)}) collective-permute-start(f32[64,128]{1,0:T(8,128)S(1)} %add_add_fusion.3), channel_id=1, source_target_pairs={{0,8},{1,9},{2,10},{3,11},{4,12},{5,13},{6,14},{7,15},{8,0},{9,1},... | collective-permute-start | bytes 98312 | tf_op jit(solution)/shard_map/ppermute | solution.py:680
  107.6 3.1 %collective-permute-start.35 = (f32[64,128]{1,0:T(8,128)S(1)}, f32[64,128]{1,0:T(8,128)S(1)}, u32[]{:S(2)}, u32[]{:S(2)}) collective-permute-start(f32[64,128]{1,0:T(8,128)S(1)} %add_add_fusion.3), channel_id=1, source_target_pairs={{0,24},{1,25},{2,26},{3,27},{4,28},{5,29},{6,30},{7,31},{8,16},{9,... | collective-permute-start | bytes 98312 | tf_op jit(solution)/shard_map/ppermute | solution.py:680
  110.6 2.1 %collective-permute-done.34 = f32[64,128]{1,0:T(8,128)S(1)} collective-permute-done((f32[64,128]{1,0:T(8,128)S(1)}, f32[64,128]{1,0:T(8,128)S(1)}, u32[]{:S(2)}, u32[]{:S(2)}) %collective-permute-start.34) | collective-permute-done | bytes 32800 | tf_op jit(solution)/shard_map/ppermute | solution.py:680
  112.7 0.6 collective-permute-done.35
  113.4 4.9 %factors.1 = (f32[64,64]{1,0:T(8,128)S(1)}, f32[64,64]{1,0:T(8,128)S(1)}, s32[1]{0:T(128)}) custom-call(f32[64,128]{1,0:T(8,128)S(1)} %add_add_fusion.2.grams), custom_call_target="tpu_custom_call" | custom-call | flops 1073741824 | bytes 65536 | tf_op jit(solution)/shard_map/factors/pallas_call | solution.py:618
  118.9 1.1 applied.3
  (31 shorter events, 0.2 us)
Async XLA Ops:
  0.0 5.7 %copy-start = (bf16[1024,768]{1,0:T(8,128)(2,1)S(1)}, bf16[1024,768]{1,0:T(8,128)(2,1)}, u32[]{:S(2)}) copy-start(bf16[1024,768]{1,0:T(8,128)(2,1)} %refs_3_.1) | copy-start | bytes 4718596
  0.0 7.8 %copy-start.1 = (f32[64,1024]{1,0:T(8,128)S(1)}, f32[64,1024]{1,0:T(8,128)}, u32[]{:S(2)}) copy-start(f32[64,1024]{1,0:T(8,128)} %start.1) | copy-start | bytes 786436
  0.0 7.8 %copy-start.2 = (s32[2]{0:T(128)S(1)}, s32[2]{0:T(128)}, u32[]{:S(2)}) copy-start(s32[2]{0:T(128)} %count_ref.3) | copy-start | bytes 28
  0.0 8.4 %copy-start.3 = (s32[64]{0:T(128)S(1)}, s32[64]{0:T(128)}, u32[]{:S(2)}) copy-start(s32[64]{0:T(128)} %rows.1) | copy-start | bytes 772
  0.0 8.4 %copy-start.4 = (s32[64]{0:T(128)S(1)}, s32[64]{0:T(128)}, u32[]{:S(2)}) copy-start(s32[64]{0:T(128)} %cols.1) | copy-start | bytes 772
  1.3 23.2 %collective-permute-start.7 = (bf16[512,768]{1,0:T(8,128)(2,1)S(1)}, bf16[512,768]{1,0:T(8,128)(2,1)S(1)}, u32[]{:S(2)}, u32[]{:S(2)}) collective-permute-start(bf16[512,768]{1,0:T(8,128)(2,1)S(1)} %slice.18), channel_id=1, source_target_pairs={{4,0},{8,4},{12,8},{16,12},{20,16},{24,20},{28,24},{5,1},{9,5},{13... | collective-permute-start | bytes 2359304 | tf_op jit(solution)/shard_map/ppermute | solution.py:37
  2.6 22.0 %collective-permute-start.8 = (bf16[512,768]{1,0:T(8,128)(2,1)S(1)}, bf16[512,768]{1,0:T(8,128)(2,1)S(1)}, u32[]{:S(2)}, u32[]{:S(2)}) collective-permute-start(bf16[512,768]{1,0:T(8,128)(2,1)S(1)} %slice.18), channel_id=1, source_target_pairs={{0,2},{1,3},{2,0},{3,1},{4,6},{5,7},{6,4},{7,5},{8,10},{9,11},{10,... | collective-permute-start | bytes 2359304 | tf_op jit(solution)/shard_map/ppermute | solution.py:31
  5.7 21.4 %collective-permute-start.13 = (bf16[1024,768]{1,0:T(8,128)(2,1)}, bf16[1024,768]{1,0:T(8,128)(2,1)S(1)}, u32[]{:S(2)}, u32[]{:S(2)}) collective-permute-start(bf16[1024,768]{1,0:T(8,128)(2,1)} %refs_3_.1), channel_id=1, source_target_pairs={{0,1},{1,0},{2,3},{3,2},{4,5},{5,4},{6,7},{7,6},{8,9},{9,8},{10,11... | collective-permute-start | bytes 4718600 | tf_op jit(solution)/shard_map/ppermute | solution.py:31
  5.7 34.3 %collective-permute-start.14 = (bf16[512,768]{1,0:T(8,128)(2,1)S(1)}, bf16[512,768]{1,0:T(8,128)(2,1)S(1)}, u32[]{:S(2)}, u32[]{:S(2)}) collective-permute-start(bf16[512,768]{1,0:T(8,128)(2,1)S(1)} %slice.19), channel_id=1, source_target_pairs={{0,2},{1,3},{2,0},{3,1},{4,6},{5,7},{6,4},{7,5},{8,10},{9,11},{10,... | collective-permute-start | bytes 2359304 | tf_op jit(solution)/shard_map/ppermute | solution.py:31
  5.9 34.7 %collective-permute-start.9 = (bf16[512,768]{1,0:T(8,128)(2,1)S(1)}, bf16[512,768]{1,0:T(8,128)(2,1)S(1)}, u32[]{:S(2)}, u32[]{:S(2)}) collective-permute-start(bf16[512,768]{1,0:T(8,128)(2,1)S(1)} %slice.19), channel_id=1, source_target_pairs={{4,0},{8,4},{12,8},{16,12},{20,16},{24,20},{28,24},{5,1},{9,5},{13... | collective-permute-start | bytes 2359304 | tf_op jit(solution)/shard_map/ppermute | solution.py:37
  24.6 1.8 %collective-permute-start.11 = (bf16[256,768]{1,0:T(8,128)(2,1)S(1)}, bf16[256,768]{1,0:T(8,128)(2,1)S(1)}, u32[]{:S(2)}, u32[]{:S(2)}) collective-permute-start(bf16[256,768]{1,0:T(8,128)(2,1)S(1)} %get-tuple-element.150), channel_id=1, source_target_pairs={{0,1},{1,0},{2,3},{3,2},{4,5},{5,4},{6,7},{7,6},{8,9},{9,8},{10,11... | collective-permute-start | bytes 1179656 | tf_op jit(solution)/shard_map/ppermute | solution.py:31
  24.7 2.3 %collective-permute-start.12 = (bf16[256,768]{1,0:T(8,128)(2,1)S(1)}, bf16[256,768]{1,0:T(8,128)(2,1)S(1)}, u32[]{:S(2)}, u32[]{:S(2)}) collective-permute-start(bf16[256,768]{1,0:T(8,128)(2,1)S(1)} %get-tuple-element.151), channel_id=1, source_target_pairs={{0,1},{1,0},{2,3},{3,2},{4,5},{5,4},{6,7},{7,6},{8,9},{9,8},{10,11... | collective-permute-start | bytes 1179656 | tf_op jit(solution)/shard_map/ppermute | solution.py:31
  26.4 9.6 %collective-permute-start.10 = (bf16[80,1024]{1,0:T(8,128)(2,1)S(1)}, bf16[80,1024]{1,0:T(8,128)(2,1)S(1)}, u32[]{:S(2)}, u32[]{:S(2)}) collective-permute-start(bf16[80,1024]{1,0:T(8,128)(2,1)S(1)} %opening.1.refs_4_), channel_id=1, source_target_pairs={{0,1},{1,0},{2,3},{3,2},{4,5},{5,4},{6,7},{7,6},{8,9},{9,8},{10,11... | collective-permute-start | bytes 491528 | tf_op jit(solution)/shard_map/ppermute | solution.py:31
  40.6 3.8 %collective-permute-start.15 = (bf16[512,768]{1,0:T(8,128)(2,1)S(1)}, bf16[512,768]{1,0:T(8,128)(2,1)S(1)}, u32[]{:S(2)}, u32[]{:S(2)}) collective-permute-start(bf16[512,768]{1,0:T(8,128)(2,1)S(1)} %collective-permute-done.14.refs_1_), channel_id=1, source_target_pairs={{0,1},{1,0},{2,3},{3,2},{4,5},{5,4},{6,7},{7,6},{8,9},{9,8},{10,11... | collective-permute-start | bytes 2359304 | tf_op jit(solution)/shard_map/ppermute | solution.py:31
  40.6 9.4 %collective-permute-start.16 = (bf16[80,1024]{1,0:T(8,128)(2,1)S(1)}, bf16[80,1024]{1,0:T(8,128)(2,1)S(1)}, u32[]{:S(2)}, u32[]{:S(2)}) collective-permute-start(bf16[80,1024]{1,0:T(8,128)(2,1)S(1)} %opening.1.refs_4_), channel_id=1, source_target_pairs={{4,0},{8,4},{12,8},{16,12},{20,16},{24,20},{28,24},{5,1},{9,5},{13... | collective-permute-start | bytes 491528 | tf_op jit(solution)/shard_map/ppermute | solution.py:37
  41.9 8.1 %collective-permute-start.17 = (bf16[80,1024]{1,0:T(8,128)(2,1)S(1)}, bf16[80,1024]{1,0:T(8,128)(2,1)S(1)}, u32[]{:S(2)}, u32[]{:S(2)}) collective-permute-start(bf16[80,1024]{1,0:T(8,128)(2,1)S(1)} %opening.1.refs_4_), channel_id=1, source_target_pairs={{0,2},{1,3},{2,0},{3,1},{4,6},{5,7},{6,4},{7,5},{8,10},{9,11},{10,... | collective-permute-start | bytes 491528 | tf_op jit(solution)/shard_map/ppermute | solution.py:31
  50.0 1.6 %collective-permute-start.18 = (bf16[80,1024]{1,0:T(8,128)(2,1)S(1)}, bf16[80,1024]{1,0:T(8,128)(2,1)S(1)}, u32[]{:S(2)}, u32[]{:S(2)}) collective-permute-start(bf16[80,1024]{1,0:T(8,128)(2,1)S(1)} %collective-permute-done.17.refs_4_), channel_id=1, source_target_pairs={{0,1},{1,0},{2,3},{3,2},{4,5},{5,4},{6,7},{7,6},{8,9},{9,8},{10,11... | collective-permute-start | bytes 491528 | tf_op jit(solution)/shard_map/ppermute | solution.py:31
  55.6 3.6 %collective-permute-start.19 = (f32[4,72,512]{2,1,0:T(8,128)S(1)}, f32[4,72,512]{2,1,0:T(8,128)S(1)}, u32[]{:S(2)}, u32[]{:S(2)}) collective-permute-start(f32[4,72,512]{2,1,0:T(8,128)S(1)} %get-tuple-element.125), channel_id=1, source_target_pairs={{0,1},{1,0},{2,3},{3,2},{4,5},{5,4},{6,7},{7,6},{8,9},{9,8},{10,11... | collective-permute-start | bytes 1769480 | tf_op jit(solution)/shard_map/ppermute | solution.py:31
  56.0 9.7 %collective-permute-start.20 = (f32[2,72,512]{2,1,0:T(8,128)S(1)}, f32[2,72,512]{2,1,0:T(8,128)S(1)}, u32[]{:S(2)}, u32[]{:S(2)}) collective-permute-start(f32[2,72,512]{2,1,0:T(8,128)S(1)} %get-tuple-element.128), channel_id=1, source_target_pairs={{0,4},{4,8},{8,12},{12,16},{16,20},{20,24},{24,28},{1,5},{5,9},{9,... | collective-permute-start | bytes 884744 | tf_op jit(solution)/shard_map/ppermute | solution.py:37
  59.3 8.8 %collective-permute-start.21 = (f32[2,72,512]{2,1,0:T(8,128)S(1)}, f32[2,72,512]{2,1,0:T(8,128)S(1)}, u32[]{:S(2)}, u32[]{:S(2)}) collective-permute-start(f32[2,72,512]{2,1,0:T(8,128)S(1)} %slice_add_fusion), channel_id=1, source_target_pairs={{0,2},{1,3},{2,0},{3,1},{4,6},{5,7},{6,4},{7,5},{8,10},{9,11},{10,... | collective-permute-start | bytes 884744 | tf_op jit(solution)/shard_map/ppermute | solution.py:31
  69.0 2.9 %collective-permute-start.22 = (bf16[128,1024]{1,0:T(8,128)(2,1)S(1)}, bf16[128,1024]{1,0:T(8,128)(2,1)S(1)}, u32[]{:S(2)}, u32[]{:S(2)}) collective-permute-start(bf16[128,1024]{1,0:T(8,128)(2,1)S(1)} %get-tuple-element.130.refs_4_), channel_id=1, source_target_pairs={{0,1},{1,0},{2,3},{3,2},{4,5},{5,4},{6,7},{7,6},{8,9},{9,8},{10,11... | collective-permute-start | bytes 786440 | tf_op jit(solution)/shard_map/ppermute | solution.py:31
  69.1 8.7 %collective-permute-start.23 = (bf16[128,1024]{1,0:T(8,128)(2,1)S(1)}, bf16[128,1024]{1,0:T(8,128)(2,1)S(1)}, u32[]{:S(2)}, u32[]{:S(2)}) collective-permute-start(bf16[128,1024]{1,0:T(8,128)(2,1)S(1)} %get-tuple-element.130.refs_4_), channel_id=1, source_target_pairs={{0,2},{1,3},{2,0},{3,1},{4,6},{5,7},{6,4},{7,5},{8,10},{9,11},{10,... | collective-permute-start | bytes 786440 | tf_op jit(solution)/shard_map/ppermute | solution.py:31
  70.7 10.3 %collective-permute-start.25 = (bf16[128,1024]{1,0:T(8,128)(2,1)S(1)}, bf16[128,1024]{1,0:T(8,128)(2,1)S(1)}, u32[]{:S(2)}, u32[]{:S(2)}) collective-permute-start(bf16[128,1024]{1,0:T(8,128)(2,1)S(1)} %get-tuple-element.130.refs_4_), channel_id=1, source_target_pairs={{4,0},{8,4},{12,8},{16,12},{20,16},{24,20},{28,24},{5,1},{9,5},{13... | collective-permute-start | bytes 786440 | tf_op jit(solution)/shard_map/ppermute | solution.py:37
  77.8 3.1 %collective-permute-start.24 = (bf16[128,1024]{1,0:T(8,128)(2,1)S(1)}, bf16[128,1024]{1,0:T(8,128)(2,1)S(1)}, u32[]{:S(2)}, u32[]{:S(2)}) collective-permute-start(bf16[128,1024]{1,0:T(8,128)(2,1)S(1)} %collective-permute-done.23.refs_4_), channel_id=1, source_target_pairs={{0,1},{1,0},{2,3},{3,2},{4,5},{5,4},{6,7},{7,6},{8,9},{9,8},{10,11... | collective-permute-start | bytes 786440 | tf_op jit(solution)/shard_map/ppermute | solution.py:31
  85.0 3.5 %collective-permute-start.26 = (f32[4,64,512]{2,1,0:T(8,128)S(1)}, f32[4,64,512]{2,1,0:T(8,128)S(1)}, u32[]{:S(2)}, u32[]{:S(2)}) collective-permute-start(f32[4,64,512]{2,1,0:T(8,128)S(1)} %get-tuple-element.137), channel_id=1, source_target_pairs={{0,1},{1,0},{2,3},{3,2},{4,5},{5,4},{6,7},{7,6},{8,9},{9,8},{10,11... | collective-permute-start | bytes 1572872 | tf_op jit(solution)/shard_map/ppermute | solution.py:31
  85.1 9.6 %collective-permute-start.27 = (f32[2,64,512]{2,1,0:T(8,128)S(1)}, f32[2,64,512]{2,1,0:T(8,128)S(1)}, u32[]{:S(2)}, u32[]{:S(2)}) collective-permute-start(f32[2,64,512]{2,1,0:T(8,128)S(1)} %get-tuple-element.140), channel_id=1, source_target_pairs={{0,4},{4,8},{8,12},{12,16},{16,20},{20,24},{24,28},{1,5},{5,9},{9,... | collective-permute-start | bytes 786440 | tf_op jit(solution)/shard_map/ppermute | solution.py:37
  88.6 8.5 %collective-permute-start.28 = (f32[2,64,512]{2,1,0:T(8,128)S(1)}, f32[2,64,512]{2,1,0:T(8,128)S(1)}, u32[]{:S(2)}, u32[]{:S(2)}) collective-permute-start(f32[2,64,512]{2,1,0:T(8,128)S(1)} %slice_add_fusion.1), channel_id=1, source_target_pairs={{0,2},{1,3},{2,0},{3,1},{4,6},{5,7},{6,4},{7,5},{8,10},{9,11},{10,... | collective-permute-start | bytes 786440 | tf_op jit(solution)/shard_map/ppermute | solution.py:31
  98.1 1.3 %collective-permute-start.29 = (f32[64,128]{1,0:T(8,128)S(1)}, f32[64,128]{1,0:T(8,128)S(1)}, u32[]{:S(2)}, u32[]{:S(2)}) collective-permute-start(f32[64,128]{1,0:T(8,128)S(1)} %get-tuple-element.145), channel_id=1, source_target_pairs={{0,1},{1,0},{2,3},{3,2},{4,5},{5,4},{6,7},{7,6},{8,9},{9,8},{10,11... | collective-permute-start | bytes 98312 | tf_op jit(solution)/shard_map/ppermute | solution.py:680
  99.3 3.9 %collective-permute-start.30 = (f32[64,128]{1,0:T(8,128)S(1)}, f32[64,128]{1,0:T(8,128)S(1)}, u32[]{:S(2)}, u32[]{:S(2)}) collective-permute-start(f32[64,128]{1,0:T(8,128)S(1)} %add.50), channel_id=1, source_target_pairs={{0,2},{1,3},{2,0},{3,1},{4,6},{5,7},{6,4},{7,5},{8,10},{9,11},{10,... | collective-permute-start | bytes 98312 | tf_op jit(solution)/shard_map/ppermute | solution.py:680
  100.4 3.9 %collective-permute-start.31 = (f32[64,128]{1,0:T(8,128)S(1)}, f32[64,128]{1,0:T(8,128)S(1)}, u32[]{:S(2)}, u32[]{:S(2)}) collective-permute-start(f32[64,128]{1,0:T(8,128)S(1)} %add.50), channel_id=1, source_target_pairs={{0,4},{1,5},{2,6},{3,7},{4,0},{5,1},{6,2},{7,3},{8,12},{9,13},{10,... | collective-permute-start | bytes 98312 | tf_op jit(solution)/shard_map/ppermute | solution.py:680
  101.4 4.8 %collective-permute-start.32 = (f32[64,128]{1,0:T(8,128)S(1)}, f32[64,128]{1,0:T(8,128)S(1)}, u32[]{:S(2)}, u32[]{:S(2)}) collective-permute-start(f32[64,128]{1,0:T(8,128)S(1)} %add.50), channel_id=1, source_target_pairs={{0,6},{1,7},{2,4},{3,5},{4,2},{5,3},{6,0},{7,1},{8,14},{9,15},{10,... | collective-permute-start | bytes 98312 | tf_op jit(solution)/shard_map/ppermute | solution.py:680
  106.2 4.5 %collective-permute-start.33 = (f32[64,128]{1,0:T(8,128)S(1)}, f32[64,128]{1,0:T(8,128)S(1)}, u32[]{:S(2)}, u32[]{:S(2)}) collective-permute-start(f32[64,128]{1,0:T(8,128)S(1)} %add_add_fusion.3), channel_id=1, source_target_pairs={{0,8},{1,9},{2,10},{3,11},{4,12},{5,13},{6,14},{7,15},{8,0},{9,1},... | collective-permute-start | bytes 98312 | tf_op jit(solution)/shard_map/ppermute | solution.py:680
  107.6 5.2 %collective-permute-start.34 = (f32[64,128]{1,0:T(8,128)S(1)}, f32[64,128]{1,0:T(8,128)S(1)}, u32[]{:S(2)}, u32[]{:S(2)}) collective-permute-start(f32[64,128]{1,0:T(8,128)S(1)} %add_add_fusion.3), channel_id=1, source_target_pairs={{0,16},{1,17},{2,18},{3,19},{4,20},{5,21},{6,22},{7,23},{8,24},{9,... | collective-permute-start | bytes 98312 | tf_op jit(solution)/shard_map/ppermute | solution.py:680
  107.6 5.8 %collective-permute-start.35 = (f32[64,128]{1,0:T(8,128)S(1)}, f32[64,128]{1,0:T(8,128)S(1)}, u32[]{:S(2)}, u32[]{:S(2)}) collective-permute-start(f32[64,128]{1,0:T(8,128)S(1)} %add_add_fusion.3), channel_id=1, source_target_pairs={{0,24},{1,25},{2,26},{3,27},{4,28},{5,29},{6,30},{7,31},{8,16},{9,... | collective-permute-start | bytes 98312 | tf_op jit(solution)/shard_map/ppermute | solution.py:680

commit v7 on v5

--- a/solution.py
+++ b/solution.py
@@ -787,7 +787,7 @@
         columns,
         2,
     )
-    at_home, *tied = lax.optimization_barrier((at_home, *crossed.values()))
+    at_home, far_part, *tied = lax.optimization_barrier((at_home, far_part, *crossed.values()))
     crossed = dict(zip(crossed, tied))
     vecs = beyond(window_of(parts, mate_part, crossed, far_part))
     results = products(entries, (TO_OTHERS,), vecs, kept, results, urgent, columns, 2)

time: 119 us -> 126 us (1.059)
  waiting for transfers between devices: 36.3 us -> 40 us
  starting transfers between devices: 25.6 us -> 28.8 us
    ppermute x6, waiting for transfers between devices: 16 us -> 20.5 us  [from_behind(): lax.ppermute(value, axis, [(source, source + steps) for source in range(i...]
    ppermute x7, starting transfers between devices: 8.19 us -> 10.2 us  [all_sum(): lax.ppermute(value, ('blk', 'grp'), [(source, source ^ move) for source i...]
  transfers between devices with their start and end apart: 29 -> 29, of which waited for: 19 -> 17; matrix products, arithmetic and copies ran while one was open for 0% -> 0% of each run, Pallas kernels for 32% -> 32%
where the time goes in v7:
time: 126 us; the launch traced here: 127 us
  Pallas kernels  54.7 us (43%)
  waiting for transfers between devices  40 us (32%)
  starting transfers between devices  28.8 us (23%)
  between operations  1.65 us (1%)
  local copies, waits for them, and re-layouts  1.44 us (1%)
    ppermute x6, waiting for transfers between devices, from_behind(): lax.ppermute(value, axis, [(source, source + steps) for source in range(i...  20.5 us
    pallas_call x7, Pallas kernels, products(): call(*entries, *[vecs[first] for first in firsts], tiles, *begun)  18.9 us
    pallas_call x4, Pallas kernels, build_tiles(): pl.pallas_call(kernel, out_shape=shapes, in_specs=[spec(SMEM)] * len(scal...  15.3 us
    pallas_call x1, Pallas kernels, listing(): pl.pallas_call(functools.partial(listing_kernel, group, cap, blocks_dev),...  12 us
    ppermute x16, waiting for transfers between devices, swap(): lax.ppermute(value, axis, [(source, source ^ bit) for source in range(cou...  11.3 us
    ppermute x7, starting transfers between devices, all_sum(): lax.ppermute(value, ('blk', 'grp'), [(source, source ^ move) for source i...  10.2 us
    ppermute x16, starting transfers between devices, swap(): lax.ppermute(value, axis, [(source, source ^ bit) for source in range(cou...  9.71 us
    ppermute x6, starting transfers between devices, from_behind(): lax.ppermute(value, axis, [(source, source + steps) for source in range(i...  8.93 us
  transfers between devices with their start and end apart: 29, of which 17 were waited for; matrix products, arithmetic and copies ran while one was open for 0% of the time, Pallas kernels for 32%

profile of v7, /device:TPU:0, one launch (start us, length us, event | category | flops | bytes accessed | tf_op | source)
XLA Modules:
  0.0 126.8 jit_solution(6743019628509978436)
XLA Ops:
  0.0 1.3 %slice.18 = bf16[512,768]{1,0:T(8,128)(2,1)S(1)} slice(bf16[1024,768]{1,0:T(8,128)(2,1)} %refs_3_.1), slice={[0:512], [0:768]} | slice | bytes 1572864 | tf_op jit(solution)/shard_map/slice | solution.py:704
  1.3 1.3 %collective-permute-start.7 = (bf16[512,768]{1,0:T(8,128)(2,1)S(1)}, bf16[512,768]{1,0:T(8,128)(2,1)S(1)}, u32[]{:S(2)}, u32[]{:S(2)}) collective-permute-start(bf16[512,768]{1,0:T(8,128)(2,1)S(1)} %slice.18), channel_id=1, source_target_pairs={{4,0},{8,4},{12,8},{16,12},{20,16},{24,20},{28,24},{5,1},{9,5},{13... | collective-permute-start | bytes 2359304 | tf_op jit(solution)/shard_map/ppermute | solution.py:37
  2.6 3.0 %collective-permute-start.8 = (bf16[512,768]{1,0:T(8,128)(2,1)S(1)}, bf16[512,768]{1,0:T(8,128)(2,1)S(1)}, u32[]{:S(2)}, u32[]{:S(2)}) collective-permute-start(bf16[512,768]{1,0:T(8,128)(2,1)S(1)} %slice.18), channel_id=1, source_target_pairs={{0,2},{1,3},{2,0},{3,1},{4,6},{5,7},{6,4},{7,5},{8,10},{9,11},{10,... | collective-permute-start | bytes 2359304 | tf_op jit(solution)/shard_map/ppermute | solution.py:31
  5.7 0.1 slice.19
  5.7 0.2 collective-permute-start.14
  5.9 1.3 %collective-permute-start.9 = (bf16[512,768]{1,0:T(8,128)(2,1)S(1)}, bf16[512,768]{1,0:T(8,128)(2,1)S(1)}, u32[]{:S(2)}, u32[]{:S(2)}) collective-permute-start(bf16[512,768]{1,0:T(8,128)(2,1)S(1)} %slice.19), channel_id=1, source_target_pairs={{4,0},{8,4},{12,8},{16,12},{20,16},{24,20},{28,24},{5,1},{9,5},{13... | collective-permute-start | bytes 2359304 | tf_op jit(solution)/shard_map/ppermute | solution.py:37
  7.8 0.6 opening.1.refs_4_
  8.4 12.0 %listing.1 = (s32[16]{0:T(128)S(1)}, s32[16]{0:T(128)S(1)}, s32[4]{0:T(128)S(1)}, s32[32]{0:T(128)S(1)}, s32[32]{0:T(128)S(1)}, /*index=5*/s32[32]{0:T(128)S(1)}, s32[9]{0:T(128)S(1)}) custom-call(s32[64]{0:T(128)S(1)} %copy-done.3, s32[64]{0:T(128)S(1)} %copy-done.4, s32[1]{0:T(128)S(6)} %copy.31.live), custom_call_target="tpu_custom_call" | custom-call | flops 1048576 | bytes 1024 | tf_op jit(solution)/shard_map/listing/pallas_call | solution.py:222
  20.4 4.1 %collective-permute-done.7.refs_5_ = bf16[512,768]{1,0:T(8,128)(2,1)S(1)} collective-permute-done((bf16[512,768]{1,0:T(8,128)(2,1)S(1)}, bf16[512,768]{1,0:T(8,128)(2,1)S(1)}, u32[]{:S(2)}, u32[]{:S(2)}) %collective-permute-start.7) | collective-permute-done | bytes 786464 | tf_op jit(solution)/shard_map/ppermute | solution.py:37
  24.6 0.0 collective-permute-done.8.refs_6_
  24.6 0.1 fusion
  24.6 0.1 collective-permute-start.11
  24.7 0.5 collective-permute-start.12
  25.2 1.2 collective-permute-done.11
  26.4 0.1 collective-permute-start.10
  26.6 0.4 collective-permute-done.12
  27.0 0.1 pad_maximum_fusion.refs_3_
  27.1 5.9 %first_tiles.1 = (bf16[5120,768]{1,0:T(8,128)(2,1)S(1)}, f32[10,8,512]{2,1,0:T(8,128)S(1)}, f32[8,512,128]{2,1,0:T(8,128)S(1)}, bf16[17,512,512]{2,1,0:T(8,128)(2,1)S(1)}) custom-call(s32[4]{0:T(128)S(1)} %get-tuple-element.91.refs_0_, s32[16]{0:T(128)S(1)} %get-tuple-element.92.refs_1_, s32[16]{0:T(128)S(1)} %get-tuple-element.93.refs_2_, ...), custom_call_target="tpu_custom_call" | custom-call | flops 1048576 | bytes 1048576 | tf_op jit(solution)/shard_map/first_tiles/pallas_call | solution.py:343
  33.0 2.1 %second_tiles.1 = (bf16[5120,768]{1,0:T(8,128)(2,1)S(1)}, f32[10,8,512]{2,1,0:T(8,128)S(1)}, f32[8,512,128]{2,1,0:T(8,128)S(1)}, bf16[17,512,512]{2,1,0:T(8,128)(2,1)S(1)}) custom-call(s32[4]{0:T(128)S(1)} %get-tuple-element.91.refs_0_, s32[16]{0:T(128)S(1)} %get-tuple-element.92.refs_1_, ...), custom_call_target="tpu_custom_call", output_to_operand_aliasing={{0}: (4, {}), {1}: (5, {}), {2}: (6, {}), {3}: (7, {})} | custom-call | flops 1048576 | bytes 1048576 | tf_op jit(solution)/shard_map/second_tiles/pallas_call | solution.py:343
  35.1 2.5 %products.7 = (f32[2,72,512]{2,1,0:T(8,128)S(1)}, f32[4,72,512]{2,1,0:T(8,128)S(1)}, f32[2,72,512]{2,1,0:T(8,128)S(1)}, f32[2,72,512]{2,1,0:T(8,128)S(1)}) custom-call(s32[32]{0:T(128)S(1)} %get-tuple-element.83.refs_0_, s32[32]{0:T(128)S(1)} %get-tuple-element.84.refs_1_, s32[32]{0:T(128)S(1)} %get-tuple-element.85.refs_2_, ...), custom_call_target="tpu_custom_call" | custom-call | flops 1048576 | bytes 1048576 | tf_op jit(solution)/shard_map/products/pallas_call | solution.py:447
  37.7 2.4 %collective-permute-done.14.refs_1_ = bf16[512,768]{1,0:T(8,128)(2,1)S(1)} collective-permute-done((bf16[512,768]{1,0:T(8,128)(2,1)S(1)}, bf16[512,768]{1,0:T(8,128)(2,1)S(1)}, u32[]{:S(2)}, u32[]{:S(2)}) %collective-permute-start.14) | collective-permute-done | bytes 786464 | tf_op jit(solution)/shard_map/ppermute | solution.py:31
  40.0 0.6 collective-permute-done.9.refs_0_
  40.6 1.7 %collective-permute-start.16 = (bf16[80,1024]{1,0:T(8,128)(2,1)S(1)}, bf16[80,1024]{1,0:T(8,128)(2,1)S(1)}, u32[]{:S(2)}, u32[]{:S(2)}) collective-permute-start(bf16[80,1024]{1,0:T(8,128)(2,1)S(1)} %opening.1.refs_4_), channel_id=1, source_target_pairs={{0,2},{1,3},{2,0},{3,1},{4,6},{5,7},{6,4},{7,5},{8,10},{9,11},{10,... | collective-permute-start | bytes 491528 | tf_op jit(solution)/shard_map/ppermute | solution.py:31
  42.3 1.3 %collective-permute-start.18 = (bf16[80,1024]{1,0:T(8,128)(2,1)S(1)}, bf16[80,1024]{1,0:T(8,128)(2,1)S(1)}, u32[]{:S(2)}, u32[]{:S(2)}) collective-permute-start(bf16[80,1024]{1,0:T(8,128)(2,1)S(1)} %opening.1.refs_4_), channel_id=1, source_target_pairs={{4,0},{8,4},{12,8},{16,12},{20,16},{24,20},{28,24},{5,1},{9,5},{13... | collective-permute-start | bytes 491528 | tf_op jit(solution)/shard_map/ppermute | solution.py:37
  43.6 0.8 more_blocks.1
  44.4 6.5 %last_tiles.1 = (bf16[5120,768]{1,0:T(8,128)(2,1)S(1)}, f32[10,8,512]{2,1,0:T(8,128)S(1)}, f32[8,512,128]{2,1,0:T(8,128)S(1)}, bf16[17,512,512]{2,1,0:T(8,128)(2,1)S(1)}) custom-call(s32[4]{0:T(128)S(1)} %get-tuple-element.91.refs_0_, s32[16]{0:T(128)S(1)} %get-tuple-element.92.refs_1_, ...), custom_call_target="tpu_custom_call", output_to_operand_aliasing={{0}: (4, {}), {1}: (5, {}), {2}: (6, {}), {3}: (7, {})} | custom-call | flops 4294967296 | bytes 1048576 | tf_op jit(solution)/shard_map/last_tiles/pallas_call | solution.py:343
  50.9 0.1 collective-permute-start.17
  51.0 1.8 %products.8 = (f32[2,72,512]{2,1,0:T(8,128)S(1)}, f32[4,72,512]{2,1,0:T(8,128)S(1)}, f32[2,72,512]{2,1,0:T(8,128)S(1)}, f32[2,72,512]{2,1,0:T(8,128)S(1)}) custom-call(s32[32]{0:T(128)S(1)} %get-tuple-element.83.refs_0_, s32[32]{0:T(128)S(1)} %get-tuple-element.84.refs_1_, s32[32]{0:T(128)S(1)} %get-tuple-element.85.refs_2_, ...), custom_call_target="tpu_custom_call" | custom-call | flops 1048576 | bytes 1048576 | tf_op jit(solution)/shard_map/products/pallas_call | solution.py:447
  52.8 3.3 %products.9 = (f32[4,72,512]{2,1,0:T(8,128)S(1)}, f32[2,72,512]{2,1,0:T(8,128)S(1)}, f32[2,72,512]{2,1,0:T(8,128)S(1)}) custom-call(s32[32]{0:T(128)S(1)} %get-tuple-element.83.refs_0_, s32[32]{0:T(128)S(1)} %get-tuple-element.84.refs_1_, s32[32]{0:T(128)S(1)} %get-tuple-element.85.refs_2_, s32[9]{0:T(128)S(1)} %get-tuple-element.86.refs_3_, ...), custom_call_target="tpu_custom_call" | custom-call | flops 2147483648 | bytes 1048576 | tf_op jit(solution)/shard_map/products/pallas_call | solution.py:447
  56.0 0.8 collective-permute-start.19
  56.9 1.3 %collective-permute-start.20 = (f32[2,72,512]{2,1,0:T(8,128)S(1)}, f32[2,72,512]{2,1,0:T(8,128)S(1)}, u32[]{:S(2)}, u32[]{:S(2)}) collective-permute-start(f32[2,72,512]{2,1,0:T(8,128)S(1)} %get-tuple-element.127), channel_id=1, source_target_pairs={{0,4},{4,8},{8,12},{12,16},{16,20},{20,24},{24,28},{1,5},{5,9},{9,... | collective-permute-start | bytes 884744 | tf_op jit(solution)/shard_map/ppermute | solution.py:37
  58.2 0.3 collective-permute-done.19.refs_2_
  58.5 0.4 collective-permute-start.21
  58.9 2.3 %products.10.refs_0_ = f32[2,72,512]{2,1,0:T(8,128)S(1)} custom-call(s32[32]{0:T(128)S(1)} %get-tuple-element.83.refs_0_, s32[32]{0:T(128)S(1)} %get-tuple-element.84.refs_1_, s32[32]{0:T(128)S(1)} %get-tuple-element.85.refs_2_, s32[9]{0:T(128)S(1)} %get-tuple-element.86.refs_3_, bf16[80,1024]{1,0:T(8,128)(2,1)S(1)} %collective-permute-done.16.refs_4_, ...), custom_call_target="tpu_custom_call" | custom-call | flops 1048576 | bytes 1048576 | tf_op jit(solution)/shard_map/products/pallas_call | solution.py:447
  61.3 3.6 %collective-permute-done.20.refs_1_ = f32[2,72,512]{2,1,0:T(8,128)S(1)} collective-permute-done((f32[2,72,512]{2,1,0:T(8,128)S(1)}, f32[2,72,512]{2,1,0:T(8,128)S(1)}, u32[]{:S(2)}, u32[]{:S(2)}) %collective-permute-start.20) | collective-permute-done | bytes 294944 | tf_op jit(solution)/shard_map/ppermute | solution.py:37
  64.9 3.0 %collective-permute-done.21.refs_3_ = f32[2,72,512]{2,1,0:T(8,128)S(1)} collective-permute-done((f32[2,72,512]{2,1,0:T(8,128)S(1)}, f32[2,72,512]{2,1,0:T(8,128)S(1)}, u32[]{:S(2)}, u32[]{:S(2)}) %collective-permute-start.21) | collective-permute-done | bytes 294944 | tf_op jit(solution)/shard_map/ppermute | solution.py:31
  67.9 0.9 scaled_gram.2
  68.8 0.1 collective-permute-start.22
  68.9 1.3 %collective-permute-start.23 = (bf16[128,1024]{1,0:T(8,128)(2,1)S(1)}, bf16[128,1024]{1,0:T(8,128)(2,1)S(1)}, u32[]{:S(2)}, u32[]{:S(2)}) collective-permute-start(bf16[128,1024]{1,0:T(8,128)(2,1)S(1)} %get-tuple-element.129.refs_4_), channel_id=1, source_target_pairs={{4,0},{8,4},{12,8},{16,12},{20,16},{24,20},{28,24},{5,1},{9,5},{13... | collective-permute-start | bytes 786440 | tf_op jit(solution)/shard_map/ppermute | solution.py:37
  70.2 0.4 collective-permute-start.24
  70.6 3.5 %products.11 = (f32[2,64,512]{2,1,0:T(8,128)S(1)}, f32[4,64,512]{2,1,0:T(8,128)S(1)}, f32[2,64,512]{2,1,0:T(8,128)S(1)}, f32[2,64,512]{2,1,0:T(8,128)S(1)}) custom-call(s32[32]{0:T(128)S(1)} %get-tuple-element.83.refs_0_, s32[32]{0:T(128)S(1)} %get-tuple-element.84.refs_1_, s32[32]{0:T(128)S(1)} %get-tuple-element.85.refs_2_, ...), custom_call_target="tpu_custom_call" | custom-call | flops 1048576 | bytes 1048576 | tf_op jit(solution)/shard_map/products/pallas_call | solution.py:447
  74.1 9.8 %collective-permute-done.23.refs_6_ = bf16[128,1024]{1,0:T(8,128)(2,1)S(1)} collective-permute-done((bf16[128,1024]{1,0:T(8,128)(2,1)S(1)}, bf16[128,1024]{1,0:T(8,128)(2,1)S(1)}, u32[]{:S(2)}, u32[]{:S(2)}) %collective-permute-start.23) | collective-permute-done | bytes 262176 | tf_op jit(solution)/shard_map/ppermute | solution.py:37
  83.9 1.5 %collective-permute-done.25.refs_5_ = bf16[128,1024]{1,0:T(8,128)(2,1)S(1)} collective-permute-done((bf16[128,1024]{1,0:T(8,128)(2,1)S(1)}, bf16[128,1024]{1,0:T(8,128)(2,1)S(1)}, u32[]{:S(2)}, u32[]{:S(2)}) %collective-permute-start.25) | collective-permute-done | bytes 262176 | tf_op jit(solution)/shard_map/ppermute | solution.py:31
  85.4 3.3 %products.12 = (f32[4,64,512]{2,1,0:T(8,128)S(1)}, f32[2,64,512]{2,1,0:T(8,128)S(1)}, f32[2,64,512]{2,1,0:T(8,128)S(1)}) custom-call(s32[32]{0:T(128)S(1)} %get-tuple-element.83.refs_0_, s32[32]{0:T(128)S(1)} %get-tuple-element.84.refs_1_, s32[32]{0:T(128)S(1)} %get-tuple-element.85.refs_2_, s32[9]{0:T(128)S(1)} %get-tuple-element.86.refs_3_, ...), custom_call_target="tpu_custom_call" | custom-call | flops 2147483648 | bytes 1048576 | tf_op jit(solution)/shard_map/products/pallas_call | solution.py:447
  88.7 1.0 collective-permute-start.26
  89.7 2.5 %collective-permute-start.27 = (f32[2,64,512]{2,1,0:T(8,128)S(1)}, f32[2,64,512]{2,1,0:T(8,128)S(1)}, u32[]{:S(2)}, u32[]{:S(2)}) collective-permute-start(f32[2,64,512]{2,1,0:T(8,128)S(1)} %get-tuple-element.140), channel_id=1, source_target_pairs={{0,4},{4,8},{8,12},{12,16},{16,20},{20,24},{24,28},{1,5},{5,9},{9,... | collective-permute-start | bytes 786440 | tf_op jit(solution)/shard_map/ppermute | solution.py:37
  92.3 1.4 %collective-permute-start.28 = (f32[2,64,512]{2,1,0:T(8,128)S(1)}, f32[2,64,512]{2,1,0:T(8,128)S(1)}, u32[]{:S(2)}, u32[]{:S(2)}) collective-permute-start(f32[2,64,512]{2,1,0:T(8,128)S(1)} %slice_add_fusion.1), channel_id=1, source_target_pairs={{0,2},{1,3},{2,0},{3,1},{4,6},{5,7},{6,4},{7,5},{8,10},{9,11},{10,... | collective-permute-start | bytes 786440 | tf_op jit(solution)/shard_map/ppermute | solution.py:31
  93.7 2.3 %products.13.refs_0_ = f32[2,64,512]{2,1,0:T(8,128)S(1)} custom-call(s32[32]{0:T(128)S(1)} %get-tuple-element.83.refs_0_, s32[32]{0:T(128)S(1)} %get-tuple-element.84.refs_1_, s32[32]{0:T(128)S(1)} %get-tuple-element.85.refs_2_, s32[9]{0:T(128)S(1)} %get-tuple-element.86.refs_3_, bf16[128,1024]{1,0:T(8,128)(2,1)S(1)} %collective-permute-done.24.refs_4_, ...), custom_call_target="tpu_custom_call" | custom-call | flops 1048576 | bytes 1048576 | tf_op jit(solution)/shard_map/products/pallas_call | solution.py:447
  95.9 2.3 %collective-permute-done.27.refs_1_ = f32[2,64,512]{2,1,0:T(8,128)S(1)} collective-permute-done((f32[2,64,512]{2,1,0:T(8,128)S(1)}, f32[2,64,512]{2,1,0:T(8,128)S(1)}, u32[]{:S(2)}, u32[]{:S(2)}) %collective-permute-start.27) | collective-permute-done | bytes 262176 | tf_op jit(solution)/shard_map/ppermute | solution.py:37
  98.3 2.4 %collective-permute-done.28.refs_3_ = f32[2,64,512]{2,1,0:T(8,128)S(1)} collective-permute-done((f32[2,64,512]{2,1,0:T(8,128)S(1)}, f32[2,64,512]{2,1,0:T(8,128)S(1)}, u32[]{:S(2)}, u32[]{:S(2)}) %collective-permute-start.28) | collective-permute-done | bytes 262176 | tf_op jit(solution)/shard_map/ppermute | solution.py:31
  100.6 1.0 scaled_gram.3
  101.6 0.1 collective-permute-start.29
  101.7 1.2 collective-permute-done.29
  102.9 1.3 %collective-permute-start.30 = (f32[64,128]{1,0:T(8,128)S(1)}, f32[64,128]{1,0:T(8,128)S(1)}, u32[]{:S(2)}, u32[]{:S(2)}) collective-permute-start(f32[64,128]{1,0:T(8,128)S(1)} %add.50), channel_id=1, source_target_pairs={{0,2},{1,3},{2,0},{3,1},{4,6},{5,7},{6,4},{7,5},{8,10},{9,11},{10,... | collective-permute-start | bytes 98312 | tf_op jit(solution)/shard_map/ppermute | solution.py:680
  104.2 4.4 %collective-permute-start.31 = (f32[64,128]{1,0:T(8,128)S(1)}, f32[64,128]{1,0:T(8,128)S(1)}, u32[]{:S(2)}, u32[]{:S(2)}) collective-permute-start(f32[64,128]{1,0:T(8,128)S(1)} %add.50), channel_id=1, source_target_pairs={{0,4},{1,5},{2,6},{3,7},{4,0},{5,1},{6,2},{7,3},{8,12},{9,13},{10,... | collective-permute-start | bytes 98312 | tf_op jit(solution)/shard_map/ppermute | solution.py:680
  108.6 1.9 %collective-permute-done.31 = f32[64,128]{1,0:T(8,128)S(1)} collective-permute-done((f32[64,128]{1,0:T(8,128)S(1)}, f32[64,128]{1,0:T(8,128)S(1)}, u32[]{:S(2)}, u32[]{:S(2)}) %collective-permute-start.31) | collective-permute-done | bytes 32800 | tf_op jit(solution)/shard_map/ppermute | solution.py:680
  110.5 2.9 %collective-permute-done.32 = f32[64,128]{1,0:T(8,128)S(1)} collective-permute-done((f32[64,128]{1,0:T(8,128)S(1)}, f32[64,128]{1,0:T(8,128)S(1)}, u32[]{:S(2)}, u32[]{:S(2)}) %collective-permute-start.32) | collective-permute-done | bytes 32800 | tf_op jit(solution)/shard_map/ppermute | solution.py:680
  113.4 0.1 collective-permute-start.33
  113.5 0.1 collective-permute-start.34
  113.6 4.3 %collective-permute-start.35 = (f32[64,128]{1,0:T(8,128)S(1)}, f32[64,128]{1,0:T(8,128)S(1)}, u32[]{:S(2)}, u32[]{:S(2)}) collective-permute-start(f32[64,128]{1,0:T(8,128)S(1)} %add_add_fusion.3), channel_id=1, source_target_pairs={{0,24},{1,25},{2,26},{3,27},{4,28},{5,29},{6,30},{7,31},{8,16},{9,... | collective-permute-start | bytes 98312 | tf_op jit(solution)/shard_map/ppermute | solution.py:680
  117.9 0.5 collective-permute-done.34
  118.4 1.7 %collective-permute-done.35 = f32[64,128]{1,0:T(8,128)S(1)} collective-permute-done((f32[64,128]{1,0:T(8,128)S(1)}, f32[64,128]{1,0:T(8,128)S(1)}, u32[]{:S(2)}, u32[]{:S(2)}) %collective-permute-start.35) | collective-permute-done | bytes 32800 | tf_op jit(solution)/shard_map/ppermute | solution.py:680
  120.1 4.9 %factors.1 = (f32[64,64]{1,0:T(8,128)S(1)}, f32[64,64]{1,0:T(8,128)S(1)}, s32[1]{0:T(128)}) custom-call(f32[64,128]{1,0:T(8,128)S(1)} %add_add_fusion.2.grams), custom_call_target="tpu_custom_call" | custom-call | flops 1073741824 | bytes 65536 | tf_op jit(solution)/shard_map/factors/pallas_call | solution.py:618
  125.7 1.1 applied.3
  (31 shorter events, 0.2 us)
Async XLA Ops:
  0.0 5.7 %copy-start = (bf16[1024,768]{1,0:T(8,128)(2,1)S(1)}, bf16[1024,768]{1,0:T(8,128)(2,1)}, u32[]{:S(2)}) copy-start(bf16[1024,768]{1,0:T(8,128)(2,1)} %refs_3_.1) | copy-start | bytes 4718596
  0.0 7.8 %copy-start.1 = (f32[64,1024]{1,0:T(8,128)S(1)}, f32[64,1024]{1,0:T(8,128)}, u32[]{:S(2)}) copy-start(f32[64,1024]{1,0:T(8,128)} %start.1) | copy-start | bytes 786436
  0.0 7.8 %copy-start.2 = (s32[2]{0:T(128)S(1)}, s32[2]{0:T(128)}, u32[]{:S(2)}) copy-start(s32[2]{0:T(128)} %count_ref.3) | copy-start | bytes 28
  0.0 8.4 %copy-start.3 = (s32[64]{0:T(128)S(1)}, s32[64]{0:T(128)}, u32[]{:S(2)}) copy-start(s32[64]{0:T(128)} %rows.1) | copy-start | bytes 772
  0.0 8.4 %copy-start.4 = (s32[64]{0:T(128)S(1)}, s32[64]{0:T(128)}, u32[]{:S(2)}) copy-start(s32[64]{0:T(128)} %cols.1) | copy-start | bytes 772
  1.3 23.2 %collective-permute-start.7 = (bf16[512,768]{1,0:T(8,128)(2,1)S(1)}, bf16[512,768]{1,0:T(8,128)(2,1)S(1)}, u32[]{:S(2)}, u32[]{:S(2)}) collective-permute-start(bf16[512,768]{1,0:T(8,128)(2,1)S(1)} %slice.18), channel_id=1, source_target_pairs={{4,0},{8,4},{12,8},{16,12},{20,16},{24,20},{28,24},{5,1},{9,5},{13... | collective-permute-start | bytes 2359304 | tf_op jit(solution)/shard_map/ppermute | solution.py:37
  2.6 22.0 %collective-permute-start.8 = (bf16[512,768]{1,0:T(8,128)(2,1)S(1)}, bf16[512,768]{1,0:T(8,128)(2,1)S(1)}, u32[]{:S(2)}, u32[]{:S(2)}) collective-permute-start(bf16[512,768]{1,0:T(8,128)(2,1)S(1)} %slice.18), channel_id=1, source_target_pairs={{0,2},{1,3},{2,0},{3,1},{4,6},{5,7},{6,4},{7,5},{8,10},{9,11},{10,... | collective-permute-start | bytes 2359304 | tf_op jit(solution)/shard_map/ppermute | solution.py:31
  5.7 21.4 %collective-permute-start.13 = (bf16[1024,768]{1,0:T(8,128)(2,1)}, bf16[1024,768]{1,0:T(8,128)(2,1)S(1)}, u32[]{:S(2)}, u32[]{:S(2)}) collective-permute-start(bf16[1024,768]{1,0:T(8,128)(2,1)} %refs_3_.1), channel_id=1, source_target_pairs={{0,1},{1,0},{2,3},{3,2},{4,5},{5,4},{6,7},{7,6},{8,9},{9,8},{10,11... | collective-permute-start | bytes 4718600 | tf_op jit(solution)/shard_map/ppermute | solution.py:31
  5.7 34.3 %collective-permute-start.14 = (bf16[512,768]{1,0:T(8,128)(2,1)S(1)}, bf16[512,768]{1,0:T(8,128)(2,1)S(1)}, u32[]{:S(2)}, u32[]{:S(2)}) collective-permute-start(bf16[512,768]{1,0:T(8,128)(2,1)S(1)} %slice.19), channel_id=1, source_target_pairs={{0,2},{1,3},{2,0},{3,1},{4,6},{5,7},{6,4},{7,5},{8,10},{9,11},{10,... | collective-permute-start | bytes 2359304 | tf_op jit(solution)/shard_map/ppermute | solution.py:31
  5.9 34.7 %collective-permute-start.9 = (bf16[512,768]{1,0:T(8,128)(2,1)S(1)}, bf16[512,768]{1,0:T(8,128)(2,1)S(1)}, u32[]{:S(2)}, u32[]{:S(2)}) collective-permute-start(bf16[512,768]{1,0:T(8,128)(2,1)S(1)} %slice.19), channel_id=1, source_target_pairs={{4,0},{8,4},{12,8},{16,12},{20,16},{24,20},{28,24},{5,1},{9,5},{13... | collective-permute-start | bytes 2359304 | tf_op jit(solution)/shard_map/ppermute | solution.py:37
  24.6 1.8 %collective-permute-start.11 = (bf16[256,768]{1,0:T(8,128)(2,1)S(1)}, bf16[256,768]{1,0:T(8,128)(2,1)S(1)}, u32[]{:S(2)}, u32[]{:S(2)}) collective-permute-start(bf16[256,768]{1,0:T(8,128)(2,1)S(1)} %get-tuple-element.150), channel_id=1, source_target_pairs={{0,1},{1,0},{2,3},{3,2},{4,5},{5,4},{6,7},{7,6},{8,9},{9,8},{10,11... | collective-permute-start | bytes 1179656 | tf_op jit(solution)/shard_map/ppermute | solution.py:31
  24.7 2.3 %collective-permute-start.12 = (bf16[256,768]{1,0:T(8,128)(2,1)S(1)}, bf16[256,768]{1,0:T(8,128)(2,1)S(1)}, u32[]{:S(2)}, u32[]{:S(2)}) collective-permute-start(bf16[256,768]{1,0:T(8,128)(2,1)S(1)} %get-tuple-element.151), channel_id=1, source_target_pairs={{0,1},{1,0},{2,3},{3,2},{4,5},{5,4},{6,7},{7,6},{8,9},{9,8},{10,11... | collective-permute-start | bytes 1179656 | tf_op jit(solution)/shard_map/ppermute | solution.py:31
  26.4 8.7 %collective-permute-start.10 = (bf16[80,1024]{1,0:T(8,128)(2,1)S(1)}, bf16[80,1024]{1,0:T(8,128)(2,1)S(1)}, u32[]{:S(2)}, u32[]{:S(2)}) collective-permute-start(bf16[80,1024]{1,0:T(8,128)(2,1)S(1)} %opening.1.refs_4_), channel_id=1, source_target_pairs={{0,1},{1,0},{2,3},{3,2},{4,5},{5,4},{6,7},{7,6},{8,9},{9,8},{10,11... | collective-permute-start | bytes 491528 | tf_op jit(solution)/shard_map/ppermute | solution.py:31
  40.6 3.8 %collective-permute-start.15 = (bf16[512,768]{1,0:T(8,128)(2,1)S(1)}, bf16[512,768]{1,0:T(8,128)(2,1)S(1)}, u32[]{:S(2)}, u32[]{:S(2)}) collective-permute-start(bf16[512,768]{1,0:T(8,128)(2,1)S(1)} %collective-permute-done.14.refs_1_), channel_id=1, source_target_pairs={{0,1},{1,0},{2,3},{3,2},{4,5},{5,4},{6,7},{7,6},{8,9},{9,8},{10,11... | collective-permute-start | bytes 2359304 | tf_op jit(solution)/shard_map/ppermute | solution.py:31
  40.6 10.3 %collective-permute-start.16 = (bf16[80,1024]{1,0:T(8,128)(2,1)S(1)}, bf16[80,1024]{1,0:T(8,128)(2,1)S(1)}, u32[]{:S(2)}, u32[]{:S(2)}) collective-permute-start(bf16[80,1024]{1,0:T(8,128)(2,1)S(1)} %opening.1.refs_4_), channel_id=1, source_target_pairs={{0,2},{1,3},{2,0},{3,1},{4,6},{5,7},{6,4},{7,5},{8,10},{9,11},{10,... | collective-permute-start | bytes 491528 | tf_op jit(solution)/shard_map/ppermute | solution.py:31
  42.3 10.4 %collective-permute-start.18 = (bf16[80,1024]{1,0:T(8,128)(2,1)S(1)}, bf16[80,1024]{1,0:T(8,128)(2,1)S(1)}, u32[]{:S(2)}, u32[]{:S(2)}) collective-permute-start(bf16[80,1024]{1,0:T(8,128)(2,1)S(1)} %opening.1.refs_4_), channel_id=1, source_target_pairs={{4,0},{8,4},{12,8},{16,12},{20,16},{24,20},{28,24},{5,1},{9,5},{13... | collective-permute-start | bytes 491528 | tf_op jit(solution)/shard_map/ppermute | solution.py:37
  50.9 1.9 %collective-permute-start.17 = (bf16[80,1024]{1,0:T(8,128)(2,1)S(1)}, bf16[80,1024]{1,0:T(8,128)(2,1)S(1)}, u32[]{:S(2)}, u32[]{:S(2)}) collective-permute-start(bf16[80,1024]{1,0:T(8,128)(2,1)S(1)} %collective-permute-done.16.refs_4_), channel_id=1, source_target_pairs={{0,1},{1,0},{2,3},{3,2},{4,5},{5,4},{6,7},{7,6},{8,9},{9,8},{10,11... | collective-permute-start | bytes 491528 | tf_op jit(solution)/shard_map/ppermute | solution.py:31
  56.0 2.5 %collective-permute-start.19 = (f32[4,72,512]{2,1,0:T(8,128)S(1)}, f32[4,72,512]{2,1,0:T(8,128)S(1)}, u32[]{:S(2)}, u32[]{:S(2)}) collective-permute-start(f32[4,72,512]{2,1,0:T(8,128)S(1)} %get-tuple-element.124), channel_id=1, source_target_pairs={{0,1},{1,0},{2,3},{3,2},{4,5},{5,4},{6,7},{7,6},{8,9},{9,8},{10,11... | collective-permute-start | bytes 1769480 | tf_op jit(solution)/shard_map/ppermute | solution.py:31
  56.9 8.0 %collective-permute-start.20 = (f32[2,72,512]{2,1,0:T(8,128)S(1)}, f32[2,72,512]{2,1,0:T(8,128)S(1)}, u32[]{:S(2)}, u32[]{:S(2)}) collective-permute-start(f32[2,72,512]{2,1,0:T(8,128)S(1)} %get-tuple-element.127), channel_id=1, source_target_pairs={{0,4},{4,8},{8,12},{12,16},{16,20},{20,24},{24,28},{1,5},{5,9},{9,... | collective-permute-start | bytes 884744 | tf_op jit(solution)/shard_map/ppermute | solution.py:37
  58.5 9.4 %collective-permute-start.21 = (f32[2,72,512]{2,1,0:T(8,128)S(1)}, f32[2,72,512]{2,1,0:T(8,128)S(1)}, u32[]{:S(2)}, u32[]{:S(2)}) collective-permute-start(f32[2,72,512]{2,1,0:T(8,128)S(1)} %slice_add_fusion), channel_id=1, source_target_pairs={{0,2},{1,3},{2,0},{3,1},{4,6},{5,7},{6,4},{7,5},{8,10},{9,11},{10,... | collective-permute-start | bytes 884744 | tf_op jit(solution)/shard_map/ppermute | solution.py:31
  68.8 1.7 %collective-permute-start.22 = (bf16[128,1024]{1,0:T(8,128)(2,1)S(1)}, bf16[128,1024]{1,0:T(8,128)(2,1)S(1)}, u32[]{:S(2)}, u32[]{:S(2)}) collective-permute-start(bf16[128,1024]{1,0:T(8,128)(2,1)S(1)} %get-tuple-element.129.refs_4_), channel_id=1, source_target_pairs={{0,1},{1,0},{2,3},{3,2},{4,5},{5,4},{6,7},{7,6},{8,9},{9,8},{10,11... | collective-permute-start | bytes 786440 | tf_op jit(solution)/shard_map/ppermute | solution.py:31
  68.9 15.0 %collective-permute-start.23 = (bf16[128,1024]{1,0:T(8,128)(2,1)S(1)}, bf16[128,1024]{1,0:T(8,128)(2,1)S(1)}, u32[]{:S(2)}, u32[]{:S(2)}) collective-permute-start(bf16[128,1024]{1,0:T(8,128)(2,1)S(1)} %get-tuple-element.129.refs_4_), channel_id=1, source_target_pairs={{4,0},{8,4},{12,8},{16,12},{20,16},{24,20},{28,24},{5,1},{9,5},{13... | collective-permute-start | bytes 786440 | tf_op jit(solution)/shard_map/ppermute | solution.py:37
  70.2 13.7 %collective-permute-start.24 = (bf16[128,1024]{1,0:T(8,128)(2,1)S(1)}, bf16[128,1024]{1,0:T(8,128)(2,1)S(1)}, u32[]{:S(2)}, u32[]{:S(2)}) collective-permute-start(bf16[128,1024]{1,0:T(8,128)(2,1)S(1)} %get-tuple-element.129.refs_4_), channel_id=1, source_target_pairs={{0,2},{1,3},{2,0},{3,1},{4,6},{5,7},{6,4},{7,5},{8,10},{9,11},{10,... | collective-permute-start | bytes 786440 | tf_op jit(solution)/shard_map/ppermute | solution.py:31
  83.9 1.5 %collective-permute-start.25 = (bf16[128,1024]{1,0:T(8,128)(2,1)S(1)}, bf16[128,1024]{1,0:T(8,128)(2,1)S(1)}, u32[]{:S(2)}, u32[]{:S(2)}) collective-permute-start(bf16[128,1024]{1,0:T(8,128)(2,1)S(1)} %collective-permute-done.24.refs_4_), channel_id=1, source_target_pairs={{0,1},{1,0},{2,3},{3,2},{4,5},{5,4},{6,7},{7,6},{8,9},{9,8},{10,11... | collective-permute-start | bytes 786440 | tf_op jit(solution)/shard_map/ppermute | solution.py:31
  88.7 3.5 %collective-permute-start.26 = (f32[4,64,512]{2,1,0:T(8,128)S(1)}, f32[4,64,512]{2,1,0:T(8,128)S(1)}, u32[]{:S(2)}, u32[]{:S(2)}) collective-permute-start(f32[4,64,512]{2,1,0:T(8,128)S(1)} %get-tuple-element.137), channel_id=1, source_target_pairs={{0,1},{1,0},{2,3},{3,2},{4,5},{5,4},{6,7},{7,6},{8,9},{9,8},{10,11... | collective-permute-start | bytes 1572872 | tf_op jit(solution)/shard_map/ppermute | solution.py:31
  89.7 8.5 %collective-permute-start.27 = (f32[2,64,512]{2,1,0:T(8,128)S(1)}, f32[2,64,512]{2,1,0:T(8,128)S(1)}, u32[]{:S(2)}, u32[]{:S(2)}) collective-permute-start(f32[2,64,512]{2,1,0:T(8,128)S(1)} %get-tuple-element.140), channel_id=1, source_target_pairs={{0,4},{4,8},{8,12},{12,16},{16,20},{20,24},{24,28},{1,5},{5,9},{9,... | collective-permute-start | bytes 786440 | tf_op jit(solution)/shard_map/ppermute | solution.py:37
  92.3 8.3 %collective-permute-start.28 = (f32[2,64,512]{2,1,0:T(8,128)S(1)}, f32[2,64,512]{2,1,0:T(8,128)S(1)}, u32[]{:S(2)}, u32[]{:S(2)}) collective-permute-start(f32[2,64,512]{2,1,0:T(8,128)S(1)} %slice_add_fusion.1), channel_id=1, source_target_pairs={{0,2},{1,3},{2,0},{3,1},{4,6},{5,7},{6,4},{7,5},{8,10},{9,11},{10,... | collective-permute-start | bytes 786440 | tf_op jit(solution)/shard_map/ppermute | solution.py:31
  101.6 1.3 %collective-permute-start.29 = (f32[64,128]{1,0:T(8,128)S(1)}, f32[64,128]{1,0:T(8,128)S(1)}, u32[]{:S(2)}, u32[]{:S(2)}) collective-permute-start(f32[64,128]{1,0:T(8,128)S(1)} %get-tuple-element.145), channel_id=1, source_target_pairs={{0,1},{1,0},{2,3},{3,2},{4,5},{5,4},{6,7},{7,6},{8,9},{9,8},{10,11... | collective-permute-start | bytes 98312 | tf_op jit(solution)/shard_map/ppermute | solution.py:680
  102.9 5.7 %collective-permute-start.30 = (f32[64,128]{1,0:T(8,128)S(1)}, f32[64,128]{1,0:T(8,128)S(1)}, u32[]{:S(2)}, u32[]{:S(2)}) collective-permute-start(f32[64,128]{1,0:T(8,128)S(1)} %add.50), channel_id=1, source_target_pairs={{0,2},{1,3},{2,0},{3,1},{4,6},{5,7},{6,4},{7,5},{8,10},{9,11},{10,... | collective-permute-start | bytes 98312 | tf_op jit(solution)/shard_map/ppermute | solution.py:680
  104.2 6.3 %collective-permute-start.31 = (f32[64,128]{1,0:T(8,128)S(1)}, f32[64,128]{1,0:T(8,128)S(1)}, u32[]{:S(2)}, u32[]{:S(2)}) collective-permute-start(f32[64,128]{1,0:T(8,128)S(1)} %add.50), channel_id=1, source_target_pairs={{0,4},{1,5},{2,6},{3,7},{4,0},{5,1},{6,2},{7,3},{8,12},{9,13},{10,... | collective-permute-start | bytes 98312 | tf_op jit(solution)/shard_map/ppermute | solution.py:680
  108.6 4.8 %collective-permute-start.32 = (f32[64,128]{1,0:T(8,128)S(1)}, f32[64,128]{1,0:T(8,128)S(1)}, u32[]{:S(2)}, u32[]{:S(2)}) collective-permute-start(f32[64,128]{1,0:T(8,128)S(1)} %add.50), channel_id=1, source_target_pairs={{0,6},{1,7},{2,4},{3,5},{4,2},{5,3},{6,0},{7,1},{8,14},{9,15},{10,... | collective-permute-start | bytes 98312 | tf_op jit(solution)/shard_map/ppermute | solution.py:680
  113.4 4.5 %collective-permute-start.33 = (f32[64,128]{1,0:T(8,128)S(1)}, f32[64,128]{1,0:T(8,128)S(1)}, u32[]{:S(2)}, u32[]{:S(2)}) collective-permute-start(f32[64,128]{1,0:T(8,128)S(1)} %add_add_fusion.3), channel_id=1, source_target_pairs={{0,8},{1,9},{2,10},{3,11},{4,12},{5,13},{6,14},{7,15},{8,0},{9,1},... | collective-permute-start | bytes 98312 | tf_op jit(solution)/shard_map/ppermute | solution.py:680
  113.5 4.9 %collective-permute-start.34 = (f32[64,128]{1,0:T(8,128)S(1)}, f32[64,128]{1,0:T(8,128)S(1)}, u32[]{:S(2)}, u32[]{:S(2)}) collective-permute-start(f32[64,128]{1,0:T(8,128)S(1)} %add_add_fusion.3), channel_id=1, source_target_pairs={{0,16},{1,17},{2,18},{3,19},{4,20},{5,21},{6,22},{7,23},{8,24},{9,... | collective-permute-start | bytes 98312 | tf_op jit(solution)/shard_map/ppermute | solution.py:680
  113.6 6.5 %collective-permute-start.35 = (f32[64,128]{1,0:T(8,128)S(1)}, f32[64,128]{1,0:T(8,128)S(1)}, u32[]{:S(2)}, u32[]{:S(2)}) collective-permute-start(f32[64,128]{1,0:T(8,128)S(1)} %add_add_fusion.3), channel_id=1, source_target_pairs={{0,24},{1,25},{2,26},{3,27},{4,28},{5,29},{6,30},{7,31},{8,16},{9,... | collective-permute-start | bytes 98312 | tf_op jit(solution)/shard_map/ppermute | solution.py:680
